TPU v7x, 32 devices: a whole 2x2x4 slice. The times are simulated.
32 devices in a mesh: ifg: 8 (over z, x), grp: 4 (over y, core).
Axes of the slice: x: 2, y: 2, z: 4, core: 2. Of those that a mesh axis runs over, the one named last changes fastest.
Arguments:
- phases: bfloat16 [1024, 4, 32768], P('ifg', 'grp'), may hold values from -6 to 6
- date_pairs: int32 [2, 1024], replicated, may hold values from 0 to 199, as said below
- pair_counts: int32 [16], replicated, may hold values from 128 to 1024, as said below
- group_ids: int32 [4, 128], P(None, 'ifg'), may hold values from 0 to 15, as said below
Outputs:
- series: float32 [4, 200, 32768], P('grp', None, 'ifg')
Inputs may be any that keep to these rules, and one draw needn't show every extreme that they name: date_pairs[0, k] < date_pairs[1, k]; the baseline date_pairs[1, k] - date_pairs[0, k] lies in 1 to 25 and never falls as k grows. `pair_counts`: each count is 128 times a power of two; some class has all 1024 interferograms and some has 128. `group_ids`: constant over each aligned run of 8 blocks of a sub-strip.
All inputs are finite; a program needn't handle non-finite values.
Results may differ from a plain program's by a relative error of at most 0.0003.
Values may be sent and summed in bfloat16 or wider, within the bound.
No kernel may reach another device: no remote copies, remote signals or barrier semaphores. Data moves between devices by JAX's collectives and lax.ppermute only.
A program may use at most 128 MiB of HBM per device.

v0:
```python
import functools

import jax
import jax.numpy as jnp
import numpy as np
from jax import lax
from jax.experimental import pallas as pl
from jax.experimental.pallas import tpu as pltpu
from jax.sharding import PartitionSpec as P

M = 200
RUN = 8
PAD = 256
SLABS = 8
DAMPING = 1.0
VMEM_BYTES = 48 * 1024 * 1024
F32 = jnp.float32
HIGHEST = lax.Precision.HIGHEST
STEADY = pl.CostEstimate(flops=10_000_000_000, bytes_accessed=30_000_000, transcendentals=0)
LITTLE = pl.CostEstimate(flops=1024, bytes_accessed=1024, transcendentals=0)
CUTS = 2
HALVES = 2
FLIGHT = 2
FIRST_SWAPS = ((0, 1), (1, 2))
SWAPS = {1: (4, 2), 2: (6, 2), 5: (8, 4), 8: (12, 2), 9: (14, 2)}
SWAP_WAITS = {5: 6, 10: 12}
RAW_STEP, RAW_WAIT = 2, 5
INVERSE_STEP = 5
FINISHED_AHEAD = 1
ME, PARTNER, NEAR, NEAR_PARTNER, INNER, FIXED = 0, 1, 2, 3, 4, 5
LANES = 128
CODE_ROWS = 16
LEVELS = 32700.0
ROUNDER = 1.5 * 2.0**23
CODES_PER_OCTAVE = 128.0
SMALLEST = 2.0**-110
CHUNK_ORDER = ((2, 3, 1, 0), (0, 2, 3, 1), (3, 1, 0, 2), (1, 0, 2, 3))
SENDS = (
    (((0, 1), (1, 0), (2, 3), (3, 2)),),
    (((0, 1), (3, 2)), ((1, 2), (2, 1))),
    (((0, 1), (1, 3), (2, 0), (3, 2)),),
)


def incidence(earlier, later, rows):
    shape = (rows, earlier.shape[1])
    date = lax.broadcasted_iota(jnp.int32, shape, 0)
    return (date == later).astype(F32) - (date == earlier).astype(F32)


def split_product(left, right):
    def halves(value):
        high = value.astype(jnp.bfloat16)
        return high, (value - high.astype(F32)).astype(jnp.bfloat16)

    left_high, left_low = halves(left)
    right_high, right_low = halves(right)
    small = jnp.dot(left_high, right_low, preferred_element_type=F32) + jnp.dot(left_low, right_high, preferred_element_type=F32)
    return jnp.dot(left_high, right_high, preferred_element_type=F32) + small


def full_product(left, right):
    return jnp.dot(left, right, precision=HIGHEST, preferred_element_type=F32)


def inverse_kernel(counts_ref, pairs_ref, *rest):
    out_ref = rest[-1]
    runs = out_ref.shape[0]
    design = incidence(pairs_ref[0:1, :], pairs_ref[1:2, :], PAD)
    pair = lax.broadcasted_iota(jnp.int32, design.shape, 1)
    contract_last = (((1,), (1,)), ((), ()))
    row = lax.broadcasted_iota(jnp.int32, (PAD, PAD), 0)
    col = lax.broadcasted_iota(jnp.int32, (PAD, PAD), 1)
    identity = (row == col).astype(F32)
    grams = []
    for run in range(runs):
        kept = jnp.where(pair < counts_ref[run], design, 0.0).astype(jnp.bfloat16)
        gram = lax.dot_general(kept, kept, contract_last, preferred_element_type=F32)
        grams.append(gram + DAMPING * identity)
    low = DAMPING
    high = 2.0 * functools.reduce(jnp.maximum, [jnp.max(gram) for gram in grams]) - DAMPING
    total, width = high + low, high - low
    scale = 2.0 * total * total - width * width
    starts = tuple((8.0 * total / scale) * identity - (8.0 / scale) * gram for gram in grams)
    needed = 18.0 * scale / (8.0 * high * low)
    steps = jnp.int32(0)
    for power in range(1, 16):
        steps += (needed > float(2**power)).astype(jnp.int32)

    def newton(product, guesses):
        products = [product(gram, guess) for gram, guess in zip(grams, guesses)]
        return tuple(2.0 * guess - product(guess, each) for guess, each in zip(guesses, products))

    full_steps = 1 + (high > 100.0).astype(jnp.int32)
    guesses = lax.fori_loop(0, steps + 1 - full_steps, lambda _, guesses: newton(split_product, guesses), starts)
    guesses = lax.fori_loop(0, full_steps, lambda _, guesses: newton(full_product, guesses), guesses)
    for run, guess in enumerate(guesses):
        out_ref[run] = guess


def invert_classes(date_pairs, run_counts, after):
    shape = (run_counts.shape[0], PAD, PAD)
    return pl.pallas_call(
        inverse_kernel,
        out_shape=jax.ShapeDtypeStruct(shape, F32),
        grid_spec=pltpu.PrefetchScalarGridSpec(
            num_scalar_prefetch=1,
            grid=(1,),
            in_specs=[pl.BlockSpec(date_pairs.shape, lambda i, c: (0, 0))] + [pl.BlockSpec(memory_space=pl.ANY)] * len(after),
            out_specs=pl.BlockSpec(shape, lambda i, c: (0, 0, 0)),
        ),
        compiler_params=pltpu.CompilerParams(vmem_limit_bytes=VMEM_BYTES),
        cost_estimate=LITTLE,
        name="invert_classes_0",
    )(run_counts, date_pairs, *after)


def sum_solve_kernel(tiles, counts_ref, pairs_ref, data_ref, inverse_ref, out_ref):
    run = pl.program_id(0) // tiles
    design = incidence(pairs_ref[0:1, :], pairs_ref[1:2, :], PAD)
    pair = lax.broadcasted_iota(jnp.int32, design.shape, 1)
    kept = jnp.where(pair < counts_ref[run], design, 0.0).astype(jnp.bfloat16)
    sums = jnp.dot(kept, data_ref[...], preferred_element_type=F32)
    out_ref[...] = jnp.dot(inverse_ref[0, :M, :], sums, precision=HIGHEST, preferred_element_type=F32)


def sum_solve(run_counts, date_pairs, received, inverse):
    runs = run_counts.shape[0]
    total_pairs, pixels = received.shape
    run_pixels = pixels // runs
    tile = run_pixels // 2
    tiles = run_pixels // tile
    return pl.pallas_call(
        functools.partial(sum_solve_kernel, tiles),
        out_shape=jax.ShapeDtypeStruct((M, pixels), F32),
        grid_spec=pltpu.PrefetchScalarGridSpec(
            num_scalar_prefetch=1,
            grid=(runs * tiles,),
            in_specs=[
                pl.BlockSpec(date_pairs.shape, lambda i, c: (0, 0)),
                pl.BlockSpec((total_pairs, tile), lambda i, c: (0, i)),
                pl.BlockSpec((1, PAD, PAD), lambda i, c: (i // tiles, 0, 0)),
            ],
            out_specs=pl.BlockSpec((M, tile), lambda i, c: (0, i)),
        ),
        compiler_params=pltpu.CompilerParams(vmem_limit_bytes=VMEM_BYTES),
        name="sum_solve",
    )(run_counts, date_pairs, received, inverse)


def coded_rows(piece):
    return M * (piece // LANES) + CODE_ROWS


def decode(coded_ref, codes_ref, lots, first):
    coded = coded_ref[...].astype(jnp.int32).astype(F32)
    values = jnp.concatenate([coded[lot * M : (lot + 1) * M, :] for lot in range(lots)], axis=1)
    codes = codes_ref[...].astype(jnp.int32).astype(F32)
    codes = jnp.concatenate([codes[first + lot : first + lot + 1, :] for lot in range(lots)], axis=1)
    return values, jnp.exp2(codes * (1.0 / CODES_PER_OCTAVE)) * (1.0 / LEVELS)


def encode(sums):
    largest = jnp.max(jnp.abs(sums), axis=0, keepdims=True)
    code = jnp.ceil(jnp.log2(jnp.maximum(largest, SMALLEST)) * CODES_PER_OCTAVE)
    scaled = (sums * (LEVELS / jnp.exp2(code * (1.0 / CODES_PER_OCTAVE))) + ROUNDER) - ROUNDER
    lots = sums.shape[1] // LANES
    return jnp.concatenate([scaled[:, lot * LANES : (lot + 1) * LANES] for lot in range(lots)], axis=0), code


def whole(values):
    return values.astype(jnp.int32).astype(jnp.int16)


def piece_count(at, layout, table, counts):
    parts, _, _, shifts = layout
    run = at % parts // CUTS
    return counts[table[shifts + at] * (parts // CUTS) + run]


def pair_sums(count, table, pairs_ref, first_ref, second_ref, members=(ME, PARTNER)):
    width = first_ref.shape[0]
    lane = lax.broadcasted_iota(jnp.int32, (1, 2 * width), 1)
    pair = jnp.where(lane < width, table[members[0]] * width + lane, table[members[1]] * width + lane - width)
    dates = pairs_ref[:, members[0] * width : (members[0] + 2) * width]
    design = incidence(dates[0:1, :], dates[1:2, :], M)
    kept = jnp.where(pair < count, design, 0.0).astype(jnp.bfloat16)
    data = jnp.concatenate([first_ref[...], second_ref[...]], axis=0)
    return jnp.dot(kept, data, preferred_element_type=F32)


def near_sums(wanted, count, table, pairs_ref, raw_refs):
    return pair_sums(jnp.where(wanted, count, 0), table, pairs_ref, *raw_refs, members=(NEAR, NEAR_PARTNER))


def step_kernel(at, layout, adds, swaps, halves, table, counts, pairs_ref, own_ref, partner_ref, *rest):
    if swaps:
        rest[-1][...] = rest[0][...]
        coded_ref, rest = rest[-2], rest[1:]
    else:
        coded_ref = rest[-1]
    count = piece_count(at, layout, table, counts)
    width = own_ref.shape[1] // halves
    lots = width // LANES
    codes = []
    for half in range(halves):
        part = pl.ds(half * width, width)
        sums = pair_sums(count, table, pairs_ref, own_ref.at[:, part], partner_ref.at[:, part])
        if adds == 1:
            rows = pl.ds(half * lots * M, lots * M)
            values, scale = decode(rest[0].at[rows, :], rest[0].at[halves * lots * M :, :], lots, half * lots)
            sums = sums + values * (scale * table[INNER].astype(F32))
        if adds == 2:
            sums = sums + near_sums(table[INNER] == 1, count, table, pairs_ref, [raw_ref.at[:, part] for raw_ref in rest[:2]])
        scaled, code = encode(sums)
        coded_ref[half * lots * M : (half + 1) * lots * M, :] = whole(scaled)
        codes += [code[:, lot * LANES : (lot + 1) * LANES] for lot in range(lots)]
    codes += [jnp.zeros((CODE_ROWS - len(codes), LANES), F32)]
    coded_ref[halves * lots * M :, :] = whole(jnp.concatenate(codes, axis=0))


def step(at, swap, layout, scalars, pairs, phases, partner, earlier, after, piece):
    partner, place_in = partner
    local_pairs = phases.shape[0]
    _, blocks, away, _ = layout
    coded_shape = (coded_rows(piece), LANES)
    in_specs = [
        pl.BlockSpec(pairs.shape, lambda i, t, c: (0, 0)),
        pl.BlockSpec((local_pairs, piece), lambda i, t, c: (0, t[blocks + at])),
        pl.BlockSpec((local_pairs, piece), lambda i, t, c: (0, place_in)),
    ]
    operands = [pairs, phases, partner]
    out_shape = [jax.ShapeDtypeStruct(coded_shape, jnp.int16)]
    out_specs = [pl.BlockSpec(coded_shape, lambda i, t, c: (0, 0))]
    if swap is not None:
        first, count = swap
        wide = piece * count
        in_specs.append(pl.BlockSpec((local_pairs, wide), lambda i, t, c: (0, t[away + first] // count)))
        operands.append(phases)
        out_shape.append(jax.ShapeDtypeStruct((local_pairs, wide), phases.dtype))
        out_specs.append(pl.BlockSpec((local_pairs, wide), lambda i, t, c: (0, 0)))
    in_specs += [pl.BlockSpec(each.shape, lambda i, t, c: (0, 0)) for each in earlier]
    operands += earlier
    in_specs += [pl.BlockSpec(memory_space=pl.ANY)] * len(after)
    results = pl.pallas_call(
        functools.partial(step_kernel, at, layout, len(earlier), swap is not None, HALVES),
        out_shape=out_shape,
        grid_spec=pltpu.PrefetchScalarGridSpec(
            num_scalar_prefetch=2,
            grid=(1,),
            in_specs=in_specs,
            out_specs=out_specs,
        ),
        compiler_params=pltpu.CompilerParams(vmem_limit_bytes=VMEM_BYTES),
        cost_estimate=STEADY,
        name=f"sum_step_{at:02d}",
    )(*scalars, *operands, *after)
    return results[0], results[1] if swap is not None else None


def coded_specs(piece, tiles, index):
    lots = piece // LANES
    return [
        pl.BlockSpec((lots // tiles * M, LANES), lambda *at: (at[index], 0)),
        pl.BlockSpec((CODE_ROWS, LANES), lambda *at: (lots * M // CODE_ROWS, 0)),
    ]


def add_arrived(sums_ref, refs, tiles):
    lots = sums_ref.shape[1] // LANES
    tile = pl.program_id(0)
    for coded_ref, codes_ref in zip(refs[::2], refs[1::2]):
        parts = [decode(coded_ref, codes_ref, lots, at * lots) for at in range(tiles)]
        scale = functools.reduce(lambda chosen, at: jnp.where(tile == at, parts[at][1], chosen), range(1, tiles), parts[0][1])
        sums_ref[...] += parts[0][0] * scale


def finish_kernel(at, layout, tiles, raw, told, table, counts, pairs_ref, own_ref, partner_ref, inverse_ref, *rest):
    first, middle, last = rest[:2], rest[2:4], rest[4:6]
    sums_ref, rest = rest[-1], rest[:-1]
    if told:
        rest[-1][...] = jnp.zeros_like(rest[-1])
        rest = rest[:-1]
    out_ref = rest[-1]
    count = piece_count(at, layout, table, counts)
    sums_ref[...] = pair_sums(count, table, pairs_ref, own_ref, partner_ref)

    @pl.when(table[INNER] == 0)
    def _():
        if raw:
            sums_ref[...] += near_sums(True, count, table, pairs_ref, first)
        else:
            add_arrived(sums_ref, first, tiles)

    @pl.when(table[INNER] == 1)
    def _():
        add_arrived(sums_ref, middle, tiles)

    add_arrived(sums_ref, last, tiles)
    out_ref[...] = split_product(inverse_ref[0, :M, :M], sums_ref[...])


def finish(at, part, layout, scalars, pairs, phases, partner, inverse, raw, arrived, series, told, pixels, piece):
    partner, place_in = partner
    local_pairs = phases.shape[0]
    blocks = layout[1]
    tiles = HALVES
    tile = piece // tiles
    in_specs = [
        pl.BlockSpec(pairs.shape, lambda i, t, c: (0, 0)),
        pl.BlockSpec((local_pairs, tile), lambda i, t, c: (0, t[blocks + at] * tiles + i)),
        pl.BlockSpec((local_pairs, tile), lambda i, t, c: (0, place_in * tiles + i)),
        pl.BlockSpec((1, PAD, PAD), lambda i, t, c: (part // CUTS, 0, 0)),
    ]
    in_specs += [pl.BlockSpec((local_pairs, tile), lambda i, t, c: (0, i))] * len(raw) + coded_specs(piece, tiles, 0) * len(arrived)
    operands = [*scalars, pairs, phases, partner, inverse, *raw] + [each for each in arrived for _ in range(2)]
    aliases = {}
    if series is not None:
        in_specs.append(pl.BlockSpec(memory_space=pl.ANY))
        aliases = {len(operands): 0}
        operands.append(series)
    out_shape = [jax.ShapeDtypeStruct((M, pixels), F32)]
    out_specs = [pl.BlockSpec((M, tile), lambda i, t, c: (0, part * tiles + i))]
    if told:
        out_shape.append(jax.ShapeDtypeStruct((8, LANES), F32))
        out_specs.append(pl.BlockSpec((8, LANES), lambda i, t, c: (0, 0)))
    return pl.pallas_call(
        functools.partial(finish_kernel, at, layout, tiles, len(raw) > 0, told),
        out_shape=out_shape,
        grid_spec=pltpu.PrefetchScalarGridSpec(
            num_scalar_prefetch=2,
            grid=(tiles,),
            in_specs=in_specs,
            out_specs=out_specs,
            scratch_shapes=[pltpu.VMEM((M, tile), F32)],
        ),
        input_output_aliases=aliases,
        compiler_params=pltpu.CompilerParams(vmem_limit_bytes=VMEM_BYTES),
        cost_estimate=LITTLE,
        name=f"finish_{part}",
    )(*operands)


def line_permutation(links):
    return [(2 * source + side, 2 * target + side) for source, target in links for side in range(2)]


def solve_by_sums(phases, date_pairs, counts_of):
    owner_count = lax.axis_size("ifg")
    line = owner_count // 2
    local_pairs, pixels = phases.shape
    owner_pixels = pixels // owner_count
    runs = counts_of(None).shape[0]
    parts = runs * CUTS
    piece = owner_pixels // parts
    steps = (line - 1) * parts
    me = lax.axis_index("ifg")

    places = np.repeat(np.array(CHUNK_ORDER), parts, axis=1)
    part_of = np.tile(np.arange(parts), line)
    rows = []
    for device in range(owner_count):
        place, side = device // 2, device % 2
        own = (places[place] * 2 + side) * parts + part_of
        away = (places[place] * 2 + 1 - side) * parts + part_of
        shift = (place - places[place]) % line
        rows.append(np.concatenate([[device, device ^ 1, device ^ 2, device ^ 3, int(0 < place < line - 1)], own, away, shift]))
    row = lax.dynamic_index_in_dim(jnp.asarray(np.stack(rows), jnp.int32), me, 0, keepdims=False)
    head, pieces = FIXED, line * parts
    layout = (parts, head, head + pieces, head + 2 * pieces)

    swap = [(i, i ^ 1) for i in range(owner_count)]
    partner_of = {}

    def swapped(away, first, count):
        here = lax.ppermute(away, "ifg", swap)
        partner_of.update({first + place: (here, place) for place in range(count)})

    place, side = me // 2, me % 2
    chunk = jnp.where(place < line // 2, 2 - 2 * place, 7 - 2 * place)

    def first_away(column, part, count, after):
        block = (chunk * 2 + column) * parts + part
        if after is not None:
            block, _ = lax.optimization_barrier((block, after))
        return lax.dynamic_slice(phases, (0, block * piece), (local_pairs, count * piece))

    away = first_away(1 - side, *FIRST_SWAPS[0], None)
    swapped(away, *FIRST_SWAPS[0])
    run_counts = counts_of(away)
    counts = [run_counts]
    for distance in range(1, line):
        links = [(i, (i + distance) % line) for i in range(line)]
        counts.append(lax.ppermute(run_counts, "ifg", line_permutation(links)))
    counts = jnp.concatenate(counts)
    raw_part = parts - 1
    near = line_permutation(SENDS[0][0])
    raw_other = lax.ppermute(first_away(1 - side, raw_part, 1, run_counts), "ifg", near)
    raw_own = lax.ppermute(first_away(side, raw_part, 1, run_counts), "ifg", near)
    swapped(first_away(1 - side, *FIRST_SWAPS[1], counts), *FIRST_SWAPS[1])
    pairs = jnp.concatenate([lax.dynamic_slice(date_pairs, (0, (me ^ at) * local_pairs), (2, local_pairs)) for at in range(4)], axis=1)
    scalars = (row, counts)

    received, sent, coded, series = {raw_part: [raw_own, raw_other]}, [raw_part], None, None

    def finished(part, series, told):
        at = steps + part
        arrived = [received[place * parts + part][-1] for place in range(1 if part == raw_part else 0, line - 1)]
        data = (layout, scalars, pairs, phases, partner_of[at], inverse, raw if part == raw_part else [], arrived)
        return finish(at, part, *data, series, told, owner_pixels, piece)

    for at in [each for each in range(steps) if each != raw_part]:
        earlier = [] if at < parts else raw if at == parts + raw_part else [received[at - parts][0]]
        after = [] if coded is None else [coded]
        after += received[sent[-FLIGHT]] if len(sent) >= FLIGHT else []
        if at in SWAP_WAITS:
            after.append(partner_of[SWAP_WAITS[at]][0])
        if at == RAW_WAIT:
            after.append(raw[1])
        if at == INVERSE_STEP:
            inverse = invert_classes(date_pairs, run_counts, [coded])
            after.append(inverse)
        if at == steps - 1:
            for part in range(FINISHED_AHEAD):
                series, told = finished(part, series, True)
                after.append(told)
        coded, away = step(at, SWAPS.get(at), layout, scalars, pairs, phases, partner_of[at], earlier, after, piece)
        received[at] = [lax.ppermute(coded, "ifg", line_permutation(links)) for links in SENDS[at // parts]]
        sent.append(at)
        if at in SWAPS:
            swapped(away, *SWAPS[at])
        if at == RAW_STEP:
            raw_other, _ = lax.optimization_barrier((raw_other, coded))
            raw = [raw_own, lax.ppermute(raw_other, "ifg", swap)]

    for part in range(FINISHED_AHEAD, parts):
        series = finished(part, series, False)[0]
    return series


def solve_by_blocks(phases, date_pairs, counts_of):
    owner_count = lax.axis_size("ifg")
    local_pairs, pixels = phases.shape
    owner_pixels = pixels // owner_count
    run_counts = counts_of(None)
    outgoing = phases.reshape(local_pairs, owner_count, owner_pixels).transpose(1, 0, 2)
    received = lax.all_to_all(outgoing, "ifg", split_axis=0, concat_axis=0, tiled=True)
    inverse = invert_classes(date_pairs, run_counts, [])
    return sum_solve(run_counts, date_pairs, received.reshape(-1, owner_pixels), inverse)


def local(phases, date_pairs, pair_counts, group_ids):
    local_pairs, _, pixels = phases.shape

    def counts_of(after):
        groups = group_ids if after is None else lax.optimization_barrier((group_ids, after))[0]
        strip_groups = lax.dynamic_index_in_dim(groups, lax.axis_index("grp"), 0, keepdims=False)[::RUN]
        chosen = strip_groups[:, None] == jnp.arange(pair_counts.shape[0], dtype=jnp.int32)
        return jnp.sum(jnp.where(chosen, pair_counts, 0), axis=1)

    line = lax.axis_size("ifg") == 2 * len(CHUNK_ORDER) and group_ids.shape[1] == 2 * RUN
    by_sums = line and 2 * local_pairs > M and local_pairs % LANES == 0 and lax.axis_size("grp") % 2 == 0
    solve = solve_by_sums if by_sums else solve_by_blocks
    return solve(phases.reshape(local_pairs, pixels), date_pairs, counts_of)[None, :, :]


def solution(mesh):
    in_specs = (P("ifg", "grp", None), P(), P(), P(None, "ifg"))
    out_specs = P("grp", None, "ifg")
    return jax.shard_map(local, mesh=mesh, in_specs=in_specs, out_specs=out_specs, check_vma=False)
```

profile of v0, /device:TPU:0, one launch (start us, length us, event | category | flops | bytes accessed | tf_op | source)
XLA Modules:
  0.0 131.1 jit_solution(12866099685714131593)
XLA Ops:
  0.0 1.0 dynamic-slice_bitcast_fusion.3
  1.1 0.8 fusion.counts_ref
  1.9 5.1 %collective-permute-start.2 = (s32[2]{0:T(128)S(1)}, s32[2]{0:T(128)S(1)}, u32[]{:S(2)}, u32[]{:S(2)}) collective-permute-start(s32[2]{0:T(128)S(1)} %fusion.counts_ref), channel_id=1, source_target_pairs={{0,24},{4,28},{8,0},{12,4},{16,8},{20,12},{24,16},{28,20},{1,25},{... | collective-permute-start | bytes 32 | tf_op jit(solution)/shard_map/ppermute | solution.py:394
  7.0 1.0 collective-permute-start
  8.1 1.5 %collective-permute-start.4 = (bf16[128,1024]{1,0:T(8,128)(2,1)S(1)}, bf16[128,1024]{1,0:T(8,128)(2,1)S(1)}, u32[]{:S(2)}, u32[]{:S(2)}) collective-permute-start(bf16[128,1024]{1,0:T(8,128)(2,1)S(1)} %dynamic-slice_bitcast_fusion.3), channel_id=1, source_target_pairs={{0,4},{4,0},{8,12},{12,8},{16,20},{20,16},{24,28},{28,24},{1,5},{5... | collective-permute-start | bytes 786440 | tf_op jit(solution)/shard_map/ppermute | solution.py:376
  9.5 1.1 dynamic-slice_bitcast_fusion.1
  10.6 2.5 %collective-permute-start.6 = (bf16[128,1024]{1,0:T(8,128)(2,1)S(1)}, bf16[128,1024]{1,0:T(8,128)(2,1)S(1)}, u32[]{:S(2)}, u32[]{:S(2)}) collective-permute-start(bf16[128,1024]{1,0:T(8,128)(2,1)S(1)} %get-tuple-element.39), channel_id=1, source_target_pairs={{0,8},{4,12},{8,0},{12,4},{16,24},{20,28},{24,16},{28,20},{1,9},{5... | collective-permute-start | bytes 786440 | tf_op jit(solution)/shard_map/ppermute | solution.py:398
  13.8 0.7 constant_dynamic-slice_fusion.3
  14.8 1.1 dynamic-slice_bitcast_fusion
  16.5 2.0 %sum_step_00.1.rest_1_ = s16[1616,128]{1,0:T(8,128)(2,1)S(1)} custom-call(s32[53]{0:T(128)S(1)} %fusion.1.table, s32[8]{0:T(128)S(1)} %pad_add_fusion.1.counts, s32[2,512]{1,0:T(2,128)S(1)} %pad_add_fusion.pairs_ref, bf16[128,32768]{1,0:T(8,128)(2,1)} %bitcast.14, bf16[128,1024]{1,0:T(8,128)(2,1)S(1)} %collective-permute-done.4.partner_ref), custom_call_target="tpu_custom_call" | custom-call | flops 10000000000 | bytes 30000000 | tf_op jit(solution)/shard_map/sum_step_00/pallas_call | solution.py:245
  18.4 2.0 %collective-permute-start.9 = (s16[1616,128]{1,0:T(8,128)(2,1)S(1)}, s16[1616,128]{1,0:T(8,128)(2,1)S(1)}, u32[]{:S(2)}, u32[]{:S(2)}) collective-permute-start(s16[1616,128]{1,0:T(8,128)(2,1)S(1)} %sum_step_00.1.rest_1_), channel_id=1, source_target_pairs={{0,8},{4,12},{8,0},{12,4},{16,24},{20,28},{24,16},{28,20},{1,9},{5... | collective-permute-start | bytes 1241096 | tf_op jit(solution)/shard_map/ppermute | solution.py:428
  20.5 5.5 %collective-permute-done.5.rest_2_.rest_0_ = bf16[128,1024]{1,0:T(8,128)(2,1)S(1)} collective-permute-done((bf16[128,1024]{1,0:T(8,128)(2,1)S(1)}, bf16[128,1024]{1,0:T(8,128)(2,1)S(1)}, u32[]{:S(2)}, u32[]{:S(2)}) %collective-permute-start.5) | collective-permute-done | bytes 262176 | tf_op jit(solution)/shard_map/ppermute | solution.py:399
  26.0 2.2 %collective-permute-done.3.partner_ref = bf16[128,2048]{1,0:T(8,128)(2,1)S(1)} collective-permute-done((bf16[128,2048]{1,0:T(8,128)(2,1)S(1)}, bf16[128,2048]{1,0:T(8,128)(2,1)S(1)}, u32[]{:S(2)}, u32[]{:S(2)}) %collective-permute-start.3) | collective-permute-done | bytes 524320 | tf_op jit(solution)/shard_map/ppermute | solution.py:376
  28.2 2.2 %sum_step_01.1 = (s16[1616,128]{1,0:T(8,128)(2,1)S(1)}, bf16[128,2048]{1,0:T(8,128)(2,1)S(1)}) custom-call(s32[53]{0:T(128)S(1)} %fusion.1.table, s32[8]{0:T(128)S(1)} %pad_add_fusion.1.counts, s32[2,512]{1,0:T(2,128)S(1)} %pad_add_fusion.pairs_ref, bf16[128,32768]{1,0:T(8,128)(2,1)} %bitcast.15, bf16[128,2048]{1,0:T(8,128)(2,1)S(1)} %collective-permute-done.3.partner_ref, ...), custom_call_target="tpu_custom_call" | custom-call | flops 10000000000 | bytes 30000000 | tf_op jit(solution)/shard_map/sum_step_01/pallas_call | solution.py:245
  30.4 1.8 %collective-permute-start.8 = (s16[1616,128]{1,0:T(8,128)(2,1)S(1)}, s16[1616,128]{1,0:T(8,128)(2,1)S(1)}, u32[]{:S(2)}, u32[]{:S(2)}) collective-permute-start(s16[1616,128]{1,0:T(8,128)(2,1)S(1)} %get-tuple-element.27.rest_1_), channel_id=1, source_target_pairs={{0,8},{4,12},{8,0},{12,4},{16,24},{20,28},{24,16},{28,20},{1,9},{5... | collective-permute-start | bytes 1241096 | tf_op jit(solution)/shard_map/ppermute | solution.py:428
  32.7 2.2 %collective-permute-done.9.rest_2_.rest_0_.rest_1_ = s16[1616,128]{1,0:T(8,128)(2,1)S(1)} collective-permute-done((s16[1616,128]{1,0:T(8,128)(2,1)S(1)}, s16[1616,128]{1,0:T(8,128)(2,1)S(1)}, u32[]{:S(2)}, u32[]{:S(2)}) %collective-permute-start.9) | collective-permute-done | bytes 413728 | tf_op jit(solution)/shard_map/ppermute | solution.py:428
  34.9 2.2 %sum_step_02.1 = (s16[1616,128]{1,0:T(8,128)(2,1)S(1)}, bf16[128,2048]{1,0:T(8,128)(2,1)S(1)}) custom-call(s32[53]{0:T(128)S(1)} %fusion.1.table, s32[8]{0:T(128)S(1)} %pad_add_fusion.1.counts, s32[2,512]{1,0:T(2,128)S(1)} %pad_add_fusion.pairs_ref, bf16[128,32768]{1,0:T(8,128)(2,1)} %bitcast.17, bf16[128,2048]{1,0:T(8,128)(2,1)S(1)} %collective-permute-done.3.partner_ref, ...), custom_call_target="tpu_custom_call" | custom-call | flops 10000000000 | bytes 30000000 | tf_op jit(solution)/shard_map/sum_step_02/pallas_call | solution.py:245
  37.0 2.1 %collective-permute-start.10 = (s16[1616,128]{1,0:T(8,128)(2,1)S(1)}, s16[1616,128]{1,0:T(8,128)(2,1)S(1)}, u32[]{:S(2)}, u32[]{:S(2)}) collective-permute-start(s16[1616,128]{1,0:T(8,128)(2,1)S(1)} %get-tuple-element.28.rest_1_), channel_id=1, source_target_pairs={{0,8},{4,12},{8,0},{12,4},{16,24},{20,28},{24,16},{28,20},{1,9},{5... | collective-permute-start | bytes 1241096 | tf_op jit(solution)/shard_map/ppermute | solution.py:428
  39.7 1.5 %collective-permute-start.11 = (bf16[128,2048]{1,0:T(8,128)(2,1)S(1)}, bf16[128,2048]{1,0:T(8,128)(2,1)S(1)}, u32[]{:S(2)}, u32[]{:S(2)}) collective-permute-start(bf16[128,2048]{1,0:T(8,128)(2,1)S(1)} %get-tuple-element.29), channel_id=1, source_target_pairs={{0,4},{4,0},{8,12},{12,8},{16,20},{20,16},{24,28},{28,24},{1,5},{5... | collective-permute-start | bytes 1572872 | tf_op jit(solution)/shard_map/ppermute | solution.py:376
  41.2 2.6 %collective-permute-done.8.rest_2_.rest_1_.rest_0_ = s16[1616,128]{1,0:T(8,128)(2,1)S(1)} collective-permute-done((s16[1616,128]{1,0:T(8,128)(2,1)S(1)}, s16[1616,128]{1,0:T(8,128)(2,1)S(1)}, u32[]{:S(2)}, u32[]{:S(2)}) %collective-permute-start.8) | collective-permute-done | bytes 413728 | tf_op jit(solution)/shard_map/ppermute | solution.py:428
  43.7 3.3 %collective-permute-done.7.partner_ref = bf16[128,2048]{1,0:T(8,128)(2,1)S(1)} collective-permute-done((bf16[128,2048]{1,0:T(8,128)(2,1)S(1)}, bf16[128,2048]{1,0:T(8,128)(2,1)S(1)}, u32[]{:S(2)}, u32[]{:S(2)}) %collective-permute-start.7) | collective-permute-done | bytes 524320 | tf_op jit(solution)/shard_map/ppermute | solution.py:376
  47.0 2.0 %sum_step_04.1.rest_0_.rest_2_ = s16[1616,128]{1,0:T(8,128)(2,1)S(1)} custom-call(s32[53]{0:T(128)S(1)} %fusion.1.table, s32[8]{0:T(128)S(1)} %pad_add_fusion.1.counts, s32[2,512]{1,0:T(2,128)S(1)} %pad_add_fusion.pairs_ref, bf16[128,32768]{1,0:T(8,128)(2,1)} %bitcast.19, bf16[128,2048]{1,0:T(8,128)(2,1)S(1)} %collective-permute-done.7.partner_ref, ...), custom_call_target="tpu_custom_call" | custom-call | flops 10000000000 | bytes 30000000 | tf_op jit(solution)/shard_map/sum_step_04/pallas_call | solution.py:245
  49.7 4.9 %collective-permute-start.15 = (s16[1616,128]{1,0:T(8,128)(2,1)S(1)}, s16[1616,128]{1,0:T(8,128)(2,1)S(1)}, u32[]{:S(2)}, u32[]{:S(2)}) collective-permute-start(s16[1616,128]{1,0:T(8,128)(2,1)S(1)} %sum_step_04.1.rest_0_.rest_2_), channel_id=1, source_target_pairs={{0,8},{4,12},{24,16},{28,20},{1,9},{5,13},{25,17},{29,21},{2,10},{... | collective-permute-start | bytes 1241096 | tf_op jit(solution)/shard_map/ppermute | solution.py:428
  54.6 6.8 %invert_classes_0.1.rest_6_.inverse_ref = f32[2,256,256]{2,1,0:T(8,128)S(1)} custom-call(s32[2]{0:T(128)S(1)} %fusion.counts_ref, s32[2,1024]{1,0:T(2,128)S(1)} %copy-done.1, s16[1616,128]{1,0:T(8,128)(2,1)S(1)} %sum_step_04.1.rest_0_.rest_2_), custom_call_target="tpu_custom_call" | custom-call | flops 1024 | bytes 1024 | tf_op jit(solution)/shard_map/invert_classes_0/pallas_call | solution.py:103
  61.4 2.4 %sum_step_05.1 = (s16[1616,128]{1,0:T(8,128)(2,1)S(1)}, bf16[128,4096]{1,0:T(8,128)(2,1)S(1)}) custom-call(s32[53]{0:T(128)S(1)} %fusion.1.table, s32[8]{0:T(128)S(1)} %pad_add_fusion.1.counts, s32[2,512]{1,0:T(2,128)S(1)} %pad_add_fusion.pairs_ref, bf16[128,32768]{1,0:T(8,128)(2,1)} %bitcast.20, bf16[128,2048]{1,0:T(8,128)(2,1)S(1)} %collective-permute-done.7.partner_ref, ...), custom_call_target="tpu_custom_call" | custom-call | flops 10000000000 | bytes 30000000 | tf_op jit(solution)/shard_map/sum_step_05/pallas_call | solution.py:245
  64.6 3.9 %collective-permute-start.14 = (s16[1616,128]{1,0:T(8,128)(2,1)S(1)}, s16[1616,128]{1,0:T(8,128)(2,1)S(1)}, u32[]{:S(2)}, u32[]{:S(2)}) collective-permute-start(s16[1616,128]{1,0:T(8,128)(2,1)S(1)} %get-tuple-element.32.rest_1_), channel_id=1, source_target_pairs={{0,8},{4,12},{24,16},{28,20},{1,9},{5,13},{25,17},{29,21},{2,10},{... | collective-permute-start | bytes 1241096 | tf_op jit(solution)/shard_map/ppermute | solution.py:428
  68.8 2.0 %sum_step_06.1.rest_2_ = s16[1616,128]{1,0:T(8,128)(2,1)S(1)} custom-call(s32[53]{0:T(128)S(1)} %fusion.1.table, s32[8]{0:T(128)S(1)} %pad_add_fusion.1.counts, s32[2,512]{1,0:T(2,128)S(1)} %pad_add_fusion.pairs_ref, bf16[128,32768]{1,0:T(8,128)(2,1)} %bitcast.22, bf16[128,2048]{1,0:T(8,128)(2,1)S(1)} %collective-permute-done.11.rest_4_.partner_ref, ...), custom_call_target="tpu_custom_call" | custom-call | flops 10000000000 | bytes 30000000 | tf_op jit(solution)/shard_map/sum_step_06/pallas_call | solution.py:245
  71.5 3.5 %collective-permute-start.18 = (s16[1616,128]{1,0:T(8,128)(2,1)S(1)}, s16[1616,128]{1,0:T(8,128)(2,1)S(1)}, u32[]{:S(2)}, u32[]{:S(2)}) collective-permute-start(s16[1616,128]{1,0:T(8,128)(2,1)S(1)} %sum_step_06.1.rest_2_), channel_id=1, source_target_pairs={{0,8},{4,12},{24,16},{28,20},{1,9},{5,13},{25,17},{29,21},{2,10},{... | collective-permute-start | bytes 1241096 | tf_op jit(solution)/shard_map/ppermute | solution.py:428
  75.0 2.9 %collective-permute-done.14.rest_3_.rest_1_ = s16[1616,128]{1,0:T(8,128)(2,1)S(1)} collective-permute-done((s16[1616,128]{1,0:T(8,128)(2,1)S(1)}, s16[1616,128]{1,0:T(8,128)(2,1)S(1)}, u32[]{:S(2)}, u32[]{:S(2)}) %collective-permute-start.14) | collective-permute-done | bytes 413728 | tf_op jit(solution)/shard_map/ppermute | solution.py:428
  77.9 2.0 %sum_step_07.1.rest_2_ = s16[1616,128]{1,0:T(8,128)(2,1)S(1)} custom-call(s32[53]{0:T(128)S(1)} %fusion.1.table, s32[8]{0:T(128)S(1)} %pad_add_fusion.1.counts, s32[2,512]{1,0:T(2,128)S(1)} %pad_add_fusion.pairs_ref, bf16[128,32768]{1,0:T(8,128)(2,1)} %bitcast.23, bf16[128,2048]{1,0:T(8,128)(2,1)S(1)} %collective-permute-done.11.rest_4_.partner_ref, ...), custom_call_target="tpu_custom_call" | custom-call | flops 10000000000 | bytes 30000000 | tf_op jit(solution)/shard_map/sum_step_07/pallas_call | solution.py:245
  80.6 5.6 %collective-permute-start.20 = (s16[1616,128]{1,0:T(8,128)(2,1)S(1)}, s16[1616,128]{1,0:T(8,128)(2,1)S(1)}, u32[]{:S(2)}, u32[]{:S(2)}) collective-permute-start(s16[1616,128]{1,0:T(8,128)(2,1)S(1)} %sum_step_07.1.rest_2_), channel_id=1, source_target_pairs={{0,8},{4,12},{24,16},{28,20},{1,9},{5,13},{25,17},{29,21},{2,10},{... | collective-permute-start | bytes 1241096 | tf_op jit(solution)/shard_map/ppermute | solution.py:428
  86.8 2.8 %collective-permute-done.13.partner_ref = bf16[128,4096]{1,0:T(8,128)(2,1)S(1)} collective-permute-done((bf16[128,4096]{1,0:T(8,128)(2,1)S(1)}, bf16[128,4096]{1,0:T(8,128)(2,1)S(1)}, u32[]{:S(2)}, u32[]{:S(2)}) %collective-permute-start.13) | collective-permute-done | bytes 1048608 | tf_op jit(solution)/shard_map/ppermute | solution.py:376
  89.5 2.2 %sum_step_08.1 = (s16[1616,128]{1,0:T(8,128)(2,1)S(1)}, bf16[128,2048]{1,0:T(8,128)(2,1)S(1)}) custom-call(s32[53]{0:T(128)S(1)} %fusion.1.table, s32[8]{0:T(128)S(1)} %pad_add_fusion.1.counts, s32[2,512]{1,0:T(2,128)S(1)} %pad_add_fusion.pairs_ref, bf16[128,32768]{1,0:T(8,128)(2,1)} %bitcast.24, bf16[128,4096]{1,0:T(8,128)(2,1)S(1)} %collective-permute-done.13.partner_ref, ...), custom_call_target="tpu_custom_call" | custom-call | flops 10000000000 | bytes 30000000 | tf_op jit(solution)/shard_map/sum_step_08/pallas_call | solution.py:245
  92.1 4.2 %collective-permute-done.20.rest_3_.rest_0_ = s16[1616,128]{1,0:T(8,128)(2,1)S(1)} collective-permute-done((s16[1616,128]{1,0:T(8,128)(2,1)S(1)}, s16[1616,128]{1,0:T(8,128)(2,1)S(1)}, u32[]{:S(2)}, u32[]{:S(2)}) %collective-permute-start.20) | collective-permute-done | bytes 413728 | tf_op jit(solution)/shard_map/ppermute | solution.py:428
  96.2 2.2 %sum_step_09.1 = (s16[1616,128]{1,0:T(8,128)(2,1)S(1)}, bf16[128,2048]{1,0:T(8,128)(2,1)S(1)}) custom-call(s32[53]{0:T(128)S(1)} %fusion.1.table, s32[8]{0:T(128)S(1)} %pad_add_fusion.1.counts, s32[2,512]{1,0:T(2,128)S(1)} %pad_add_fusion.pairs_ref, bf16[128,32768]{1,0:T(8,128)(2,1)} %bitcast.26, bf16[128,4096]{1,0:T(8,128)(2,1)S(1)} %collective-permute-done.13.partner_ref, ...), custom_call_target="tpu_custom_call" | custom-call | flops 10000000000 | bytes 30000000 | tf_op jit(solution)/shard_map/sum_step_09/pallas_call | solution.py:245
  98.5 2.5 %collective-permute-start.25 = (s16[1616,128]{1,0:T(8,128)(2,1)S(1)}, s16[1616,128]{1,0:T(8,128)(2,1)S(1)}, u32[]{:S(2)}, u32[]{:S(2)}) collective-permute-start(s16[1616,128]{1,0:T(8,128)(2,1)S(1)} %get-tuple-element.35.rest_1_), channel_id=1, source_target_pairs={{0,8},{4,12},{8,24},{12,28},{16,0},{20,4},{24,16},{28,20},{1,9},{5... | collective-permute-start | bytes 1241096 | tf_op jit(solution)/shard_map/ppermute | solution.py:428
  101.0 4.2 %collective-permute-done.23.rest_2_.rest_4_.rest_5_ = s16[1616,128]{1,0:T(8,128)(2,1)S(1)} collective-permute-done((s16[1616,128]{1,0:T(8,128)(2,1)S(1)}, s16[1616,128]{1,0:T(8,128)(2,1)S(1)}, u32[]{:S(2)}, u32[]{:S(2)}) %collective-permute-start.23) | collective-permute-done | bytes 413728 | tf_op jit(solution)/shard_map/ppermute | solution.py:428
  105.8 2.0 %sum_step_10.1.rest_1_ = s16[1616,128]{1,0:T(8,128)(2,1)S(1)} custom-call(s32[53]{0:T(128)S(1)} %fusion.1.table, s32[8]{0:T(128)S(1)} %pad_add_fusion.1.counts, s32[2,512]{1,0:T(2,128)S(1)} %pad_add_fusion.pairs_ref, bf16[128,32768]{1,0:T(8,128)(2,1)} %bitcast.28, bf16[128,4096]{1,0:T(8,128)(2,1)S(1)} %collective-permute-done.13.partner_ref, ...), custom_call_target="tpu_custom_call" | custom-call | flops 10000000000 | bytes 30000000 | tf_op jit(solution)/shard_map/sum_step_10/pallas_call | solution.py:245
  107.8 1.8 %collective-permute-start.27 = (s16[1616,128]{1,0:T(8,128)(2,1)S(1)}, s16[1616,128]{1,0:T(8,128)(2,1)S(1)}, u32[]{:S(2)}, u32[]{:S(2)}) collective-permute-start(s16[1616,128]{1,0:T(8,128)(2,1)S(1)} %sum_step_10.1.rest_1_), channel_id=1, source_target_pairs={{0,8},{4,12},{8,24},{12,28},{16,0},{20,4},{24,16},{28,20},{1,9},{5... | collective-permute-start | bytes 1241096 | tf_op jit(solution)/shard_map/ppermute | solution.py:428
  109.7 3.6 %finish_0.1 = (f32[200,4096]{1,0:T(8,128)}, f32[8,128]{1,0:T(8,128)S(1)}) custom-call(s32[53]{0:T(128)S(1)} %fusion.1.table, s32[8]{0:T(128)S(1)} %pad_add_fusion.1.counts, s32[2,512]{1,0:T(2,128)S(1)} %pad_add_fusion.pairs_ref, bf16[128,32768]{1,0:T(8,128)(2,1)} %bitcast.29, bf16[128,2048]{1,0:T(8,128)(2,1)S(1)} %collective-permute-done.24.rest_3_.partner_ref, ...), custom_call_target="tpu_custom_call" | custom-call | flops 1024 | bytes 1024 | tf_op jit(solution)/shard_map/finish_0/pallas_call | solution.py:327
  113.2 0.8 collective-permute-done.25.rest_2_.rest_4_.rest_5_
  114.0 2.0 %sum_step_11.1 = s16[1616,128]{1,0:T(8,128)(2,1)S(1)} custom-call(s32[53]{0:T(128)S(1)} %fusion.1.table, s32[8]{0:T(128)S(1)} %pad_add_fusion.1.counts, s32[2,512]{1,0:T(2,128)S(1)} %pad_add_fusion.pairs_ref, bf16[128,32768]{1,0:T(8,128)(2,1)} %bitcast.30, bf16[128,4096]{1,0:T(8,128)(2,1)S(1)} %collective-permute-done.13.partner_ref, ...), custom_call_target="tpu_custom_call" | custom-call | flops 10000000000 | bytes 30000000 | tf_op jit(solution)/shard_map/sum_step_11/pallas_call | solution.py:245
  116.0 2.5 %collective-permute-start.26 = (s16[1616,128]{1,0:T(8,128)(2,1)S(1)}, s16[1616,128]{1,0:T(8,128)(2,1)S(1)}, u32[]{:S(2)}, u32[]{:S(2)}) collective-permute-start(s16[1616,128]{1,0:T(8,128)(2,1)S(1)} %sum_step_11.1), channel_id=1, source_target_pairs={{0,8},{4,12},{8,24},{12,28},{16,0},{20,4},{24,16},{28,20},{1,9},{5... | collective-permute-start | bytes 1241096 | tf_op jit(solution)/shard_map/ppermute | solution.py:428
  118.5 3.5 %finish_1.1.rest_6_ = f32[200,4096]{1,0:T(8,128)} custom-call(s32[53]{0:T(128)S(1)} %fusion.1.table, s32[8]{0:T(128)S(1)} %pad_add_fusion.1.counts, s32[2,512]{1,0:T(2,128)S(1)} %pad_add_fusion.pairs_ref, bf16[128,32768]{1,0:T(8,128)(2,1)} %bitcast.31, ...), custom_call_target="tpu_custom_call", output_to_operand_aliasing={{}: (12, {})} | custom-call | flops 1024 | bytes 1024 | tf_op jit(solution)/shard_map/finish_1/pallas_call | solution.py:327
  122.1 0.7 collective-permute-done.27.rest_4_.rest_5_
  122.8 3.6 %finish_2.1.rest_6_ = f32[200,4096]{1,0:T(8,128)} custom-call(s32[53]{0:T(128)S(1)} %fusion.1.table, s32[8]{0:T(128)S(1)} %pad_add_fusion.1.counts, s32[2,512]{1,0:T(2,128)S(1)} %pad_add_fusion.pairs_ref, bf16[128,32768]{1,0:T(8,128)(2,1)} %bitcast.32, bf16[128,2048]{1,0:T(8,128)(2,1)S(1)} %collective-permute-done.22.partner_ref, ...), custom_call_target="tpu_custom_call", output_to_operand_aliasing={{}: (12, {})} | custom-call | flops 1024 | bytes 1024 | tf_op jit(solution)/shard_map/finish_2/pallas_call | solution.py:327
  126.3 0.9 collective-permute-done.26.rest_4_.rest_5_
  127.2 3.9 %finish_3.1 = f32[200,4096]{1,0:T(8,128)} custom-call(s32[53]{0:T(128)S(1)} %fusion.1.table, s32[8]{0:T(128)S(1)} %pad_add_fusion.1.counts, s32[2,512]{1,0:T(2,128)S(1)} %pad_add_fusion.pairs_ref, bf16[128,32768]{1,0:T(8,128)(2,1)} %bitcast.33, bf16[128,2048]{1,0:T(8,128)(2,1)S(1)} %collective-permute-done.22.partner_ref, ...), custom_call_target="tpu_custom_call", output_to_operand_aliasing={{}: (12, {})} | custom-call | flops 1024 | bytes 1024 | tf_op jit(solution)/shard_map/finish_3/pallas_call | solution.py:327
  (38 shorter events, 7.2 us)
Async XLA Ops:
  0.0 1.0 copy-start
  1.9 12.6 %collective-permute-start.2 = (s32[2]{0:T(128)S(1)}, s32[2]{0:T(128)S(1)}, u32[]{:S(2)}, u32[]{:S(2)}) collective-permute-start(s32[2]{0:T(128)S(1)} %fusion.counts_ref), channel_id=1, source_target_pairs={{0,24},{4,28},{8,0},{12,4},{16,8},{20,12},{24,16},{28,20},{1,25},{... | collective-permute-start | bytes 32 | tf_op jit(solution)/shard_map/ppermute | solution.py:394
  7.0 7.7 %collective-permute-start.1 = (s32[2]{0:T(128)S(1)}, s32[2]{0:T(128)S(1)}, u32[]{:S(2)}, u32[]{:S(2)}) collective-permute-start(s32[2]{0:T(128)S(1)} %fusion.counts_ref), channel_id=1, source_target_pairs={{0,16},{4,20},{8,24},{12,28},{16,0},{20,4},{24,8},{28,12},{1,17},{... | collective-permute-start | bytes 32 | tf_op jit(solution)/shard_map/ppermute | solution.py:394
  7.0 7.7 %collective-permute-start = (s32[2]{0:T(128)S(1)}, s32[2]{0:T(128)S(1)}, u32[]{:S(2)}, u32[]{:S(2)}) collective-permute-start(s32[2]{0:T(128)S(1)} %fusion.counts_ref), channel_id=1, source_target_pairs={{0,8},{4,12},{8,16},{12,20},{16,24},{20,28},{24,0},{28,4},{1,9},{5... | collective-permute-start | bytes 32 | tf_op jit(solution)/shard_map/ppermute | solution.py:394
  8.1 8.4 %collective-permute-start.4 = (bf16[128,1024]{1,0:T(8,128)(2,1)S(1)}, bf16[128,1024]{1,0:T(8,128)(2,1)S(1)}, u32[]{:S(2)}, u32[]{:S(2)}) collective-permute-start(bf16[128,1024]{1,0:T(8,128)(2,1)S(1)} %dynamic-slice_bitcast_fusion.3), channel_id=1, source_target_pairs={{0,4},{4,0},{8,12},{12,8},{16,20},{20,16},{24,28},{28,24},{1,5},{5... | collective-permute-start | bytes 786440 | tf_op jit(solution)/shard_map/ppermute | solution.py:376
  10.6 9.9 %collective-permute-start.6 = (bf16[128,1024]{1,0:T(8,128)(2,1)S(1)}, bf16[128,1024]{1,0:T(8,128)(2,1)S(1)}, u32[]{:S(2)}, u32[]{:S(2)}) collective-permute-start(bf16[128,1024]{1,0:T(8,128)(2,1)S(1)} %get-tuple-element.39), channel_id=1, source_target_pairs={{0,8},{4,12},{8,0},{12,4},{16,24},{20,28},{24,16},{28,20},{1,9},{5... | collective-permute-start | bytes 786440 | tf_op jit(solution)/shard_map/ppermute | solution.py:398
  14.6 11.4 %collective-permute-start.5 = (bf16[128,1024]{1,0:T(8,128)(2,1)S(1)}, bf16[128,1024]{1,0:T(8,128)(2,1)S(1)}, u32[]{:S(2)}, u32[]{:S(2)}) collective-permute-start(bf16[128,1024]{1,0:T(8,128)(2,1)S(1)} %get-tuple-element.40), channel_id=1, source_target_pairs={{0,8},{4,12},{8,0},{12,4},{16,24},{20,28},{24,16},{28,20},{1,9},{5... | collective-permute-start | bytes 786440 | tf_op jit(solution)/shard_map/ppermute | solution.py:399
  15.9 12.3 %collective-permute-start.3 = (bf16[128,2048]{1,0:T(8,128)(2,1)S(1)}, bf16[128,2048]{1,0:T(8,128)(2,1)S(1)}, u32[]{:S(2)}, u32[]{:S(2)}) collective-permute-start(bf16[128,2048]{1,0:T(8,128)(2,1)S(1)} %dynamic-slice_bitcast_fusion), channel_id=1, source_target_pairs={{0,4},{4,0},{8,12},{12,8},{16,20},{20,16},{24,28},{28,24},{1,5},{5... | collective-permute-start | bytes 1572872 | tf_op jit(solution)/shard_map/ppermute | solution.py:376
  18.4 16.4 %collective-permute-start.9 = (s16[1616,128]{1,0:T(8,128)(2,1)S(1)}, s16[1616,128]{1,0:T(8,128)(2,1)S(1)}, u32[]{:S(2)}, u32[]{:S(2)}) collective-permute-start(s16[1616,128]{1,0:T(8,128)(2,1)S(1)} %sum_step_00.1.rest_1_), channel_id=1, source_target_pairs={{0,8},{4,12},{8,0},{12,4},{16,24},{20,28},{24,16},{28,20},{1,9},{5... | collective-permute-start | bytes 1241096 | tf_op jit(solution)/shard_map/ppermute | solution.py:428
  30.4 13.4 %collective-permute-start.8 = (s16[1616,128]{1,0:T(8,128)(2,1)S(1)}, s16[1616,128]{1,0:T(8,128)(2,1)S(1)}, u32[]{:S(2)}, u32[]{:S(2)}) collective-permute-start(s16[1616,128]{1,0:T(8,128)(2,1)S(1)} %get-tuple-element.27.rest_1_), channel_id=1, source_target_pairs={{0,8},{4,12},{8,0},{12,4},{16,24},{20,28},{24,16},{28,20},{1,9},{5... | collective-permute-start | bytes 1241096 | tf_op jit(solution)/shard_map/ppermute | solution.py:428
  32.1 14.9 %collective-permute-start.7 = (bf16[128,2048]{1,0:T(8,128)(2,1)S(1)}, bf16[128,2048]{1,0:T(8,128)(2,1)S(1)}, u32[]{:S(2)}, u32[]{:S(2)}) collective-permute-start(bf16[128,2048]{1,0:T(8,128)(2,1)S(1)} %get-tuple-element.26), channel_id=1, source_target_pairs={{0,4},{4,0},{8,12},{12,8},{16,20},{20,16},{24,28},{28,24},{1,5},{5... | collective-permute-start | bytes 1572872 | tf_op jit(solution)/shard_map/ppermute | solution.py:376
  37.0 24.4 %collective-permute-start.10 = (s16[1616,128]{1,0:T(8,128)(2,1)S(1)}, s16[1616,128]{1,0:T(8,128)(2,1)S(1)}, u32[]{:S(2)}, u32[]{:S(2)}) collective-permute-start(s16[1616,128]{1,0:T(8,128)(2,1)S(1)} %get-tuple-element.28.rest_1_), channel_id=1, source_target_pairs={{0,8},{4,12},{8,0},{12,4},{16,24},{20,28},{24,16},{28,20},{1,9},{5... | collective-permute-start | bytes 1241096 | tf_op jit(solution)/shard_map/ppermute | solution.py:428
  39.1 22.3 %collective-permute-start.12 = (bf16[128,1024]{1,0:T(8,128)(2,1)S(1)}, bf16[128,1024]{1,0:T(8,128)(2,1)S(1)}, u32[]{:S(2)}, u32[]{:S(2)}) collective-permute-start(bf16[128,1024]{1,0:T(8,128)(2,1)S(1)} %collective-permute-done.6.rest_3_), channel_id=1, source_target_pairs={{0,4},{4,0},{8,12},{12,8},{16,20},{20,16},{24,28},{28,24},{1,5},{5... | collective-permute-start | bytes 786440 | tf_op jit(solution)/shard_map/ppermute | solution.py:434
  39.7 15.0 %copy-start.1 = (s32[2,1024]{1,0:T(2,128)S(1)}, s32[2,1024]{1,0:T(2,128)}, u32[]{:S(2)}) copy-start(s32[2,1024]{1,0:T(2,128)} %pairs_ref.1) | copy-start | bytes 24580
  39.7 21.8 %collective-permute-start.11 = (bf16[128,2048]{1,0:T(8,128)(2,1)S(1)}, bf16[128,2048]{1,0:T(8,128)(2,1)S(1)}, u32[]{:S(2)}, u32[]{:S(2)}) collective-permute-start(bf16[128,2048]{1,0:T(8,128)(2,1)S(1)} %get-tuple-element.29), channel_id=1, source_target_pairs={{0,4},{4,0},{8,12},{12,8},{16,20},{20,16},{24,28},{28,24},{1,5},{5... | collective-permute-start | bytes 1572872 | tf_op jit(solution)/shard_map/ppermute | solution.py:376
  49.0 19.8 %collective-permute-start.16 = (s16[1616,128]{1,0:T(8,128)(2,1)S(1)}, s16[1616,128]{1,0:T(8,128)(2,1)S(1)}, u32[]{:S(2)}, u32[]{:S(2)}) collective-permute-start(s16[1616,128]{1,0:T(8,128)(2,1)S(1)} %sum_step_04.1.rest_0_.rest_2_), channel_id=1, source_target_pairs={{8,16},{12,20},{16,8},{20,12},{9,17},{13,21},{17,9},{21,13},{10,18... | collective-permute-start | bytes 1241096 | tf_op jit(solution)/shard_map/ppermute | solution.py:428
  49.7 19.1 %collective-permute-start.15 = (s16[1616,128]{1,0:T(8,128)(2,1)S(1)}, s16[1616,128]{1,0:T(8,128)(2,1)S(1)}, u32[]{:S(2)}, u32[]{:S(2)}) collective-permute-start(s16[1616,128]{1,0:T(8,128)(2,1)S(1)} %sum_step_04.1.rest_0_.rest_2_), channel_id=1, source_target_pairs={{0,8},{4,12},{24,16},{28,20},{1,9},{5,13},{25,17},{29,21},{2,10},{... | collective-permute-start | bytes 1241096 | tf_op jit(solution)/shard_map/ppermute | solution.py:428
  63.9 11.1 %collective-permute-start.17 = (s16[1616,128]{1,0:T(8,128)(2,1)S(1)}, s16[1616,128]{1,0:T(8,128)(2,1)S(1)}, u32[]{:S(2)}, u32[]{:S(2)}) collective-permute-start(s16[1616,128]{1,0:T(8,128)(2,1)S(1)} %get-tuple-element.32.rest_1_), channel_id=1, source_target_pairs={{8,16},{12,20},{16,8},{20,12},{9,17},{13,21},{17,9},{21,13},{10,18... | collective-permute-start | bytes 1241096 | tf_op jit(solution)/shard_map/ppermute | solution.py:428
  64.6 13.3 %collective-permute-start.14 = (s16[1616,128]{1,0:T(8,128)(2,1)S(1)}, s16[1616,128]{1,0:T(8,128)(2,1)S(1)}, u32[]{:S(2)}, u32[]{:S(2)}) collective-permute-start(s16[1616,128]{1,0:T(8,128)(2,1)S(1)} %get-tuple-element.32.rest_1_), channel_id=1, source_target_pairs={{0,8},{4,12},{24,16},{28,20},{1,9},{5,13},{25,17},{29,21},{2,10},{... | collective-permute-start | bytes 1241096 | tf_op jit(solution)/shard_map/ppermute | solution.py:428
  68.5 21.1 %collective-permute-start.13 = (bf16[128,4096]{1,0:T(8,128)(2,1)S(1)}, bf16[128,4096]{1,0:T(8,128)(2,1)S(1)}, u32[]{:S(2)}, u32[]{:S(2)}) collective-permute-start(bf16[128,4096]{1,0:T(8,128)(2,1)S(1)} %get-tuple-element.31), channel_id=1, source_target_pairs={{0,4},{4,0},{8,12},{12,8},{16,20},{20,16},{24,28},{28,24},{1,5},{5... | collective-permute-start | bytes 3145736 | tf_op jit(solution)/shard_map/ppermute | solution.py:376
  70.8 15.5 %collective-permute-start.19 = (s16[1616,128]{1,0:T(8,128)(2,1)S(1)}, s16[1616,128]{1,0:T(8,128)(2,1)S(1)}, u32[]{:S(2)}, u32[]{:S(2)}) collective-permute-start(s16[1616,128]{1,0:T(8,128)(2,1)S(1)} %sum_step_06.1.rest_2_), channel_id=1, source_target_pairs={{8,16},{12,20},{16,8},{20,12},{9,17},{13,21},{17,9},{21,13},{10,18... | collective-permute-start | bytes 1241096 | tf_op jit(solution)/shard_map/ppermute | solution.py:428
  71.5 15.3 %collective-permute-start.18 = (s16[1616,128]{1,0:T(8,128)(2,1)S(1)}, s16[1616,128]{1,0:T(8,128)(2,1)S(1)}, u32[]{:S(2)}, u32[]{:S(2)}) collective-permute-start(s16[1616,128]{1,0:T(8,128)(2,1)S(1)} %sum_step_06.1.rest_2_), channel_id=1, source_target_pairs={{0,8},{4,12},{24,16},{28,20},{1,9},{5,13},{25,17},{29,21},{2,10},{... | collective-permute-start | bytes 1241096 | tf_op jit(solution)/shard_map/ppermute | solution.py:428
  79.9 12.2 %collective-permute-start.21 = (s16[1616,128]{1,0:T(8,128)(2,1)S(1)}, s16[1616,128]{1,0:T(8,128)(2,1)S(1)}, u32[]{:S(2)}, u32[]{:S(2)}) collective-permute-start(s16[1616,128]{1,0:T(8,128)(2,1)S(1)} %sum_step_07.1.rest_2_), channel_id=1, source_target_pairs={{8,16},{12,20},{16,8},{20,12},{9,17},{13,21},{17,9},{21,13},{10,18... | collective-permute-start | bytes 1241096 | tf_op jit(solution)/shard_map/ppermute | solution.py:428
  80.6 15.6 %collective-permute-start.20 = (s16[1616,128]{1,0:T(8,128)(2,1)S(1)}, s16[1616,128]{1,0:T(8,128)(2,1)S(1)}, u32[]{:S(2)}, u32[]{:S(2)}) collective-permute-start(s16[1616,128]{1,0:T(8,128)(2,1)S(1)} %sum_step_07.1.rest_2_), channel_id=1, source_target_pairs={{0,8},{4,12},{24,16},{28,20},{1,9},{5,13},{25,17},{29,21},{2,10},{... | collective-permute-start | bytes 1241096 | tf_op jit(solution)/shard_map/ppermute | solution.py:428
  91.7 13.4 %collective-permute-start.23 = (s16[1616,128]{1,0:T(8,128)(2,1)S(1)}, s16[1616,128]{1,0:T(8,128)(2,1)S(1)}, u32[]{:S(2)}, u32[]{:S(2)}) collective-permute-start(s16[1616,128]{1,0:T(8,128)(2,1)S(1)} %get-tuple-element.33.rest_2_), channel_id=1, source_target_pairs={{0,8},{4,12},{8,24},{12,28},{16,0},{20,4},{24,16},{28,20},{1,9},{5... | collective-permute-start | bytes 1241096 | tf_op jit(solution)/shard_map/ppermute | solution.py:428
  91.8 14.0 %collective-permute-start.24 = (bf16[128,2048]{1,0:T(8,128)(2,1)S(1)}, bf16[128,2048]{1,0:T(8,128)(2,1)S(1)}, u32[]{:S(2)}, u32[]{:S(2)}) collective-permute-start(bf16[128,2048]{1,0:T(8,128)(2,1)S(1)} %get-tuple-element.36), channel_id=1, source_target_pairs={{0,4},{4,0},{8,12},{12,8},{16,20},{20,16},{24,28},{28,24},{1,5},{5... | collective-permute-start | bytes 1572872 | tf_op jit(solution)/shard_map/ppermute | solution.py:376
  98.5 15.6 %collective-permute-start.25 = (s16[1616,128]{1,0:T(8,128)(2,1)S(1)}, s16[1616,128]{1,0:T(8,128)(2,1)S(1)}, u32[]{:S(2)}, u32[]{:S(2)}) collective-permute-start(s16[1616,128]{1,0:T(8,128)(2,1)S(1)} %get-tuple-element.35.rest_1_), channel_id=1, source_target_pairs={{0,8},{4,12},{8,24},{12,28},{16,0},{20,4},{24,16},{28,20},{1,9},{5... | collective-permute-start | bytes 1241096 | tf_op jit(solution)/shard_map/ppermute | solution.py:428
  101.0 21.1 %collective-permute-start.22 = (bf16[128,2048]{1,0:T(8,128)(2,1)S(1)}, bf16[128,2048]{1,0:T(8,128)(2,1)S(1)}, u32[]{:S(2)}, u32[]{:S(2)}) collective-permute-start(bf16[128,2048]{1,0:T(8,128)(2,1)S(1)} %get-tuple-element.34), channel_id=1, source_target_pairs={{0,4},{4,0},{8,12},{12,8},{16,20},{20,16},{24,28},{28,24},{1,5},{5... | collective-permute-start | bytes 1572872 | tf_op jit(solution)/shard_map/ppermute | solution.py:376
  107.8 14.9 %collective-permute-start.27 = (s16[1616,128]{1,0:T(8,128)(2,1)S(1)}, s16[1616,128]{1,0:T(8,128)(2,1)S(1)}, u32[]{:S(2)}, u32[]{:S(2)}) collective-permute-start(s16[1616,128]{1,0:T(8,128)(2,1)S(1)} %sum_step_10.1.rest_1_), channel_id=1, source_target_pairs={{0,8},{4,12},{8,24},{12,28},{16,0},{20,4},{24,16},{28,20},{1,9},{5... | collective-permute-start | bytes 1241096 | tf_op jit(solution)/shard_map/ppermute | solution.py:428
  116.0 11.1 %collective-permute-start.26 = (s16[1616,128]{1,0:T(8,128)(2,1)S(1)}, s16[1616,128]{1,0:T(8,128)(2,1)S(1)}, u32[]{:S(2)}, u32[]{:S(2)}) collective-permute-start(s16[1616,128]{1,0:T(8,128)(2,1)S(1)} %sum_step_11.1), channel_id=1, source_target_pairs={{0,8},{4,12},{8,24},{12,28},{16,0},{20,4},{24,16},{28,20},{1,9},{5... | collective-permute-start | bytes 1241096 | tf_op jit(solution)/shard_map/ppermute | solution.py:428
where the time goes:
time: 132 us; the launch traced here: 131 us
  starting transfers between devices  47.5 us (36%)
  Pallas kernels  44.5 us (34%)
  waiting for transfers between devices  33.3 us (25%)
  local copies, waits for them, and re-layouts  4.66 us (4%)
    ppermute x15, starting transfers between devices, solve_by_sums(): lax.ppermute(coded, 'ifg', line_permutation(links))  33.5 us
    pallas_call x11, Pallas kernels, step(): pl.pallas_call(functools.partial(step_kernel, at, layout, len(earlier), s...  23.2 us
    ppermute x15, waiting for transfers between devices, solve_by_sums(): lax.ppermute(coded, 'ifg', line_permutation(links))  18.9 us
    pallas_call x4, Pallas kernels, finish(): pl.pallas_call(functools.partial(finish_kernel, at, layout, tiles, len(ra...  14.5 us
    ppermute x7, waiting for transfers between devices, swapped(): here = lax.ppermute(away, 'ifg', swap)  8.85 us
    pallas_call x1, Pallas kernels, invert_classes(): pl.pallas_call(inverse_kernel, out_shape=jax.ShapeDtypeStruct(shape, F32)...  6.77 us
    ppermute x3, starting transfers between devices, solve_by_sums(): counts.append(lax.ppermute(run_counts, 'ifg', line_permutation(links)))  6.11 us
    ppermute x1, waiting for transfers between devices, solve_by_sums(): lax.ppermute(first_away(side, raw_part, 1, run_counts), 'ifg', near)  5.51 us
  transfers between devices with their start and end apart: 28, of which 14 were waited for; matrix products, arithmetic and copies ran while one was open for 3% of the time, Pallas kernels for 31%

commit v1 on v0

--- a/solution.py
+++ b/solution.py
@@ -21,8 +21,8 @@
 CUTS = 2
 HALVES = 2
 FLIGHT = 2
-FIRST_SWAPS = ((0, 1), (1, 2))
-SWAPS = {1: (4, 2), 2: (6, 2), 5: (8, 4), 8: (12, 2), 9: (14, 2)}
+FIRST_SWAP = (0, 2)
+SWAPS = {0: (2, 1), 1: (4, 2), 2: (6, 2), 5: (8, 4), 8: (12, 2), 9: (14, 2)}
 SWAP_WAITS = {5: 6, 10: 12}
 RAW_STEP, RAW_WAIT = 2, 5
 INVERSE_STEP = 5
@@ -385,8 +385,8 @@
             block, _ = lax.optimization_barrier((block, after))
         return lax.dynamic_slice(phases, (0, block * piece), (local_pairs, count * piece))
 
-    away = first_away(1 - side, *FIRST_SWAPS[0], None)
-    swapped(away, *FIRST_SWAPS[0])
+    away = first_away(1 - side, *FIRST_SWAP, None)
+    swapped(away, *FIRST_SWAP)
     run_counts = counts_of(away)
     counts = [run_counts]
     for distance in range(1, line):
@@ -397,7 +397,6 @@
     near = line_permutation(SENDS[0][0])
     raw_other = lax.ppermute(first_away(1 - side, raw_part, 1, run_counts), "ifg", near)
     raw_own = lax.ppermute(first_away(side, raw_part, 1, run_counts), "ifg", near)
-    swapped(first_away(1 - side, *FIRST_SWAPS[1], counts), *FIRST_SWAPS[1])
     pairs = jnp.concatenate([lax.dynamic_slice(date_pairs, (0, (me ^ at) * local_pairs), (2, local_pairs)) for at in range(4)], axis=1)
     scalars = (row, counts)
 

time: 132 us -> 133 us (level)
  starting transfers between devices: 47.5 us -> 52.2 us
  waiting for transfers between devices: 33.3 us -> 29.7 us
    ppermute x1, waiting for transfers between devices: 5.51 us -> 0.01 us  [solve_by_sums(): lax.ppermute(first_away(side, raw_part, 1, run_counts), 'ifg', near)]
    ppermute x7, starting transfers between devices: 4.72 us -> 10 us  [swapped(): here = lax.ppermute(away, 'ifg', swap)]
    dynamic_slice x3 -> x2, local copies, waits for them, and re-layouts: 3.12 us -> 2.15 us  [first_away(): lax.dynamic_slice(phases, (0, block * piece), (local_pairs, count * piece))]
  transfers between devices with their start and end apart: 28 -> 28, of which waited for: 14 -> 11; matrix products, arithmetic and copies ran while one was open for 3% -> 2% of each run, Pallas kernels for 31% -> 31%
where the time goes in v1:
time: 133 us; the launch traced here: 132 us
  starting transfers between devices  52.2 us (39%)
  Pallas kernels  45.4 us (34%)
  waiting for transfers between devices  29.7 us (22%)
  local copies, waits for them, and re-layouts  3.68 us (3%)
    ppermute x15, starting transfers between devices, solve_by_sums(): lax.ppermute(coded, 'ifg', line_permutation(links))  32.9 us
    pallas_call x11, Pallas kernels, step(): pl.pallas_call(functools.partial(step_kernel, at, layout, len(earlier), s...  23.3 us
    ppermute x15, waiting for transfers between devices, solve_by_sums(): lax.ppermute(coded, 'ifg', line_permutation(links))  19.8 us
    pallas_call x4, Pallas kernels, finish(): pl.pallas_call(functools.partial(finish_kernel, at, layout, tiles, len(ra...  14.5 us
    ppermute x7, starting transfers between devices, swapped(): here = lax.ppermute(away, 'ifg', swap)  10 us
    ppermute x7, waiting for transfers between devices, swapped(): here = lax.ppermute(away, 'ifg', swap)  9.82 us
    pallas_call x1, Pallas kernels, invert_classes(): pl.pallas_call(inverse_kernel, out_shape=jax.ShapeDtypeStruct(shape, F32)...  7.56 us
    ppermute x3, starting transfers between devices, solve_by_sums(): counts.append(lax.ppermute(run_counts, 'ifg', line_permutation(links)))  6.11 us
  transfers between devices with their start and end apart: 28, of which 11 were waited for; matrix products, arithmetic and copies ran while one was open for 2% of the time, Pallas kernels for 31%

profile of v1, /device:TPU:0, one launch (start us, length us, event | category | flops | bytes accessed | tf_op | source)
XLA Modules:
  0.0 132.1 jit_solution(13831227048238471213)
XLA Ops:
  0.0 1.1 dynamic-slice_bitcast_fusion
  1.2 0.8 fusion.counts_ref
  2.1 5.1 %collective-permute-start.2 = (s32[2]{0:T(128)S(1)}, s32[2]{0:T(128)S(1)}, u32[]{:S(2)}, u32[]{:S(2)}) collective-permute-start(s32[2]{0:T(128)S(1)} %fusion.counts_ref), channel_id=1, source_target_pairs={{0,24},{4,28},{8,0},{12,4},{16,8},{20,12},{24,16},{28,20},{1,25},{... | collective-permute-start | bytes 32 | tf_op jit(solution)/shard_map/ppermute | solution.py:394
  7.2 1.0 collective-permute-start
  8.2 1.5 %collective-permute-start.3 = (bf16[128,2048]{1,0:T(8,128)(2,1)S(1)}, bf16[128,2048]{1,0:T(8,128)(2,1)S(1)}, u32[]{:S(2)}, u32[]{:S(2)}) collective-permute-start(bf16[128,2048]{1,0:T(8,128)(2,1)S(1)} %dynamic-slice_bitcast_fusion), channel_id=1, source_target_pairs={{0,4},{4,0},{8,12},{12,8},{16,20},{20,16},{24,28},{28,24},{1,5},{5... | collective-permute-start | bytes 1572872 | tf_op jit(solution)/shard_map/ppermute | solution.py:376
  9.7 1.1 dynamic-slice_bitcast_fusion.1
  10.7 2.5 %collective-permute-start.5 = (bf16[128,1024]{1,0:T(8,128)(2,1)S(1)}, bf16[128,1024]{1,0:T(8,128)(2,1)S(1)}, u32[]{:S(2)}, u32[]{:S(2)}) collective-permute-start(bf16[128,1024]{1,0:T(8,128)(2,1)S(1)} %get-tuple-element.41), channel_id=1, source_target_pairs={{0,8},{4,12},{8,0},{12,4},{16,24},{20,28},{24,16},{28,20},{1,9},{5... | collective-permute-start | bytes 786440 | tf_op jit(solution)/shard_map/ppermute | solution.py:398
  13.3 0.7 fusion.1.table
  14.0 0.7 constant_dynamic-slice_fusion.3
  14.9 6.1 %collective-permute-done.3.partner_ref = bf16[128,2048]{1,0:T(8,128)(2,1)S(1)} collective-permute-done((bf16[128,2048]{1,0:T(8,128)(2,1)S(1)}, bf16[128,2048]{1,0:T(8,128)(2,1)S(1)}, u32[]{:S(2)}, u32[]{:S(2)}) %collective-permute-start.3) | collective-permute-done | bytes 524320 | tf_op jit(solution)/shard_map/ppermute | solution.py:376
  21.0 2.1 %sum_step_00.1 = (s16[1616,128]{1,0:T(8,128)(2,1)S(1)}, bf16[128,1024]{1,0:T(8,128)(2,1)S(1)}) custom-call(s32[53]{0:T(128)S(1)} %fusion.1.table, s32[8]{0:T(128)S(1)} %pad_add_fusion.1.counts, s32[2,512]{1,0:T(2,128)S(1)} %pad_add_fusion.pairs_ref, bf16[128,32768]{1,0:T(8,128)(2,1)} %bitcast.12, bf16[128,2048]{1,0:T(8,128)(2,1)S(1)} %collective-permute-done.3.partner_ref, ...), custom_call_target="tpu_custom_call" | custom-call | flops 10000000000 | bytes 30000000 | tf_op jit(solution)/shard_map/sum_step_00/pallas_call | solution.py:245
  23.1 1.6 %collective-permute-start.9 = (bf16[128,1024]{1,0:T(8,128)(2,1)S(1)}, bf16[128,1024]{1,0:T(8,128)(2,1)S(1)}, u32[]{:S(2)}, u32[]{:S(2)}) collective-permute-start(bf16[128,1024]{1,0:T(8,128)(2,1)S(1)} %get-tuple-element.29), channel_id=1, source_target_pairs={{0,4},{4,0},{8,12},{12,8},{16,20},{20,16},{24,28},{28,24},{1,5},{5... | collective-permute-start | bytes 786440 | tf_op jit(solution)/shard_map/ppermute | solution.py:376
  24.6 2.5 %collective-permute-start.8 = (s16[1616,128]{1,0:T(8,128)(2,1)S(1)}, s16[1616,128]{1,0:T(8,128)(2,1)S(1)}, u32[]{:S(2)}, u32[]{:S(2)}) collective-permute-start(s16[1616,128]{1,0:T(8,128)(2,1)S(1)} %get-tuple-element.24.rest_1_), channel_id=1, source_target_pairs={{0,8},{4,12},{8,0},{12,4},{16,24},{20,28},{24,16},{28,20},{1,9},{5... | collective-permute-start | bytes 1241096 | tf_op jit(solution)/shard_map/ppermute | solution.py:427
  27.1 2.2 %sum_step_01.1 = (s16[1616,128]{1,0:T(8,128)(2,1)S(1)}, bf16[128,2048]{1,0:T(8,128)(2,1)S(1)}) custom-call(s32[53]{0:T(128)S(1)} %fusion.1.table, s32[8]{0:T(128)S(1)} %pad_add_fusion.1.counts, s32[2,512]{1,0:T(2,128)S(1)} %pad_add_fusion.pairs_ref, bf16[128,32768]{1,0:T(8,128)(2,1)} %bitcast.14, bf16[128,2048]{1,0:T(8,128)(2,1)S(1)} %collective-permute-done.3.partner_ref, ...), custom_call_target="tpu_custom_call" | custom-call | flops 10000000000 | bytes 30000000 | tf_op jit(solution)/shard_map/sum_step_01/pallas_call | solution.py:245
  30.0 7.6 %collective-permute-done.8.rest_2_.rest_0_.rest_1_ = s16[1616,128]{1,0:T(8,128)(2,1)S(1)} collective-permute-done((s16[1616,128]{1,0:T(8,128)(2,1)S(1)}, s16[1616,128]{1,0:T(8,128)(2,1)S(1)}, u32[]{:S(2)}, u32[]{:S(2)}) %collective-permute-start.8) | collective-permute-done | bytes 413728 | tf_op jit(solution)/shard_map/ppermute | solution.py:427
  37.6 2.2 %sum_step_02.1 = (s16[1616,128]{1,0:T(8,128)(2,1)S(1)}, bf16[128,2048]{1,0:T(8,128)(2,1)S(1)}) custom-call(s32[53]{0:T(128)S(1)} %fusion.1.table, s32[8]{0:T(128)S(1)} %pad_add_fusion.1.counts, s32[2,512]{1,0:T(2,128)S(1)} %pad_add_fusion.pairs_ref, bf16[128,32768]{1,0:T(8,128)(2,1)} %bitcast.16, bf16[128,1024]{1,0:T(8,128)(2,1)S(1)} %collective-permute-done.9.partner_ref, ...), custom_call_target="tpu_custom_call" | custom-call | flops 10000000000 | bytes 30000000 | tf_op jit(solution)/shard_map/sum_step_02/pallas_call | solution.py:245
  39.7 2.1 %collective-permute-start.10 = (s16[1616,128]{1,0:T(8,128)(2,1)S(1)}, s16[1616,128]{1,0:T(8,128)(2,1)S(1)}, u32[]{:S(2)}, u32[]{:S(2)}) collective-permute-start(s16[1616,128]{1,0:T(8,128)(2,1)S(1)} %get-tuple-element.30.rest_1_), channel_id=1, source_target_pairs={{0,8},{4,12},{8,0},{12,4},{16,24},{20,28},{24,16},{28,20},{1,9},{5... | collective-permute-start | bytes 1241096 | tf_op jit(solution)/shard_map/ppermute | solution.py:427
  42.4 1.5 %collective-permute-start.11 = (bf16[128,2048]{1,0:T(8,128)(2,1)S(1)}, bf16[128,2048]{1,0:T(8,128)(2,1)S(1)}, u32[]{:S(2)}, u32[]{:S(2)}) collective-permute-start(bf16[128,2048]{1,0:T(8,128)(2,1)S(1)} %get-tuple-element.31), channel_id=1, source_target_pairs={{0,4},{4,0},{8,12},{12,8},{16,20},{20,16},{24,28},{28,24},{1,5},{5... | collective-permute-start | bytes 1572872 | tf_op jit(solution)/shard_map/ppermute | solution.py:376
  43.8 2.6 %collective-permute-done.7.rest_2_.rest_1_.rest_0_ = s16[1616,128]{1,0:T(8,128)(2,1)S(1)} collective-permute-done((s16[1616,128]{1,0:T(8,128)(2,1)S(1)}, s16[1616,128]{1,0:T(8,128)(2,1)S(1)}, u32[]{:S(2)}, u32[]{:S(2)}) %collective-permute-start.7) | collective-permute-done | bytes 413728 | tf_op jit(solution)/shard_map/ppermute | solution.py:427
  46.4 2.0 %sum_step_04.1.rest_0_.rest_2_ = s16[1616,128]{1,0:T(8,128)(2,1)S(1)} custom-call(s32[53]{0:T(128)S(1)} %fusion.1.table, s32[8]{0:T(128)S(1)} %pad_add_fusion.1.counts, s32[2,512]{1,0:T(2,128)S(1)} %pad_add_fusion.pairs_ref, bf16[128,32768]{1,0:T(8,128)(2,1)} %bitcast.18, bf16[128,2048]{1,0:T(8,128)(2,1)S(1)} %collective-permute-done.6.partner_ref, ...), custom_call_target="tpu_custom_call" | custom-call | flops 10000000000 | bytes 30000000 | tf_op jit(solution)/shard_map/sum_step_04/pallas_call | solution.py:245
  49.1 5.5 %collective-permute-start.15 = (s16[1616,128]{1,0:T(8,128)(2,1)S(1)}, s16[1616,128]{1,0:T(8,128)(2,1)S(1)}, u32[]{:S(2)}, u32[]{:S(2)}) collective-permute-start(s16[1616,128]{1,0:T(8,128)(2,1)S(1)} %sum_step_04.1.rest_0_.rest_2_), channel_id=1, source_target_pairs={{0,8},{4,12},{24,16},{28,20},{1,9},{5,13},{25,17},{29,21},{2,10},{... | collective-permute-start | bytes 1241096 | tf_op jit(solution)/shard_map/ppermute | solution.py:427
  54.6 7.6 %invert_classes_0.1.rest_6_.inverse_ref = f32[2,256,256]{2,1,0:T(8,128)S(1)} custom-call(s32[2]{0:T(128)S(1)} %fusion.counts_ref, s32[2,1024]{1,0:T(2,128)S(1)} %copy-done.1, s16[1616,128]{1,0:T(8,128)(2,1)S(1)} %sum_step_04.1.rest_0_.rest_2_), custom_call_target="tpu_custom_call" | custom-call | flops 1024 | bytes 1024 | tf_op jit(solution)/shard_map/invert_classes_0/pallas_call | solution.py:103
  62.2 2.4 %sum_step_05.1 = (s16[1616,128]{1,0:T(8,128)(2,1)S(1)}, bf16[128,4096]{1,0:T(8,128)(2,1)S(1)}) custom-call(s32[53]{0:T(128)S(1)} %fusion.1.table, s32[8]{0:T(128)S(1)} %pad_add_fusion.1.counts, s32[2,512]{1,0:T(2,128)S(1)} %pad_add_fusion.pairs_ref, bf16[128,32768]{1,0:T(8,128)(2,1)} %bitcast.19, bf16[128,2048]{1,0:T(8,128)(2,1)S(1)} %collective-permute-done.6.partner_ref, ...), custom_call_target="tpu_custom_call" | custom-call | flops 10000000000 | bytes 30000000 | tf_op jit(solution)/shard_map/sum_step_05/pallas_call | solution.py:245
  65.3 4.2 %collective-permute-start.14 = (s16[1616,128]{1,0:T(8,128)(2,1)S(1)}, s16[1616,128]{1,0:T(8,128)(2,1)S(1)}, u32[]{:S(2)}, u32[]{:S(2)}) collective-permute-start(s16[1616,128]{1,0:T(8,128)(2,1)S(1)} %get-tuple-element.34.rest_1_), channel_id=1, source_target_pairs={{0,8},{4,12},{24,16},{28,20},{1,9},{5,13},{25,17},{29,21},{2,10},{... | collective-permute-start | bytes 1241096 | tf_op jit(solution)/shard_map/ppermute | solution.py:427
  70.2 2.0 %sum_step_06.1.rest_2_ = s16[1616,128]{1,0:T(8,128)(2,1)S(1)} custom-call(s32[53]{0:T(128)S(1)} %fusion.1.table, s32[8]{0:T(128)S(1)} %pad_add_fusion.1.counts, s32[2,512]{1,0:T(2,128)S(1)} %pad_add_fusion.pairs_ref, bf16[128,32768]{1,0:T(8,128)(2,1)} %bitcast.21, bf16[128,2048]{1,0:T(8,128)(2,1)S(1)} %collective-permute-done.11.rest_4_.partner_ref, ...), custom_call_target="tpu_custom_call" | custom-call | flops 10000000000 | bytes 30000000 | tf_op jit(solution)/shard_map/sum_step_06/pallas_call | solution.py:245
  72.9 2.8 %collective-permute-start.18 = (s16[1616,128]{1,0:T(8,128)(2,1)S(1)}, s16[1616,128]{1,0:T(8,128)(2,1)S(1)}, u32[]{:S(2)}, u32[]{:S(2)}) collective-permute-start(s16[1616,128]{1,0:T(8,128)(2,1)S(1)} %sum_step_06.1.rest_2_), channel_id=1, source_target_pairs={{0,8},{4,12},{24,16},{28,20},{1,9},{5,13},{25,17},{29,21},{2,10},{... | collective-permute-start | bytes 1241096 | tf_op jit(solution)/shard_map/ppermute | solution.py:427
  75.7 1.9 %collective-permute-done.14.rest_3_.rest_1_ = s16[1616,128]{1,0:T(8,128)(2,1)S(1)} collective-permute-done((s16[1616,128]{1,0:T(8,128)(2,1)S(1)}, s16[1616,128]{1,0:T(8,128)(2,1)S(1)}, u32[]{:S(2)}, u32[]{:S(2)}) %collective-permute-start.14) | collective-permute-done | bytes 413728 | tf_op jit(solution)/shard_map/ppermute | solution.py:427
  77.6 2.0 %sum_step_07.1.rest_2_ = s16[1616,128]{1,0:T(8,128)(2,1)S(1)} custom-call(s32[53]{0:T(128)S(1)} %fusion.1.table, s32[8]{0:T(128)S(1)} %pad_add_fusion.1.counts, s32[2,512]{1,0:T(2,128)S(1)} %pad_add_fusion.pairs_ref, bf16[128,32768]{1,0:T(8,128)(2,1)} %bitcast.22, bf16[128,2048]{1,0:T(8,128)(2,1)S(1)} %collective-permute-done.11.rest_4_.partner_ref, ...), custom_call_target="tpu_custom_call" | custom-call | flops 10000000000 | bytes 30000000 | tf_op jit(solution)/shard_map/sum_step_07/pallas_call | solution.py:245
  80.4 5.6 %collective-permute-start.20 = (s16[1616,128]{1,0:T(8,128)(2,1)S(1)}, s16[1616,128]{1,0:T(8,128)(2,1)S(1)}, u32[]{:S(2)}, u32[]{:S(2)}) collective-permute-start(s16[1616,128]{1,0:T(8,128)(2,1)S(1)} %sum_step_07.1.rest_2_), channel_id=1, source_target_pairs={{0,8},{4,12},{24,16},{28,20},{1,9},{5,13},{25,17},{29,21},{2,10},{... | collective-permute-start | bytes 1241096 | tf_op jit(solution)/shard_map/ppermute | solution.py:427
  86.5 2.9 %collective-permute-done.13.partner_ref = bf16[128,4096]{1,0:T(8,128)(2,1)S(1)} collective-permute-done((bf16[128,4096]{1,0:T(8,128)(2,1)S(1)}, bf16[128,4096]{1,0:T(8,128)(2,1)S(1)}, u32[]{:S(2)}, u32[]{:S(2)}) %collective-permute-start.13) | collective-permute-done | bytes 1048608 | tf_op jit(solution)/shard_map/ppermute | solution.py:376
  89.4 2.2 %sum_step_08.1 = (s16[1616,128]{1,0:T(8,128)(2,1)S(1)}, bf16[128,2048]{1,0:T(8,128)(2,1)S(1)}) custom-call(s32[53]{0:T(128)S(1)} %fusion.1.table, s32[8]{0:T(128)S(1)} %pad_add_fusion.1.counts, s32[2,512]{1,0:T(2,128)S(1)} %pad_add_fusion.pairs_ref, bf16[128,32768]{1,0:T(8,128)(2,1)} %bitcast.23, bf16[128,4096]{1,0:T(8,128)(2,1)S(1)} %collective-permute-done.13.partner_ref, ...), custom_call_target="tpu_custom_call" | custom-call | flops 10000000000 | bytes 30000000 | tf_op jit(solution)/shard_map/sum_step_08/pallas_call | solution.py:245
  91.7 1.9 %collective-permute-start.24 = (bf16[128,2048]{1,0:T(8,128)(2,1)S(1)}, bf16[128,2048]{1,0:T(8,128)(2,1)S(1)}, u32[]{:S(2)}, u32[]{:S(2)}) collective-permute-start(bf16[128,2048]{1,0:T(8,128)(2,1)S(1)} %get-tuple-element.38), channel_id=1, source_target_pairs={{0,4},{4,0},{8,12},{12,8},{16,20},{20,16},{24,28},{28,24},{1,5},{5... | collective-permute-start | bytes 1572872 | tf_op jit(solution)/shard_map/ppermute | solution.py:376
  93.6 2.4 %collective-permute-done.20.rest_3_.rest_0_ = s16[1616,128]{1,0:T(8,128)(2,1)S(1)} collective-permute-done((s16[1616,128]{1,0:T(8,128)(2,1)S(1)}, s16[1616,128]{1,0:T(8,128)(2,1)S(1)}, u32[]{:S(2)}, u32[]{:S(2)}) %collective-permute-start.20) | collective-permute-done | bytes 413728 | tf_op jit(solution)/shard_map/ppermute | solution.py:427
  96.0 2.2 %sum_step_09.1 = (s16[1616,128]{1,0:T(8,128)(2,1)S(1)}, bf16[128,2048]{1,0:T(8,128)(2,1)S(1)}) custom-call(s32[53]{0:T(128)S(1)} %fusion.1.table, s32[8]{0:T(128)S(1)} %pad_add_fusion.1.counts, s32[2,512]{1,0:T(2,128)S(1)} %pad_add_fusion.pairs_ref, bf16[128,32768]{1,0:T(8,128)(2,1)} %bitcast.25, bf16[128,4096]{1,0:T(8,128)(2,1)S(1)} %collective-permute-done.13.partner_ref, ...), custom_call_target="tpu_custom_call" | custom-call | flops 10000000000 | bytes 30000000 | tf_op jit(solution)/shard_map/sum_step_09/pallas_call | solution.py:245
  98.2 2.5 %collective-permute-start.25 = (s16[1616,128]{1,0:T(8,128)(2,1)S(1)}, s16[1616,128]{1,0:T(8,128)(2,1)S(1)}, u32[]{:S(2)}, u32[]{:S(2)}) collective-permute-start(s16[1616,128]{1,0:T(8,128)(2,1)S(1)} %get-tuple-element.37.rest_1_), channel_id=1, source_target_pairs={{0,8},{4,12},{8,24},{12,28},{16,0},{20,4},{24,16},{28,20},{1,9},{5... | collective-permute-start | bytes 1241096 | tf_op jit(solution)/shard_map/ppermute | solution.py:427
  100.7 2.4 %collective-permute-start.22 = (bf16[128,2048]{1,0:T(8,128)(2,1)S(1)}, bf16[128,2048]{1,0:T(8,128)(2,1)S(1)}, u32[]{:S(2)}, u32[]{:S(2)}) collective-permute-start(bf16[128,2048]{1,0:T(8,128)(2,1)S(1)} %get-tuple-element.36), channel_id=1, source_target_pairs={{0,4},{4,0},{8,12},{12,8},{16,20},{20,16},{24,28},{28,24},{1,5},{5... | collective-permute-start | bytes 1572872 | tf_op jit(solution)/shard_map/ppermute | solution.py:376
  103.1 2.0 %collective-permute-done.23.rest_2_.rest_4_.rest_5_ = s16[1616,128]{1,0:T(8,128)(2,1)S(1)} collective-permute-done((s16[1616,128]{1,0:T(8,128)(2,1)S(1)}, s16[1616,128]{1,0:T(8,128)(2,1)S(1)}, u32[]{:S(2)}, u32[]{:S(2)}) %collective-permute-start.23) | collective-permute-done | bytes 413728 | tf_op jit(solution)/shard_map/ppermute | solution.py:427
  105.1 0.8 collective-permute-done.24.rest_3_.partner_ref
  105.9 2.0 %sum_step_10.1.rest_1_ = s16[1616,128]{1,0:T(8,128)(2,1)S(1)} custom-call(s32[53]{0:T(128)S(1)} %fusion.1.table, s32[8]{0:T(128)S(1)} %pad_add_fusion.1.counts, s32[2,512]{1,0:T(2,128)S(1)} %pad_add_fusion.pairs_ref, bf16[128,32768]{1,0:T(8,128)(2,1)} %bitcast.27, bf16[128,4096]{1,0:T(8,128)(2,1)S(1)} %collective-permute-done.13.partner_ref, ...), custom_call_target="tpu_custom_call" | custom-call | flops 10000000000 | bytes 30000000 | tf_op jit(solution)/shard_map/sum_step_10/pallas_call | solution.py:245
  107.9 3.5 %collective-permute-start.27 = (s16[1616,128]{1,0:T(8,128)(2,1)S(1)}, s16[1616,128]{1,0:T(8,128)(2,1)S(1)}, u32[]{:S(2)}, u32[]{:S(2)}) collective-permute-start(s16[1616,128]{1,0:T(8,128)(2,1)S(1)} %sum_step_10.1.rest_1_), channel_id=1, source_target_pairs={{0,8},{4,12},{8,24},{12,28},{16,0},{20,4},{24,16},{28,20},{1,9},{5... | collective-permute-start | bytes 1241096 | tf_op jit(solution)/shard_map/ppermute | solution.py:427
  111.4 3.6 %finish_0.1 = (f32[200,4096]{1,0:T(8,128)}, f32[8,128]{1,0:T(8,128)S(1)}) custom-call(s32[53]{0:T(128)S(1)} %fusion.1.table, s32[8]{0:T(128)S(1)} %pad_add_fusion.1.counts, s32[2,512]{1,0:T(2,128)S(1)} %pad_add_fusion.pairs_ref, bf16[128,32768]{1,0:T(8,128)(2,1)} %bitcast.28, bf16[128,2048]{1,0:T(8,128)(2,1)S(1)} %collective-permute-done.24.rest_3_.partner_ref, ...), custom_call_target="tpu_custom_call" | custom-call | flops 1024 | bytes 1024 | tf_op jit(solution)/shard_map/finish_0/pallas_call | solution.py:327
  114.9 2.0 %sum_step_11.1 = s16[1616,128]{1,0:T(8,128)(2,1)S(1)} custom-call(s32[53]{0:T(128)S(1)} %fusion.1.table, s32[8]{0:T(128)S(1)} %pad_add_fusion.1.counts, s32[2,512]{1,0:T(2,128)S(1)} %pad_add_fusion.pairs_ref, bf16[128,32768]{1,0:T(8,128)(2,1)} %bitcast.29, bf16[128,4096]{1,0:T(8,128)(2,1)S(1)} %collective-permute-done.13.partner_ref, ...), custom_call_target="tpu_custom_call" | custom-call | flops 10000000000 | bytes 30000000 | tf_op jit(solution)/shard_map/sum_step_11/pallas_call | solution.py:245
  116.9 1.3 collective-permute-start.26
  118.2 3.6 %finish_1.1.rest_6_ = f32[200,4096]{1,0:T(8,128)} custom-call(s32[53]{0:T(128)S(1)} %fusion.1.table, s32[8]{0:T(128)S(1)} %pad_add_fusion.1.counts, s32[2,512]{1,0:T(2,128)S(1)} %pad_add_fusion.pairs_ref, bf16[128,32768]{1,0:T(8,128)(2,1)} %bitcast.30, ...), custom_call_target="tpu_custom_call", output_to_operand_aliasing={{}: (12, {})} | custom-call | flops 1024 | bytes 1024 | tf_op jit(solution)/shard_map/finish_1/pallas_call | solution.py:327
  121.8 0.8 collective-permute-done.27.rest_4_.rest_5_
  122.6 3.6 %finish_2.1.rest_6_ = f32[200,4096]{1,0:T(8,128)} custom-call(s32[53]{0:T(128)S(1)} %fusion.1.table, s32[8]{0:T(128)S(1)} %pad_add_fusion.1.counts, s32[2,512]{1,0:T(2,128)S(1)} %pad_add_fusion.pairs_ref, bf16[128,32768]{1,0:T(8,128)(2,1)} %bitcast.31, bf16[128,2048]{1,0:T(8,128)(2,1)S(1)} %collective-permute-done.22.partner_ref, ...), custom_call_target="tpu_custom_call", output_to_operand_aliasing={{}: (12, {})} | custom-call | flops 1024 | bytes 1024 | tf_op jit(solution)/shard_map/finish_2/pallas_call | solution.py:327
  126.1 2.1 %collective-permute-done.26.rest_4_.rest_5_ = s16[1616,128]{1,0:T(8,128)(2,1)S(1)} collective-permute-done((s16[1616,128]{1,0:T(8,128)(2,1)S(1)}, s16[1616,128]{1,0:T(8,128)(2,1)S(1)}, u32[]{:S(2)}, u32[]{:S(2)}) %collective-permute-start.26) | collective-permute-done | bytes 413728 | tf_op jit(solution)/shard_map/ppermute | solution.py:427
  128.3 3.9 %finish_3.1 = f32[200,4096]{1,0:T(8,128)} custom-call(s32[53]{0:T(128)S(1)} %fusion.1.table, s32[8]{0:T(128)S(1)} %pad_add_fusion.1.counts, s32[2,512]{1,0:T(2,128)S(1)} %pad_add_fusion.pairs_ref, bf16[128,32768]{1,0:T(8,128)(2,1)} %bitcast.32, bf16[128,2048]{1,0:T(8,128)(2,1)S(1)} %collective-permute-done.22.partner_ref, ...), custom_call_target="tpu_custom_call", output_to_operand_aliasing={{}: (12, {})} | custom-call | flops 1024 | bytes 1024 | tf_op jit(solution)/shard_map/finish_3/pallas_call | solution.py:327
  (37 shorter events, 5.5 us)
Async XLA Ops:
  0.0 1.1 copy-start
  2.1 12.6 %collective-permute-start.2 = (s32[2]{0:T(128)S(1)}, s32[2]{0:T(128)S(1)}, u32[]{:S(2)}, u32[]{:S(2)}) collective-permute-start(s32[2]{0:T(128)S(1)} %fusion.counts_ref), channel_id=1, source_target_pairs={{0,24},{4,28},{8,0},{12,4},{16,8},{20,12},{24,16},{28,20},{1,25},{... | collective-permute-start | bytes 32 | tf_op jit(solution)/shard_map/ppermute | solution.py:394
  7.1 7.7 %collective-permute-start.1 = (s32[2]{0:T(128)S(1)}, s32[2]{0:T(128)S(1)}, u32[]{:S(2)}, u32[]{:S(2)}) collective-permute-start(s32[2]{0:T(128)S(1)} %fusion.counts_ref), channel_id=1, source_target_pairs={{0,16},{4,20},{8,24},{12,28},{16,0},{20,4},{24,8},{28,12},{1,17},{... | collective-permute-start | bytes 32 | tf_op jit(solution)/shard_map/ppermute | solution.py:394
  7.2 7.7 %collective-permute-start = (s32[2]{0:T(128)S(1)}, s32[2]{0:T(128)S(1)}, u32[]{:S(2)}, u32[]{:S(2)}) collective-permute-start(s32[2]{0:T(128)S(1)} %fusion.counts_ref), channel_id=1, source_target_pairs={{0,8},{4,12},{8,16},{12,20},{16,24},{20,28},{24,0},{28,4},{1,9},{5... | collective-permute-start | bytes 32 | tf_op jit(solution)/shard_map/ppermute | solution.py:394
  8.2 12.8 %collective-permute-start.3 = (bf16[128,2048]{1,0:T(8,128)(2,1)S(1)}, bf16[128,2048]{1,0:T(8,128)(2,1)S(1)}, u32[]{:S(2)}, u32[]{:S(2)}) collective-permute-start(bf16[128,2048]{1,0:T(8,128)(2,1)S(1)} %dynamic-slice_bitcast_fusion), channel_id=1, source_target_pairs={{0,4},{4,0},{8,12},{12,8},{16,20},{20,16},{24,28},{28,24},{1,5},{5... | collective-permute-start | bytes 1572872 | tf_op jit(solution)/shard_map/ppermute | solution.py:376
  10.7 16.4 %collective-permute-start.5 = (bf16[128,1024]{1,0:T(8,128)(2,1)S(1)}, bf16[128,1024]{1,0:T(8,128)(2,1)S(1)}, u32[]{:S(2)}, u32[]{:S(2)}) collective-permute-start(bf16[128,1024]{1,0:T(8,128)(2,1)S(1)} %get-tuple-element.41), channel_id=1, source_target_pairs={{0,8},{4,12},{8,0},{12,4},{16,24},{20,28},{24,16},{28,20},{1,9},{5... | collective-permute-start | bytes 786440 | tf_op jit(solution)/shard_map/ppermute | solution.py:398
  14.7 12.4 %collective-permute-start.4 = (bf16[128,1024]{1,0:T(8,128)(2,1)S(1)}, bf16[128,1024]{1,0:T(8,128)(2,1)S(1)}, u32[]{:S(2)}, u32[]{:S(2)}) collective-permute-start(bf16[128,1024]{1,0:T(8,128)(2,1)S(1)} %get-tuple-element.42), channel_id=1, source_target_pairs={{0,8},{4,12},{8,0},{12,4},{16,24},{20,28},{24,16},{28,20},{1,9},{5... | collective-permute-start | bytes 786440 | tf_op jit(solution)/shard_map/ppermute | solution.py:399
  23.1 6.9 %collective-permute-start.9 = (bf16[128,1024]{1,0:T(8,128)(2,1)S(1)}, bf16[128,1024]{1,0:T(8,128)(2,1)S(1)}, u32[]{:S(2)}, u32[]{:S(2)}) collective-permute-start(bf16[128,1024]{1,0:T(8,128)(2,1)S(1)} %get-tuple-element.29), channel_id=1, source_target_pairs={{0,4},{4,0},{8,12},{12,8},{16,20},{20,16},{24,28},{28,24},{1,5},{5... | collective-permute-start | bytes 786440 | tf_op jit(solution)/shard_map/ppermute | solution.py:376
  24.6 12.9 %collective-permute-start.8 = (s16[1616,128]{1,0:T(8,128)(2,1)S(1)}, s16[1616,128]{1,0:T(8,128)(2,1)S(1)}, u32[]{:S(2)}, u32[]{:S(2)}) collective-permute-start(s16[1616,128]{1,0:T(8,128)(2,1)S(1)} %get-tuple-element.24.rest_1_), channel_id=1, source_target_pairs={{0,8},{4,12},{8,0},{12,4},{16,24},{20,28},{24,16},{28,20},{1,9},{5... | collective-permute-start | bytes 1241096 | tf_op jit(solution)/shard_map/ppermute | solution.py:427
  29.3 17.1 %collective-permute-start.7 = (s16[1616,128]{1,0:T(8,128)(2,1)S(1)}, s16[1616,128]{1,0:T(8,128)(2,1)S(1)}, u32[]{:S(2)}, u32[]{:S(2)}) collective-permute-start(s16[1616,128]{1,0:T(8,128)(2,1)S(1)} %get-tuple-element.28.rest_1_), channel_id=1, source_target_pairs={{0,8},{4,12},{8,0},{12,4},{16,24},{20,28},{24,16},{28,20},{1,9},{5... | collective-permute-start | bytes 1241096 | tf_op jit(solution)/shard_map/ppermute | solution.py:427
  29.3 17.1 %collective-permute-start.6 = (bf16[128,2048]{1,0:T(8,128)(2,1)S(1)}, bf16[128,2048]{1,0:T(8,128)(2,1)S(1)}, u32[]{:S(2)}, u32[]{:S(2)}) collective-permute-start(bf16[128,2048]{1,0:T(8,128)(2,1)S(1)} %get-tuple-element.27), channel_id=1, source_target_pairs={{0,4},{4,0},{8,12},{12,8},{16,20},{20,16},{24,28},{28,24},{1,5},{5... | collective-permute-start | bytes 1572872 | tf_op jit(solution)/shard_map/ppermute | solution.py:376
  39.7 22.5 %collective-permute-start.10 = (s16[1616,128]{1,0:T(8,128)(2,1)S(1)}, s16[1616,128]{1,0:T(8,128)(2,1)S(1)}, u32[]{:S(2)}, u32[]{:S(2)}) collective-permute-start(s16[1616,128]{1,0:T(8,128)(2,1)S(1)} %get-tuple-element.30.rest_1_), channel_id=1, source_target_pairs={{0,8},{4,12},{8,0},{12,4},{16,24},{20,28},{24,16},{28,20},{1,9},{5... | collective-permute-start | bytes 1241096 | tf_op jit(solution)/shard_map/ppermute | solution.py:427
  41.8 20.4 %collective-permute-start.12 = (bf16[128,1024]{1,0:T(8,128)(2,1)S(1)}, bf16[128,1024]{1,0:T(8,128)(2,1)S(1)}, u32[]{:S(2)}, u32[]{:S(2)}) collective-permute-start(bf16[128,1024]{1,0:T(8,128)(2,1)S(1)} %collective-permute-done.5.rest_3_), channel_id=1, source_target_pairs={{0,4},{4,0},{8,12},{12,8},{16,20},{20,16},{24,28},{28,24},{1,5},{5... | collective-permute-start | bytes 786440 | tf_op jit(solution)/shard_map/ppermute | solution.py:433
  42.4 12.2 %copy-start.1 = (s32[2,1024]{1,0:T(2,128)S(1)}, s32[2,1024]{1,0:T(2,128)}, u32[]{:S(2)}) copy-start(s32[2,1024]{1,0:T(2,128)} %pairs_ref.1) | copy-start | bytes 24580
  42.4 19.8 %collective-permute-start.11 = (bf16[128,2048]{1,0:T(8,128)(2,1)S(1)}, bf16[128,2048]{1,0:T(8,128)(2,1)S(1)}, u32[]{:S(2)}, u32[]{:S(2)}) collective-permute-start(bf16[128,2048]{1,0:T(8,128)(2,1)S(1)} %get-tuple-element.31), channel_id=1, source_target_pairs={{0,4},{4,0},{8,12},{12,8},{16,20},{20,16},{24,28},{28,24},{1,5},{5... | collective-permute-start | bytes 1572872 | tf_op jit(solution)/shard_map/ppermute | solution.py:376
  48.4 21.8 %collective-permute-start.16 = (s16[1616,128]{1,0:T(8,128)(2,1)S(1)}, s16[1616,128]{1,0:T(8,128)(2,1)S(1)}, u32[]{:S(2)}, u32[]{:S(2)}) collective-permute-start(s16[1616,128]{1,0:T(8,128)(2,1)S(1)} %sum_step_04.1.rest_0_.rest_2_), channel_id=1, source_target_pairs={{8,16},{12,20},{16,8},{20,12},{9,17},{13,21},{17,9},{21,13},{10,18... | collective-permute-start | bytes 1241096 | tf_op jit(solution)/shard_map/ppermute | solution.py:427
  49.1 21.1 %collective-permute-start.15 = (s16[1616,128]{1,0:T(8,128)(2,1)S(1)}, s16[1616,128]{1,0:T(8,128)(2,1)S(1)}, u32[]{:S(2)}, u32[]{:S(2)}) collective-permute-start(s16[1616,128]{1,0:T(8,128)(2,1)S(1)} %sum_step_04.1.rest_0_.rest_2_), channel_id=1, source_target_pairs={{0,8},{4,12},{24,16},{28,20},{1,9},{5,13},{25,17},{29,21},{2,10},{... | collective-permute-start | bytes 1241096 | tf_op jit(solution)/shard_map/ppermute | solution.py:427
  64.7 11.1 %collective-permute-start.17 = (s16[1616,128]{1,0:T(8,128)(2,1)S(1)}, s16[1616,128]{1,0:T(8,128)(2,1)S(1)}, u32[]{:S(2)}, u32[]{:S(2)}) collective-permute-start(s16[1616,128]{1,0:T(8,128)(2,1)S(1)} %get-tuple-element.34.rest_1_), channel_id=1, source_target_pairs={{8,16},{12,20},{16,8},{20,12},{9,17},{13,21},{17,9},{21,13},{10,18... | collective-permute-start | bytes 1241096 | tf_op jit(solution)/shard_map/ppermute | solution.py:427
  65.3 12.3 %collective-permute-start.14 = (s16[1616,128]{1,0:T(8,128)(2,1)S(1)}, s16[1616,128]{1,0:T(8,128)(2,1)S(1)}, u32[]{:S(2)}, u32[]{:S(2)}) collective-permute-start(s16[1616,128]{1,0:T(8,128)(2,1)S(1)} %get-tuple-element.34.rest_1_), channel_id=1, source_target_pairs={{0,8},{4,12},{24,16},{28,20},{1,9},{5,13},{25,17},{29,21},{2,10},{... | collective-permute-start | bytes 1241096 | tf_op jit(solution)/shard_map/ppermute | solution.py:427
  69.6 19.8 %collective-permute-start.13 = (bf16[128,4096]{1,0:T(8,128)(2,1)S(1)}, bf16[128,4096]{1,0:T(8,128)(2,1)S(1)}, u32[]{:S(2)}, u32[]{:S(2)}) collective-permute-start(bf16[128,4096]{1,0:T(8,128)(2,1)S(1)} %get-tuple-element.33), channel_id=1, source_target_pairs={{0,4},{4,0},{8,12},{12,8},{16,20},{20,16},{24,28},{28,24},{1,5},{5... | collective-permute-start | bytes 3145736 | tf_op jit(solution)/shard_map/ppermute | solution.py:376
  72.2 13.8 %collective-permute-start.19 = (s16[1616,128]{1,0:T(8,128)(2,1)S(1)}, s16[1616,128]{1,0:T(8,128)(2,1)S(1)}, u32[]{:S(2)}, u32[]{:S(2)}) collective-permute-start(s16[1616,128]{1,0:T(8,128)(2,1)S(1)} %sum_step_06.1.rest_2_), channel_id=1, source_target_pairs={{8,16},{12,20},{16,8},{20,12},{9,17},{13,21},{17,9},{21,13},{10,18... | collective-permute-start | bytes 1241096 | tf_op jit(solution)/shard_map/ppermute | solution.py:427
  72.9 13.6 %collective-permute-start.18 = (s16[1616,128]{1,0:T(8,128)(2,1)S(1)}, s16[1616,128]{1,0:T(8,128)(2,1)S(1)}, u32[]{:S(2)}, u32[]{:S(2)}) collective-permute-start(s16[1616,128]{1,0:T(8,128)(2,1)S(1)} %sum_step_06.1.rest_2_), channel_id=1, source_target_pairs={{0,8},{4,12},{24,16},{28,20},{1,9},{5,13},{25,17},{29,21},{2,10},{... | collective-permute-start | bytes 1241096 | tf_op jit(solution)/shard_map/ppermute | solution.py:427
  79.7 13.9 %collective-permute-start.21 = (s16[1616,128]{1,0:T(8,128)(2,1)S(1)}, s16[1616,128]{1,0:T(8,128)(2,1)S(1)}, u32[]{:S(2)}, u32[]{:S(2)}) collective-permute-start(s16[1616,128]{1,0:T(8,128)(2,1)S(1)} %sum_step_07.1.rest_2_), channel_id=1, source_target_pairs={{8,16},{12,20},{16,8},{20,12},{9,17},{13,21},{17,9},{21,13},{10,18... | collective-permute-start | bytes 1241096 | tf_op jit(solution)/shard_map/ppermute | solution.py:427
  80.4 15.6 %collective-permute-start.20 = (s16[1616,128]{1,0:T(8,128)(2,1)S(1)}, s16[1616,128]{1,0:T(8,128)(2,1)S(1)}, u32[]{:S(2)}, u32[]{:S(2)}) collective-permute-start(s16[1616,128]{1,0:T(8,128)(2,1)S(1)} %sum_step_07.1.rest_2_), channel_id=1, source_target_pairs={{0,8},{4,12},{24,16},{28,20},{1,9},{5,13},{25,17},{29,21},{2,10},{... | collective-permute-start | bytes 1241096 | tf_op jit(solution)/shard_map/ppermute | solution.py:427
  91.6 13.4 %collective-permute-start.23 = (s16[1616,128]{1,0:T(8,128)(2,1)S(1)}, s16[1616,128]{1,0:T(8,128)(2,1)S(1)}, u32[]{:S(2)}, u32[]{:S(2)}) collective-permute-start(s16[1616,128]{1,0:T(8,128)(2,1)S(1)} %get-tuple-element.35.rest_2_), channel_id=1, source_target_pairs={{0,8},{4,12},{8,24},{12,28},{16,0},{20,4},{24,16},{28,20},{1,9},{5... | collective-permute-start | bytes 1241096 | tf_op jit(solution)/shard_map/ppermute | solution.py:427
  91.7 14.2 %collective-permute-start.24 = (bf16[128,2048]{1,0:T(8,128)(2,1)S(1)}, bf16[128,2048]{1,0:T(8,128)(2,1)S(1)}, u32[]{:S(2)}, u32[]{:S(2)}) collective-permute-start(bf16[128,2048]{1,0:T(8,128)(2,1)S(1)} %get-tuple-element.38), channel_id=1, source_target_pairs={{0,4},{4,0},{8,12},{12,8},{16,20},{20,16},{24,28},{28,24},{1,5},{5... | collective-permute-start | bytes 1572872 | tf_op jit(solution)/shard_map/ppermute | solution.py:376
  98.2 16.8 %collective-permute-start.25 = (s16[1616,128]{1,0:T(8,128)(2,1)S(1)}, s16[1616,128]{1,0:T(8,128)(2,1)S(1)}, u32[]{:S(2)}, u32[]{:S(2)}) collective-permute-start(s16[1616,128]{1,0:T(8,128)(2,1)S(1)} %get-tuple-element.37.rest_1_), channel_id=1, source_target_pairs={{0,8},{4,12},{8,24},{12,28},{16,0},{20,4},{24,16},{28,20},{1,9},{5... | collective-permute-start | bytes 1241096 | tf_op jit(solution)/shard_map/ppermute | solution.py:427
  100.7 21.1 %collective-permute-start.22 = (bf16[128,2048]{1,0:T(8,128)(2,1)S(1)}, bf16[128,2048]{1,0:T(8,128)(2,1)S(1)}, u32[]{:S(2)}, u32[]{:S(2)}) collective-permute-start(bf16[128,2048]{1,0:T(8,128)(2,1)S(1)} %get-tuple-element.36), channel_id=1, source_target_pairs={{0,4},{4,0},{8,12},{12,8},{16,20},{20,16},{24,28},{28,24},{1,5},{5... | collective-permute-start | bytes 1572872 | tf_op jit(solution)/shard_map/ppermute | solution.py:376
  107.9 14.7 %collective-permute-start.27 = (s16[1616,128]{1,0:T(8,128)(2,1)S(1)}, s16[1616,128]{1,0:T(8,128)(2,1)S(1)}, u32[]{:S(2)}, u32[]{:S(2)}) collective-permute-start(s16[1616,128]{1,0:T(8,128)(2,1)S(1)} %sum_step_10.1.rest_1_), channel_id=1, source_target_pairs={{0,8},{4,12},{8,24},{12,28},{16,0},{20,4},{24,16},{28,20},{1,9},{5... | collective-permute-start | bytes 1241096 | tf_op jit(solution)/shard_map/ppermute | solution.py:427
  116.9 11.3 %collective-permute-start.26 = (s16[1616,128]{1,0:T(8,128)(2,1)S(1)}, s16[1616,128]{1,0:T(8,128)(2,1)S(1)}, u32[]{:S(2)}, u32[]{:S(2)}) collective-permute-start(s16[1616,128]{1,0:T(8,128)(2,1)S(1)} %sum_step_11.1), channel_id=1, source_target_pairs={{0,8},{4,12},{8,24},{12,28},{16,0},{20,4},{24,16},{28,20},{1,9},{5... | collective-permute-start | bytes 1241096 | tf_op jit(solution)/shard_map/ppermute | solution.py:427

commit v2 on v1

--- a/solution.py
+++ b/solution.py
@@ -22,10 +22,10 @@
 HALVES = 2
 FLIGHT = 2
 FIRST_SWAP = (0, 2)
-SWAPS = {0: (2, 1), 1: (4, 2), 2: (6, 2), 5: (8, 4), 8: (12, 2), 9: (14, 2)}
-SWAP_WAITS = {5: 6, 10: 12}
+SWAPS = {0: (2, 1), 1: (4, 2), 2: (6, 2), 6: (8, 2), 8: (10, 2), 9: (12, 2), 10: (14, 2)}
+SWAP_WAITS = {}
 RAW_STEP, RAW_WAIT = 2, 5
-INVERSE_STEP = 5
+INVERSE_STEP = 0
 FINISHED_AHEAD = 1
 ME, PARTNER, NEAR, NEAR_PARTNER, INNER, FIXED = 0, 1, 2, 3, 4, 5
 LANES = 128
@@ -417,7 +417,7 @@
         if at == RAW_WAIT:
             after.append(raw[1])
         if at == INVERSE_STEP:
-            inverse = invert_classes(date_pairs, run_counts, [coded])
+            inverse = invert_classes(date_pairs, run_counts, [counts if coded is None else coded])
             after.append(inverse)
         if at == steps - 1:
             for part in range(FINISHED_AHEAD):

time: 133 us -> 133 us (level)
    ppermute x15, waiting for transfers between devices: 19.8 us -> 16.3 us  [solve_by_sums(): lax.ppermute(coded, 'ifg', line_permutation(links))]
    ppermute x7 -> x8, waiting for transfers between devices: 9.82 us -> 13 us  [swapped(): here = lax.ppermute(away, 'ifg', swap)]
    ppermute x7 -> x8, starting transfers between devices: 10 us -> 6.85 us  [swapped(): here = lax.ppermute(away, 'ifg', swap)]
    ppermute x15, starting transfers between devices: 32.9 us -> 35.2 us  [solve_by_sums(): lax.ppermute(coded, 'ifg', line_permutation(links))]
  transfers between devices with their start and end apart: 28 -> 29, of which waited for: 11 -> 10; matrix products, arithmetic and copies ran while one was open for 2% -> 2% of each run, Pallas kernels for 31% -> 31%
where the time goes in v2:
time: 133 us
  starting transfers between devices  52.3 us (39%)
  Pallas kernels  45.3 us (34%)
  waiting for transfers between devices  29.4 us (22%)
  local copies, waits for them, and re-layouts  4.38 us (3%)
    ppermute x15, starting transfers between devices, solve_by_sums(): lax.ppermute(coded, 'ifg', line_permutation(links))  35.2 us
    pallas_call x11, Pallas kernels, step(): pl.pallas_call(functools.partial(step_kernel, at, layout, len(earlier), s...  23.3 us
    ppermute x15, waiting for transfers between devices, solve_by_sums(): lax.ppermute(coded, 'ifg', line_permutation(links))  16.3 us
    pallas_call x4, Pallas kernels, finish(): pl.pallas_call(functools.partial(finish_kernel, at, layout, tiles, len(ra...  14.5 us
    ppermute x8, waiting for transfers between devices, swapped(): here = lax.ppermute(away, 'ifg', swap)  13 us
    pallas_call x1, Pallas kernels, invert_classes(): pl.pallas_call(inverse_kernel, out_shape=jax.ShapeDtypeStruct(shape, F32)...  7.56 us
    ppermute x8, starting transfers between devices, swapped(): here = lax.ppermute(away, 'ifg', swap)  6.85 us
    ppermute x3, starting transfers between devices, solve_by_sums(): counts.append(lax.ppermute(run_counts, 'ifg', line_permutation(links)))  6.11 us
  transfers between devices with their start and end apart: 29, of which 10 were waited for; matrix products, arithmetic and copies ran while one was open for 2% of the time, Pallas kernels for 31%

profile of v2, /device:TPU:0, one launch (start us, length us, event | category | flops | bytes accessed | tf_op | source)
XLA Modules:
  0.0 132.6 jit_solution(2084278986238046172)
XLA Ops:
  0.0 1.1 dynamic-slice_bitcast_fusion
  1.2 0.8 fusion.counts_ref
  2.1 5.1 %collective-permute-start.2 = (s32[2]{0:T(128)S(1)}, s32[2]{0:T(128)S(1)}, u32[]{:S(2)}, u32[]{:S(2)}) collective-permute-start(s32[2]{0:T(128)S(1)} %fusion.counts_ref), channel_id=1, source_target_pairs={{0,24},{4,28},{8,0},{12,4},{16,8},{20,12},{24,16},{28,20},{1,25},{... | collective-permute-start | bytes 32 | tf_op jit(solution)/shard_map/ppermute | solution.py:394
  7.2 1.0 collective-permute-start
  8.2 1.5 %collective-permute-start.3 = (bf16[128,2048]{1,0:T(8,128)(2,1)S(1)}, bf16[128,2048]{1,0:T(8,128)(2,1)S(1)}, u32[]{:S(2)}, u32[]{:S(2)}) collective-permute-start(bf16[128,2048]{1,0:T(8,128)(2,1)S(1)} %dynamic-slice_bitcast_fusion), channel_id=1, source_target_pairs={{0,4},{4,0},{8,12},{12,8},{16,20},{20,16},{24,28},{28,24},{1,5},{5... | collective-permute-start | bytes 1572872 | tf_op jit(solution)/shard_map/ppermute | solution.py:376
  9.7 1.1 dynamic-slice_bitcast_fusion.1
  10.7 2.5 %collective-permute-start.6 = (bf16[128,1024]{1,0:T(8,128)(2,1)S(1)}, bf16[128,1024]{1,0:T(8,128)(2,1)S(1)}, u32[]{:S(2)}, u32[]{:S(2)}) collective-permute-start(bf16[128,1024]{1,0:T(8,128)(2,1)S(1)} %get-tuple-element.45), channel_id=1, source_target_pairs={{0,8},{4,12},{8,0},{12,4},{16,24},{20,28},{24,16},{28,20},{1,9},{5... | collective-permute-start | bytes 786440 | tf_op jit(solution)/shard_map/ppermute | solution.py:398
  13.3 0.7 constant_dynamic-slice_fusion.3
  14.2 0.7 fusion.1.table
  14.9 0.7 copy-done.1
  15.6 7.6 %invert_classes_0.1.rest_1_.inverse_ref = f32[2,256,256]{2,1,0:T(8,128)S(1)} custom-call(s32[2]{0:T(128)S(1)} %fusion.counts_ref, s32[2,1024]{1,0:T(2,128)S(1)} %copy-done.1, s32[8]{0:T(128)S(1)} %pad_add_fusion.1.rest_0_.counts), custom_call_target="tpu_custom_call" | custom-call | flops 1024 | bytes 1024 | tf_op jit(solution)/shard_map/invert_classes_0/pallas_call | solution.py:103
  23.2 2.1 %sum_step_00.1 = (s16[1616,128]{1,0:T(8,128)(2,1)S(1)}, bf16[128,1024]{1,0:T(8,128)(2,1)S(1)}) custom-call(s32[53]{0:T(128)S(1)} %fusion.1.table, s32[8]{0:T(128)S(1)} %pad_add_fusion.1.rest_0_.counts, s32[2,512]{1,0:T(2,128)S(1)} %pad_add_fusion.pairs_ref, bf16[128,32768]{1,0:T(8,128)(2,1)} %bitcast.12, ...), custom_call_target="tpu_custom_call" | custom-call | flops 10000000000 | bytes 30000000 | tf_op jit(solution)/shard_map/sum_step_00/pallas_call | solution.py:245
  25.3 2.5 %collective-permute-start.7 = (s16[1616,128]{1,0:T(8,128)(2,1)S(1)}, s16[1616,128]{1,0:T(8,128)(2,1)S(1)}, u32[]{:S(2)}, u32[]{:S(2)}) collective-permute-start(s16[1616,128]{1,0:T(8,128)(2,1)S(1)} %get-tuple-element.27.rest_1_), channel_id=1, source_target_pairs={{0,8},{4,12},{8,0},{12,4},{16,24},{20,28},{24,16},{28,20},{1,9},{5... | collective-permute-start | bytes 1241096 | tf_op jit(solution)/shard_map/ppermute | solution.py:427
  27.8 2.2 %sum_step_01.1 = (s16[1616,128]{1,0:T(8,128)(2,1)S(1)}, bf16[128,2048]{1,0:T(8,128)(2,1)S(1)}) custom-call(s32[53]{0:T(128)S(1)} %fusion.1.table, s32[8]{0:T(128)S(1)} %pad_add_fusion.1.rest_0_.counts, s32[2,512]{1,0:T(2,128)S(1)} %pad_add_fusion.pairs_ref, bf16[128,32768]{1,0:T(8,128)(2,1)} %bitcast.14, ...), custom_call_target="tpu_custom_call" | custom-call | flops 10000000000 | bytes 30000000 | tf_op jit(solution)/shard_map/sum_step_01/pallas_call | solution.py:245
  30.1 1.6 %collective-permute-start.10 = (bf16[128,2048]{1,0:T(8,128)(2,1)S(1)}, bf16[128,2048]{1,0:T(8,128)(2,1)S(1)}, u32[]{:S(2)}, u32[]{:S(2)}) collective-permute-start(bf16[128,2048]{1,0:T(8,128)(2,1)S(1)} %get-tuple-element.33), channel_id=1, source_target_pairs={{0,4},{4,0},{8,12},{12,8},{16,20},{20,16},{24,28},{28,24},{1,5},{5... | collective-permute-start | bytes 1572872 | tf_op jit(solution)/shard_map/ppermute | solution.py:376
  31.6 2.2 %collective-permute-done.4.partner_ref = bf16[128,1024]{1,0:T(8,128)(2,1)S(1)} collective-permute-done((bf16[128,1024]{1,0:T(8,128)(2,1)S(1)}, bf16[128,1024]{1,0:T(8,128)(2,1)S(1)}, u32[]{:S(2)}, u32[]{:S(2)}) %collective-permute-start.4) | collective-permute-done | bytes 262176 | tf_op jit(solution)/shard_map/ppermute | solution.py:376
  33.8 4.5 %collective-permute-done.7.rest_2_.rest_0_.rest_1_ = s16[1616,128]{1,0:T(8,128)(2,1)S(1)} collective-permute-done((s16[1616,128]{1,0:T(8,128)(2,1)S(1)}, s16[1616,128]{1,0:T(8,128)(2,1)S(1)}, u32[]{:S(2)}, u32[]{:S(2)}) %collective-permute-start.7) | collective-permute-done | bytes 413728 | tf_op jit(solution)/shard_map/ppermute | solution.py:427
  38.3 2.2 %sum_step_02.1 = (s16[1616,128]{1,0:T(8,128)(2,1)S(1)}, bf16[128,2048]{1,0:T(8,128)(2,1)S(1)}) custom-call(s32[53]{0:T(128)S(1)} %fusion.1.table, s32[8]{0:T(128)S(1)} %pad_add_fusion.1.rest_0_.counts, s32[2,512]{1,0:T(2,128)S(1)} %pad_add_fusion.pairs_ref, bf16[128,32768]{1,0:T(8,128)(2,1)} %bitcast.16, ...), custom_call_target="tpu_custom_call" | custom-call | flops 10000000000 | bytes 30000000 | tf_op jit(solution)/shard_map/sum_step_02/pallas_call | solution.py:245
  40.5 2.1 %collective-permute-start.9 = (s16[1616,128]{1,0:T(8,128)(2,1)S(1)}, s16[1616,128]{1,0:T(8,128)(2,1)S(1)}, u32[]{:S(2)}, u32[]{:S(2)}) collective-permute-start(s16[1616,128]{1,0:T(8,128)(2,1)S(1)} %get-tuple-element.32.rest_1_), channel_id=1, source_target_pairs={{0,8},{4,12},{8,0},{12,4},{16,24},{20,28},{24,16},{28,20},{1,9},{5... | collective-permute-start | bytes 1241096 | tf_op jit(solution)/shard_map/ppermute | solution.py:427
  42.6 1.5 %collective-permute-start.12 = (bf16[128,1024]{1,0:T(8,128)(2,1)S(1)}, bf16[128,1024]{1,0:T(8,128)(2,1)S(1)}, u32[]{:S(2)}, u32[]{:S(2)}) collective-permute-start(bf16[128,1024]{1,0:T(8,128)(2,1)S(1)} %collective-permute-done.6.rest_3_), channel_id=1, source_target_pairs={{0,4},{4,0},{8,12},{12,8},{16,20},{20,16},{24,28},{28,24},{1,5},{5... | collective-permute-start | bytes 786440 | tf_op jit(solution)/shard_map/ppermute | solution.py:433
  44.6 2.6 %collective-permute-done.11.rest_2_.rest_0_.rest_1_ = s16[1616,128]{1,0:T(8,128)(2,1)S(1)} collective-permute-done((s16[1616,128]{1,0:T(8,128)(2,1)S(1)}, s16[1616,128]{1,0:T(8,128)(2,1)S(1)}, u32[]{:S(2)}, u32[]{:S(2)}) %collective-permute-start.11) | collective-permute-done | bytes 413728 | tf_op jit(solution)/shard_map/ppermute | solution.py:427
  47.2 2.0 %sum_step_04.1.rest_1_ = s16[1616,128]{1,0:T(8,128)(2,1)S(1)} custom-call(s32[53]{0:T(128)S(1)} %fusion.1.table, s32[8]{0:T(128)S(1)} %pad_add_fusion.1.rest_0_.counts, s32[2,512]{1,0:T(2,128)S(1)} %pad_add_fusion.pairs_ref, bf16[128,32768]{1,0:T(8,128)(2,1)} %bitcast.18, bf16[128,2048]{1,0:T(8,128)(2,1)S(1)} %collective-permute-done.10.partner_ref, ...), custom_call_target="tpu_custom_call" | custom-call | flops 10000000000 | bytes 30000000 | tf_op jit(solution)/shard_map/sum_step_04/pallas_call | solution.py:245
  49.9 5.2 %collective-permute-start.13 = (s16[1616,128]{1,0:T(8,128)(2,1)S(1)}, s16[1616,128]{1,0:T(8,128)(2,1)S(1)}, u32[]{:S(2)}, u32[]{:S(2)}) collective-permute-start(s16[1616,128]{1,0:T(8,128)(2,1)S(1)} %sum_step_04.1.rest_1_), channel_id=1, source_target_pairs={{0,8},{4,12},{24,16},{28,20},{1,9},{5,13},{25,17},{29,21},{2,10},{... | collective-permute-start | bytes 1241096 | tf_op jit(solution)/shard_map/ppermute | solution.py:427
  55.1 2.0 %sum_step_05.1.rest_2_ = s16[1616,128]{1,0:T(8,128)(2,1)S(1)} custom-call(s32[53]{0:T(128)S(1)} %fusion.1.table, s32[8]{0:T(128)S(1)} %pad_add_fusion.1.rest_0_.counts, s32[2,512]{1,0:T(2,128)S(1)} %pad_add_fusion.pairs_ref, bf16[128,32768]{1,0:T(8,128)(2,1)} %bitcast.19, bf16[128,2048]{1,0:T(8,128)(2,1)S(1)} %collective-permute-done.10.partner_ref, ...), custom_call_target="tpu_custom_call" | custom-call | flops 10000000000 | bytes 30000000 | tf_op jit(solution)/shard_map/sum_step_05/pallas_call | solution.py:245
  57.8 5.7 %collective-permute-start.16 = (s16[1616,128]{1,0:T(8,128)(2,1)S(1)}, s16[1616,128]{1,0:T(8,128)(2,1)S(1)}, u32[]{:S(2)}, u32[]{:S(2)}) collective-permute-start(s16[1616,128]{1,0:T(8,128)(2,1)S(1)} %sum_step_05.1.rest_2_), channel_id=1, source_target_pairs={{0,8},{4,12},{24,16},{28,20},{1,9},{5,13},{25,17},{29,21},{2,10},{... | collective-permute-start | bytes 1241096 | tf_op jit(solution)/shard_map/ppermute | solution.py:427
  63.5 2.2 %sum_step_06.1 = (s16[1616,128]{1,0:T(8,128)(2,1)S(1)}, bf16[128,2048]{1,0:T(8,128)(2,1)S(1)}) custom-call(s32[53]{0:T(128)S(1)} %fusion.1.table, s32[8]{0:T(128)S(1)} %pad_add_fusion.1.rest_0_.counts, s32[2,512]{1,0:T(2,128)S(1)} %pad_add_fusion.pairs_ref, bf16[128,32768]{1,0:T(8,128)(2,1)} %bitcast.21, ...), custom_call_target="tpu_custom_call" | custom-call | flops 10000000000 | bytes 30000000 | tf_op jit(solution)/shard_map/sum_step_06/pallas_call | solution.py:245
  66.4 8.9 %collective-permute-start.18 = (s16[1616,128]{1,0:T(8,128)(2,1)S(1)}, s16[1616,128]{1,0:T(8,128)(2,1)S(1)}, u32[]{:S(2)}, u32[]{:S(2)}) collective-permute-start(s16[1616,128]{1,0:T(8,128)(2,1)S(1)} %get-tuple-element.36.rest_2_), channel_id=1, source_target_pairs={{0,8},{4,12},{24,16},{28,20},{1,9},{5,13},{25,17},{29,21},{2,10},{... | collective-permute-start | bytes 1241096 | tf_op jit(solution)/shard_map/ppermute | solution.py:427
  75.3 1.0 collective-permute-start.15
  76.3 2.0 %sum_step_07.1.rest_2_ = s16[1616,128]{1,0:T(8,128)(2,1)S(1)} custom-call(s32[53]{0:T(128)S(1)} %fusion.1.table, s32[8]{0:T(128)S(1)} %pad_add_fusion.1.rest_0_.counts, s32[2,512]{1,0:T(2,128)S(1)} %pad_add_fusion.pairs_ref, bf16[128,32768]{1,0:T(8,128)(2,1)} %bitcast.22, bf16[128,2048]{1,0:T(8,128)(2,1)S(1)} %collective-permute-done.8.partner_ref, ...), custom_call_target="tpu_custom_call" | custom-call | flops 10000000000 | bytes 30000000 | tf_op jit(solution)/shard_map/sum_step_07/pallas_call | solution.py:245
  79.1 4.8 %collective-permute-start.21 = (s16[1616,128]{1,0:T(8,128)(2,1)S(1)}, s16[1616,128]{1,0:T(8,128)(2,1)S(1)}, u32[]{:S(2)}, u32[]{:S(2)}) collective-permute-start(s16[1616,128]{1,0:T(8,128)(2,1)S(1)} %sum_step_07.1.rest_2_), channel_id=1, source_target_pairs={{0,8},{4,12},{24,16},{28,20},{1,9},{5,13},{25,17},{29,21},{2,10},{... | collective-permute-start | bytes 1241096 | tf_op jit(solution)/shard_map/ppermute | solution.py:427
  83.9 1.3 collective-permute-done.18.rest_3_.rest_1_
  85.2 2.8 %collective-permute-done.15.partner_ref = bf16[128,2048]{1,0:T(8,128)(2,1)S(1)} collective-permute-done((bf16[128,2048]{1,0:T(8,128)(2,1)S(1)}, bf16[128,2048]{1,0:T(8,128)(2,1)S(1)}, u32[]{:S(2)}, u32[]{:S(2)}) %collective-permute-start.15) | collective-permute-done | bytes 524320 | tf_op jit(solution)/shard_map/ppermute | solution.py:376
  88.0 2.2 %sum_step_08.1 = (s16[1616,128]{1,0:T(8,128)(2,1)S(1)}, bf16[128,2048]{1,0:T(8,128)(2,1)S(1)}) custom-call(s32[53]{0:T(128)S(1)} %fusion.1.table, s32[8]{0:T(128)S(1)} %pad_add_fusion.1.rest_0_.counts, s32[2,512]{1,0:T(2,128)S(1)} %pad_add_fusion.pairs_ref, bf16[128,32768]{1,0:T(8,128)(2,1)} %bitcast.23, ...), custom_call_target="tpu_custom_call" | custom-call | flops 10000000000 | bytes 30000000 | tf_op jit(solution)/shard_map/sum_step_08/pallas_call | solution.py:245
  90.8 3.3 %collective-permute-done.21.rest_3_.rest_0_ = s16[1616,128]{1,0:T(8,128)(2,1)S(1)} collective-permute-done((s16[1616,128]{1,0:T(8,128)(2,1)S(1)}, s16[1616,128]{1,0:T(8,128)(2,1)S(1)}, u32[]{:S(2)}, u32[]{:S(2)}) %collective-permute-start.21) | collective-permute-done | bytes 413728 | tf_op jit(solution)/shard_map/ppermute | solution.py:427
  94.1 2.2 %sum_step_09.1 = (s16[1616,128]{1,0:T(8,128)(2,1)S(1)}, bf16[128,2048]{1,0:T(8,128)(2,1)S(1)}) custom-call(s32[53]{0:T(128)S(1)} %fusion.1.table, s32[8]{0:T(128)S(1)} %pad_add_fusion.1.rest_0_.counts, s32[2,512]{1,0:T(2,128)S(1)} %pad_add_fusion.pairs_ref, bf16[128,32768]{1,0:T(8,128)(2,1)} %bitcast.25, ...), custom_call_target="tpu_custom_call" | custom-call | flops 10000000000 | bytes 30000000 | tf_op jit(solution)/shard_map/sum_step_09/pallas_call | solution.py:245
  96.3 2.5 %collective-permute-start.25 = (s16[1616,128]{1,0:T(8,128)(2,1)S(1)}, s16[1616,128]{1,0:T(8,128)(2,1)S(1)}, u32[]{:S(2)}, u32[]{:S(2)}) collective-permute-start(s16[1616,128]{1,0:T(8,128)(2,1)S(1)} %get-tuple-element.39.rest_2_), channel_id=1, source_target_pairs={{0,8},{4,12},{8,24},{12,28},{16,0},{20,4},{24,16},{28,20},{1,9},{5... | collective-permute-start | bytes 1241096 | tf_op jit(solution)/shard_map/ppermute | solution.py:427
  98.8 0.9 collective-permute-start.26
  99.7 3.3 %collective-permute-done.23.rest_3_.rest_4_.rest_5_ = s16[1616,128]{1,0:T(8,128)(2,1)S(1)} collective-permute-done((s16[1616,128]{1,0:T(8,128)(2,1)S(1)}, s16[1616,128]{1,0:T(8,128)(2,1)S(1)}, u32[]{:S(2)}, u32[]{:S(2)}) %collective-permute-start.23) | collective-permute-done | bytes 413728 | tf_op jit(solution)/shard_map/ppermute | solution.py:427
  102.9 2.3 %collective-permute-done.20.partner_ref = bf16[128,2048]{1,0:T(8,128)(2,1)S(1)} collective-permute-done((bf16[128,2048]{1,0:T(8,128)(2,1)S(1)}, bf16[128,2048]{1,0:T(8,128)(2,1)S(1)}, u32[]{:S(2)}, u32[]{:S(2)}) %collective-permute-start.20) | collective-permute-done | bytes 524320 | tf_op jit(solution)/shard_map/ppermute | solution.py:376
  105.3 2.2 %sum_step_10.1 = (s16[1616,128]{1,0:T(8,128)(2,1)S(1)}, bf16[128,2048]{1,0:T(8,128)(2,1)S(1)}) custom-call(s32[53]{0:T(128)S(1)} %fusion.1.table, s32[8]{0:T(128)S(1)} %pad_add_fusion.1.rest_0_.counts, s32[2,512]{1,0:T(2,128)S(1)} %pad_add_fusion.pairs_ref, bf16[128,32768]{1,0:T(8,128)(2,1)} %bitcast.27, ...), custom_call_target="tpu_custom_call" | custom-call | flops 10000000000 | bytes 30000000 | tf_op jit(solution)/shard_map/sum_step_10/pallas_call | solution.py:245
  107.7 0.8 collective-permute-start.24
  108.5 5.7 %collective-permute-done.26.partner_ref = bf16[128,2048]{1,0:T(8,128)(2,1)S(1)} collective-permute-done((bf16[128,2048]{1,0:T(8,128)(2,1)S(1)}, bf16[128,2048]{1,0:T(8,128)(2,1)S(1)}, u32[]{:S(2)}, u32[]{:S(2)}) %collective-permute-start.26) | collective-permute-done | bytes 524320 | tf_op jit(solution)/shard_map/ppermute | solution.py:376
  114.2 3.5 %finish_0.1 = (f32[200,4096]{1,0:T(8,128)}, f32[8,128]{1,0:T(8,128)S(1)}) custom-call(s32[53]{0:T(128)S(1)} %fusion.1.table, s32[8]{0:T(128)S(1)} %pad_add_fusion.1.rest_0_.counts, s32[2,512]{1,0:T(2,128)S(1)} %pad_add_fusion.pairs_ref, bf16[128,32768]{1,0:T(8,128)(2,1)} %bitcast.29, bf16[128,2048]{1,0:T(8,128)(2,1)S(1)} %collective-permute-done.26.partner_ref, ...), custom_call_target="tpu_custom_call" | custom-call | flops 1024 | bytes 1024 | tf_op jit(solution)/shard_map/finish_0/pallas_call | solution.py:327
  117.8 2.0 %sum_step_11.1 = s16[1616,128]{1,0:T(8,128)(2,1)S(1)} custom-call(s32[53]{0:T(128)S(1)} %fusion.1.table, s32[8]{0:T(128)S(1)} %pad_add_fusion.1.rest_0_.counts, s32[2,512]{1,0:T(2,128)S(1)} %pad_add_fusion.pairs_ref, bf16[128,32768]{1,0:T(8,128)(2,1)} %bitcast.30, bf16[128,2048]{1,0:T(8,128)(2,1)S(1)} %collective-permute-done.20.partner_ref, ...), custom_call_target="tpu_custom_call" | custom-call | flops 10000000000 | bytes 30000000 | tf_op jit(solution)/shard_map/sum_step_11/pallas_call | solution.py:245
  120.2 3.6 %finish_1.1.rest_6_ = f32[200,4096]{1,0:T(8,128)} custom-call(s32[53]{0:T(128)S(1)} %fusion.1.table, s32[8]{0:T(128)S(1)} %pad_add_fusion.1.rest_0_.counts, s32[2,512]{1,0:T(2,128)S(1)} %pad_add_fusion.pairs_ref, bf16[128,32768]{1,0:T(8,128)(2,1)} %bitcast.31, ...), custom_call_target="tpu_custom_call", output_to_operand_aliasing={{}: (12, {})} | custom-call | flops 1024 | bytes 1024 | tf_op jit(solution)/shard_map/finish_1/pallas_call | solution.py:327
  123.7 3.6 %finish_2.1.rest_6_ = f32[200,4096]{1,0:T(8,128)} custom-call(s32[53]{0:T(128)S(1)} %fusion.1.table, s32[8]{0:T(128)S(1)} %pad_add_fusion.1.rest_0_.counts, s32[2,512]{1,0:T(2,128)S(1)} %pad_add_fusion.pairs_ref, bf16[128,32768]{1,0:T(8,128)(2,1)} %bitcast.32, ...), custom_call_target="tpu_custom_call", output_to_operand_aliasing={{}: (12, {})} | custom-call | flops 1024 | bytes 1024 | tf_op jit(solution)/shard_map/finish_2/pallas_call | solution.py:327
  127.3 1.4 %collective-permute-done.27.rest_4_.rest_5_ = s16[1616,128]{1,0:T(8,128)(2,1)S(1)} collective-permute-done((s16[1616,128]{1,0:T(8,128)(2,1)S(1)}, s16[1616,128]{1,0:T(8,128)(2,1)S(1)}, u32[]{:S(2)}, u32[]{:S(2)}) %collective-permute-start.27) | collective-permute-done | bytes 413728 | tf_op jit(solution)/shard_map/ppermute | solution.py:427
  128.7 3.9 %finish_3.1 = f32[200,4096]{1,0:T(8,128)} custom-call(s32[53]{0:T(128)S(1)} %fusion.1.table, s32[8]{0:T(128)S(1)} %pad_add_fusion.1.rest_0_.counts, s32[2,512]{1,0:T(2,128)S(1)} %pad_add_fusion.pairs_ref, bf16[128,32768]{1,0:T(8,128)(2,1)} %bitcast.33, bf16[128,2048]{1,0:T(8,128)(2,1)S(1)} %collective-permute-done.24.partner_ref, ...), custom_call_target="tpu_custom_call", output_to_operand_aliasing={{}: (12, {})} | custom-call | flops 1024 | bytes 1024 | tf_op jit(solution)/shard_map/finish_3/pallas_call | solution.py:327
  (39 shorter events, 4.9 us)
Async XLA Ops:
  0.0 1.1 copy-start
  2.1 11.9 %collective-permute-start.2 = (s32[2]{0:T(128)S(1)}, s32[2]{0:T(128)S(1)}, u32[]{:S(2)}, u32[]{:S(2)}) collective-permute-start(s32[2]{0:T(128)S(1)} %fusion.counts_ref), channel_id=1, source_target_pairs={{0,24},{4,28},{8,0},{12,4},{16,8},{20,12},{24,16},{28,20},{1,25},{... | collective-permute-start | bytes 32 | tf_op jit(solution)/shard_map/ppermute | solution.py:394
  7.1 7.0 %collective-permute-start.1 = (s32[2]{0:T(128)S(1)}, s32[2]{0:T(128)S(1)}, u32[]{:S(2)}, u32[]{:S(2)}) collective-permute-start(s32[2]{0:T(128)S(1)} %fusion.counts_ref), channel_id=1, source_target_pairs={{0,16},{4,20},{8,24},{12,28},{16,0},{20,4},{24,8},{28,12},{1,17},{... | collective-permute-start | bytes 32 | tf_op jit(solution)/shard_map/ppermute | solution.py:394
  7.2 7.0 %collective-permute-start = (s32[2]{0:T(128)S(1)}, s32[2]{0:T(128)S(1)}, u32[]{:S(2)}, u32[]{:S(2)}) collective-permute-start(s32[2]{0:T(128)S(1)} %fusion.counts_ref), channel_id=1, source_target_pairs={{0,8},{4,12},{8,16},{12,20},{16,24},{20,28},{24,0},{28,4},{1,9},{5... | collective-permute-start | bytes 32 | tf_op jit(solution)/shard_map/ppermute | solution.py:394
  8.2 15.0 %collective-permute-start.3 = (bf16[128,2048]{1,0:T(8,128)(2,1)S(1)}, bf16[128,2048]{1,0:T(8,128)(2,1)S(1)}, u32[]{:S(2)}, u32[]{:S(2)}) collective-permute-start(bf16[128,2048]{1,0:T(8,128)(2,1)S(1)} %dynamic-slice_bitcast_fusion), channel_id=1, source_target_pairs={{0,4},{4,0},{8,12},{12,8},{16,20},{20,16},{24,28},{28,24},{1,5},{5... | collective-permute-start | bytes 1572872 | tf_op jit(solution)/shard_map/ppermute | solution.py:376
  10.7 17.1 %collective-permute-start.6 = (bf16[128,1024]{1,0:T(8,128)(2,1)S(1)}, bf16[128,1024]{1,0:T(8,128)(2,1)S(1)}, u32[]{:S(2)}, u32[]{:S(2)}) collective-permute-start(bf16[128,1024]{1,0:T(8,128)(2,1)S(1)} %get-tuple-element.45), channel_id=1, source_target_pairs={{0,8},{4,12},{8,0},{12,4},{16,24},{20,28},{24,16},{28,20},{1,9},{5... | collective-permute-start | bytes 786440 | tf_op jit(solution)/shard_map/ppermute | solution.py:398
  14.0 13.8 %collective-permute-start.5 = (bf16[128,1024]{1,0:T(8,128)(2,1)S(1)}, bf16[128,1024]{1,0:T(8,128)(2,1)S(1)}, u32[]{:S(2)}, u32[]{:S(2)}) collective-permute-start(bf16[128,1024]{1,0:T(8,128)(2,1)S(1)} %get-tuple-element.46), channel_id=1, source_target_pairs={{0,8},{4,12},{8,0},{12,4},{16,24},{20,28},{24,16},{28,20},{1,9},{5... | collective-permute-start | bytes 786440 | tf_op jit(solution)/shard_map/ppermute | solution.py:399
  14.9 0.7 copy-start.1
  25.2 8.6 %collective-permute-start.4 = (bf16[128,1024]{1,0:T(8,128)(2,1)S(1)}, bf16[128,1024]{1,0:T(8,128)(2,1)S(1)}, u32[]{:S(2)}, u32[]{:S(2)}) collective-permute-start(bf16[128,1024]{1,0:T(8,128)(2,1)S(1)} %get-tuple-element.26), channel_id=1, source_target_pairs={{0,4},{4,0},{8,12},{12,8},{16,20},{20,16},{24,28},{28,24},{1,5},{5... | collective-permute-start | bytes 786440 | tf_op jit(solution)/shard_map/ppermute | solution.py:376
  25.3 13.0 %collective-permute-start.7 = (s16[1616,128]{1,0:T(8,128)(2,1)S(1)}, s16[1616,128]{1,0:T(8,128)(2,1)S(1)}, u32[]{:S(2)}, u32[]{:S(2)}) collective-permute-start(s16[1616,128]{1,0:T(8,128)(2,1)S(1)} %get-tuple-element.27.rest_1_), channel_id=1, source_target_pairs={{0,8},{4,12},{8,0},{12,4},{16,24},{20,28},{24,16},{28,20},{1,9},{5... | collective-permute-start | bytes 1241096 | tf_op jit(solution)/shard_map/ppermute | solution.py:427
  30.0 17.2 %collective-permute-start.11 = (s16[1616,128]{1,0:T(8,128)(2,1)S(1)}, s16[1616,128]{1,0:T(8,128)(2,1)S(1)}, u32[]{:S(2)}, u32[]{:S(2)}) collective-permute-start(s16[1616,128]{1,0:T(8,128)(2,1)S(1)} %get-tuple-element.30.rest_1_), channel_id=1, source_target_pairs={{0,8},{4,12},{8,0},{12,4},{16,24},{20,28},{24,16},{28,20},{1,9},{5... | collective-permute-start | bytes 1241096 | tf_op jit(solution)/shard_map/ppermute | solution.py:427
  30.1 17.1 %collective-permute-start.10 = (bf16[128,2048]{1,0:T(8,128)(2,1)S(1)}, bf16[128,2048]{1,0:T(8,128)(2,1)S(1)}, u32[]{:S(2)}, u32[]{:S(2)}) collective-permute-start(bf16[128,2048]{1,0:T(8,128)(2,1)S(1)} %get-tuple-element.33), channel_id=1, source_target_pairs={{0,4},{4,0},{8,12},{12,8},{16,20},{20,16},{24,28},{28,24},{1,5},{5... | collective-permute-start | bytes 1572872 | tf_op jit(solution)/shard_map/ppermute | solution.py:376
  40.5 14.6 %collective-permute-start.9 = (s16[1616,128]{1,0:T(8,128)(2,1)S(1)}, s16[1616,128]{1,0:T(8,128)(2,1)S(1)}, u32[]{:S(2)}, u32[]{:S(2)}) collective-permute-start(s16[1616,128]{1,0:T(8,128)(2,1)S(1)} %get-tuple-element.32.rest_1_), channel_id=1, source_target_pairs={{0,8},{4,12},{8,0},{12,4},{16,24},{20,28},{24,16},{28,20},{1,9},{5... | collective-permute-start | bytes 1241096 | tf_op jit(solution)/shard_map/ppermute | solution.py:427
  42.6 12.5 %collective-permute-start.12 = (bf16[128,1024]{1,0:T(8,128)(2,1)S(1)}, bf16[128,1024]{1,0:T(8,128)(2,1)S(1)}, u32[]{:S(2)}, u32[]{:S(2)}) collective-permute-start(bf16[128,1024]{1,0:T(8,128)(2,1)S(1)} %collective-permute-done.6.rest_3_), channel_id=1, source_target_pairs={{0,4},{4,0},{8,12},{12,8},{16,20},{20,16},{24,28},{28,24},{1,5},{5... | collective-permute-start | bytes 786440 | tf_op jit(solution)/shard_map/ppermute | solution.py:433
  44.0 19.4 %collective-permute-start.8 = (bf16[128,2048]{1,0:T(8,128)(2,1)S(1)}, bf16[128,2048]{1,0:T(8,128)(2,1)S(1)}, u32[]{:S(2)}, u32[]{:S(2)}) collective-permute-start(bf16[128,2048]{1,0:T(8,128)(2,1)S(1)} %get-tuple-element.31), channel_id=1, source_target_pairs={{0,4},{4,0},{8,12},{12,8},{16,20},{20,16},{24,28},{28,24},{1,5},{5... | collective-permute-start | bytes 1572872 | tf_op jit(solution)/shard_map/ppermute | solution.py:376
  49.2 14.3 %collective-permute-start.14 = (s16[1616,128]{1,0:T(8,128)(2,1)S(1)}, s16[1616,128]{1,0:T(8,128)(2,1)S(1)}, u32[]{:S(2)}, u32[]{:S(2)}) collective-permute-start(s16[1616,128]{1,0:T(8,128)(2,1)S(1)} %sum_step_04.1.rest_1_), channel_id=1, source_target_pairs={{8,16},{12,20},{16,8},{20,12},{9,17},{13,21},{17,9},{21,13},{10,18... | collective-permute-start | bytes 1241096 | tf_op jit(solution)/shard_map/ppermute | solution.py:427
  49.9 13.6 %collective-permute-start.13 = (s16[1616,128]{1,0:T(8,128)(2,1)S(1)}, s16[1616,128]{1,0:T(8,128)(2,1)S(1)}, u32[]{:S(2)}, u32[]{:S(2)}) collective-permute-start(s16[1616,128]{1,0:T(8,128)(2,1)S(1)} %sum_step_04.1.rest_1_), channel_id=1, source_target_pairs={{0,8},{4,12},{24,16},{28,20},{1,9},{5,13},{25,17},{29,21},{2,10},{... | collective-permute-start | bytes 1241096 | tf_op jit(solution)/shard_map/ppermute | solution.py:427
  57.1 19.2 %collective-permute-start.17 = (s16[1616,128]{1,0:T(8,128)(2,1)S(1)}, s16[1616,128]{1,0:T(8,128)(2,1)S(1)}, u32[]{:S(2)}, u32[]{:S(2)}) collective-permute-start(s16[1616,128]{1,0:T(8,128)(2,1)S(1)} %sum_step_05.1.rest_2_), channel_id=1, source_target_pairs={{8,16},{12,20},{16,8},{20,12},{9,17},{13,21},{17,9},{21,13},{10,18... | collective-permute-start | bytes 1241096 | tf_op jit(solution)/shard_map/ppermute | solution.py:427
  57.8 18.6 %collective-permute-start.16 = (s16[1616,128]{1,0:T(8,128)(2,1)S(1)}, s16[1616,128]{1,0:T(8,128)(2,1)S(1)}, u32[]{:S(2)}, u32[]{:S(2)}) collective-permute-start(s16[1616,128]{1,0:T(8,128)(2,1)S(1)} %sum_step_05.1.rest_2_), channel_id=1, source_target_pairs={{0,8},{4,12},{24,16},{28,20},{1,9},{5,13},{25,17},{29,21},{2,10},{... | collective-permute-start | bytes 1241096 | tf_op jit(solution)/shard_map/ppermute | solution.py:427
  65.7 18.2 %collective-permute-start.19 = (s16[1616,128]{1,0:T(8,128)(2,1)S(1)}, s16[1616,128]{1,0:T(8,128)(2,1)S(1)}, u32[]{:S(2)}, u32[]{:S(2)}) collective-permute-start(s16[1616,128]{1,0:T(8,128)(2,1)S(1)} %get-tuple-element.36.rest_2_), channel_id=1, source_target_pairs={{8,16},{12,20},{16,8},{20,12},{9,17},{13,21},{17,9},{21,13},{10,18... | collective-permute-start | bytes 1241096 | tf_op jit(solution)/shard_map/ppermute | solution.py:427
  66.4 18.8 %collective-permute-start.18 = (s16[1616,128]{1,0:T(8,128)(2,1)S(1)}, s16[1616,128]{1,0:T(8,128)(2,1)S(1)}, u32[]{:S(2)}, u32[]{:S(2)}) collective-permute-start(s16[1616,128]{1,0:T(8,128)(2,1)S(1)} %get-tuple-element.36.rest_2_), channel_id=1, source_target_pairs={{0,8},{4,12},{24,16},{28,20},{1,9},{5,13},{25,17},{29,21},{2,10},{... | collective-permute-start | bytes 1241096 | tf_op jit(solution)/shard_map/ppermute | solution.py:427
  75.3 12.7 %collective-permute-start.15 = (bf16[128,2048]{1,0:T(8,128)(2,1)S(1)}, bf16[128,2048]{1,0:T(8,128)(2,1)S(1)}, u32[]{:S(2)}, u32[]{:S(2)}) collective-permute-start(bf16[128,2048]{1,0:T(8,128)(2,1)S(1)} %get-tuple-element.35), channel_id=1, source_target_pairs={{0,4},{4,0},{8,12},{12,8},{16,20},{20,16},{24,28},{28,24},{1,5},{5... | collective-permute-start | bytes 1572872 | tf_op jit(solution)/shard_map/ppermute | solution.py:376
  78.4 12.4 %collective-permute-start.22 = (s16[1616,128]{1,0:T(8,128)(2,1)S(1)}, s16[1616,128]{1,0:T(8,128)(2,1)S(1)}, u32[]{:S(2)}, u32[]{:S(2)}) collective-permute-start(s16[1616,128]{1,0:T(8,128)(2,1)S(1)} %sum_step_07.1.rest_2_), channel_id=1, source_target_pairs={{8,16},{12,20},{16,8},{20,12},{9,17},{13,21},{17,9},{21,13},{10,18... | collective-permute-start | bytes 1241096 | tf_op jit(solution)/shard_map/ppermute | solution.py:427
  79.1 15.0 %collective-permute-start.21 = (s16[1616,128]{1,0:T(8,128)(2,1)S(1)}, s16[1616,128]{1,0:T(8,128)(2,1)S(1)}, u32[]{:S(2)}, u32[]{:S(2)}) collective-permute-start(s16[1616,128]{1,0:T(8,128)(2,1)S(1)} %sum_step_07.1.rest_2_), channel_id=1, source_target_pairs={{0,8},{4,12},{24,16},{28,20},{1,9},{5,13},{25,17},{29,21},{2,10},{... | collective-permute-start | bytes 1241096 | tf_op jit(solution)/shard_map/ppermute | solution.py:427
  90.3 12.7 %collective-permute-start.23 = (s16[1616,128]{1,0:T(8,128)(2,1)S(1)}, s16[1616,128]{1,0:T(8,128)(2,1)S(1)}, u32[]{:S(2)}, u32[]{:S(2)}) collective-permute-start(s16[1616,128]{1,0:T(8,128)(2,1)S(1)} %get-tuple-element.38.rest_2_), channel_id=1, source_target_pairs={{0,8},{4,12},{8,24},{12,28},{16,0},{20,4},{24,16},{28,20},{1,9},{5... | collective-permute-start | bytes 1241096 | tf_op jit(solution)/shard_map/ppermute | solution.py:427
  90.3 14.9 %collective-permute-start.20 = (bf16[128,2048]{1,0:T(8,128)(2,1)S(1)}, bf16[128,2048]{1,0:T(8,128)(2,1)S(1)}, u32[]{:S(2)}, u32[]{:S(2)}) collective-permute-start(bf16[128,2048]{1,0:T(8,128)(2,1)S(1)} %get-tuple-element.37), channel_id=1, source_target_pairs={{0,4},{4,0},{8,12},{12,8},{16,20},{20,16},{24,28},{28,24},{1,5},{5... | collective-permute-start | bytes 1572872 | tf_op jit(solution)/shard_map/ppermute | solution.py:376
  96.3 21.5 %collective-permute-start.25 = (s16[1616,128]{1,0:T(8,128)(2,1)S(1)}, s16[1616,128]{1,0:T(8,128)(2,1)S(1)}, u32[]{:S(2)}, u32[]{:S(2)}) collective-permute-start(s16[1616,128]{1,0:T(8,128)(2,1)S(1)} %get-tuple-element.39.rest_2_), channel_id=1, source_target_pairs={{0,8},{4,12},{8,24},{12,28},{16,0},{20,4},{24,16},{28,20},{1,9},{5... | collective-permute-start | bytes 1241096 | tf_op jit(solution)/shard_map/ppermute | solution.py:427
  98.8 15.4 %collective-permute-start.26 = (bf16[128,2048]{1,0:T(8,128)(2,1)S(1)}, bf16[128,2048]{1,0:T(8,128)(2,1)S(1)}, u32[]{:S(2)}, u32[]{:S(2)}) collective-permute-start(bf16[128,2048]{1,0:T(8,128)(2,1)S(1)} %get-tuple-element.42), channel_id=1, source_target_pairs={{0,4},{4,0},{8,12},{12,8},{16,20},{20,16},{24,28},{28,24},{1,5},{5... | collective-permute-start | bytes 1572872 | tf_op jit(solution)/shard_map/ppermute | solution.py:376
  107.5 16.3 %collective-permute-start.28 = (s16[1616,128]{1,0:T(8,128)(2,1)S(1)}, s16[1616,128]{1,0:T(8,128)(2,1)S(1)}, u32[]{:S(2)}, u32[]{:S(2)}) collective-permute-start(s16[1616,128]{1,0:T(8,128)(2,1)S(1)} %get-tuple-element.41.rest_1_), channel_id=1, source_target_pairs={{0,8},{4,12},{8,24},{12,28},{16,0},{20,4},{24,16},{28,20},{1,9},{5... | collective-permute-start | bytes 1241096 | tf_op jit(solution)/shard_map/ppermute | solution.py:427
  107.7 16.1 %collective-permute-start.24 = (bf16[128,2048]{1,0:T(8,128)(2,1)S(1)}, bf16[128,2048]{1,0:T(8,128)(2,1)S(1)}, u32[]{:S(2)}, u32[]{:S(2)}) collective-permute-start(bf16[128,2048]{1,0:T(8,128)(2,1)S(1)} %get-tuple-element.40), channel_id=1, source_target_pairs={{0,4},{4,0},{8,12},{12,8},{16,20},{20,16},{24,28},{28,24},{1,5},{5... | collective-permute-start | bytes 1572872 | tf_op jit(solution)/shard_map/ppermute | solution.py:376
  119.8 8.9 %collective-permute-start.27 = (s16[1616,128]{1,0:T(8,128)(2,1)S(1)}, s16[1616,128]{1,0:T(8,128)(2,1)S(1)}, u32[]{:S(2)}, u32[]{:S(2)}) collective-permute-start(s16[1616,128]{1,0:T(8,128)(2,1)S(1)} %sum_step_11.1), channel_id=1, source_target_pairs={{0,8},{4,12},{8,24},{12,28},{16,0},{20,4},{24,16},{28,20},{1,9},{5... | collective-permute-start | bytes 1241096 | tf_op jit(solution)/shard_map/ppermute | solution.py:427

commit v3 on v2

--- a/solution.py
+++ b/solution.py
@@ -22,11 +22,11 @@
 HALVES = 2
 FLIGHT = 2
 FIRST_SWAP = (0, 2)
-SWAPS = {0: (2, 1), 1: (4, 2), 2: (6, 2), 6: (8, 2), 8: (10, 2), 9: (12, 2), 10: (14, 2)}
+SWAPS = {0: (2, 1), 1: (4, 2), 2: (6, 2), 6: (8, 2), 7: (10, 2), 8: (12, 2), 9: (14, 2)}
 SWAP_WAITS = {}
 RAW_STEP, RAW_WAIT = 2, 5
 INVERSE_STEP = 0
-FINISHED_AHEAD = 1
+FINISHED_AHEAD = 0
 ME, PARTNER, NEAR, NEAR_PARTNER, INNER, FIXED = 0, 1, 2, 3, 4, 5
 LANES = 128
 CODE_ROWS = 16

time: 133 us -> 131 us (0.985)
  waiting for transfers between devices: 29.4 us -> 23.6 us
  starting transfers between devices: 52.3 us -> 55.7 us
    ppermute x8, waiting for transfers between devices: 13 us -> 6.15 us  [swapped(): here = lax.ppermute(away, 'ifg', swap)]
    ppermute x8, starting transfers between devices: 6.85 us -> 10.4 us  [swapped(): here = lax.ppermute(away, 'ifg', swap)]
  transfers between devices with their start and end apart: 29 -> 29, of which waited for: 10 -> 10; matrix products, arithmetic and copies ran while one was open for 2% -> 2% of each run, Pallas kernels for 31% -> 32%
where the time goes in v3:
time: 131 us; the launch traced here: 130 us
  starting transfers between devices  55.7 us (43%)
  Pallas kernels  45.3 us (35%)
  waiting for transfers between devices  23.6 us (18%)
  local copies, waits for them, and re-layouts  4.38 us (3%)
    ppermute x15, starting transfers between devices, solve_by_sums(): lax.ppermute(coded, 'ifg', line_permutation(links))  35.1 us
    pallas_call x11, Pallas kernels, step(): pl.pallas_call(functools.partial(step_kernel, at, layout, len(earlier), s...  23.3 us
    ppermute x15, waiting for transfers between devices, solve_by_sums(): lax.ppermute(coded, 'ifg', line_permutation(links))  17.4 us
    pallas_call x4, Pallas kernels, finish(): pl.pallas_call(functools.partial(finish_kernel, at, layout, tiles, len(ra...  14.5 us
    ppermute x8, starting transfers between devices, swapped(): here = lax.ppermute(away, 'ifg', swap)  10.4 us
    pallas_call x1, Pallas kernels, invert_classes(): pl.pallas_call(inverse_kernel, out_shape=jax.ShapeDtypeStruct(shape, F32)...  7.56 us
    ppermute x8, waiting for transfers between devices, swapped(): here = lax.ppermute(away, 'ifg', swap)  6.15 us
    ppermute x3, starting transfers between devices, solve_by_sums(): counts.append(lax.ppermute(run_counts, 'ifg', line_permutation(links)))  6.11 us
  transfers between devices with their start and end apart: 29, of which 10 were waited for; matrix products, arithmetic and copies ran while one was open for 2% of the time, Pallas kernels for 32%

profile of v3, /device:TPU:0, one launch (start us, length us, event | category | flops | bytes accessed | tf_op | source)
XLA Modules:
  0.0 130.2 jit_solution(5898507701262670049)
XLA Ops:
  0.0 1.1 dynamic-slice_bitcast_fusion
  1.2 0.8 fusion.counts_ref
  2.1 5.1 %collective-permute-start.2 = (s32[2]{0:T(128)S(1)}, s32[2]{0:T(128)S(1)}, u32[]{:S(2)}, u32[]{:S(2)}) collective-permute-start(s32[2]{0:T(128)S(1)} %fusion.counts_ref), channel_id=1, source_target_pairs={{0,24},{4,28},{8,0},{12,4},{16,8},{20,12},{24,16},{28,20},{1,25},{... | collective-permute-start | bytes 32 | tf_op jit(solution)/shard_map/ppermute | solution.py:394
  7.2 1.0 collective-permute-start
  8.2 1.5 %collective-permute-start.3 = (bf16[128,2048]{1,0:T(8,128)(2,1)S(1)}, bf16[128,2048]{1,0:T(8,128)(2,1)S(1)}, u32[]{:S(2)}, u32[]{:S(2)}) collective-permute-start(bf16[128,2048]{1,0:T(8,128)(2,1)S(1)} %dynamic-slice_bitcast_fusion), channel_id=1, source_target_pairs={{0,4},{4,0},{8,12},{12,8},{16,20},{20,16},{24,28},{28,24},{1,5},{5... | collective-permute-start | bytes 1572872 | tf_op jit(solution)/shard_map/ppermute | solution.py:376
  9.7 1.1 dynamic-slice_bitcast_fusion.1
  10.7 2.5 %collective-permute-start.6 = (bf16[128,1024]{1,0:T(8,128)(2,1)S(1)}, bf16[128,1024]{1,0:T(8,128)(2,1)S(1)}, u32[]{:S(2)}, u32[]{:S(2)}) collective-permute-start(bf16[128,1024]{1,0:T(8,128)(2,1)S(1)} %get-tuple-element.41), channel_id=1, source_target_pairs={{0,8},{4,12},{8,0},{12,4},{16,24},{20,28},{24,16},{28,20},{1,9},{5... | collective-permute-start | bytes 786440 | tf_op jit(solution)/shard_map/ppermute | solution.py:398
  13.3 0.7 constant_dynamic-slice_fusion.3
  14.2 0.7 fusion.1.table
  14.9 0.7 copy-done.1
  15.6 7.6 %invert_classes_0.1.rest_1_.inverse_ref = f32[2,256,256]{2,1,0:T(8,128)S(1)} custom-call(s32[2]{0:T(128)S(1)} %fusion.counts_ref, s32[2,1024]{1,0:T(2,128)S(1)} %copy-done.1, s32[8]{0:T(128)S(1)} %pad_add_fusion.1.rest_0_.counts), custom_call_target="tpu_custom_call" | custom-call | flops 1024 | bytes 1024 | tf_op jit(solution)/shard_map/invert_classes_0/pallas_call | solution.py:103
  23.2 2.1 %sum_step_00.1 = (s16[1616,128]{1,0:T(8,128)(2,1)S(1)}, bf16[128,1024]{1,0:T(8,128)(2,1)S(1)}) custom-call(s32[53]{0:T(128)S(1)} %fusion.1.table, s32[8]{0:T(128)S(1)} %pad_add_fusion.1.rest_0_.counts, s32[2,512]{1,0:T(2,128)S(1)} %pad_add_fusion.pairs_ref, bf16[128,32768]{1,0:T(8,128)(2,1)} %bitcast.12, ...), custom_call_target="tpu_custom_call" | custom-call | flops 10000000000 | bytes 30000000 | tf_op jit(solution)/shard_map/sum_step_00/pallas_call | solution.py:245
  25.8 2.0 %collective-permute-start.7 = (s16[1616,128]{1,0:T(8,128)(2,1)S(1)}, s16[1616,128]{1,0:T(8,128)(2,1)S(1)}, u32[]{:S(2)}, u32[]{:S(2)}) collective-permute-start(s16[1616,128]{1,0:T(8,128)(2,1)S(1)} %get-tuple-element.25.rest_1_), channel_id=1, source_target_pairs={{0,8},{4,12},{8,0},{12,4},{16,24},{20,28},{24,16},{28,20},{1,9},{5... | collective-permute-start | bytes 1241096 | tf_op jit(solution)/shard_map/ppermute | solution.py:427
  27.8 2.2 %sum_step_01.1 = (s16[1616,128]{1,0:T(8,128)(2,1)S(1)}, bf16[128,2048]{1,0:T(8,128)(2,1)S(1)}) custom-call(s32[53]{0:T(128)S(1)} %fusion.1.table, s32[8]{0:T(128)S(1)} %pad_add_fusion.1.rest_0_.counts, s32[2,512]{1,0:T(2,128)S(1)} %pad_add_fusion.pairs_ref, bf16[128,32768]{1,0:T(8,128)(2,1)} %bitcast.14, ...), custom_call_target="tpu_custom_call" | custom-call | flops 10000000000 | bytes 30000000 | tf_op jit(solution)/shard_map/sum_step_01/pallas_call | solution.py:245
  30.1 1.5 %collective-permute-start.10 = (bf16[128,2048]{1,0:T(8,128)(2,1)S(1)}, bf16[128,2048]{1,0:T(8,128)(2,1)S(1)}, u32[]{:S(2)}, u32[]{:S(2)}) collective-permute-start(bf16[128,2048]{1,0:T(8,128)(2,1)S(1)} %get-tuple-element.31), channel_id=1, source_target_pairs={{0,4},{4,0},{8,12},{12,8},{16,20},{20,16},{24,28},{28,24},{1,5},{5... | collective-permute-start | bytes 1572872 | tf_op jit(solution)/shard_map/ppermute | solution.py:376
  31.6 1.8 %collective-permute-done.4.partner_ref = bf16[128,1024]{1,0:T(8,128)(2,1)S(1)} collective-permute-done((bf16[128,1024]{1,0:T(8,128)(2,1)S(1)}, bf16[128,1024]{1,0:T(8,128)(2,1)S(1)}, u32[]{:S(2)}, u32[]{:S(2)}) %collective-permute-start.4) | collective-permute-done | bytes 262176 | tf_op jit(solution)/shard_map/ppermute | solution.py:376
  33.5 4.8 %collective-permute-done.7.rest_2_.rest_0_.rest_1_ = s16[1616,128]{1,0:T(8,128)(2,1)S(1)} collective-permute-done((s16[1616,128]{1,0:T(8,128)(2,1)S(1)}, s16[1616,128]{1,0:T(8,128)(2,1)S(1)}, u32[]{:S(2)}, u32[]{:S(2)}) %collective-permute-start.7) | collective-permute-done | bytes 413728 | tf_op jit(solution)/shard_map/ppermute | solution.py:427
  38.3 2.2 %sum_step_02.1 = (s16[1616,128]{1,0:T(8,128)(2,1)S(1)}, bf16[128,2048]{1,0:T(8,128)(2,1)S(1)}) custom-call(s32[53]{0:T(128)S(1)} %fusion.1.table, s32[8]{0:T(128)S(1)} %pad_add_fusion.1.rest_0_.counts, s32[2,512]{1,0:T(2,128)S(1)} %pad_add_fusion.pairs_ref, bf16[128,32768]{1,0:T(8,128)(2,1)} %bitcast.16, ...), custom_call_target="tpu_custom_call" | custom-call | flops 10000000000 | bytes 30000000 | tf_op jit(solution)/shard_map/sum_step_02/pallas_call | solution.py:245
  40.5 2.1 %collective-permute-start.9 = (s16[1616,128]{1,0:T(8,128)(2,1)S(1)}, s16[1616,128]{1,0:T(8,128)(2,1)S(1)}, u32[]{:S(2)}, u32[]{:S(2)}) collective-permute-start(s16[1616,128]{1,0:T(8,128)(2,1)S(1)} %get-tuple-element.30.rest_1_), channel_id=1, source_target_pairs={{0,8},{4,12},{8,0},{12,4},{16,24},{20,28},{24,16},{28,20},{1,9},{5... | collective-permute-start | bytes 1241096 | tf_op jit(solution)/shard_map/ppermute | solution.py:427
  42.6 1.5 %collective-permute-start.12 = (bf16[128,1024]{1,0:T(8,128)(2,1)S(1)}, bf16[128,1024]{1,0:T(8,128)(2,1)S(1)}, u32[]{:S(2)}, u32[]{:S(2)}) collective-permute-start(bf16[128,1024]{1,0:T(8,128)(2,1)S(1)} %collective-permute-done.6.rest_3_), channel_id=1, source_target_pairs={{0,4},{4,0},{8,12},{12,8},{16,20},{20,16},{24,28},{28,24},{1,5},{5... | collective-permute-start | bytes 786440 | tf_op jit(solution)/shard_map/ppermute | solution.py:433
  44.6 2.6 %collective-permute-done.11.rest_2_.rest_0_.rest_1_ = s16[1616,128]{1,0:T(8,128)(2,1)S(1)} collective-permute-done((s16[1616,128]{1,0:T(8,128)(2,1)S(1)}, s16[1616,128]{1,0:T(8,128)(2,1)S(1)}, u32[]{:S(2)}, u32[]{:S(2)}) %collective-permute-start.11) | collective-permute-done | bytes 413728 | tf_op jit(solution)/shard_map/ppermute | solution.py:427
  47.2 2.0 %sum_step_04.1.rest_1_ = s16[1616,128]{1,0:T(8,128)(2,1)S(1)} custom-call(s32[53]{0:T(128)S(1)} %fusion.1.table, s32[8]{0:T(128)S(1)} %pad_add_fusion.1.rest_0_.counts, s32[2,512]{1,0:T(2,128)S(1)} %pad_add_fusion.pairs_ref, bf16[128,32768]{1,0:T(8,128)(2,1)} %bitcast.18, bf16[128,2048]{1,0:T(8,128)(2,1)S(1)} %collective-permute-done.10.partner_ref, ...), custom_call_target="tpu_custom_call" | custom-call | flops 10000000000 | bytes 30000000 | tf_op jit(solution)/shard_map/sum_step_04/pallas_call | solution.py:245
  49.2 0.7 collective-permute-start.14
  49.9 5.2 %collective-permute-start.13 = (s16[1616,128]{1,0:T(8,128)(2,1)S(1)}, s16[1616,128]{1,0:T(8,128)(2,1)S(1)}, u32[]{:S(2)}, u32[]{:S(2)}) collective-permute-start(s16[1616,128]{1,0:T(8,128)(2,1)S(1)} %sum_step_04.1.rest_1_), channel_id=1, source_target_pairs={{0,8},{4,12},{24,16},{28,20},{1,9},{5,13},{25,17},{29,21},{2,10},{... | collective-permute-start | bytes 1241096 | tf_op jit(solution)/shard_map/ppermute | solution.py:427
  55.6 2.0 %sum_step_05.1.rest_2_ = s16[1616,128]{1,0:T(8,128)(2,1)S(1)} custom-call(s32[53]{0:T(128)S(1)} %fusion.1.table, s32[8]{0:T(128)S(1)} %pad_add_fusion.1.rest_0_.counts, s32[2,512]{1,0:T(2,128)S(1)} %pad_add_fusion.pairs_ref, bf16[128,32768]{1,0:T(8,128)(2,1)} %bitcast.19, bf16[128,2048]{1,0:T(8,128)(2,1)S(1)} %collective-permute-done.10.partner_ref, ...), custom_call_target="tpu_custom_call" | custom-call | flops 10000000000 | bytes 30000000 | tf_op jit(solution)/shard_map/sum_step_05/pallas_call | solution.py:245
  58.3 5.7 %collective-permute-start.16 = (s16[1616,128]{1,0:T(8,128)(2,1)S(1)}, s16[1616,128]{1,0:T(8,128)(2,1)S(1)}, u32[]{:S(2)}, u32[]{:S(2)}) collective-permute-start(s16[1616,128]{1,0:T(8,128)(2,1)S(1)} %sum_step_05.1.rest_2_), channel_id=1, source_target_pairs={{0,8},{4,12},{24,16},{28,20},{1,9},{5,13},{25,17},{29,21},{2,10},{... | collective-permute-start | bytes 1241096 | tf_op jit(solution)/shard_map/ppermute | solution.py:427
  64.4 2.2 %sum_step_06.1 = (s16[1616,128]{1,0:T(8,128)(2,1)S(1)}, bf16[128,2048]{1,0:T(8,128)(2,1)S(1)}) custom-call(s32[53]{0:T(128)S(1)} %fusion.1.table, s32[8]{0:T(128)S(1)} %pad_add_fusion.1.rest_0_.counts, s32[2,512]{1,0:T(2,128)S(1)} %pad_add_fusion.pairs_ref, bf16[128,32768]{1,0:T(8,128)(2,1)} %bitcast.21, ...), custom_call_target="tpu_custom_call" | custom-call | flops 10000000000 | bytes 30000000 | tf_op jit(solution)/shard_map/sum_step_06/pallas_call | solution.py:245
  67.3 6.7 %collective-permute-start.18 = (s16[1616,128]{1,0:T(8,128)(2,1)S(1)}, s16[1616,128]{1,0:T(8,128)(2,1)S(1)}, u32[]{:S(2)}, u32[]{:S(2)}) collective-permute-start(s16[1616,128]{1,0:T(8,128)(2,1)S(1)} %get-tuple-element.34.rest_3_), channel_id=1, source_target_pairs={{0,8},{4,12},{24,16},{28,20},{1,9},{5,13},{25,17},{29,21},{2,10},{... | collective-permute-start | bytes 1241096 | tf_op jit(solution)/shard_map/ppermute | solution.py:427
  74.1 1.6 %collective-permute-start.15 = (bf16[128,2048]{1,0:T(8,128)(2,1)S(1)}, bf16[128,2048]{1,0:T(8,128)(2,1)S(1)}, u32[]{:S(2)}, u32[]{:S(2)}) collective-permute-start(bf16[128,2048]{1,0:T(8,128)(2,1)S(1)} %get-tuple-element.33), channel_id=1, source_target_pairs={{0,4},{4,0},{8,12},{12,8},{16,20},{20,16},{24,28},{28,24},{1,5},{5... | collective-permute-start | bytes 1572872 | tf_op jit(solution)/shard_map/ppermute | solution.py:376
  75.6 2.2 %sum_step_07.1 = (s16[1616,128]{1,0:T(8,128)(2,1)S(1)}, bf16[128,2048]{1,0:T(8,128)(2,1)S(1)}) custom-call(s32[53]{0:T(128)S(1)} %fusion.1.table, s32[8]{0:T(128)S(1)} %pad_add_fusion.1.rest_0_.counts, s32[2,512]{1,0:T(2,128)S(1)} %pad_add_fusion.pairs_ref, bf16[128,32768]{1,0:T(8,128)(2,1)} %bitcast.22, ...), custom_call_target="tpu_custom_call" | custom-call | flops 10000000000 | bytes 30000000 | tf_op jit(solution)/shard_map/sum_step_07/pallas_call | solution.py:245
  78.6 4.8 %collective-permute-start.20 = (s16[1616,128]{1,0:T(8,128)(2,1)S(1)}, s16[1616,128]{1,0:T(8,128)(2,1)S(1)}, u32[]{:S(2)}, u32[]{:S(2)}) collective-permute-start(s16[1616,128]{1,0:T(8,128)(2,1)S(1)} %get-tuple-element.35.rest_2_), channel_id=1, source_target_pairs={{0,8},{4,12},{24,16},{28,20},{1,9},{5,13},{25,17},{29,21},{2,10},{... | collective-permute-start | bytes 1241096 | tf_op jit(solution)/shard_map/ppermute | solution.py:427
  83.4 1.6 %collective-permute-start.23 = (bf16[128,2048]{1,0:T(8,128)(2,1)S(1)}, bf16[128,2048]{1,0:T(8,128)(2,1)S(1)}, u32[]{:S(2)}, u32[]{:S(2)}) collective-permute-start(bf16[128,2048]{1,0:T(8,128)(2,1)S(1)} %get-tuple-element.38), channel_id=1, source_target_pairs={{0,4},{4,0},{8,12},{12,8},{16,20},{20,16},{24,28},{28,24},{1,5},{5... | collective-permute-start | bytes 1572872 | tf_op jit(solution)/shard_map/ppermute | solution.py:376
  85.0 3.9 %collective-permute-done.15.partner_ref = bf16[128,2048]{1,0:T(8,128)(2,1)S(1)} collective-permute-done((bf16[128,2048]{1,0:T(8,128)(2,1)S(1)}, bf16[128,2048]{1,0:T(8,128)(2,1)S(1)}, u32[]{:S(2)}, u32[]{:S(2)}) %collective-permute-start.15) | collective-permute-done | bytes 524320 | tf_op jit(solution)/shard_map/ppermute | solution.py:376
  88.8 2.2 %sum_step_08.1 = (s16[1616,128]{1,0:T(8,128)(2,1)S(1)}, bf16[128,2048]{1,0:T(8,128)(2,1)S(1)}) custom-call(s32[53]{0:T(128)S(1)} %fusion.1.table, s32[8]{0:T(128)S(1)} %pad_add_fusion.1.rest_0_.counts, s32[2,512]{1,0:T(2,128)S(1)} %pad_add_fusion.pairs_ref, bf16[128,32768]{1,0:T(8,128)(2,1)} %bitcast.24, ...), custom_call_target="tpu_custom_call" | custom-call | flops 10000000000 | bytes 30000000 | tf_op jit(solution)/shard_map/sum_step_08/pallas_call | solution.py:245
  91.1 1.6 %collective-permute-start.28 = (bf16[128,2048]{1,0:T(8,128)(2,1)S(1)}, bf16[128,2048]{1,0:T(8,128)(2,1)S(1)}, u32[]{:S(2)}, u32[]{:S(2)}) collective-permute-start(bf16[128,2048]{1,0:T(8,128)(2,1)S(1)} %get-tuple-element.40), channel_id=1, source_target_pairs={{0,4},{4,0},{8,12},{12,8},{16,20},{20,16},{24,28},{28,24},{1,5},{5... | collective-permute-start | bytes 1572872 | tf_op jit(solution)/shard_map/ppermute | solution.py:376
  93.4 2.2 %sum_step_09.1 = (s16[1616,128]{1,0:T(8,128)(2,1)S(1)}, bf16[128,2048]{1,0:T(8,128)(2,1)S(1)}) custom-call(s32[53]{0:T(128)S(1)} %fusion.1.table, s32[8]{0:T(128)S(1)} %pad_add_fusion.1.rest_0_.counts, s32[2,512]{1,0:T(2,128)S(1)} %pad_add_fusion.pairs_ref, bf16[128,32768]{1,0:T(8,128)(2,1)} %bitcast.26, ...), custom_call_target="tpu_custom_call" | custom-call | flops 10000000000 | bytes 30000000 | tf_op jit(solution)/shard_map/sum_step_09/pallas_call | solution.py:245
  95.6 2.5 %collective-permute-start.25 = (s16[1616,128]{1,0:T(8,128)(2,1)S(1)}, s16[1616,128]{1,0:T(8,128)(2,1)S(1)}, u32[]{:S(2)}, u32[]{:S(2)}) collective-permute-start(s16[1616,128]{1,0:T(8,128)(2,1)S(1)} %get-tuple-element.39.rest_1_), channel_id=1, source_target_pairs={{0,8},{4,12},{8,24},{12,28},{16,0},{20,4},{24,16},{28,20},{1,9},{5... | collective-permute-start | bytes 1241096 | tf_op jit(solution)/shard_map/ppermute | solution.py:427
  98.1 1.5 %collective-permute-start.22 = (bf16[128,2048]{1,0:T(8,128)(2,1)S(1)}, bf16[128,2048]{1,0:T(8,128)(2,1)S(1)}, u32[]{:S(2)}, u32[]{:S(2)}) collective-permute-start(bf16[128,2048]{1,0:T(8,128)(2,1)S(1)} %get-tuple-element.37), channel_id=1, source_target_pairs={{0,4},{4,0},{8,12},{12,8},{16,20},{20,16},{24,28},{28,24},{1,5},{5... | collective-permute-start | bytes 1572872 | tf_op jit(solution)/shard_map/ppermute | solution.py:376
  100.1 3.1 %collective-permute-done.24.rest_2_.rest_4_.rest_5_ = s16[1616,128]{1,0:T(8,128)(2,1)S(1)} collective-permute-done((s16[1616,128]{1,0:T(8,128)(2,1)S(1)}, s16[1616,128]{1,0:T(8,128)(2,1)S(1)}, u32[]{:S(2)}, u32[]{:S(2)}) %collective-permute-start.24) | collective-permute-done | bytes 413728 | tf_op jit(solution)/shard_map/ppermute | solution.py:427
  103.1 2.0 %sum_step_10.1.rest_1_ = s16[1616,128]{1,0:T(8,128)(2,1)S(1)} custom-call(s32[53]{0:T(128)S(1)} %fusion.1.table, s32[8]{0:T(128)S(1)} %pad_add_fusion.1.rest_0_.counts, s32[2,512]{1,0:T(2,128)S(1)} %pad_add_fusion.pairs_ref, bf16[128,32768]{1,0:T(8,128)(2,1)} %bitcast.28, bf16[128,2048]{1,0:T(8,128)(2,1)S(1)} %collective-permute-done.23.partner_ref, ...), custom_call_target="tpu_custom_call" | custom-call | flops 10000000000 | bytes 30000000 | tf_op jit(solution)/shard_map/sum_step_10/pallas_call | solution.py:245
  105.1 1.6 %collective-permute-start.27 = (s16[1616,128]{1,0:T(8,128)(2,1)S(1)}, s16[1616,128]{1,0:T(8,128)(2,1)S(1)}, u32[]{:S(2)}, u32[]{:S(2)}) collective-permute-start(s16[1616,128]{1,0:T(8,128)(2,1)S(1)} %sum_step_10.1.rest_1_), channel_id=1, source_target_pairs={{0,8},{4,12},{8,24},{12,28},{16,0},{20,4},{24,16},{28,20},{1,9},{5... | collective-permute-start | bytes 1241096 | tf_op jit(solution)/shard_map/ppermute | solution.py:427
  106.8 5.2 %collective-permute-done.25.rest_2_.rest_4_.rest_5_ = s16[1616,128]{1,0:T(8,128)(2,1)S(1)} collective-permute-done((s16[1616,128]{1,0:T(8,128)(2,1)S(1)}, s16[1616,128]{1,0:T(8,128)(2,1)S(1)}, u32[]{:S(2)}, u32[]{:S(2)}) %collective-permute-start.25) | collective-permute-done | bytes 413728 | tf_op jit(solution)/shard_map/ppermute | solution.py:427
  112.0 2.0 %sum_step_11.1 = s16[1616,128]{1,0:T(8,128)(2,1)S(1)} custom-call(s32[53]{0:T(128)S(1)} %fusion.1.table, s32[8]{0:T(128)S(1)} %pad_add_fusion.1.rest_0_.counts, s32[2,512]{1,0:T(2,128)S(1)} %pad_add_fusion.pairs_ref, bf16[128,32768]{1,0:T(8,128)(2,1)} %bitcast.29, bf16[128,2048]{1,0:T(8,128)(2,1)S(1)} %collective-permute-done.23.partner_ref, ...), custom_call_target="tpu_custom_call" | custom-call | flops 10000000000 | bytes 30000000 | tf_op jit(solution)/shard_map/sum_step_11/pallas_call | solution.py:245
  114.0 1.6 %collective-permute-start.26 = (s16[1616,128]{1,0:T(8,128)(2,1)S(1)}, s16[1616,128]{1,0:T(8,128)(2,1)S(1)}, u32[]{:S(2)}, u32[]{:S(2)}) collective-permute-start(s16[1616,128]{1,0:T(8,128)(2,1)S(1)} %sum_step_11.1), channel_id=1, source_target_pairs={{0,8},{4,12},{8,24},{12,28},{16,0},{20,4},{24,16},{28,20},{1,9},{5... | collective-permute-start | bytes 1241096 | tf_op jit(solution)/shard_map/ppermute | solution.py:427
  115.6 3.6 %finish_0.1.rest_6_ = f32[200,4096]{1,0:T(8,128)} custom-call(s32[53]{0:T(128)S(1)} %fusion.1.table, s32[8]{0:T(128)S(1)} %pad_add_fusion.1.rest_0_.counts, s32[2,512]{1,0:T(2,128)S(1)} %pad_add_fusion.pairs_ref, bf16[128,32768]{1,0:T(8,128)(2,1)} %bitcast.30, bf16[128,2048]{1,0:T(8,128)(2,1)S(1)} %collective-permute-done.28.partner_ref, ...), custom_call_target="tpu_custom_call" | custom-call | flops 1024 | bytes 1024 | tf_op jit(solution)/shard_map/finish_0/pallas_call | solution.py:327
  119.2 3.6 %finish_1.1.rest_6_ = f32[200,4096]{1,0:T(8,128)} custom-call(s32[53]{0:T(128)S(1)} %fusion.1.table, s32[8]{0:T(128)S(1)} %pad_add_fusion.1.rest_0_.counts, s32[2,512]{1,0:T(2,128)S(1)} %pad_add_fusion.pairs_ref, bf16[128,32768]{1,0:T(8,128)(2,1)} %bitcast.31, ...), custom_call_target="tpu_custom_call", output_to_operand_aliasing={{}: (12, {})} | custom-call | flops 1024 | bytes 1024 | tf_op jit(solution)/shard_map/finish_1/pallas_call | solution.py:327
  122.8 3.6 %finish_2.1.rest_6_ = f32[200,4096]{1,0:T(8,128)} custom-call(s32[53]{0:T(128)S(1)} %fusion.1.table, s32[8]{0:T(128)S(1)} %pad_add_fusion.1.rest_0_.counts, s32[2,512]{1,0:T(2,128)S(1)} %pad_add_fusion.pairs_ref, bf16[128,32768]{1,0:T(8,128)(2,1)} %bitcast.32, ...), custom_call_target="tpu_custom_call", output_to_operand_aliasing={{}: (12, {})} | custom-call | flops 1024 | bytes 1024 | tf_op jit(solution)/shard_map/finish_2/pallas_call | solution.py:327
  126.3 3.9 %finish_3.1 = f32[200,4096]{1,0:T(8,128)} custom-call(s32[53]{0:T(128)S(1)} %fusion.1.table, s32[8]{0:T(128)S(1)} %pad_add_fusion.1.rest_0_.counts, s32[2,512]{1,0:T(2,128)S(1)} %pad_add_fusion.pairs_ref, bf16[128,32768]{1,0:T(8,128)(2,1)} %bitcast.33, bf16[128,2048]{1,0:T(8,128)(2,1)S(1)} %collective-permute-done.22.partner_ref, ...), custom_call_target="tpu_custom_call", output_to_operand_aliasing={{}: (12, {})} | custom-call | flops 1024 | bytes 1024 | tf_op jit(solution)/shard_map/finish_3/pallas_call | solution.py:327
  (39 shorter events, 5.8 us)
Async XLA Ops:
  0.0 1.1 copy-start
  2.1 11.9 %collective-permute-start.2 = (s32[2]{0:T(128)S(1)}, s32[2]{0:T(128)S(1)}, u32[]{:S(2)}, u32[]{:S(2)}) collective-permute-start(s32[2]{0:T(128)S(1)} %fusion.counts_ref), channel_id=1, source_target_pairs={{0,24},{4,28},{8,0},{12,4},{16,8},{20,12},{24,16},{28,20},{1,25},{... | collective-permute-start | bytes 32 | tf_op jit(solution)/shard_map/ppermute | solution.py:394
  7.1 7.0 %collective-permute-start.1 = (s32[2]{0:T(128)S(1)}, s32[2]{0:T(128)S(1)}, u32[]{:S(2)}, u32[]{:S(2)}) collective-permute-start(s32[2]{0:T(128)S(1)} %fusion.counts_ref), channel_id=1, source_target_pairs={{0,16},{4,20},{8,24},{12,28},{16,0},{20,4},{24,8},{28,12},{1,17},{... | collective-permute-start | bytes 32 | tf_op jit(solution)/shard_map/ppermute | solution.py:394
  7.2 7.0 %collective-permute-start = (s32[2]{0:T(128)S(1)}, s32[2]{0:T(128)S(1)}, u32[]{:S(2)}, u32[]{:S(2)}) collective-permute-start(s32[2]{0:T(128)S(1)} %fusion.counts_ref), channel_id=1, source_target_pairs={{0,8},{4,12},{8,16},{12,20},{16,24},{20,28},{24,0},{28,4},{1,9},{5... | collective-permute-start | bytes 32 | tf_op jit(solution)/shard_map/ppermute | solution.py:394
  8.2 15.0 %collective-permute-start.3 = (bf16[128,2048]{1,0:T(8,128)(2,1)S(1)}, bf16[128,2048]{1,0:T(8,128)(2,1)S(1)}, u32[]{:S(2)}, u32[]{:S(2)}) collective-permute-start(bf16[128,2048]{1,0:T(8,128)(2,1)S(1)} %dynamic-slice_bitcast_fusion), channel_id=1, source_target_pairs={{0,4},{4,0},{8,12},{12,8},{16,20},{20,16},{24,28},{28,24},{1,5},{5... | collective-permute-start | bytes 1572872 | tf_op jit(solution)/shard_map/ppermute | solution.py:376
  10.7 17.1 %collective-permute-start.6 = (bf16[128,1024]{1,0:T(8,128)(2,1)S(1)}, bf16[128,1024]{1,0:T(8,128)(2,1)S(1)}, u32[]{:S(2)}, u32[]{:S(2)}) collective-permute-start(bf16[128,1024]{1,0:T(8,128)(2,1)S(1)} %get-tuple-element.41), channel_id=1, source_target_pairs={{0,8},{4,12},{8,0},{12,4},{16,24},{20,28},{24,16},{28,20},{1,9},{5... | collective-permute-start | bytes 786440 | tf_op jit(solution)/shard_map/ppermute | solution.py:398
  14.0 13.8 %collective-permute-start.5 = (bf16[128,1024]{1,0:T(8,128)(2,1)S(1)}, bf16[128,1024]{1,0:T(8,128)(2,1)S(1)}, u32[]{:S(2)}, u32[]{:S(2)}) collective-permute-start(bf16[128,1024]{1,0:T(8,128)(2,1)S(1)} %get-tuple-element.42), channel_id=1, source_target_pairs={{0,8},{4,12},{8,0},{12,4},{16,24},{20,28},{24,16},{28,20},{1,9},{5... | collective-permute-start | bytes 786440 | tf_op jit(solution)/shard_map/ppermute | solution.py:399
  14.9 0.7 copy-start.1
  25.2 8.2 %collective-permute-start.4 = (bf16[128,1024]{1,0:T(8,128)(2,1)S(1)}, bf16[128,1024]{1,0:T(8,128)(2,1)S(1)}, u32[]{:S(2)}, u32[]{:S(2)}) collective-permute-start(bf16[128,1024]{1,0:T(8,128)(2,1)S(1)} %get-tuple-element.24), channel_id=1, source_target_pairs={{0,4},{4,0},{8,12},{12,8},{16,20},{20,16},{24,28},{28,24},{1,5},{5... | collective-permute-start | bytes 786440 | tf_op jit(solution)/shard_map/ppermute | solution.py:376
  25.8 12.5 %collective-permute-start.7 = (s16[1616,128]{1,0:T(8,128)(2,1)S(1)}, s16[1616,128]{1,0:T(8,128)(2,1)S(1)}, u32[]{:S(2)}, u32[]{:S(2)}) collective-permute-start(s16[1616,128]{1,0:T(8,128)(2,1)S(1)} %get-tuple-element.25.rest_1_), channel_id=1, source_target_pairs={{0,8},{4,12},{8,0},{12,4},{16,24},{20,28},{24,16},{28,20},{1,9},{5... | collective-permute-start | bytes 1241096 | tf_op jit(solution)/shard_map/ppermute | solution.py:427
  30.0 17.2 %collective-permute-start.11 = (s16[1616,128]{1,0:T(8,128)(2,1)S(1)}, s16[1616,128]{1,0:T(8,128)(2,1)S(1)}, u32[]{:S(2)}, u32[]{:S(2)}) collective-permute-start(s16[1616,128]{1,0:T(8,128)(2,1)S(1)} %get-tuple-element.28.rest_1_), channel_id=1, source_target_pairs={{0,8},{4,12},{8,0},{12,4},{16,24},{20,28},{24,16},{28,20},{1,9},{5... | collective-permute-start | bytes 1241096 | tf_op jit(solution)/shard_map/ppermute | solution.py:427
  30.1 17.1 %collective-permute-start.10 = (bf16[128,2048]{1,0:T(8,128)(2,1)S(1)}, bf16[128,2048]{1,0:T(8,128)(2,1)S(1)}, u32[]{:S(2)}, u32[]{:S(2)}) collective-permute-start(bf16[128,2048]{1,0:T(8,128)(2,1)S(1)} %get-tuple-element.31), channel_id=1, source_target_pairs={{0,4},{4,0},{8,12},{12,8},{16,20},{20,16},{24,28},{28,24},{1,5},{5... | collective-permute-start | bytes 1572872 | tf_op jit(solution)/shard_map/ppermute | solution.py:376
  40.5 15.1 %collective-permute-start.9 = (s16[1616,128]{1,0:T(8,128)(2,1)S(1)}, s16[1616,128]{1,0:T(8,128)(2,1)S(1)}, u32[]{:S(2)}, u32[]{:S(2)}) collective-permute-start(s16[1616,128]{1,0:T(8,128)(2,1)S(1)} %get-tuple-element.30.rest_1_), channel_id=1, source_target_pairs={{0,8},{4,12},{8,0},{12,4},{16,24},{20,28},{24,16},{28,20},{1,9},{5... | collective-permute-start | bytes 1241096 | tf_op jit(solution)/shard_map/ppermute | solution.py:427
  42.6 12.5 %collective-permute-start.12 = (bf16[128,1024]{1,0:T(8,128)(2,1)S(1)}, bf16[128,1024]{1,0:T(8,128)(2,1)S(1)}, u32[]{:S(2)}, u32[]{:S(2)}) collective-permute-start(bf16[128,1024]{1,0:T(8,128)(2,1)S(1)} %collective-permute-done.6.rest_3_), channel_id=1, source_target_pairs={{0,4},{4,0},{8,12},{12,8},{16,20},{20,16},{24,28},{28,24},{1,5},{5... | collective-permute-start | bytes 786440 | tf_op jit(solution)/shard_map/ppermute | solution.py:433
  44.1 19.9 %collective-permute-start.8 = (bf16[128,2048]{1,0:T(8,128)(2,1)S(1)}, bf16[128,2048]{1,0:T(8,128)(2,1)S(1)}, u32[]{:S(2)}, u32[]{:S(2)}) collective-permute-start(bf16[128,2048]{1,0:T(8,128)(2,1)S(1)} %get-tuple-element.29), channel_id=1, source_target_pairs={{0,4},{4,0},{8,12},{12,8},{16,20},{20,16},{24,28},{28,24},{1,5},{5... | collective-permute-start | bytes 1572872 | tf_op jit(solution)/shard_map/ppermute | solution.py:376
  49.2 14.7 %collective-permute-start.14 = (s16[1616,128]{1,0:T(8,128)(2,1)S(1)}, s16[1616,128]{1,0:T(8,128)(2,1)S(1)}, u32[]{:S(2)}, u32[]{:S(2)}) collective-permute-start(s16[1616,128]{1,0:T(8,128)(2,1)S(1)} %sum_step_04.1.rest_1_), channel_id=1, source_target_pairs={{8,16},{12,20},{16,8},{20,12},{9,17},{13,21},{17,9},{21,13},{10,18... | collective-permute-start | bytes 1241096 | tf_op jit(solution)/shard_map/ppermute | solution.py:427
  49.9 14.5 %collective-permute-start.13 = (s16[1616,128]{1,0:T(8,128)(2,1)S(1)}, s16[1616,128]{1,0:T(8,128)(2,1)S(1)}, u32[]{:S(2)}, u32[]{:S(2)}) collective-permute-start(s16[1616,128]{1,0:T(8,128)(2,1)S(1)} %sum_step_04.1.rest_1_), channel_id=1, source_target_pairs={{0,8},{4,12},{24,16},{28,20},{1,9},{5,13},{25,17},{29,21},{2,10},{... | collective-permute-start | bytes 1241096 | tf_op jit(solution)/shard_map/ppermute | solution.py:427
  57.6 18.1 %collective-permute-start.17 = (s16[1616,128]{1,0:T(8,128)(2,1)S(1)}, s16[1616,128]{1,0:T(8,128)(2,1)S(1)}, u32[]{:S(2)}, u32[]{:S(2)}) collective-permute-start(s16[1616,128]{1,0:T(8,128)(2,1)S(1)} %sum_step_05.1.rest_2_), channel_id=1, source_target_pairs={{8,16},{12,20},{16,8},{20,12},{9,17},{13,21},{17,9},{21,13},{10,18... | collective-permute-start | bytes 1241096 | tf_op jit(solution)/shard_map/ppermute | solution.py:427
  58.3 17.4 %collective-permute-start.16 = (s16[1616,128]{1,0:T(8,128)(2,1)S(1)}, s16[1616,128]{1,0:T(8,128)(2,1)S(1)}, u32[]{:S(2)}, u32[]{:S(2)}) collective-permute-start(s16[1616,128]{1,0:T(8,128)(2,1)S(1)} %sum_step_05.1.rest_2_), channel_id=1, source_target_pairs={{0,8},{4,12},{24,16},{28,20},{1,9},{5,13},{25,17},{29,21},{2,10},{... | collective-permute-start | bytes 1241096 | tf_op jit(solution)/shard_map/ppermute | solution.py:427
  66.7 16.8 %collective-permute-start.19 = (s16[1616,128]{1,0:T(8,128)(2,1)S(1)}, s16[1616,128]{1,0:T(8,128)(2,1)S(1)}, u32[]{:S(2)}, u32[]{:S(2)}) collective-permute-start(s16[1616,128]{1,0:T(8,128)(2,1)S(1)} %get-tuple-element.34.rest_3_), channel_id=1, source_target_pairs={{8,16},{12,20},{16,8},{20,12},{9,17},{13,21},{17,9},{21,13},{10,18... | collective-permute-start | bytes 1241096 | tf_op jit(solution)/shard_map/ppermute | solution.py:427
  67.3 17.6 %collective-permute-start.18 = (s16[1616,128]{1,0:T(8,128)(2,1)S(1)}, s16[1616,128]{1,0:T(8,128)(2,1)S(1)}, u32[]{:S(2)}, u32[]{:S(2)}) collective-permute-start(s16[1616,128]{1,0:T(8,128)(2,1)S(1)} %get-tuple-element.34.rest_3_), channel_id=1, source_target_pairs={{0,8},{4,12},{24,16},{28,20},{1,9},{5,13},{25,17},{29,21},{2,10},{... | collective-permute-start | bytes 1241096 | tf_op jit(solution)/shard_map/ppermute | solution.py:427
  74.1 14.8 %collective-permute-start.15 = (bf16[128,2048]{1,0:T(8,128)(2,1)S(1)}, bf16[128,2048]{1,0:T(8,128)(2,1)S(1)}, u32[]{:S(2)}, u32[]{:S(2)}) collective-permute-start(bf16[128,2048]{1,0:T(8,128)(2,1)S(1)} %get-tuple-element.33), channel_id=1, source_target_pairs={{0,4},{4,0},{8,12},{12,8},{16,20},{20,16},{24,28},{28,24},{1,5},{5... | collective-permute-start | bytes 1572872 | tf_op jit(solution)/shard_map/ppermute | solution.py:376
  77.9 14.8 %collective-permute-start.21 = (s16[1616,128]{1,0:T(8,128)(2,1)S(1)}, s16[1616,128]{1,0:T(8,128)(2,1)S(1)}, u32[]{:S(2)}, u32[]{:S(2)}) collective-permute-start(s16[1616,128]{1,0:T(8,128)(2,1)S(1)} %get-tuple-element.35.rest_2_), channel_id=1, source_target_pairs={{8,16},{12,20},{16,8},{20,12},{9,17},{13,21},{17,9},{21,13},{10,18... | collective-permute-start | bytes 1241096 | tf_op jit(solution)/shard_map/ppermute | solution.py:427
  78.6 14.8 %collective-permute-start.20 = (s16[1616,128]{1,0:T(8,128)(2,1)S(1)}, s16[1616,128]{1,0:T(8,128)(2,1)S(1)}, u32[]{:S(2)}, u32[]{:S(2)}) collective-permute-start(s16[1616,128]{1,0:T(8,128)(2,1)S(1)} %get-tuple-element.35.rest_2_), channel_id=1, source_target_pairs={{0,8},{4,12},{24,16},{28,20},{1,9},{5,13},{25,17},{29,21},{2,10},{... | collective-permute-start | bytes 1241096 | tf_op jit(solution)/shard_map/ppermute | solution.py:427
  83.4 16.6 %collective-permute-start.23 = (bf16[128,2048]{1,0:T(8,128)(2,1)S(1)}, bf16[128,2048]{1,0:T(8,128)(2,1)S(1)}, u32[]{:S(2)}, u32[]{:S(2)}) collective-permute-start(bf16[128,2048]{1,0:T(8,128)(2,1)S(1)} %get-tuple-element.38), channel_id=1, source_target_pairs={{0,4},{4,0},{8,12},{12,8},{16,20},{20,16},{24,28},{28,24},{1,5},{5... | collective-permute-start | bytes 1572872 | tf_op jit(solution)/shard_map/ppermute | solution.py:376
  91.0 12.1 %collective-permute-start.24 = (s16[1616,128]{1,0:T(8,128)(2,1)S(1)}, s16[1616,128]{1,0:T(8,128)(2,1)S(1)}, u32[]{:S(2)}, u32[]{:S(2)}) collective-permute-start(s16[1616,128]{1,0:T(8,128)(2,1)S(1)} %get-tuple-element.36.rest_2_), channel_id=1, source_target_pairs={{0,8},{4,12},{8,24},{12,28},{16,0},{20,4},{24,16},{28,20},{1,9},{5... | collective-permute-start | bytes 1241096 | tf_op jit(solution)/shard_map/ppermute | solution.py:427
  91.1 24.5 %collective-permute-start.28 = (bf16[128,2048]{1,0:T(8,128)(2,1)S(1)}, bf16[128,2048]{1,0:T(8,128)(2,1)S(1)}, u32[]{:S(2)}, u32[]{:S(2)}) collective-permute-start(bf16[128,2048]{1,0:T(8,128)(2,1)S(1)} %get-tuple-element.40), channel_id=1, source_target_pairs={{0,4},{4,0},{8,12},{12,8},{16,20},{20,16},{24,28},{28,24},{1,5},{5... | collective-permute-start | bytes 1572872 | tf_op jit(solution)/shard_map/ppermute | solution.py:376
  95.6 16.4 %collective-permute-start.25 = (s16[1616,128]{1,0:T(8,128)(2,1)S(1)}, s16[1616,128]{1,0:T(8,128)(2,1)S(1)}, u32[]{:S(2)}, u32[]{:S(2)}) collective-permute-start(s16[1616,128]{1,0:T(8,128)(2,1)S(1)} %get-tuple-element.39.rest_1_), channel_id=1, source_target_pairs={{0,8},{4,12},{8,24},{12,28},{16,0},{20,4},{24,16},{28,20},{1,9},{5... | collective-permute-start | bytes 1241096 | tf_op jit(solution)/shard_map/ppermute | solution.py:427
  98.1 24.6 %collective-permute-start.22 = (bf16[128,2048]{1,0:T(8,128)(2,1)S(1)}, bf16[128,2048]{1,0:T(8,128)(2,1)S(1)}, u32[]{:S(2)}, u32[]{:S(2)}) collective-permute-start(bf16[128,2048]{1,0:T(8,128)(2,1)S(1)} %get-tuple-element.37), channel_id=1, source_target_pairs={{0,4},{4,0},{8,12},{12,8},{16,20},{20,16},{24,28},{28,24},{1,5},{5... | collective-permute-start | bytes 1572872 | tf_op jit(solution)/shard_map/ppermute | solution.py:376
  105.1 17.6 %collective-permute-start.27 = (s16[1616,128]{1,0:T(8,128)(2,1)S(1)}, s16[1616,128]{1,0:T(8,128)(2,1)S(1)}, u32[]{:S(2)}, u32[]{:S(2)}) collective-permute-start(s16[1616,128]{1,0:T(8,128)(2,1)S(1)} %sum_step_10.1.rest_1_), channel_id=1, source_target_pairs={{0,8},{4,12},{8,24},{12,28},{16,0},{20,4},{24,16},{28,20},{1,9},{5... | collective-permute-start | bytes 1241096 | tf_op jit(solution)/shard_map/ppermute | solution.py:427
  114.0 12.3 %collective-permute-start.26 = (s16[1616,128]{1,0:T(8,128)(2,1)S(1)}, s16[1616,128]{1,0:T(8,128)(2,1)S(1)}, u32[]{:S(2)}, u32[]{:S(2)}) collective-permute-start(s16[1616,128]{1,0:T(8,128)(2,1)S(1)} %sum_step_11.1), channel_id=1, source_target_pairs={{0,8},{4,12},{8,24},{12,28},{16,0},{20,4},{24,16},{28,20},{1,9},{5... | collective-permute-start | bytes 1241096 | tf_op jit(solution)/shard_map/ppermute | solution.py:427

commit v4 on v2

--- a/solution.py
+++ b/solution.py
@@ -22,7 +22,7 @@
 HALVES = 2
 FLIGHT = 2
 FIRST_SWAP = (0, 2)
-SWAPS = {0: (2, 1), 1: (4, 2), 2: (6, 2), 6: (8, 2), 8: (10, 2), 9: (12, 2), 10: (14, 2)}
+SWAPS = {0: (2, 1), 1: (4, 2), 2: (6, 2), 5: (8, 2), 7: (10, 2), 8: (12, 2), 9: (14, 2)}
 SWAP_WAITS = {}
 RAW_STEP, RAW_WAIT = 2, 5
 INVERSE_STEP = 0

time: 133 us -> 128 us (0.962)
  waiting for transfers between devices: 29.4 us -> 20.3 us
  starting transfers between devices: 52.3 us -> 56.1 us
    ppermute x8, waiting for transfers between devices: 13 us -> 1.9 us  [swapped(): here = lax.ppermute(away, 'ifg', swap)]
    ppermute x15, starting transfers between devices: 35.2 us -> 39.9 us  [solve_by_sums(): lax.ppermute(coded, 'ifg', line_permutation(links))]
    ppermute x15, waiting for transfers between devices: 16.3 us -> 18.4 us  [solve_by_sums(): lax.ppermute(coded, 'ifg', line_permutation(links))]
  transfers between devices with their start and end apart: 29 -> 29, of which waited for: 10 -> 7; matrix products, arithmetic and copies ran while one was open for 2% -> 2% of each run, Pallas kernels for 31% -> 33%
where the time goes in v4:
time: 128 us; the launch traced here: 127 us
  starting transfers between devices  56.1 us (44%)
  Pallas kernels  45.3 us (35%)
  waiting for transfers between devices  20.3 us (16%)
  local copies, waits for them, and re-layouts  4.38 us (3%)
    ppermute x15, starting transfers between devices, solve_by_sums(): lax.ppermute(coded, 'ifg', line_permutation(links))  39.9 us
    pallas_call x11, Pallas kernels, step(): pl.pallas_call(functools.partial(step_kernel, at, layout, len(earlier), s...  23.3 us
    ppermute x15, waiting for transfers between devices, solve_by_sums(): lax.ppermute(coded, 'ifg', line_permutation(links))  18.4 us
    pallas_call x4, Pallas kernels, finish(): pl.pallas_call(functools.partial(finish_kernel, at, layout, tiles, len(ra...  14.5 us
    pallas_call x1, Pallas kernels, invert_classes(): pl.pallas_call(inverse_kernel, out_shape=jax.ShapeDtypeStruct(shape, F32)...  7.56 us
    ppermute x8, starting transfers between devices, swapped(): here = lax.ppermute(away, 'ifg', swap)  6.7 us
    ppermute x3, starting transfers between devices, solve_by_sums(): counts.append(lax.ppermute(run_counts, 'ifg', line_permutation(links)))  6.11 us
  transfers between devices with their start and end apart: 29, of which 7 were waited for; matrix products, arithmetic and copies ran while one was open for 2% of the time, Pallas kernels for 33%

profile of v4, /device:TPU:0, one launch (start us, length us, event | category | flops | bytes accessed | tf_op | source)
XLA Modules:
  0.0 127.3 jit_solution(17476567839233966568)
XLA Ops:
  0.0 1.1 dynamic-slice_bitcast_fusion
  1.2 0.8 fusion.counts_ref
  2.1 5.1 %collective-permute-start.2 = (s32[2]{0:T(128)S(1)}, s32[2]{0:T(128)S(1)}, u32[]{:S(2)}, u32[]{:S(2)}) collective-permute-start(s32[2]{0:T(128)S(1)} %fusion.counts_ref), channel_id=1, source_target_pairs={{0,24},{4,28},{8,0},{12,4},{16,8},{20,12},{24,16},{28,20},{1,25},{... | collective-permute-start | bytes 32 | tf_op jit(solution)/shard_map/ppermute | solution.py:394
  7.2 1.0 collective-permute-start
  8.2 1.5 %collective-permute-start.3 = (bf16[128,2048]{1,0:T(8,128)(2,1)S(1)}, bf16[128,2048]{1,0:T(8,128)(2,1)S(1)}, u32[]{:S(2)}, u32[]{:S(2)}) collective-permute-start(bf16[128,2048]{1,0:T(8,128)(2,1)S(1)} %dynamic-slice_bitcast_fusion), channel_id=1, source_target_pairs={{0,4},{4,0},{8,12},{12,8},{16,20},{20,16},{24,28},{28,24},{1,5},{5... | collective-permute-start | bytes 1572872 | tf_op jit(solution)/shard_map/ppermute | solution.py:376
  9.7 1.1 dynamic-slice_bitcast_fusion.1
  10.7 2.5 %collective-permute-start.5 = (bf16[128,1024]{1,0:T(8,128)(2,1)S(1)}, bf16[128,1024]{1,0:T(8,128)(2,1)S(1)}, u32[]{:S(2)}, u32[]{:S(2)}) collective-permute-start(bf16[128,1024]{1,0:T(8,128)(2,1)S(1)} %get-tuple-element.45), channel_id=1, source_target_pairs={{0,8},{4,12},{8,0},{12,4},{16,24},{20,28},{24,16},{28,20},{1,9},{5... | collective-permute-start | bytes 786440 | tf_op jit(solution)/shard_map/ppermute | solution.py:398
  13.3 0.7 constant_dynamic-slice_fusion.3
  14.2 0.7 fusion.1.table
  14.9 0.7 copy-done.1
  15.6 7.6 %invert_classes_0.1.rest_1_.inverse_ref = f32[2,256,256]{2,1,0:T(8,128)S(1)} custom-call(s32[2]{0:T(128)S(1)} %fusion.counts_ref, s32[2,1024]{1,0:T(2,128)S(1)} %copy-done.1, s32[8]{0:T(128)S(1)} %pad_add_fusion.1.rest_0_.counts), custom_call_target="tpu_custom_call" | custom-call | flops 1024 | bytes 1024 | tf_op jit(solution)/shard_map/invert_classes_0/pallas_call | solution.py:103
  23.2 2.1 %sum_step_00.1 = (s16[1616,128]{1,0:T(8,128)(2,1)S(1)}, bf16[128,1024]{1,0:T(8,128)(2,1)S(1)}) custom-call(s32[53]{0:T(128)S(1)} %fusion.1.table, s32[8]{0:T(128)S(1)} %pad_add_fusion.1.rest_0_.counts, s32[2,512]{1,0:T(2,128)S(1)} %pad_add_fusion.pairs_ref, bf16[128,32768]{1,0:T(8,128)(2,1)} %bitcast.12, ...), custom_call_target="tpu_custom_call" | custom-call | flops 10000000000 | bytes 30000000 | tf_op jit(solution)/shard_map/sum_step_00/pallas_call | solution.py:245
  25.8 2.0 %collective-permute-start.8 = (s16[1616,128]{1,0:T(8,128)(2,1)S(1)}, s16[1616,128]{1,0:T(8,128)(2,1)S(1)}, u32[]{:S(2)}, u32[]{:S(2)}) collective-permute-start(s16[1616,128]{1,0:T(8,128)(2,1)S(1)} %get-tuple-element.26.rest_1_), channel_id=1, source_target_pairs={{0,8},{4,12},{8,0},{12,4},{16,24},{20,28},{24,16},{28,20},{1,9},{5... | collective-permute-start | bytes 1241096 | tf_op jit(solution)/shard_map/ppermute | solution.py:427
  27.8 2.2 %sum_step_01.1 = (s16[1616,128]{1,0:T(8,128)(2,1)S(1)}, bf16[128,2048]{1,0:T(8,128)(2,1)S(1)}) custom-call(s32[53]{0:T(128)S(1)} %fusion.1.table, s32[8]{0:T(128)S(1)} %pad_add_fusion.1.rest_0_.counts, s32[2,512]{1,0:T(2,128)S(1)} %pad_add_fusion.pairs_ref, bf16[128,32768]{1,0:T(8,128)(2,1)} %bitcast.14, ...), custom_call_target="tpu_custom_call" | custom-call | flops 10000000000 | bytes 30000000 | tf_op jit(solution)/shard_map/sum_step_01/pallas_call | solution.py:245
  30.1 1.5 %collective-permute-start.6 = (bf16[128,2048]{1,0:T(8,128)(2,1)S(1)}, bf16[128,2048]{1,0:T(8,128)(2,1)S(1)}, u32[]{:S(2)}, u32[]{:S(2)}) collective-permute-start(bf16[128,2048]{1,0:T(8,128)(2,1)S(1)} %get-tuple-element.29), channel_id=1, source_target_pairs={{0,4},{4,0},{8,12},{12,8},{16,20},{20,16},{24,28},{28,24},{1,5},{5... | collective-permute-start | bytes 1572872 | tf_op jit(solution)/shard_map/ppermute | solution.py:376
  31.6 1.9 %collective-permute-done.9.partner_ref = bf16[128,1024]{1,0:T(8,128)(2,1)S(1)} collective-permute-done((bf16[128,1024]{1,0:T(8,128)(2,1)S(1)}, bf16[128,1024]{1,0:T(8,128)(2,1)S(1)}, u32[]{:S(2)}, u32[]{:S(2)}) %collective-permute-start.9) | collective-permute-done | bytes 262176 | tf_op jit(solution)/shard_map/ppermute | solution.py:376
  33.5 4.8 %collective-permute-done.8.rest_2_.rest_0_.rest_1_ = s16[1616,128]{1,0:T(8,128)(2,1)S(1)} collective-permute-done((s16[1616,128]{1,0:T(8,128)(2,1)S(1)}, s16[1616,128]{1,0:T(8,128)(2,1)S(1)}, u32[]{:S(2)}, u32[]{:S(2)}) %collective-permute-start.8) | collective-permute-done | bytes 413728 | tf_op jit(solution)/shard_map/ppermute | solution.py:427
  38.3 2.2 %sum_step_02.1 = (s16[1616,128]{1,0:T(8,128)(2,1)S(1)}, bf16[128,2048]{1,0:T(8,128)(2,1)S(1)}) custom-call(s32[53]{0:T(128)S(1)} %fusion.1.table, s32[8]{0:T(128)S(1)} %pad_add_fusion.1.rest_0_.counts, s32[2,512]{1,0:T(2,128)S(1)} %pad_add_fusion.pairs_ref, bf16[128,32768]{1,0:T(8,128)(2,1)} %bitcast.16, ...), custom_call_target="tpu_custom_call" | custom-call | flops 10000000000 | bytes 30000000 | tf_op jit(solution)/shard_map/sum_step_02/pallas_call | solution.py:245
  40.5 2.0 %collective-permute-start.10 = (s16[1616,128]{1,0:T(8,128)(2,1)S(1)}, s16[1616,128]{1,0:T(8,128)(2,1)S(1)}, u32[]{:S(2)}, u32[]{:S(2)}) collective-permute-start(s16[1616,128]{1,0:T(8,128)(2,1)S(1)} %get-tuple-element.32.rest_1_), channel_id=1, source_target_pairs={{0,8},{4,12},{8,0},{12,4},{16,24},{20,28},{24,16},{28,20},{1,9},{5... | collective-permute-start | bytes 1241096 | tf_op jit(solution)/shard_map/ppermute | solution.py:427
  42.6 0.7 collective-permute-start.11
  43.3 1.3 %collective-permute-start.15 = (bf16[128,2048]{1,0:T(8,128)(2,1)S(1)}, bf16[128,2048]{1,0:T(8,128)(2,1)S(1)}, u32[]{:S(2)}, u32[]{:S(2)}) collective-permute-start(bf16[128,2048]{1,0:T(8,128)(2,1)S(1)} %get-tuple-element.36), channel_id=1, source_target_pairs={{0,4},{4,0},{8,12},{12,8},{16,20},{20,16},{24,28},{28,24},{1,5},{5... | collective-permute-start | bytes 1572872 | tf_op jit(solution)/shard_map/ppermute | solution.py:376
  44.6 2.6 %collective-permute-done.7.rest_2_.rest_1_.rest_0_ = s16[1616,128]{1,0:T(8,128)(2,1)S(1)} collective-permute-done((s16[1616,128]{1,0:T(8,128)(2,1)S(1)}, s16[1616,128]{1,0:T(8,128)(2,1)S(1)}, u32[]{:S(2)}, u32[]{:S(2)}) %collective-permute-start.7) | collective-permute-done | bytes 413728 | tf_op jit(solution)/shard_map/ppermute | solution.py:427
  47.2 2.0 %sum_step_04.1.rest_2_ = s16[1616,128]{1,0:T(8,128)(2,1)S(1)} custom-call(s32[53]{0:T(128)S(1)} %fusion.1.table, s32[8]{0:T(128)S(1)} %pad_add_fusion.1.rest_0_.counts, s32[2,512]{1,0:T(2,128)S(1)} %pad_add_fusion.pairs_ref, bf16[128,32768]{1,0:T(8,128)(2,1)} %bitcast.18, bf16[128,2048]{1,0:T(8,128)(2,1)S(1)} %collective-permute-done.6.partner_ref, ...), custom_call_target="tpu_custom_call" | custom-call | flops 10000000000 | bytes 30000000 | tf_op jit(solution)/shard_map/sum_step_04/pallas_call | solution.py:245
  49.2 0.7 collective-permute-start.16
  49.9 5.2 %collective-permute-start.14 = (s16[1616,128]{1,0:T(8,128)(2,1)S(1)}, s16[1616,128]{1,0:T(8,128)(2,1)S(1)}, u32[]{:S(2)}, u32[]{:S(2)}) collective-permute-start(s16[1616,128]{1,0:T(8,128)(2,1)S(1)} %sum_step_04.1.rest_2_), channel_id=1, source_target_pairs={{0,8},{4,12},{24,16},{28,20},{1,9},{5,13},{25,17},{29,21},{2,10},{... | collective-permute-start | bytes 1241096 | tf_op jit(solution)/shard_map/ppermute | solution.py:427
  55.6 2.2 %sum_step_05.1 = (s16[1616,128]{1,0:T(8,128)(2,1)S(1)}, bf16[128,2048]{1,0:T(8,128)(2,1)S(1)}) custom-call(s32[53]{0:T(128)S(1)} %fusion.1.table, s32[8]{0:T(128)S(1)} %pad_add_fusion.1.rest_0_.counts, s32[2,512]{1,0:T(2,128)S(1)} %pad_add_fusion.pairs_ref, bf16[128,32768]{1,0:T(8,128)(2,1)} %bitcast.19, ...), custom_call_target="tpu_custom_call" | custom-call | flops 10000000000 | bytes 30000000 | tf_op jit(solution)/shard_map/sum_step_05/pallas_call | solution.py:245
  58.5 5.6 %collective-permute-start.13 = (s16[1616,128]{1,0:T(8,128)(2,1)S(1)}, s16[1616,128]{1,0:T(8,128)(2,1)S(1)}, u32[]{:S(2)}, u32[]{:S(2)}) collective-permute-start(s16[1616,128]{1,0:T(8,128)(2,1)S(1)} %get-tuple-element.35.rest_1_), channel_id=1, source_target_pairs={{0,8},{4,12},{24,16},{28,20},{1,9},{5,13},{25,17},{29,21},{2,10},{... | collective-permute-start | bytes 1241096 | tf_op jit(solution)/shard_map/ppermute | solution.py:427
  64.1 0.8 collective-permute-start.12
  64.9 2.0 %sum_step_06.1.rest_3_ = s16[1616,128]{1,0:T(8,128)(2,1)S(1)} custom-call(s32[53]{0:T(128)S(1)} %fusion.1.table, s32[8]{0:T(128)S(1)} %pad_add_fusion.1.rest_0_.counts, s32[2,512]{1,0:T(2,128)S(1)} %pad_add_fusion.pairs_ref, bf16[128,32768]{1,0:T(8,128)(2,1)} %bitcast.21, bf16[128,2048]{1,0:T(8,128)(2,1)S(1)} %collective-permute-done.15.partner_ref, ...), custom_call_target="tpu_custom_call" | custom-call | flops 10000000000 | bytes 30000000 | tf_op jit(solution)/shard_map/sum_step_06/pallas_call | solution.py:245
  67.6 6.0 %collective-permute-start.18 = (s16[1616,128]{1,0:T(8,128)(2,1)S(1)}, s16[1616,128]{1,0:T(8,128)(2,1)S(1)}, u32[]{:S(2)}, u32[]{:S(2)}) collective-permute-start(s16[1616,128]{1,0:T(8,128)(2,1)S(1)} %sum_step_06.1.rest_3_), channel_id=1, source_target_pairs={{0,8},{4,12},{24,16},{28,20},{1,9},{5,13},{25,17},{29,21},{2,10},{... | collective-permute-start | bytes 1241096 | tf_op jit(solution)/shard_map/ppermute | solution.py:427
  73.7 2.2 %sum_step_07.1 = (s16[1616,128]{1,0:T(8,128)(2,1)S(1)}, bf16[128,2048]{1,0:T(8,128)(2,1)S(1)}) custom-call(s32[53]{0:T(128)S(1)} %fusion.1.table, s32[8]{0:T(128)S(1)} %pad_add_fusion.1.rest_0_.counts, s32[2,512]{1,0:T(2,128)S(1)} %pad_add_fusion.pairs_ref, bf16[128,32768]{1,0:T(8,128)(2,1)} %bitcast.22, ...), custom_call_target="tpu_custom_call" | custom-call | flops 10000000000 | bytes 30000000 | tf_op jit(solution)/shard_map/sum_step_07/pallas_call | solution.py:245
  76.6 7.4 %collective-permute-start.20 = (s16[1616,128]{1,0:T(8,128)(2,1)S(1)}, s16[1616,128]{1,0:T(8,128)(2,1)S(1)}, u32[]{:S(2)}, u32[]{:S(2)}) collective-permute-start(s16[1616,128]{1,0:T(8,128)(2,1)S(1)} %get-tuple-element.37.rest_2_), channel_id=1, source_target_pairs={{0,8},{4,12},{24,16},{28,20},{1,9},{5,13},{25,17},{29,21},{2,10},{... | collective-permute-start | bytes 1241096 | tf_op jit(solution)/shard_map/ppermute | solution.py:427
  84.2 2.2 %sum_step_08.1 = (s16[1616,128]{1,0:T(8,128)(2,1)S(1)}, bf16[128,2048]{1,0:T(8,128)(2,1)S(1)}) custom-call(s32[53]{0:T(128)S(1)} %fusion.1.table, s32[8]{0:T(128)S(1)} %pad_add_fusion.1.rest_0_.counts, s32[2,512]{1,0:T(2,128)S(1)} %pad_add_fusion.pairs_ref, bf16[128,32768]{1,0:T(8,128)(2,1)} %bitcast.24, ...), custom_call_target="tpu_custom_call" | custom-call | flops 10000000000 | bytes 30000000 | tf_op jit(solution)/shard_map/sum_step_08/pallas_call | solution.py:245
  86.4 1.2 collective-permute-start.24
  87.6 0.9 collective-permute-start.26
  88.5 5.5 %collective-permute-done.20.rest_3_.rest_0_ = s16[1616,128]{1,0:T(8,128)(2,1)S(1)} collective-permute-done((s16[1616,128]{1,0:T(8,128)(2,1)S(1)}, s16[1616,128]{1,0:T(8,128)(2,1)S(1)}, u32[]{:S(2)}, u32[]{:S(2)}) %collective-permute-start.20) | collective-permute-done | bytes 413728 | tf_op jit(solution)/shard_map/ppermute | solution.py:427
  94.0 2.2 %sum_step_09.1 = (s16[1616,128]{1,0:T(8,128)(2,1)S(1)}, bf16[128,2048]{1,0:T(8,128)(2,1)S(1)}) custom-call(s32[53]{0:T(128)S(1)} %fusion.1.table, s32[8]{0:T(128)S(1)} %pad_add_fusion.1.rest_0_.counts, s32[2,512]{1,0:T(2,128)S(1)} %pad_add_fusion.pairs_ref, bf16[128,32768]{1,0:T(8,128)(2,1)} %bitcast.26, ...), custom_call_target="tpu_custom_call" | custom-call | flops 10000000000 | bytes 30000000 | tf_op jit(solution)/shard_map/sum_step_09/pallas_call | solution.py:245
  96.2 2.5 %collective-permute-start.25 = (s16[1616,128]{1,0:T(8,128)(2,1)S(1)}, s16[1616,128]{1,0:T(8,128)(2,1)S(1)}, u32[]{:S(2)}, u32[]{:S(2)}) collective-permute-start(s16[1616,128]{1,0:T(8,128)(2,1)S(1)} %get-tuple-element.41.rest_1_), channel_id=1, source_target_pairs={{0,8},{4,12},{8,24},{12,28},{16,0},{20,4},{24,16},{28,20},{1,9},{5... | collective-permute-start | bytes 1241096 | tf_op jit(solution)/shard_map/ppermute | solution.py:427
  98.8 4.1 %collective-permute-done.24.rest_2_.rest_4_.rest_5_ = s16[1616,128]{1,0:T(8,128)(2,1)S(1)} collective-permute-done((s16[1616,128]{1,0:T(8,128)(2,1)S(1)}, s16[1616,128]{1,0:T(8,128)(2,1)S(1)}, u32[]{:S(2)}, u32[]{:S(2)}) %collective-permute-start.24) | collective-permute-done | bytes 413728 | tf_op jit(solution)/shard_map/ppermute | solution.py:427
  102.9 2.0 %sum_step_10.1.rest_1_ = s16[1616,128]{1,0:T(8,128)(2,1)S(1)} custom-call(s32[53]{0:T(128)S(1)} %fusion.1.table, s32[8]{0:T(128)S(1)} %pad_add_fusion.1.rest_0_.counts, s32[2,512]{1,0:T(2,128)S(1)} %pad_add_fusion.pairs_ref, bf16[128,32768]{1,0:T(8,128)(2,1)} %bitcast.28, bf16[128,2048]{1,0:T(8,128)(2,1)S(1)} %collective-permute-done.23.partner_ref, ...), custom_call_target="tpu_custom_call" | custom-call | flops 10000000000 | bytes 30000000 | tf_op jit(solution)/shard_map/sum_step_10/pallas_call | solution.py:245
  104.9 2.5 %collective-permute-start.28 = (s16[1616,128]{1,0:T(8,128)(2,1)S(1)}, s16[1616,128]{1,0:T(8,128)(2,1)S(1)}, u32[]{:S(2)}, u32[]{:S(2)}) collective-permute-start(s16[1616,128]{1,0:T(8,128)(2,1)S(1)} %sum_step_10.1.rest_1_), channel_id=1, source_target_pairs={{0,8},{4,12},{8,24},{12,28},{16,0},{20,4},{24,16},{28,20},{1,9},{5... | collective-permute-start | bytes 1241096 | tf_op jit(solution)/shard_map/ppermute | solution.py:427
  107.4 3.5 %finish_0.1 = (f32[200,4096]{1,0:T(8,128)}, f32[8,128]{1,0:T(8,128)S(1)}) custom-call(s32[53]{0:T(128)S(1)} %fusion.1.table, s32[8]{0:T(128)S(1)} %pad_add_fusion.1.rest_0_.counts, s32[2,512]{1,0:T(2,128)S(1)} %pad_add_fusion.pairs_ref, bf16[128,32768]{1,0:T(8,128)(2,1)} %bitcast.29, bf16[128,2048]{1,0:T(8,128)(2,1)S(1)} %collective-permute-done.26.partner_ref, ...), custom_call_target="tpu_custom_call" | custom-call | flops 1024 | bytes 1024 | tf_op jit(solution)/shard_map/finish_0/pallas_call | solution.py:327
  111.0 0.8 collective-permute-done.25.rest_2_.rest_4_.rest_5_
  111.8 2.0 %sum_step_11.1 = s16[1616,128]{1,0:T(8,128)(2,1)S(1)} custom-call(s32[53]{0:T(128)S(1)} %fusion.1.table, s32[8]{0:T(128)S(1)} %pad_add_fusion.1.rest_0_.counts, s32[2,512]{1,0:T(2,128)S(1)} %pad_add_fusion.pairs_ref, bf16[128,32768]{1,0:T(8,128)(2,1)} %bitcast.30, bf16[128,2048]{1,0:T(8,128)(2,1)S(1)} %collective-permute-done.23.partner_ref, ...), custom_call_target="tpu_custom_call" | custom-call | flops 10000000000 | bytes 30000000 | tf_op jit(solution)/shard_map/sum_step_11/pallas_call | solution.py:245
  113.8 2.5 %collective-permute-start.27 = (s16[1616,128]{1,0:T(8,128)(2,1)S(1)}, s16[1616,128]{1,0:T(8,128)(2,1)S(1)}, u32[]{:S(2)}, u32[]{:S(2)}) collective-permute-start(s16[1616,128]{1,0:T(8,128)(2,1)S(1)} %sum_step_11.1), channel_id=1, source_target_pairs={{0,8},{4,12},{8,24},{12,28},{16,0},{20,4},{24,16},{28,20},{1,9},{5... | collective-permute-start | bytes 1241096 | tf_op jit(solution)/shard_map/ppermute | solution.py:427
  116.3 3.6 %finish_1.1.rest_6_ = f32[200,4096]{1,0:T(8,128)} custom-call(s32[53]{0:T(128)S(1)} %fusion.1.table, s32[8]{0:T(128)S(1)} %pad_add_fusion.1.rest_0_.counts, s32[2,512]{1,0:T(2,128)S(1)} %pad_add_fusion.pairs_ref, bf16[128,32768]{1,0:T(8,128)(2,1)} %bitcast.31, ...), custom_call_target="tpu_custom_call", output_to_operand_aliasing={{}: (12, {})} | custom-call | flops 1024 | bytes 1024 | tf_op jit(solution)/shard_map/finish_1/pallas_call | solution.py:327
  119.9 3.6 %finish_2.1.rest_6_ = f32[200,4096]{1,0:T(8,128)} custom-call(s32[53]{0:T(128)S(1)} %fusion.1.table, s32[8]{0:T(128)S(1)} %pad_add_fusion.1.rest_0_.counts, s32[2,512]{1,0:T(2,128)S(1)} %pad_add_fusion.pairs_ref, bf16[128,32768]{1,0:T(8,128)(2,1)} %bitcast.32, ...), custom_call_target="tpu_custom_call", output_to_operand_aliasing={{}: (12, {})} | custom-call | flops 1024 | bytes 1024 | tf_op jit(solution)/shard_map/finish_2/pallas_call | solution.py:327
  123.5 3.9 %finish_3.1 = f32[200,4096]{1,0:T(8,128)} custom-call(s32[53]{0:T(128)S(1)} %fusion.1.table, s32[8]{0:T(128)S(1)} %pad_add_fusion.1.rest_0_.counts, s32[2,512]{1,0:T(2,128)S(1)} %pad_add_fusion.pairs_ref, bf16[128,32768]{1,0:T(8,128)(2,1)} %bitcast.33, bf16[128,2048]{1,0:T(8,128)(2,1)S(1)} %collective-permute-done.22.partner_ref, ...), custom_call_target="tpu_custom_call", output_to_operand_aliasing={{}: (12, {})} | custom-call | flops 1024 | bytes 1024 | tf_op jit(solution)/shard_map/finish_3/pallas_call | solution.py:327
  (39 shorter events, 3.7 us)
Async XLA Ops:
  0.0 1.1 copy-start
  2.1 11.9 %collective-permute-start.2 = (s32[2]{0:T(128)S(1)}, s32[2]{0:T(128)S(1)}, u32[]{:S(2)}, u32[]{:S(2)}) collective-permute-start(s32[2]{0:T(128)S(1)} %fusion.counts_ref), channel_id=1, source_target_pairs={{0,24},{4,28},{8,0},{12,4},{16,8},{20,12},{24,16},{28,20},{1,25},{... | collective-permute-start | bytes 32 | tf_op jit(solution)/shard_map/ppermute | solution.py:394
  7.1 7.0 %collective-permute-start.1 = (s32[2]{0:T(128)S(1)}, s32[2]{0:T(128)S(1)}, u32[]{:S(2)}, u32[]{:S(2)}) collective-permute-start(s32[2]{0:T(128)S(1)} %fusion.counts_ref), channel_id=1, source_target_pairs={{0,16},{4,20},{8,24},{12,28},{16,0},{20,4},{24,8},{28,12},{1,17},{... | collective-permute-start | bytes 32 | tf_op jit(solution)/shard_map/ppermute | solution.py:394
  7.2 7.0 %collective-permute-start = (s32[2]{0:T(128)S(1)}, s32[2]{0:T(128)S(1)}, u32[]{:S(2)}, u32[]{:S(2)}) collective-permute-start(s32[2]{0:T(128)S(1)} %fusion.counts_ref), channel_id=1, source_target_pairs={{0,8},{4,12},{8,16},{12,20},{16,24},{20,28},{24,0},{28,4},{1,9},{5... | collective-permute-start | bytes 32 | tf_op jit(solution)/shard_map/ppermute | solution.py:394
  8.2 15.0 %collective-permute-start.3 = (bf16[128,2048]{1,0:T(8,128)(2,1)S(1)}, bf16[128,2048]{1,0:T(8,128)(2,1)S(1)}, u32[]{:S(2)}, u32[]{:S(2)}) collective-permute-start(bf16[128,2048]{1,0:T(8,128)(2,1)S(1)} %dynamic-slice_bitcast_fusion), channel_id=1, source_target_pairs={{0,4},{4,0},{8,12},{12,8},{16,20},{20,16},{24,28},{28,24},{1,5},{5... | collective-permute-start | bytes 1572872 | tf_op jit(solution)/shard_map/ppermute | solution.py:376
  10.7 17.1 %collective-permute-start.5 = (bf16[128,1024]{1,0:T(8,128)(2,1)S(1)}, bf16[128,1024]{1,0:T(8,128)(2,1)S(1)}, u32[]{:S(2)}, u32[]{:S(2)}) collective-permute-start(bf16[128,1024]{1,0:T(8,128)(2,1)S(1)} %get-tuple-element.45), channel_id=1, source_target_pairs={{0,8},{4,12},{8,0},{12,4},{16,24},{20,28},{24,16},{28,20},{1,9},{5... | collective-permute-start | bytes 786440 | tf_op jit(solution)/shard_map/ppermute | solution.py:398
  14.0 13.8 %collective-permute-start.4 = (bf16[128,1024]{1,0:T(8,128)(2,1)S(1)}, bf16[128,1024]{1,0:T(8,128)(2,1)S(1)}, u32[]{:S(2)}, u32[]{:S(2)}) collective-permute-start(bf16[128,1024]{1,0:T(8,128)(2,1)S(1)} %get-tuple-element.46), channel_id=1, source_target_pairs={{0,8},{4,12},{8,0},{12,4},{16,24},{20,28},{24,16},{28,20},{1,9},{5... | collective-permute-start | bytes 786440 | tf_op jit(solution)/shard_map/ppermute | solution.py:399
  14.9 0.7 copy-start.1
  25.2 8.2 %collective-permute-start.9 = (bf16[128,1024]{1,0:T(8,128)(2,1)S(1)}, bf16[128,1024]{1,0:T(8,128)(2,1)S(1)}, u32[]{:S(2)}, u32[]{:S(2)}) collective-permute-start(bf16[128,1024]{1,0:T(8,128)(2,1)S(1)} %get-tuple-element.31), channel_id=1, source_target_pairs={{0,4},{4,0},{8,12},{12,8},{16,20},{20,16},{24,28},{28,24},{1,5},{5... | collective-permute-start | bytes 786440 | tf_op jit(solution)/shard_map/ppermute | solution.py:376
  25.8 12.5 %collective-permute-start.8 = (s16[1616,128]{1,0:T(8,128)(2,1)S(1)}, s16[1616,128]{1,0:T(8,128)(2,1)S(1)}, u32[]{:S(2)}, u32[]{:S(2)}) collective-permute-start(s16[1616,128]{1,0:T(8,128)(2,1)S(1)} %get-tuple-element.26.rest_1_), channel_id=1, source_target_pairs={{0,8},{4,12},{8,0},{12,4},{16,24},{20,28},{24,16},{28,20},{1,9},{5... | collective-permute-start | bytes 1241096 | tf_op jit(solution)/shard_map/ppermute | solution.py:427
  30.0 17.2 %collective-permute-start.7 = (s16[1616,128]{1,0:T(8,128)(2,1)S(1)}, s16[1616,128]{1,0:T(8,128)(2,1)S(1)}, u32[]{:S(2)}, u32[]{:S(2)}) collective-permute-start(s16[1616,128]{1,0:T(8,128)(2,1)S(1)} %get-tuple-element.30.rest_1_), channel_id=1, source_target_pairs={{0,8},{4,12},{8,0},{12,4},{16,24},{20,28},{24,16},{28,20},{1,9},{5... | collective-permute-start | bytes 1241096 | tf_op jit(solution)/shard_map/ppermute | solution.py:427
  30.1 17.1 %collective-permute-start.6 = (bf16[128,2048]{1,0:T(8,128)(2,1)S(1)}, bf16[128,2048]{1,0:T(8,128)(2,1)S(1)}, u32[]{:S(2)}, u32[]{:S(2)}) collective-permute-start(bf16[128,2048]{1,0:T(8,128)(2,1)S(1)} %get-tuple-element.29), channel_id=1, source_target_pairs={{0,4},{4,0},{8,12},{12,8},{16,20},{20,16},{24,28},{28,24},{1,5},{5... | collective-permute-start | bytes 1572872 | tf_op jit(solution)/shard_map/ppermute | solution.py:376
  40.5 15.1 %collective-permute-start.10 = (s16[1616,128]{1,0:T(8,128)(2,1)S(1)}, s16[1616,128]{1,0:T(8,128)(2,1)S(1)}, u32[]{:S(2)}, u32[]{:S(2)}) collective-permute-start(s16[1616,128]{1,0:T(8,128)(2,1)S(1)} %get-tuple-element.32.rest_1_), channel_id=1, source_target_pairs={{0,8},{4,12},{8,0},{12,4},{16,24},{20,28},{24,16},{28,20},{1,9},{5... | collective-permute-start | bytes 1241096 | tf_op jit(solution)/shard_map/ppermute | solution.py:427
  42.6 12.5 %collective-permute-start.11 = (bf16[128,1024]{1,0:T(8,128)(2,1)S(1)}, bf16[128,1024]{1,0:T(8,128)(2,1)S(1)}, u32[]{:S(2)}, u32[]{:S(2)}) collective-permute-start(bf16[128,1024]{1,0:T(8,128)(2,1)S(1)} %collective-permute-done.5.rest_3_), channel_id=1, source_target_pairs={{0,4},{4,0},{8,12},{12,8},{16,20},{20,16},{24,28},{28,24},{1,5},{5... | collective-permute-start | bytes 786440 | tf_op jit(solution)/shard_map/ppermute | solution.py:433
  43.3 20.9 %collective-permute-start.15 = (bf16[128,2048]{1,0:T(8,128)(2,1)S(1)}, bf16[128,2048]{1,0:T(8,128)(2,1)S(1)}, u32[]{:S(2)}, u32[]{:S(2)}) collective-permute-start(bf16[128,2048]{1,0:T(8,128)(2,1)S(1)} %get-tuple-element.36), channel_id=1, source_target_pairs={{0,4},{4,0},{8,12},{12,8},{16,20},{20,16},{24,28},{28,24},{1,5},{5... | collective-permute-start | bytes 1572872 | tf_op jit(solution)/shard_map/ppermute | solution.py:376
  49.2 15.7 %collective-permute-start.16 = (s16[1616,128]{1,0:T(8,128)(2,1)S(1)}, s16[1616,128]{1,0:T(8,128)(2,1)S(1)}, u32[]{:S(2)}, u32[]{:S(2)}) collective-permute-start(s16[1616,128]{1,0:T(8,128)(2,1)S(1)} %sum_step_04.1.rest_2_), channel_id=1, source_target_pairs={{8,16},{12,20},{16,8},{20,12},{9,17},{13,21},{17,9},{21,13},{10,18... | collective-permute-start | bytes 1241096 | tf_op jit(solution)/shard_map/ppermute | solution.py:427
  49.9 15.0 %collective-permute-start.14 = (s16[1616,128]{1,0:T(8,128)(2,1)S(1)}, s16[1616,128]{1,0:T(8,128)(2,1)S(1)}, u32[]{:S(2)}, u32[]{:S(2)}) collective-permute-start(s16[1616,128]{1,0:T(8,128)(2,1)S(1)} %sum_step_04.1.rest_2_), channel_id=1, source_target_pairs={{0,8},{4,12},{24,16},{28,20},{1,9},{5,13},{25,17},{29,21},{2,10},{... | collective-permute-start | bytes 1241096 | tf_op jit(solution)/shard_map/ppermute | solution.py:427
  57.8 15.9 %collective-permute-start.17 = (s16[1616,128]{1,0:T(8,128)(2,1)S(1)}, s16[1616,128]{1,0:T(8,128)(2,1)S(1)}, u32[]{:S(2)}, u32[]{:S(2)}) collective-permute-start(s16[1616,128]{1,0:T(8,128)(2,1)S(1)} %get-tuple-element.35.rest_1_), channel_id=1, source_target_pairs={{8,16},{12,20},{16,8},{20,12},{9,17},{13,21},{17,9},{21,13},{10,18... | collective-permute-start | bytes 1241096 | tf_op jit(solution)/shard_map/ppermute | solution.py:427
  58.5 15.2 %collective-permute-start.13 = (s16[1616,128]{1,0:T(8,128)(2,1)S(1)}, s16[1616,128]{1,0:T(8,128)(2,1)S(1)}, u32[]{:S(2)}, u32[]{:S(2)}) collective-permute-start(s16[1616,128]{1,0:T(8,128)(2,1)S(1)} %get-tuple-element.35.rest_1_), channel_id=1, source_target_pairs={{0,8},{4,12},{24,16},{28,20},{1,9},{5,13},{25,17},{29,21},{2,10},{... | collective-permute-start | bytes 1241096 | tf_op jit(solution)/shard_map/ppermute | solution.py:427
  64.1 20.0 %collective-permute-start.12 = (bf16[128,2048]{1,0:T(8,128)(2,1)S(1)}, bf16[128,2048]{1,0:T(8,128)(2,1)S(1)}, u32[]{:S(2)}, u32[]{:S(2)}) collective-permute-start(bf16[128,2048]{1,0:T(8,128)(2,1)S(1)} %get-tuple-element.34), channel_id=1, source_target_pairs={{0,4},{4,0},{8,12},{12,8},{16,20},{20,16},{24,28},{28,24},{1,5},{5... | collective-permute-start | bytes 1572872 | tf_op jit(solution)/shard_map/ppermute | solution.py:376
  66.9 17.1 %collective-permute-start.19 = (s16[1616,128]{1,0:T(8,128)(2,1)S(1)}, s16[1616,128]{1,0:T(8,128)(2,1)S(1)}, u32[]{:S(2)}, u32[]{:S(2)}) collective-permute-start(s16[1616,128]{1,0:T(8,128)(2,1)S(1)} %sum_step_06.1.rest_3_), channel_id=1, source_target_pairs={{8,16},{12,20},{16,8},{20,12},{9,17},{13,21},{17,9},{21,13},{10,18... | collective-permute-start | bytes 1241096 | tf_op jit(solution)/shard_map/ppermute | solution.py:427
  67.6 16.5 %collective-permute-start.18 = (s16[1616,128]{1,0:T(8,128)(2,1)S(1)}, s16[1616,128]{1,0:T(8,128)(2,1)S(1)}, u32[]{:S(2)}, u32[]{:S(2)}) collective-permute-start(s16[1616,128]{1,0:T(8,128)(2,1)S(1)} %sum_step_06.1.rest_3_), channel_id=1, source_target_pairs={{0,8},{4,12},{24,16},{28,20},{1,9},{5,13},{25,17},{29,21},{2,10},{... | collective-permute-start | bytes 1241096 | tf_op jit(solution)/shard_map/ppermute | solution.py:427
  75.9 12.6 %collective-permute-start.21 = (s16[1616,128]{1,0:T(8,128)(2,1)S(1)}, s16[1616,128]{1,0:T(8,128)(2,1)S(1)}, u32[]{:S(2)}, u32[]{:S(2)}) collective-permute-start(s16[1616,128]{1,0:T(8,128)(2,1)S(1)} %get-tuple-element.37.rest_2_), channel_id=1, source_target_pairs={{8,16},{12,20},{16,8},{20,12},{9,17},{13,21},{17,9},{21,13},{10,18... | collective-permute-start | bytes 1241096 | tf_op jit(solution)/shard_map/ppermute | solution.py:427
  76.6 17.4 %collective-permute-start.20 = (s16[1616,128]{1,0:T(8,128)(2,1)S(1)}, s16[1616,128]{1,0:T(8,128)(2,1)S(1)}, u32[]{:S(2)}, u32[]{:S(2)}) collective-permute-start(s16[1616,128]{1,0:T(8,128)(2,1)S(1)} %get-tuple-element.37.rest_2_), channel_id=1, source_target_pairs={{0,8},{4,12},{24,16},{28,20},{1,9},{5,13},{25,17},{29,21},{2,10},{... | collective-permute-start | bytes 1241096 | tf_op jit(solution)/shard_map/ppermute | solution.py:427
  84.1 14.7 %collective-permute-start.23 = (bf16[128,2048]{1,0:T(8,128)(2,1)S(1)}, bf16[128,2048]{1,0:T(8,128)(2,1)S(1)}, u32[]{:S(2)}, u32[]{:S(2)}) collective-permute-start(bf16[128,2048]{1,0:T(8,128)(2,1)S(1)} %get-tuple-element.40), channel_id=1, source_target_pairs={{0,4},{4,0},{8,12},{12,8},{16,20},{20,16},{24,28},{28,24},{1,5},{5... | collective-permute-start | bytes 1572872 | tf_op jit(solution)/shard_map/ppermute | solution.py:376
  86.4 16.5 %collective-permute-start.24 = (s16[1616,128]{1,0:T(8,128)(2,1)S(1)}, s16[1616,128]{1,0:T(8,128)(2,1)S(1)}, u32[]{:S(2)}, u32[]{:S(2)}) collective-permute-start(s16[1616,128]{1,0:T(8,128)(2,1)S(1)} %get-tuple-element.38.rest_2_), channel_id=1, source_target_pairs={{0,8},{4,12},{8,24},{12,28},{16,0},{20,4},{24,16},{28,20},{1,9},{5... | collective-permute-start | bytes 1241096 | tf_op jit(solution)/shard_map/ppermute | solution.py:427
  87.6 19.9 %collective-permute-start.26 = (bf16[128,2048]{1,0:T(8,128)(2,1)S(1)}, bf16[128,2048]{1,0:T(8,128)(2,1)S(1)}, u32[]{:S(2)}, u32[]{:S(2)}) collective-permute-start(bf16[128,2048]{1,0:T(8,128)(2,1)S(1)} %get-tuple-element.42), channel_id=1, source_target_pairs={{0,4},{4,0},{8,12},{12,8},{16,20},{20,16},{24,28},{28,24},{1,5},{5... | collective-permute-start | bytes 1572872 | tf_op jit(solution)/shard_map/ppermute | solution.py:376
  96.2 15.5 %collective-permute-start.25 = (s16[1616,128]{1,0:T(8,128)(2,1)S(1)}, s16[1616,128]{1,0:T(8,128)(2,1)S(1)}, u32[]{:S(2)}, u32[]{:S(2)}) collective-permute-start(s16[1616,128]{1,0:T(8,128)(2,1)S(1)} %get-tuple-element.41.rest_1_), channel_id=1, source_target_pairs={{0,8},{4,12},{8,24},{12,28},{16,0},{20,4},{24,16},{28,20},{1,9},{5... | collective-permute-start | bytes 1241096 | tf_op jit(solution)/shard_map/ppermute | solution.py:427
  98.8 21.1 %collective-permute-start.22 = (bf16[128,2048]{1,0:T(8,128)(2,1)S(1)}, bf16[128,2048]{1,0:T(8,128)(2,1)S(1)}, u32[]{:S(2)}, u32[]{:S(2)}) collective-permute-start(bf16[128,2048]{1,0:T(8,128)(2,1)S(1)} %get-tuple-element.39), channel_id=1, source_target_pairs={{0,4},{4,0},{8,12},{12,8},{16,20},{20,16},{24,28},{28,24},{1,5},{5... | collective-permute-start | bytes 1572872 | tf_op jit(solution)/shard_map/ppermute | solution.py:376
  104.9 15.0 %collective-permute-start.28 = (s16[1616,128]{1,0:T(8,128)(2,1)S(1)}, s16[1616,128]{1,0:T(8,128)(2,1)S(1)}, u32[]{:S(2)}, u32[]{:S(2)}) collective-permute-start(s16[1616,128]{1,0:T(8,128)(2,1)S(1)} %sum_step_10.1.rest_1_), channel_id=1, source_target_pairs={{0,8},{4,12},{8,24},{12,28},{16,0},{20,4},{24,16},{28,20},{1,9},{5... | collective-permute-start | bytes 1241096 | tf_op jit(solution)/shard_map/ppermute | solution.py:427
  113.8 9.7 %collective-permute-start.27 = (s16[1616,128]{1,0:T(8,128)(2,1)S(1)}, s16[1616,128]{1,0:T(8,128)(2,1)S(1)}, u32[]{:S(2)}, u32[]{:S(2)}) collective-permute-start(s16[1616,128]{1,0:T(8,128)(2,1)S(1)} %sum_step_11.1), channel_id=1, source_target_pairs={{0,8},{4,12},{8,24},{12,28},{16,0},{20,4},{24,16},{28,20},{1,9},{5... | collective-permute-start | bytes 1241096 | tf_op jit(solution)/shard_map/ppermute | solution.py:427

commit v5 on v4

--- a/solution.py
+++ b/solution.py
@@ -270,9 +270,26 @@
     lots = sums_ref.shape[1] // LANES
     tile = pl.program_id(0)
     for coded_ref, codes_ref in zip(refs[::2], refs[1::2]):
-        parts = [decode(coded_ref, codes_ref, lots, at * lots) for at in range(tiles)]
-        scale = functools.reduce(lambda chosen, at: jnp.where(tile == at, parts[at][1], chosen), range(1, tiles), parts[0][1])
-        sums_ref[...] += parts[0][0] * scale
+        codes = codes_ref[...].astype(jnp.int32).astype(F32)
+        pieces = [codes[at * lots : (at + 1) * lots, :] for at in range(tiles)]
+        codes = functools.reduce(lambda chosen, at: jnp.where(tile == at, pieces[at], chosen), range(1, tiles), pieces[0])
+        scale = jnp.exp2(codes * (1.0 / CODES_PER_OCTAVE)) * (1.0 / LEVELS)
+        coded = coded_ref[...].astype(jnp.int32).astype(F32)
+        for lot in range(lots):
+            lanes = slice(lot * LANES, (lot + 1) * LANES)
+            sums_ref[:M, lanes] += coded[lot * M : (lot + 1) * M, :] * scale[lot : lot + 1, :]
+
+
+def solve_product(inverse, sums):
+    def halves(value):
+        high = value.astype(jnp.bfloat16)
+        return high, (value - high.astype(F32)).astype(jnp.bfloat16)
+
+    inverse_high, inverse_low = halves(inverse)
+    sums_high, sums_low = halves(sums)
+    left = jnp.concatenate([inverse_high, inverse_high, inverse_low], axis=1)
+    right = jnp.concatenate([sums_high, sums_low, sums_high], axis=0)
+    return jnp.dot(left, right, preferred_element_type=F32)
 
 
 def finish_kernel(at, layout, tiles, raw, told, table, counts, pairs_ref, own_ref, partner_ref, inverse_ref, *rest):
@@ -283,12 +300,13 @@
         rest = rest[:-1]
     out_ref = rest[-1]
     count = piece_count(at, layout, table, counts)
-    sums_ref[...] = pair_sums(count, table, pairs_ref, own_ref, partner_ref)
+    sums_ref[:M, :] = pair_sums(count, table, pairs_ref, own_ref, partner_ref)
+    sums_ref[M:, :] = jnp.zeros((PAD - M, sums_ref.shape[1]), F32)
 
     @pl.when(table[INNER] == 0)
     def _():
         if raw:
-            sums_ref[...] += near_sums(True, count, table, pairs_ref, first)
+            sums_ref[:M, :] += near_sums(True, count, table, pairs_ref, first)
         else:
             add_arrived(sums_ref, first, tiles)
 
@@ -297,7 +315,7 @@
         add_arrived(sums_ref, middle, tiles)
 
     add_arrived(sums_ref, last, tiles)
-    out_ref[...] = split_product(inverse_ref[0, :M, :M], sums_ref[...])
+    out_ref[...] = solve_product(inverse_ref[0, :M, :], sums_ref[...])
 
 
 def finish(at, part, layout, scalars, pairs, phases, partner, inverse, raw, arrived, series, told, pixels, piece):
@@ -332,7 +350,7 @@
             grid=(tiles,),
             in_specs=in_specs,
             out_specs=out_specs,
-            scratch_shapes=[pltpu.VMEM((M, tile), F32)],
+            scratch_shapes=[pltpu.VMEM((PAD, tile), F32)],
         ),
         input_output_aliases=aliases,
         compiler_params=pltpu.CompilerParams(vmem_limit_bytes=VMEM_BYTES),

time: 128 us -> 128 us (level)
  waiting for transfers between devices: 20.3 us -> 15.3 us
  starting transfers between devices: 56.1 us -> 60.8 us
    ppermute x8, starting transfers between devices: 6.7 us -> 13.6 us  [swapped(): here = lax.ppermute(away, 'ifg', swap)]
    ppermute x15, waiting for transfers between devices: 18.4 us -> 13.5 us  [solve_by_sums(): lax.ppermute(coded, 'ifg', line_permutation(links))]
    ppermute x15, starting transfers between devices: 39.9 us -> 36.4 us  [solve_by_sums(): lax.ppermute(coded, 'ifg', line_permutation(links))]
  transfers between devices with their start and end apart: 29 -> 29, of which waited for: 7 -> 10; matrix products, arithmetic and copies ran while one was open for 2% -> 2% of each run, Pallas kernels for 33% -> 33%
where the time goes in v5:
time: 128 us; the launch traced here: 127 us
  starting transfers between devices  60.8 us (48%)
  Pallas kernels  45.5 us (36%)
  waiting for transfers between devices  15.3 us (12%)
  local copies, waits for them, and re-layouts  4.38 us (3%)
    ppermute x15, starting transfers between devices, solve_by_sums(): lax.ppermute(coded, 'ifg', line_permutation(links))  36.4 us
    pallas_call x11, Pallas kernels, step(): pl.pallas_call(functools.partial(step_kernel, at, layout, len(earlier), s...  23.3 us
    pallas_call x4, Pallas kernels, finish(): pl.pallas_call(functools.partial(finish_kernel, at, layout, tiles, len(ra...  14.7 us
    ppermute x8, starting transfers between devices, swapped(): here = lax.ppermute(away, 'ifg', swap)  13.6 us
    ppermute x15, waiting for transfers between devices, solve_by_sums(): lax.ppermute(coded, 'ifg', line_permutation(links))  13.5 us
    pallas_call x1, Pallas kernels, invert_classes(): pl.pallas_call(inverse_kernel, out_shape=jax.ShapeDtypeStruct(shape, F32)...  7.56 us
    ppermute x3, starting transfers between devices, solve_by_sums(): counts.append(lax.ppermute(run_counts, 'ifg', line_permutation(links)))  6.11 us
  transfers between devices with their start and end apart: 29, of which 10 were waited for; matrix products, arithmetic and copies ran while one was open for 2% of the time, Pallas kernels for 33%

profile of v5, /device:TPU:0, one launch (start us, length us, event | category | flops | bytes accessed | tf_op | source)
XLA Modules:
  0.0 127.2 jit_solution(10061570438508991749)
XLA Ops:
  0.0 1.1 dynamic-slice_bitcast_fusion
  1.2 0.8 fusion.counts_ref
  2.1 5.1 %collective-permute-start.2 = (s32[2]{0:T(128)S(1)}, s32[2]{0:T(128)S(1)}, u32[]{:S(2)}, u32[]{:S(2)}) collective-permute-start(s32[2]{0:T(128)S(1)} %fusion.counts_ref), channel_id=1, source_target_pairs={{0,24},{4,28},{8,0},{12,4},{16,8},{20,12},{24,16},{28,20},{1,25},{... | collective-permute-start | bytes 32 | tf_op jit(solution)/shard_map/ppermute | solution.py:412
  7.2 1.0 collective-permute-start
  8.2 1.5 %collective-permute-start.3 = (bf16[128,2048]{1,0:T(8,128)(2,1)S(1)}, bf16[128,2048]{1,0:T(8,128)(2,1)S(1)}, u32[]{:S(2)}, u32[]{:S(2)}) collective-permute-start(bf16[128,2048]{1,0:T(8,128)(2,1)S(1)} %dynamic-slice_bitcast_fusion), channel_id=1, source_target_pairs={{0,4},{4,0},{8,12},{12,8},{16,20},{20,16},{24,28},{28,24},{1,5},{5... | collective-permute-start | bytes 1572872 | tf_op jit(solution)/shard_map/ppermute | solution.py:394
  9.7 1.1 dynamic-slice_bitcast_fusion.1
  10.7 2.5 %collective-permute-start.5 = (bf16[128,1024]{1,0:T(8,128)(2,1)S(1)}, bf16[128,1024]{1,0:T(8,128)(2,1)S(1)}, u32[]{:S(2)}, u32[]{:S(2)}) collective-permute-start(bf16[128,1024]{1,0:T(8,128)(2,1)S(1)} %get-tuple-element.45), channel_id=1, source_target_pairs={{0,8},{4,12},{8,0},{12,4},{16,24},{20,28},{24,16},{28,20},{1,9},{5... | collective-permute-start | bytes 786440 | tf_op jit(solution)/shard_map/ppermute | solution.py:416
  13.3 0.7 constant_dynamic-slice_fusion.3
  14.2 0.7 fusion.1.table
  15.6 7.6 %invert_classes_0.1.rest_1_.inverse_ref = f32[2,256,256]{2,1,0:T(8,128)S(1)} custom-call(s32[2]{0:T(128)S(1)} %fusion.counts_ref, s32[2,1024]{1,0:T(2,128)S(1)} %copy-done.1, s32[8]{0:T(128)S(1)} %pad_add_fusion.1.rest_0_.counts), custom_call_target="tpu_custom_call" | custom-call | flops 1024 | bytes 1024 | tf_op jit(solution)/shard_map/invert_classes_0/pallas_call | solution.py:103
  23.2 2.1 %sum_step_00.1 = (s16[1616,128]{1,0:T(8,128)(2,1)S(1)}, bf16[128,1024]{1,0:T(8,128)(2,1)S(1)}) custom-call(s32[53]{0:T(128)S(1)} %fusion.1.table, s32[8]{0:T(128)S(1)} %pad_add_fusion.1.rest_0_.counts, s32[2,512]{1,0:T(2,128)S(1)} %pad_add_fusion.pairs_ref, bf16[128,32768]{1,0:T(8,128)(2,1)} %bitcast.12, ...), custom_call_target="tpu_custom_call" | custom-call | flops 10000000000 | bytes 30000000 | tf_op jit(solution)/shard_map/sum_step_00/pallas_call | solution.py:245
  25.3 2.1 %collective-permute-start.8 = (s16[1616,128]{1,0:T(8,128)(2,1)S(1)}, s16[1616,128]{1,0:T(8,128)(2,1)S(1)}, u32[]{:S(2)}, u32[]{:S(2)}) collective-permute-start(s16[1616,128]{1,0:T(8,128)(2,1)S(1)} %get-tuple-element.26.rest_1_), channel_id=1, source_target_pairs={{0,8},{4,12},{8,0},{12,4},{16,24},{20,28},{24,16},{28,20},{1,9},{5... | collective-permute-start | bytes 1241096 | tf_op jit(solution)/shard_map/ppermute | solution.py:445
  27.4 2.2 %sum_step_01.1 = (s16[1616,128]{1,0:T(8,128)(2,1)S(1)}, bf16[128,2048]{1,0:T(8,128)(2,1)S(1)}) custom-call(s32[53]{0:T(128)S(1)} %fusion.1.table, s32[8]{0:T(128)S(1)} %pad_add_fusion.1.rest_0_.counts, s32[2,512]{1,0:T(2,128)S(1)} %pad_add_fusion.pairs_ref, bf16[128,32768]{1,0:T(8,128)(2,1)} %bitcast.14, ...), custom_call_target="tpu_custom_call" | custom-call | flops 10000000000 | bytes 30000000 | tf_op jit(solution)/shard_map/sum_step_01/pallas_call | solution.py:245
  29.7 2.0 %collective-permute-start.6 = (bf16[128,2048]{1,0:T(8,128)(2,1)S(1)}, bf16[128,2048]{1,0:T(8,128)(2,1)S(1)}, u32[]{:S(2)}, u32[]{:S(2)}) collective-permute-start(bf16[128,2048]{1,0:T(8,128)(2,1)S(1)} %get-tuple-element.29), channel_id=1, source_target_pairs={{0,4},{4,0},{8,12},{12,8},{16,20},{20,16},{24,28},{28,24},{1,5},{5... | collective-permute-start | bytes 1572872 | tf_op jit(solution)/shard_map/ppermute | solution.py:394
  31.6 1.8 %collective-permute-done.9.partner_ref = bf16[128,1024]{1,0:T(8,128)(2,1)S(1)} collective-permute-done((bf16[128,1024]{1,0:T(8,128)(2,1)S(1)}, bf16[128,1024]{1,0:T(8,128)(2,1)S(1)}, u32[]{:S(2)}, u32[]{:S(2)}) %collective-permute-start.9) | collective-permute-done | bytes 262176 | tf_op jit(solution)/shard_map/ppermute | solution.py:394
  33.5 4.4 %collective-permute-done.8.rest_2_.rest_0_.rest_1_ = s16[1616,128]{1,0:T(8,128)(2,1)S(1)} collective-permute-done((s16[1616,128]{1,0:T(8,128)(2,1)S(1)}, s16[1616,128]{1,0:T(8,128)(2,1)S(1)}, u32[]{:S(2)}, u32[]{:S(2)}) %collective-permute-start.8) | collective-permute-done | bytes 413728 | tf_op jit(solution)/shard_map/ppermute | solution.py:445
  37.9 2.2 %sum_step_02.1 = (s16[1616,128]{1,0:T(8,128)(2,1)S(1)}, bf16[128,2048]{1,0:T(8,128)(2,1)S(1)}) custom-call(s32[53]{0:T(128)S(1)} %fusion.1.table, s32[8]{0:T(128)S(1)} %pad_add_fusion.1.rest_0_.counts, s32[2,512]{1,0:T(2,128)S(1)} %pad_add_fusion.pairs_ref, bf16[128,32768]{1,0:T(8,128)(2,1)} %bitcast.16, ...), custom_call_target="tpu_custom_call" | custom-call | flops 10000000000 | bytes 30000000 | tf_op jit(solution)/shard_map/sum_step_02/pallas_call | solution.py:245
  40.0 2.1 %collective-permute-start.10 = (s16[1616,128]{1,0:T(8,128)(2,1)S(1)}, s16[1616,128]{1,0:T(8,128)(2,1)S(1)}, u32[]{:S(2)}, u32[]{:S(2)}) collective-permute-start(s16[1616,128]{1,0:T(8,128)(2,1)S(1)} %get-tuple-element.32.rest_1_), channel_id=1, source_target_pairs={{0,8},{4,12},{8,0},{12,4},{16,24},{20,28},{24,16},{28,20},{1,9},{5... | collective-permute-start | bytes 1241096 | tf_op jit(solution)/shard_map/ppermute | solution.py:445
  42.1 1.9 %collective-permute-start.11 = (bf16[128,1024]{1,0:T(8,128)(2,1)S(1)}, bf16[128,1024]{1,0:T(8,128)(2,1)S(1)}, u32[]{:S(2)}, u32[]{:S(2)}) collective-permute-start(bf16[128,1024]{1,0:T(8,128)(2,1)S(1)} %collective-permute-done.5.rest_3_), channel_id=1, source_target_pairs={{0,4},{4,0},{8,12},{12,8},{16,20},{20,16},{24,28},{28,24},{1,5},{5... | collective-permute-start | bytes 786440 | tf_op jit(solution)/shard_map/ppermute | solution.py:451
  44.1 2.6 %collective-permute-done.7.rest_2_.rest_1_.rest_0_ = s16[1616,128]{1,0:T(8,128)(2,1)S(1)} collective-permute-done((s16[1616,128]{1,0:T(8,128)(2,1)S(1)}, s16[1616,128]{1,0:T(8,128)(2,1)S(1)}, u32[]{:S(2)}, u32[]{:S(2)}) %collective-permute-start.7) | collective-permute-done | bytes 413728 | tf_op jit(solution)/shard_map/ppermute | solution.py:445
  46.7 2.0 %sum_step_04.1.rest_2_ = s16[1616,128]{1,0:T(8,128)(2,1)S(1)} custom-call(s32[53]{0:T(128)S(1)} %fusion.1.table, s32[8]{0:T(128)S(1)} %pad_add_fusion.1.rest_0_.counts, s32[2,512]{1,0:T(2,128)S(1)} %pad_add_fusion.pairs_ref, bf16[128,32768]{1,0:T(8,128)(2,1)} %bitcast.18, bf16[128,2048]{1,0:T(8,128)(2,1)S(1)} %collective-permute-done.6.partner_ref, ...), custom_call_target="tpu_custom_call" | custom-call | flops 10000000000 | bytes 30000000 | tf_op jit(solution)/shard_map/sum_step_04/pallas_call | solution.py:245
  49.5 5.6 %collective-permute-start.14 = (s16[1616,128]{1,0:T(8,128)(2,1)S(1)}, s16[1616,128]{1,0:T(8,128)(2,1)S(1)}, u32[]{:S(2)}, u32[]{:S(2)}) collective-permute-start(s16[1616,128]{1,0:T(8,128)(2,1)S(1)} %sum_step_04.1.rest_2_), channel_id=1, source_target_pairs={{0,8},{4,12},{24,16},{28,20},{1,9},{5,13},{25,17},{29,21},{2,10},{... | collective-permute-start | bytes 1241096 | tf_op jit(solution)/shard_map/ppermute | solution.py:445
  55.1 2.2 %sum_step_05.1 = (s16[1616,128]{1,0:T(8,128)(2,1)S(1)}, bf16[128,2048]{1,0:T(8,128)(2,1)S(1)}) custom-call(s32[53]{0:T(128)S(1)} %fusion.1.table, s32[8]{0:T(128)S(1)} %pad_add_fusion.1.rest_0_.counts, s32[2,512]{1,0:T(2,128)S(1)} %pad_add_fusion.pairs_ref, bf16[128,32768]{1,0:T(8,128)(2,1)} %bitcast.19, ...), custom_call_target="tpu_custom_call" | custom-call | flops 10000000000 | bytes 30000000 | tf_op jit(solution)/shard_map/sum_step_05/pallas_call | solution.py:245
  58.0 5.6 %collective-permute-start.13 = (s16[1616,128]{1,0:T(8,128)(2,1)S(1)}, s16[1616,128]{1,0:T(8,128)(2,1)S(1)}, u32[]{:S(2)}, u32[]{:S(2)}) collective-permute-start(s16[1616,128]{1,0:T(8,128)(2,1)S(1)} %get-tuple-element.35.rest_1_), channel_id=1, source_target_pairs={{0,8},{4,12},{24,16},{28,20},{1,9},{5,13},{25,17},{29,21},{2,10},{... | collective-permute-start | bytes 1241096 | tf_op jit(solution)/shard_map/ppermute | solution.py:445
  63.7 2.0 %collective-permute-start.12 = (bf16[128,2048]{1,0:T(8,128)(2,1)S(1)}, bf16[128,2048]{1,0:T(8,128)(2,1)S(1)}, u32[]{:S(2)}, u32[]{:S(2)}) collective-permute-start(bf16[128,2048]{1,0:T(8,128)(2,1)S(1)} %get-tuple-element.34), channel_id=1, source_target_pairs={{0,4},{4,0},{8,12},{12,8},{16,20},{20,16},{24,28},{28,24},{1,5},{5... | collective-permute-start | bytes 1572872 | tf_op jit(solution)/shard_map/ppermute | solution.py:394
  65.7 2.0 %sum_step_06.1.rest_3_ = s16[1616,128]{1,0:T(8,128)(2,1)S(1)} custom-call(s32[53]{0:T(128)S(1)} %fusion.1.table, s32[8]{0:T(128)S(1)} %pad_add_fusion.1.rest_0_.counts, s32[2,512]{1,0:T(2,128)S(1)} %pad_add_fusion.pairs_ref, bf16[128,32768]{1,0:T(8,128)(2,1)} %bitcast.21, bf16[128,2048]{1,0:T(8,128)(2,1)S(1)} %collective-permute-done.15.partner_ref, ...), custom_call_target="tpu_custom_call" | custom-call | flops 10000000000 | bytes 30000000 | tf_op jit(solution)/shard_map/sum_step_06/pallas_call | solution.py:245
  68.4 4.0 %collective-permute-start.18 = (s16[1616,128]{1,0:T(8,128)(2,1)S(1)}, s16[1616,128]{1,0:T(8,128)(2,1)S(1)}, u32[]{:S(2)}, u32[]{:S(2)}) collective-permute-start(s16[1616,128]{1,0:T(8,128)(2,1)S(1)} %sum_step_06.1.rest_3_), channel_id=1, source_target_pairs={{0,8},{4,12},{24,16},{28,20},{1,9},{5,13},{25,17},{29,21},{2,10},{... | collective-permute-start | bytes 1241096 | tf_op jit(solution)/shard_map/ppermute | solution.py:445
  72.4 1.2 collective-permute-done.13.rest_4_.rest_1_
  73.6 2.2 %sum_step_07.1 = (s16[1616,128]{1,0:T(8,128)(2,1)S(1)}, bf16[128,2048]{1,0:T(8,128)(2,1)S(1)}) custom-call(s32[53]{0:T(128)S(1)} %fusion.1.table, s32[8]{0:T(128)S(1)} %pad_add_fusion.1.rest_0_.counts, s32[2,512]{1,0:T(2,128)S(1)} %pad_add_fusion.pairs_ref, bf16[128,32768]{1,0:T(8,128)(2,1)} %bitcast.22, ...), custom_call_target="tpu_custom_call" | custom-call | flops 10000000000 | bytes 30000000 | tf_op jit(solution)/shard_map/sum_step_07/pallas_call | solution.py:245
  76.6 6.3 %collective-permute-start.20 = (s16[1616,128]{1,0:T(8,128)(2,1)S(1)}, s16[1616,128]{1,0:T(8,128)(2,1)S(1)}, u32[]{:S(2)}, u32[]{:S(2)}) collective-permute-start(s16[1616,128]{1,0:T(8,128)(2,1)S(1)} %get-tuple-element.37.rest_2_), channel_id=1, source_target_pairs={{0,8},{4,12},{24,16},{28,20},{1,9},{5,13},{25,17},{29,21},{2,10},{... | collective-permute-start | bytes 1241096 | tf_op jit(solution)/shard_map/ppermute | solution.py:445
  82.9 1.8 %collective-permute-start.23 = (bf16[128,2048]{1,0:T(8,128)(2,1)S(1)}, bf16[128,2048]{1,0:T(8,128)(2,1)S(1)}, u32[]{:S(2)}, u32[]{:S(2)}) collective-permute-start(bf16[128,2048]{1,0:T(8,128)(2,1)S(1)} %get-tuple-element.40), channel_id=1, source_target_pairs={{0,4},{4,0},{8,12},{12,8},{16,20},{20,16},{24,28},{28,24},{1,5},{5... | collective-permute-start | bytes 1572872 | tf_op jit(solution)/shard_map/ppermute | solution.py:394
  84.7 2.2 %sum_step_08.1 = (s16[1616,128]{1,0:T(8,128)(2,1)S(1)}, bf16[128,2048]{1,0:T(8,128)(2,1)S(1)}) custom-call(s32[53]{0:T(128)S(1)} %fusion.1.table, s32[8]{0:T(128)S(1)} %pad_add_fusion.1.rest_0_.counts, s32[2,512]{1,0:T(2,128)S(1)} %pad_add_fusion.pairs_ref, bf16[128,32768]{1,0:T(8,128)(2,1)} %bitcast.24, ...), custom_call_target="tpu_custom_call" | custom-call | flops 10000000000 | bytes 30000000 | tf_op jit(solution)/shard_map/sum_step_08/pallas_call | solution.py:245
  87.3 3.9 %collective-permute-start.26 = (bf16[128,2048]{1,0:T(8,128)(2,1)S(1)}, bf16[128,2048]{1,0:T(8,128)(2,1)S(1)}, u32[]{:S(2)}, u32[]{:S(2)}) collective-permute-start(bf16[128,2048]{1,0:T(8,128)(2,1)S(1)} %get-tuple-element.42), channel_id=1, source_target_pairs={{0,4},{4,0},{8,12},{12,8},{16,20},{20,16},{24,28},{28,24},{1,5},{5... | collective-permute-start | bytes 1572872 | tf_op jit(solution)/shard_map/ppermute | solution.py:394
  91.1 1.8 %collective-permute-done.20.rest_3_.rest_0_ = s16[1616,128]{1,0:T(8,128)(2,1)S(1)} collective-permute-done((s16[1616,128]{1,0:T(8,128)(2,1)S(1)}, s16[1616,128]{1,0:T(8,128)(2,1)S(1)}, u32[]{:S(2)}, u32[]{:S(2)}) %collective-permute-start.20) | collective-permute-done | bytes 413728 | tf_op jit(solution)/shard_map/ppermute | solution.py:445
  92.9 2.2 %sum_step_09.1 = (s16[1616,128]{1,0:T(8,128)(2,1)S(1)}, bf16[128,2048]{1,0:T(8,128)(2,1)S(1)}) custom-call(s32[53]{0:T(128)S(1)} %fusion.1.table, s32[8]{0:T(128)S(1)} %pad_add_fusion.1.rest_0_.counts, s32[2,512]{1,0:T(2,128)S(1)} %pad_add_fusion.pairs_ref, bf16[128,32768]{1,0:T(8,128)(2,1)} %bitcast.26, ...), custom_call_target="tpu_custom_call" | custom-call | flops 10000000000 | bytes 30000000 | tf_op jit(solution)/shard_map/sum_step_09/pallas_call | solution.py:245
  95.1 2.5 %collective-permute-start.25 = (s16[1616,128]{1,0:T(8,128)(2,1)S(1)}, s16[1616,128]{1,0:T(8,128)(2,1)S(1)}, u32[]{:S(2)}, u32[]{:S(2)}) collective-permute-start(s16[1616,128]{1,0:T(8,128)(2,1)S(1)} %get-tuple-element.41.rest_1_), channel_id=1, source_target_pairs={{0,8},{4,12},{8,24},{12,28},{16,0},{20,4},{24,16},{28,20},{1,9},{5... | collective-permute-start | bytes 1241096 | tf_op jit(solution)/shard_map/ppermute | solution.py:445
  97.7 2.3 %collective-permute-start.22 = (bf16[128,2048]{1,0:T(8,128)(2,1)S(1)}, bf16[128,2048]{1,0:T(8,128)(2,1)S(1)}, u32[]{:S(2)}, u32[]{:S(2)}) collective-permute-start(bf16[128,2048]{1,0:T(8,128)(2,1)S(1)} %get-tuple-element.39), channel_id=1, source_target_pairs={{0,4},{4,0},{8,12},{12,8},{16,20},{20,16},{24,28},{28,24},{1,5},{5... | collective-permute-start | bytes 1572872 | tf_op jit(solution)/shard_map/ppermute | solution.py:394
  100.0 1.8 %collective-permute-done.24.rest_2_.rest_4_.rest_5_ = s16[1616,128]{1,0:T(8,128)(2,1)S(1)} collective-permute-done((s16[1616,128]{1,0:T(8,128)(2,1)S(1)}, s16[1616,128]{1,0:T(8,128)(2,1)S(1)}, u32[]{:S(2)}, u32[]{:S(2)}) %collective-permute-start.24) | collective-permute-done | bytes 413728 | tf_op jit(solution)/shard_map/ppermute | solution.py:445
  101.8 2.0 %sum_step_10.1.rest_1_ = s16[1616,128]{1,0:T(8,128)(2,1)S(1)} custom-call(s32[53]{0:T(128)S(1)} %fusion.1.table, s32[8]{0:T(128)S(1)} %pad_add_fusion.1.rest_0_.counts, s32[2,512]{1,0:T(2,128)S(1)} %pad_add_fusion.pairs_ref, bf16[128,32768]{1,0:T(8,128)(2,1)} %bitcast.28, bf16[128,2048]{1,0:T(8,128)(2,1)S(1)} %collective-permute-done.23.partner_ref, ...), custom_call_target="tpu_custom_call" | custom-call | flops 10000000000 | bytes 30000000 | tf_op jit(solution)/shard_map/sum_step_10/pallas_call | solution.py:245
  103.8 2.5 %collective-permute-start.28 = (s16[1616,128]{1,0:T(8,128)(2,1)S(1)}, s16[1616,128]{1,0:T(8,128)(2,1)S(1)}, u32[]{:S(2)}, u32[]{:S(2)}) collective-permute-start(s16[1616,128]{1,0:T(8,128)(2,1)S(1)} %sum_step_10.1.rest_1_), channel_id=1, source_target_pairs={{0,8},{4,12},{8,24},{12,28},{16,0},{20,4},{24,16},{28,20},{1,9},{5... | collective-permute-start | bytes 1241096 | tf_op jit(solution)/shard_map/ppermute | solution.py:445
  106.3 3.6 %finish_0.1 = (f32[200,4096]{1,0:T(8,128)}, f32[8,128]{1,0:T(8,128)S(1)}) custom-call(s32[53]{0:T(128)S(1)} %fusion.1.table, s32[8]{0:T(128)S(1)} %pad_add_fusion.1.rest_0_.counts, s32[2,512]{1,0:T(2,128)S(1)} %pad_add_fusion.pairs_ref, bf16[128,32768]{1,0:T(8,128)(2,1)} %bitcast.29, bf16[128,2048]{1,0:T(8,128)(2,1)S(1)} %collective-permute-done.26.partner_ref, ...), custom_call_target="tpu_custom_call" | custom-call | flops 1024 | bytes 1024 | tf_op jit(solution)/shard_map/finish_0/pallas_call | solution.py:345
  109.9 0.7 collective-permute-done.25.rest_2_.rest_4_.rest_5_
  110.6 2.0 %sum_step_11.1 = s16[1616,128]{1,0:T(8,128)(2,1)S(1)} custom-call(s32[53]{0:T(128)S(1)} %fusion.1.table, s32[8]{0:T(128)S(1)} %pad_add_fusion.1.rest_0_.counts, s32[2,512]{1,0:T(2,128)S(1)} %pad_add_fusion.pairs_ref, bf16[128,32768]{1,0:T(8,128)(2,1)} %bitcast.30, bf16[128,2048]{1,0:T(8,128)(2,1)S(1)} %collective-permute-done.23.partner_ref, ...), custom_call_target="tpu_custom_call" | custom-call | flops 10000000000 | bytes 30000000 | tf_op jit(solution)/shard_map/sum_step_11/pallas_call | solution.py:245
  112.6 2.5 %collective-permute-start.27 = (s16[1616,128]{1,0:T(8,128)(2,1)S(1)}, s16[1616,128]{1,0:T(8,128)(2,1)S(1)}, u32[]{:S(2)}, u32[]{:S(2)}) collective-permute-start(s16[1616,128]{1,0:T(8,128)(2,1)S(1)} %sum_step_11.1), channel_id=1, source_target_pairs={{0,8},{4,12},{8,24},{12,28},{16,0},{20,4},{24,16},{28,20},{1,9},{5... | collective-permute-start | bytes 1241096 | tf_op jit(solution)/shard_map/ppermute | solution.py:445
  115.2 3.6 %finish_1.1.rest_6_ = f32[200,4096]{1,0:T(8,128)} custom-call(s32[53]{0:T(128)S(1)} %fusion.1.table, s32[8]{0:T(128)S(1)} %pad_add_fusion.1.rest_0_.counts, s32[2,512]{1,0:T(2,128)S(1)} %pad_add_fusion.pairs_ref, bf16[128,32768]{1,0:T(8,128)(2,1)} %bitcast.31, ...), custom_call_target="tpu_custom_call", output_to_operand_aliasing={{}: (12, {})} | custom-call | flops 1024 | bytes 1024 | tf_op jit(solution)/shard_map/finish_1/pallas_call | solution.py:345
  118.9 3.6 %finish_2.1.rest_6_ = f32[200,4096]{1,0:T(8,128)} custom-call(s32[53]{0:T(128)S(1)} %fusion.1.table, s32[8]{0:T(128)S(1)} %pad_add_fusion.1.rest_0_.counts, s32[2,512]{1,0:T(2,128)S(1)} %pad_add_fusion.pairs_ref, bf16[128,32768]{1,0:T(8,128)(2,1)} %bitcast.32, ...), custom_call_target="tpu_custom_call", output_to_operand_aliasing={{}: (12, {})} | custom-call | flops 1024 | bytes 1024 | tf_op jit(solution)/shard_map/finish_2/pallas_call | solution.py:345
  122.5 0.8 collective-permute-done.27.rest_4_.rest_5_
  123.3 3.9 %finish_3.1 = f32[200,4096]{1,0:T(8,128)} custom-call(s32[53]{0:T(128)S(1)} %fusion.1.table, s32[8]{0:T(128)S(1)} %pad_add_fusion.1.rest_0_.counts, s32[2,512]{1,0:T(2,128)S(1)} %pad_add_fusion.pairs_ref, bf16[128,32768]{1,0:T(8,128)(2,1)} %bitcast.33, bf16[128,2048]{1,0:T(8,128)(2,1)S(1)} %collective-permute-done.22.partner_ref, ...), custom_call_target="tpu_custom_call", output_to_operand_aliasing={{}: (12, {})} | custom-call | flops 1024 | bytes 1024 | tf_op jit(solution)/shard_map/finish_3/pallas_call | solution.py:345
  (39 shorter events, 4.5 us)
Async XLA Ops:
  0.0 1.1 copy-start
  2.1 11.9 %collective-permute-start.2 = (s32[2]{0:T(128)S(1)}, s32[2]{0:T(128)S(1)}, u32[]{:S(2)}, u32[]{:S(2)}) collective-permute-start(s32[2]{0:T(128)S(1)} %fusion.counts_ref), channel_id=1, source_target_pairs={{0,24},{4,28},{8,0},{12,4},{16,8},{20,12},{24,16},{28,20},{1,25},{... | collective-permute-start | bytes 32 | tf_op jit(solution)/shard_map/ppermute | solution.py:412
  7.1 7.0 %collective-permute-start.1 = (s32[2]{0:T(128)S(1)}, s32[2]{0:T(128)S(1)}, u32[]{:S(2)}, u32[]{:S(2)}) collective-permute-start(s32[2]{0:T(128)S(1)} %fusion.counts_ref), channel_id=1, source_target_pairs={{0,16},{4,20},{8,24},{12,28},{16,0},{20,4},{24,8},{28,12},{1,17},{... | collective-permute-start | bytes 32 | tf_op jit(solution)/shard_map/ppermute | solution.py:412
  7.2 7.0 %collective-permute-start = (s32[2]{0:T(128)S(1)}, s32[2]{0:T(128)S(1)}, u32[]{:S(2)}, u32[]{:S(2)}) collective-permute-start(s32[2]{0:T(128)S(1)} %fusion.counts_ref), channel_id=1, source_target_pairs={{0,8},{4,12},{8,16},{12,20},{16,24},{20,28},{24,0},{28,4},{1,9},{5... | collective-permute-start | bytes 32 | tf_op jit(solution)/shard_map/ppermute | solution.py:412
  8.2 15.0 %collective-permute-start.3 = (bf16[128,2048]{1,0:T(8,128)(2,1)S(1)}, bf16[128,2048]{1,0:T(8,128)(2,1)S(1)}, u32[]{:S(2)}, u32[]{:S(2)}) collective-permute-start(bf16[128,2048]{1,0:T(8,128)(2,1)S(1)} %dynamic-slice_bitcast_fusion), channel_id=1, source_target_pairs={{0,4},{4,0},{8,12},{12,8},{16,20},{20,16},{24,28},{28,24},{1,5},{5... | collective-permute-start | bytes 1572872 | tf_op jit(solution)/shard_map/ppermute | solution.py:394
  10.7 16.7 %collective-permute-start.5 = (bf16[128,1024]{1,0:T(8,128)(2,1)S(1)}, bf16[128,1024]{1,0:T(8,128)(2,1)S(1)}, u32[]{:S(2)}, u32[]{:S(2)}) collective-permute-start(bf16[128,1024]{1,0:T(8,128)(2,1)S(1)} %get-tuple-element.45), channel_id=1, source_target_pairs={{0,8},{4,12},{8,0},{12,4},{16,24},{20,28},{24,16},{28,20},{1,9},{5... | collective-permute-start | bytes 786440 | tf_op jit(solution)/shard_map/ppermute | solution.py:416
  14.0 13.4 %collective-permute-start.4 = (bf16[128,1024]{1,0:T(8,128)(2,1)S(1)}, bf16[128,1024]{1,0:T(8,128)(2,1)S(1)}, u32[]{:S(2)}, u32[]{:S(2)}) collective-permute-start(bf16[128,1024]{1,0:T(8,128)(2,1)S(1)} %get-tuple-element.46), channel_id=1, source_target_pairs={{0,8},{4,12},{8,0},{12,4},{16,24},{20,28},{24,16},{28,20},{1,9},{5... | collective-permute-start | bytes 786440 | tf_op jit(solution)/shard_map/ppermute | solution.py:417
  14.9 0.7 copy-start.1
  25.2 8.2 %collective-permute-start.9 = (bf16[128,1024]{1,0:T(8,128)(2,1)S(1)}, bf16[128,1024]{1,0:T(8,128)(2,1)S(1)}, u32[]{:S(2)}, u32[]{:S(2)}) collective-permute-start(bf16[128,1024]{1,0:T(8,128)(2,1)S(1)} %get-tuple-element.31), channel_id=1, source_target_pairs={{0,4},{4,0},{8,12},{12,8},{16,20},{20,16},{24,28},{28,24},{1,5},{5... | collective-permute-start | bytes 786440 | tf_op jit(solution)/shard_map/ppermute | solution.py:394
  25.3 12.6 %collective-permute-start.8 = (s16[1616,128]{1,0:T(8,128)(2,1)S(1)}, s16[1616,128]{1,0:T(8,128)(2,1)S(1)}, u32[]{:S(2)}, u32[]{:S(2)}) collective-permute-start(s16[1616,128]{1,0:T(8,128)(2,1)S(1)} %get-tuple-element.26.rest_1_), channel_id=1, source_target_pairs={{0,8},{4,12},{8,0},{12,4},{16,24},{20,28},{24,16},{28,20},{1,9},{5... | collective-permute-start | bytes 1241096 | tf_op jit(solution)/shard_map/ppermute | solution.py:445
  29.6 17.2 %collective-permute-start.7 = (s16[1616,128]{1,0:T(8,128)(2,1)S(1)}, s16[1616,128]{1,0:T(8,128)(2,1)S(1)}, u32[]{:S(2)}, u32[]{:S(2)}) collective-permute-start(s16[1616,128]{1,0:T(8,128)(2,1)S(1)} %get-tuple-element.30.rest_1_), channel_id=1, source_target_pairs={{0,8},{4,12},{8,0},{12,4},{16,24},{20,28},{24,16},{28,20},{1,9},{5... | collective-permute-start | bytes 1241096 | tf_op jit(solution)/shard_map/ppermute | solution.py:445
  29.7 17.1 %collective-permute-start.6 = (bf16[128,2048]{1,0:T(8,128)(2,1)S(1)}, bf16[128,2048]{1,0:T(8,128)(2,1)S(1)}, u32[]{:S(2)}, u32[]{:S(2)}) collective-permute-start(bf16[128,2048]{1,0:T(8,128)(2,1)S(1)} %get-tuple-element.29), channel_id=1, source_target_pairs={{0,4},{4,0},{8,12},{12,8},{16,20},{20,16},{24,28},{28,24},{1,5},{5... | collective-permute-start | bytes 1572872 | tf_op jit(solution)/shard_map/ppermute | solution.py:394
  40.0 15.1 %collective-permute-start.10 = (s16[1616,128]{1,0:T(8,128)(2,1)S(1)}, s16[1616,128]{1,0:T(8,128)(2,1)S(1)}, u32[]{:S(2)}, u32[]{:S(2)}) collective-permute-start(s16[1616,128]{1,0:T(8,128)(2,1)S(1)} %get-tuple-element.32.rest_1_), channel_id=1, source_target_pairs={{0,8},{4,12},{8,0},{12,4},{16,24},{20,28},{24,16},{28,20},{1,9},{5... | collective-permute-start | bytes 1241096 | tf_op jit(solution)/shard_map/ppermute | solution.py:445
  42.1 12.9 %collective-permute-start.11 = (bf16[128,1024]{1,0:T(8,128)(2,1)S(1)}, bf16[128,1024]{1,0:T(8,128)(2,1)S(1)}, u32[]{:S(2)}, u32[]{:S(2)}) collective-permute-start(bf16[128,1024]{1,0:T(8,128)(2,1)S(1)} %collective-permute-done.5.rest_3_), channel_id=1, source_target_pairs={{0,4},{4,0},{8,12},{12,8},{16,20},{20,16},{24,28},{28,24},{1,5},{5... | collective-permute-start | bytes 786440 | tf_op jit(solution)/shard_map/ppermute | solution.py:451
  44.0 19.6 %collective-permute-start.15 = (bf16[128,2048]{1,0:T(8,128)(2,1)S(1)}, bf16[128,2048]{1,0:T(8,128)(2,1)S(1)}, u32[]{:S(2)}, u32[]{:S(2)}) collective-permute-start(bf16[128,2048]{1,0:T(8,128)(2,1)S(1)} %get-tuple-element.36), channel_id=1, source_target_pairs={{0,4},{4,0},{8,12},{12,8},{16,20},{20,16},{24,28},{28,24},{1,5},{5... | collective-permute-start | bytes 1572872 | tf_op jit(solution)/shard_map/ppermute | solution.py:394
  48.8 16.9 %collective-permute-start.16 = (s16[1616,128]{1,0:T(8,128)(2,1)S(1)}, s16[1616,128]{1,0:T(8,128)(2,1)S(1)}, u32[]{:S(2)}, u32[]{:S(2)}) collective-permute-start(s16[1616,128]{1,0:T(8,128)(2,1)S(1)} %sum_step_04.1.rest_2_), channel_id=1, source_target_pairs={{8,16},{12,20},{16,8},{20,12},{9,17},{13,21},{17,9},{21,13},{10,18... | collective-permute-start | bytes 1241096 | tf_op jit(solution)/shard_map/ppermute | solution.py:445
  49.5 16.2 %collective-permute-start.14 = (s16[1616,128]{1,0:T(8,128)(2,1)S(1)}, s16[1616,128]{1,0:T(8,128)(2,1)S(1)}, u32[]{:S(2)}, u32[]{:S(2)}) collective-permute-start(s16[1616,128]{1,0:T(8,128)(2,1)S(1)} %sum_step_04.1.rest_2_), channel_id=1, source_target_pairs={{0,8},{4,12},{24,16},{28,20},{1,9},{5,13},{25,17},{29,21},{2,10},{... | collective-permute-start | bytes 1241096 | tf_op jit(solution)/shard_map/ppermute | solution.py:445
  57.3 15.1 %collective-permute-start.17 = (s16[1616,128]{1,0:T(8,128)(2,1)S(1)}, s16[1616,128]{1,0:T(8,128)(2,1)S(1)}, u32[]{:S(2)}, u32[]{:S(2)}) collective-permute-start(s16[1616,128]{1,0:T(8,128)(2,1)S(1)} %get-tuple-element.35.rest_1_), channel_id=1, source_target_pairs={{8,16},{12,20},{16,8},{20,12},{9,17},{13,21},{17,9},{21,13},{10,18... | collective-permute-start | bytes 1241096 | tf_op jit(solution)/shard_map/ppermute | solution.py:445
  58.0 15.6 %collective-permute-start.13 = (s16[1616,128]{1,0:T(8,128)(2,1)S(1)}, s16[1616,128]{1,0:T(8,128)(2,1)S(1)}, u32[]{:S(2)}, u32[]{:S(2)}) collective-permute-start(s16[1616,128]{1,0:T(8,128)(2,1)S(1)} %get-tuple-element.35.rest_1_), channel_id=1, source_target_pairs={{0,8},{4,12},{24,16},{28,20},{1,9},{5,13},{25,17},{29,21},{2,10},{... | collective-permute-start | bytes 1241096 | tf_op jit(solution)/shard_map/ppermute | solution.py:445
  63.7 21.0 %collective-permute-start.12 = (bf16[128,2048]{1,0:T(8,128)(2,1)S(1)}, bf16[128,2048]{1,0:T(8,128)(2,1)S(1)}, u32[]{:S(2)}, u32[]{:S(2)}) collective-permute-start(bf16[128,2048]{1,0:T(8,128)(2,1)S(1)} %get-tuple-element.34), channel_id=1, source_target_pairs={{0,4},{4,0},{8,12},{12,8},{16,20},{20,16},{24,28},{28,24},{1,5},{5... | collective-permute-start | bytes 1572872 | tf_op jit(solution)/shard_map/ppermute | solution.py:394
  67.7 15.2 %collective-permute-start.19 = (s16[1616,128]{1,0:T(8,128)(2,1)S(1)}, s16[1616,128]{1,0:T(8,128)(2,1)S(1)}, u32[]{:S(2)}, u32[]{:S(2)}) collective-permute-start(s16[1616,128]{1,0:T(8,128)(2,1)S(1)} %sum_step_06.1.rest_3_), channel_id=1, source_target_pairs={{8,16},{12,20},{16,8},{20,12},{9,17},{13,21},{17,9},{21,13},{10,18... | collective-permute-start | bytes 1241096 | tf_op jit(solution)/shard_map/ppermute | solution.py:445
  68.4 16.3 %collective-permute-start.18 = (s16[1616,128]{1,0:T(8,128)(2,1)S(1)}, s16[1616,128]{1,0:T(8,128)(2,1)S(1)}, u32[]{:S(2)}, u32[]{:S(2)}) collective-permute-start(s16[1616,128]{1,0:T(8,128)(2,1)S(1)} %sum_step_06.1.rest_3_), channel_id=1, source_target_pairs={{0,8},{4,12},{24,16},{28,20},{1,9},{5,13},{25,17},{29,21},{2,10},{... | collective-permute-start | bytes 1241096 | tf_op jit(solution)/shard_map/ppermute | solution.py:445
  75.9 15.3 %collective-permute-start.21 = (s16[1616,128]{1,0:T(8,128)(2,1)S(1)}, s16[1616,128]{1,0:T(8,128)(2,1)S(1)}, u32[]{:S(2)}, u32[]{:S(2)}) collective-permute-start(s16[1616,128]{1,0:T(8,128)(2,1)S(1)} %get-tuple-element.37.rest_2_), channel_id=1, source_target_pairs={{8,16},{12,20},{16,8},{20,12},{9,17},{13,21},{17,9},{21,13},{10,18... | collective-permute-start | bytes 1241096 | tf_op jit(solution)/shard_map/ppermute | solution.py:445
  76.6 16.3 %collective-permute-start.20 = (s16[1616,128]{1,0:T(8,128)(2,1)S(1)}, s16[1616,128]{1,0:T(8,128)(2,1)S(1)}, u32[]{:S(2)}, u32[]{:S(2)}) collective-permute-start(s16[1616,128]{1,0:T(8,128)(2,1)S(1)} %get-tuple-element.37.rest_2_), channel_id=1, source_target_pairs={{0,8},{4,12},{24,16},{28,20},{1,9},{5,13},{25,17},{29,21},{2,10},{... | collective-permute-start | bytes 1241096 | tf_op jit(solution)/shard_map/ppermute | solution.py:445
  82.9 17.1 %collective-permute-start.23 = (bf16[128,2048]{1,0:T(8,128)(2,1)S(1)}, bf16[128,2048]{1,0:T(8,128)(2,1)S(1)}, u32[]{:S(2)}, u32[]{:S(2)}) collective-permute-start(bf16[128,2048]{1,0:T(8,128)(2,1)S(1)} %get-tuple-element.40), channel_id=1, source_target_pairs={{0,4},{4,0},{8,12},{12,8},{16,20},{20,16},{24,28},{28,24},{1,5},{5... | collective-permute-start | bytes 1572872 | tf_op jit(solution)/shard_map/ppermute | solution.py:394
  86.9 14.8 %collective-permute-start.24 = (s16[1616,128]{1,0:T(8,128)(2,1)S(1)}, s16[1616,128]{1,0:T(8,128)(2,1)S(1)}, u32[]{:S(2)}, u32[]{:S(2)}) collective-permute-start(s16[1616,128]{1,0:T(8,128)(2,1)S(1)} %get-tuple-element.38.rest_2_), channel_id=1, source_target_pairs={{0,8},{4,12},{8,24},{12,28},{16,0},{20,4},{24,16},{28,20},{1,9},{5... | collective-permute-start | bytes 1241096 | tf_op jit(solution)/shard_map/ppermute | solution.py:445
  87.3 19.1 %collective-permute-start.26 = (bf16[128,2048]{1,0:T(8,128)(2,1)S(1)}, bf16[128,2048]{1,0:T(8,128)(2,1)S(1)}, u32[]{:S(2)}, u32[]{:S(2)}) collective-permute-start(bf16[128,2048]{1,0:T(8,128)(2,1)S(1)} %get-tuple-element.42), channel_id=1, source_target_pairs={{0,4},{4,0},{8,12},{12,8},{16,20},{20,16},{24,28},{28,24},{1,5},{5... | collective-permute-start | bytes 1572872 | tf_op jit(solution)/shard_map/ppermute | solution.py:394
  95.1 15.5 %collective-permute-start.25 = (s16[1616,128]{1,0:T(8,128)(2,1)S(1)}, s16[1616,128]{1,0:T(8,128)(2,1)S(1)}, u32[]{:S(2)}, u32[]{:S(2)}) collective-permute-start(s16[1616,128]{1,0:T(8,128)(2,1)S(1)} %get-tuple-element.41.rest_1_), channel_id=1, source_target_pairs={{0,8},{4,12},{8,24},{12,28},{16,0},{20,4},{24,16},{28,20},{1,9},{5... | collective-permute-start | bytes 1241096 | tf_op jit(solution)/shard_map/ppermute | solution.py:445
  97.7 21.3 %collective-permute-start.22 = (bf16[128,2048]{1,0:T(8,128)(2,1)S(1)}, bf16[128,2048]{1,0:T(8,128)(2,1)S(1)}, u32[]{:S(2)}, u32[]{:S(2)}) collective-permute-start(bf16[128,2048]{1,0:T(8,128)(2,1)S(1)} %get-tuple-element.39), channel_id=1, source_target_pairs={{0,4},{4,0},{8,12},{12,8},{16,20},{20,16},{24,28},{28,24},{1,5},{5... | collective-permute-start | bytes 1572872 | tf_op jit(solution)/shard_map/ppermute | solution.py:394
  103.8 15.1 %collective-permute-start.28 = (s16[1616,128]{1,0:T(8,128)(2,1)S(1)}, s16[1616,128]{1,0:T(8,128)(2,1)S(1)}, u32[]{:S(2)}, u32[]{:S(2)}) collective-permute-start(s16[1616,128]{1,0:T(8,128)(2,1)S(1)} %sum_step_10.1.rest_1_), channel_id=1, source_target_pairs={{0,8},{4,12},{8,24},{12,28},{16,0},{20,4},{24,16},{28,20},{1,9},{5... | collective-permute-start | bytes 1241096 | tf_op jit(solution)/shard_map/ppermute | solution.py:445
  112.6 10.7 %collective-permute-start.27 = (s16[1616,128]{1,0:T(8,128)(2,1)S(1)}, s16[1616,128]{1,0:T(8,128)(2,1)S(1)}, u32[]{:S(2)}, u32[]{:S(2)}) collective-permute-start(s16[1616,128]{1,0:T(8,128)(2,1)S(1)} %sum_step_11.1), channel_id=1, source_target_pairs={{0,8},{4,12},{8,24},{12,28},{16,0},{20,4},{24,16},{28,20},{1,9},{5... | collective-permute-start | bytes 1241096 | tf_op jit(solution)/shard_map/ppermute | solution.py:445

commit v6 on v5

--- a/solution.py
+++ b/solution.py
@@ -258,26 +258,15 @@
     return results[0], results[1] if swap is not None else None
 
 
-def coded_specs(piece, tiles, index):
-    lots = piece // LANES
-    return [
-        pl.BlockSpec((lots // tiles * M, LANES), lambda *at: (at[index], 0)),
-        pl.BlockSpec((CODE_ROWS, LANES), lambda *at: (lots * M // CODE_ROWS, 0)),
-    ]
-
-
-def add_arrived(sums_ref, refs, tiles):
+def add_coded(sums_ref, coded_ref, half, halves):
     lots = sums_ref.shape[1] // LANES
-    tile = pl.program_id(0)
-    for coded_ref, codes_ref in zip(refs[::2], refs[1::2]):
-        codes = codes_ref[...].astype(jnp.int32).astype(F32)
-        pieces = [codes[at * lots : (at + 1) * lots, :] for at in range(tiles)]
-        codes = functools.reduce(lambda chosen, at: jnp.where(tile == at, pieces[at], chosen), range(1, tiles), pieces[0])
-        scale = jnp.exp2(codes * (1.0 / CODES_PER_OCTAVE)) * (1.0 / LEVELS)
-        coded = coded_ref[...].astype(jnp.int32).astype(F32)
-        for lot in range(lots):
-            lanes = slice(lot * LANES, (lot + 1) * LANES)
-            sums_ref[:M, lanes] += coded[lot * M : (lot + 1) * M, :] * scale[lot : lot + 1, :]
+    first = half * lots
+    coded = coded_ref[first * M : (first + lots) * M, :].astype(jnp.int32).astype(F32)
+    codes = coded_ref[halves * lots * M :, :].astype(jnp.int32).astype(F32)
+    scale = jnp.exp2(codes * (1.0 / CODES_PER_OCTAVE)) * (1.0 / LEVELS)
+    for lot in range(lots):
+        lanes = slice(lot * LANES, (lot + 1) * LANES)
+        sums_ref[:M, lanes] += coded[lot * M : (lot + 1) * M, :] * scale[first + lot : first + lot + 1, :]
 
 
 def solve_product(inverse, sums):
@@ -292,65 +281,67 @@
     return jnp.dot(left, right, preferred_element_type=F32)
 
 
-def finish_kernel(at, layout, tiles, raw, told, table, counts, pairs_ref, own_ref, partner_ref, inverse_ref, *rest):
-    first, middle, last = rest[:2], rest[2:4], rest[4:6]
+def finish_kernel(at, layout, halves, raw, told, table, counts, pairs_ref, own_ref, partner_ref, inverse_ref, *rest):
+    first, middle_ref, last_ref = rest[: max(raw, 1)], rest[max(raw, 1)], rest[max(raw, 1) + 1]
     sums_ref, rest = rest[-1], rest[:-1]
     if told:
         rest[-1][...] = jnp.zeros_like(rest[-1])
         rest = rest[:-1]
     out_ref = rest[-1]
     count = piece_count(at, layout, table, counts)
-    sums_ref[:M, :] = pair_sums(count, table, pairs_ref, own_ref, partner_ref)
-    sums_ref[M:, :] = jnp.zeros((PAD - M, sums_ref.shape[1]), F32)
-
-    @pl.when(table[INNER] == 0)
-    def _():
-        if raw:
-            sums_ref[:M, :] += near_sums(True, count, table, pairs_ref, first)
-        else:
-            add_arrived(sums_ref, first, tiles)
-
-    @pl.when(table[INNER] == 1)
-    def _():
-        add_arrived(sums_ref, middle, tiles)
-
-    add_arrived(sums_ref, last, tiles)
-    out_ref[...] = solve_product(inverse_ref[0, :M, :], sums_ref[...])
+    width = sums_ref.shape[1]
+    sums_ref[M:, :] = jnp.zeros((PAD - M, width), F32)
+    for half in range(halves):
+        part = pl.ds(half * width, width)
+        sums_ref[:M, :] = pair_sums(count, table, pairs_ref, own_ref.at[:, part], partner_ref.at[:, part])
+
+        @pl.when(table[INNER] == 0)
+        def _():
+            if raw:
+                sums_ref[:M, :] += near_sums(True, count, table, pairs_ref, [each.at[:, part] for each in first])
+            else:
+                add_coded(sums_ref, first[0], half, halves)
+
+        @pl.when(table[INNER] == 1)
+        def _():
+            add_coded(sums_ref, middle_ref, half, halves)
+
+        add_coded(sums_ref, last_ref, half, halves)
+        out_ref[:, part] = solve_product(inverse_ref[0, :M, :], sums_ref[...])
 
 
 def finish(at, part, layout, scalars, pairs, phases, partner, inverse, raw, arrived, series, told, pixels, piece):
     partner, place_in = partner
     local_pairs = phases.shape[0]
     blocks = layout[1]
-    tiles = HALVES
-    tile = piece // tiles
+    whole_block = lambda i, t, c: (0, 0)
     in_specs = [
-        pl.BlockSpec(pairs.shape, lambda i, t, c: (0, 0)),
-        pl.BlockSpec((local_pairs, tile), lambda i, t, c: (0, t[blocks + at] * tiles + i)),
-        pl.BlockSpec((local_pairs, tile), lambda i, t, c: (0, place_in * tiles + i)),
+        pl.BlockSpec(pairs.shape, whole_block),
+        pl.BlockSpec((local_pairs, piece), lambda i, t, c: (0, t[blocks + at])),
+        pl.BlockSpec((local_pairs, piece), lambda i, t, c: (0, place_in)),
         pl.BlockSpec((1, PAD, PAD), lambda i, t, c: (part // CUTS, 0, 0)),
     ]
-    in_specs += [pl.BlockSpec((local_pairs, tile), lambda i, t, c: (0, i))] * len(raw) + coded_specs(piece, tiles, 0) * len(arrived)
-    operands = [*scalars, pairs, phases, partner, inverse, *raw] + [each for each in arrived for _ in range(2)]
+    in_specs += [pl.BlockSpec(each.shape, whole_block) for each in [*raw, *arrived]]
+    operands = [*scalars, pairs, phases, partner, inverse, *raw, *arrived]
     aliases = {}
     if series is not None:
         in_specs.append(pl.BlockSpec(memory_space=pl.ANY))
         aliases = {len(operands): 0}
         operands.append(series)
     out_shape = [jax.ShapeDtypeStruct((M, pixels), F32)]
-    out_specs = [pl.BlockSpec((M, tile), lambda i, t, c: (0, part * tiles + i))]
+    out_specs = [pl.BlockSpec((M, piece), lambda i, t, c: (0, part))]
     if told:
         out_shape.append(jax.ShapeDtypeStruct((8, LANES), F32))
         out_specs.append(pl.BlockSpec((8, LANES), lambda i, t, c: (0, 0)))
     return pl.pallas_call(
-        functools.partial(finish_kernel, at, layout, tiles, len(raw) > 0, told),
+        functools.partial(finish_kernel, at, layout, HALVES, len(raw), told),
         out_shape=out_shape,
         grid_spec=pltpu.PrefetchScalarGridSpec(
             num_scalar_prefetch=2,
-            grid=(tiles,),
+            grid=(1,),
             in_specs=in_specs,
             out_specs=out_specs,
-            scratch_shapes=[pltpu.VMEM((PAD, tile), F32)],
+            scratch_shapes=[pltpu.VMEM((PAD, piece // HALVES), F32)],
         ),
         input_output_aliases=aliases,
         compiler_params=pltpu.CompilerParams(vmem_limit_bytes=VMEM_BYTES),

time: 128 us -> 129 us (level)
  starting transfers between devices: 60.8 us -> 55.7 us
  waiting for transfers between devices: 15.3 us -> 20.1 us
    ppermute x15, waiting for transfers between devices: 13.5 us -> 18.5 us  [solve_by_sums(): lax.ppermute(coded, 'ifg', line_permutation(links))]
    ppermute x8, starting transfers between devices: 13.6 us -> 9.06 us  [swapped(): here = lax.ppermute(away, 'ifg', swap)]
  transfers between devices with their start and end apart: 29 -> 29, of which waited for: 10 -> 9; matrix products, arithmetic and copies ran while one was open for 2% -> 2% of each run, Pallas kernels for 33% -> 33%
where the time goes in v6:
time: 129 us; the launch traced here: 127 us
  starting transfers between devices  55.7 us (43%)
  Pallas kernels  45.6 us (35%)
  waiting for transfers between devices  20.1 us (16%)
  local copies, waits for them, and re-layouts  4.38 us (3%)
    ppermute x15, starting transfers between devices, solve_by_sums(): lax.ppermute(coded, 'ifg', line_permutation(links))  36.5 us
    pallas_call x11, Pallas kernels, step(): pl.pallas_call(functools.partial(step_kernel, at, layout, len(earlier), s...  23.3 us
    ppermute x15, waiting for transfers between devices, solve_by_sums(): lax.ppermute(coded, 'ifg', line_permutation(links))  18.5 us
    pallas_call x4, Pallas kernels, finish(): pl.pallas_call(functools.partial(finish_kernel, at, layout, HALVES, len(r...  14.8 us
    ppermute x8, starting transfers between devices, swapped(): here = lax.ppermute(away, 'ifg', swap)  9.06 us
    pallas_call x1, Pallas kernels, invert_classes(): pl.pallas_call(inverse_kernel, out_shape=jax.ShapeDtypeStruct(shape, F32)...  7.56 us
    ppermute x3, starting transfers between devices, solve_by_sums(): counts.append(lax.ppermute(run_counts, 'ifg', line_permutation(links)))  6.11 us
  transfers between devices with their start and end apart: 29, of which 9 were waited for; matrix products, arithmetic and copies ran while one was open for 2% of the time, Pallas kernels for 33%

profile of v6, /device:TPU:0, one launch (start us, length us, event | category | flops | bytes accessed | tf_op | source)
XLA Modules:
  0.0 127.0 jit_solution(1153822218669492360)
XLA Ops:
  0.0 1.1 dynamic-slice_bitcast_fusion
  1.2 0.8 fusion.counts_ref
  2.1 5.1 %collective-permute-start.2 = (s32[2]{0:T(128)S(1)}, s32[2]{0:T(128)S(1)}, u32[]{:S(2)}, u32[]{:S(2)}) collective-permute-start(s32[2]{0:T(128)S(1)} %fusion.counts_ref), channel_id=1, source_target_pairs={{0,24},{4,28},{8,0},{12,4},{16,8},{20,12},{24,16},{28,20},{1,25},{... | collective-permute-start | bytes 32 | tf_op jit(solution)/shard_map/ppermute | solution.py:403
  7.2 1.0 collective-permute-start
  8.2 1.5 %collective-permute-start.3 = (bf16[128,2048]{1,0:T(8,128)(2,1)S(1)}, bf16[128,2048]{1,0:T(8,128)(2,1)S(1)}, u32[]{:S(2)}, u32[]{:S(2)}) collective-permute-start(bf16[128,2048]{1,0:T(8,128)(2,1)S(1)} %dynamic-slice_bitcast_fusion), channel_id=1, source_target_pairs={{0,4},{4,0},{8,12},{12,8},{16,20},{20,16},{24,28},{28,24},{1,5},{5... | collective-permute-start | bytes 1572872 | tf_op jit(solution)/shard_map/ppermute | solution.py:385
  9.7 1.1 dynamic-slice_bitcast_fusion.1
  10.7 2.5 %collective-permute-start.5 = (bf16[128,1024]{1,0:T(8,128)(2,1)S(1)}, bf16[128,1024]{1,0:T(8,128)(2,1)S(1)}, u32[]{:S(2)}, u32[]{:S(2)}) collective-permute-start(bf16[128,1024]{1,0:T(8,128)(2,1)S(1)} %get-tuple-element.45), channel_id=1, source_target_pairs={{0,8},{4,12},{8,0},{12,4},{16,24},{20,28},{24,16},{28,20},{1,9},{5... | collective-permute-start | bytes 786440 | tf_op jit(solution)/shard_map/ppermute | solution.py:407
  13.3 0.7 constant_dynamic-slice_fusion.3
  15.6 7.6 %invert_classes_0.1.rest_1_.inverse_ref = f32[2,256,256]{2,1,0:T(8,128)S(1)} custom-call(s32[2]{0:T(128)S(1)} %fusion.counts_ref, s32[2,1024]{1,0:T(2,128)S(1)} %copy-done.1, s32[8]{0:T(128)S(1)} %pad_add_fusion.1.rest_0_.counts), custom_call_target="tpu_custom_call" | custom-call | flops 1024 | bytes 1024 | tf_op jit(solution)/shard_map/invert_classes_0/pallas_call | solution.py:103
  23.2 2.1 %sum_step_00.1 = (s16[1616,128]{1,0:T(8,128)(2,1)S(1)}, bf16[128,1024]{1,0:T(8,128)(2,1)S(1)}) custom-call(s32[53]{0:T(128)S(1)} %fusion.1.table, s32[8]{0:T(128)S(1)} %pad_add_fusion.1.rest_0_.counts, s32[2,512]{1,0:T(2,128)S(1)} %pad_add_fusion.pairs_ref, bf16[128,32768]{1,0:T(8,128)(2,1)} %bitcast.12, ...), custom_call_target="tpu_custom_call" | custom-call | flops 10000000000 | bytes 30000000 | tf_op jit(solution)/shard_map/sum_step_00/pallas_call | solution.py:245
  25.8 1.2 collective-permute-start.8
  27.1 2.2 %sum_step_01.1 = (s16[1616,128]{1,0:T(8,128)(2,1)S(1)}, bf16[128,2048]{1,0:T(8,128)(2,1)S(1)}) custom-call(s32[53]{0:T(128)S(1)} %fusion.1.table, s32[8]{0:T(128)S(1)} %pad_add_fusion.1.rest_0_.counts, s32[2,512]{1,0:T(2,128)S(1)} %pad_add_fusion.pairs_ref, bf16[128,32768]{1,0:T(8,128)(2,1)} %bitcast.14, ...), custom_call_target="tpu_custom_call" | custom-call | flops 10000000000 | bytes 30000000 | tf_op jit(solution)/shard_map/sum_step_01/pallas_call | solution.py:245
  29.3 0.8 collective-permute-start.7
  30.1 1.5 %collective-permute-start.6 = (bf16[128,2048]{1,0:T(8,128)(2,1)S(1)}, bf16[128,2048]{1,0:T(8,128)(2,1)S(1)}, u32[]{:S(2)}, u32[]{:S(2)}) collective-permute-start(bf16[128,2048]{1,0:T(8,128)(2,1)S(1)} %get-tuple-element.29), channel_id=1, source_target_pairs={{0,4},{4,0},{8,12},{12,8},{16,20},{20,16},{24,28},{28,24},{1,5},{5... | collective-permute-start | bytes 1572872 | tf_op jit(solution)/shard_map/ppermute | solution.py:385
  31.6 1.5 %collective-permute-done.9.partner_ref = bf16[128,1024]{1,0:T(8,128)(2,1)S(1)} collective-permute-done((bf16[128,1024]{1,0:T(8,128)(2,1)S(1)}, bf16[128,1024]{1,0:T(8,128)(2,1)S(1)}, u32[]{:S(2)}, u32[]{:S(2)}) %collective-permute-start.9) | collective-permute-done | bytes 262176 | tf_op jit(solution)/shard_map/ppermute | solution.py:385
  33.1 5.2 %collective-permute-done.8.rest_2_.rest_0_ = s16[1616,128]{1,0:T(8,128)(2,1)S(1)} collective-permute-done((s16[1616,128]{1,0:T(8,128)(2,1)S(1)}, s16[1616,128]{1,0:T(8,128)(2,1)S(1)}, u32[]{:S(2)}, u32[]{:S(2)}) %collective-permute-start.8) | collective-permute-done | bytes 413728 | tf_op jit(solution)/shard_map/ppermute | solution.py:436
  38.3 2.2 %sum_step_02.1 = (s16[1616,128]{1,0:T(8,128)(2,1)S(1)}, bf16[128,2048]{1,0:T(8,128)(2,1)S(1)}) custom-call(s32[53]{0:T(128)S(1)} %fusion.1.table, s32[8]{0:T(128)S(1)} %pad_add_fusion.1.rest_0_.counts, s32[2,512]{1,0:T(2,128)S(1)} %pad_add_fusion.pairs_ref, bf16[128,32768]{1,0:T(8,128)(2,1)} %bitcast.16, ...), custom_call_target="tpu_custom_call" | custom-call | flops 10000000000 | bytes 30000000 | tf_op jit(solution)/shard_map/sum_step_02/pallas_call | solution.py:245
  40.5 1.3 %collective-permute-start.10 = (s16[1616,128]{1,0:T(8,128)(2,1)S(1)}, s16[1616,128]{1,0:T(8,128)(2,1)S(1)}, u32[]{:S(2)}, u32[]{:S(2)}) collective-permute-start(s16[1616,128]{1,0:T(8,128)(2,1)S(1)} %get-tuple-element.32.rest_1_), channel_id=1, source_target_pairs={{0,8},{4,12},{8,0},{12,4},{16,24},{20,28},{24,16},{28,20},{1,9},{5... | collective-permute-start | bytes 1241096 | tf_op jit(solution)/shard_map/ppermute | solution.py:436
  41.8 1.4 %collective-permute-start.11 = (bf16[128,1024]{1,0:T(8,128)(2,1)S(1)}, bf16[128,1024]{1,0:T(8,128)(2,1)S(1)}, u32[]{:S(2)}, u32[]{:S(2)}) collective-permute-start(bf16[128,1024]{1,0:T(8,128)(2,1)S(1)} %collective-permute-done.5.rest_3_), channel_id=1, source_target_pairs={{0,4},{4,0},{8,12},{12,8},{16,20},{20,16},{24,28},{28,24},{1,5},{5... | collective-permute-start | bytes 786440 | tf_op jit(solution)/shard_map/ppermute | solution.py:442
  43.8 3.3 %collective-permute-done.7.rest_2_.rest_1_.rest_0_ = s16[1616,128]{1,0:T(8,128)(2,1)S(1)} collective-permute-done((s16[1616,128]{1,0:T(8,128)(2,1)S(1)}, s16[1616,128]{1,0:T(8,128)(2,1)S(1)}, u32[]{:S(2)}, u32[]{:S(2)}) %collective-permute-start.7) | collective-permute-done | bytes 413728 | tf_op jit(solution)/shard_map/ppermute | solution.py:436
  47.2 2.0 %sum_step_04.1.rest_2_ = s16[1616,128]{1,0:T(8,128)(2,1)S(1)} custom-call(s32[53]{0:T(128)S(1)} %fusion.1.table, s32[8]{0:T(128)S(1)} %pad_add_fusion.1.rest_0_.counts, s32[2,512]{1,0:T(2,128)S(1)} %pad_add_fusion.pairs_ref, bf16[128,32768]{1,0:T(8,128)(2,1)} %bitcast.18, bf16[128,2048]{1,0:T(8,128)(2,1)S(1)} %collective-permute-done.6.partner_ref, ...), custom_call_target="tpu_custom_call" | custom-call | flops 10000000000 | bytes 30000000 | tf_op jit(solution)/shard_map/sum_step_04/pallas_call | solution.py:245
  49.9 5.1 %collective-permute-start.14 = (s16[1616,128]{1,0:T(8,128)(2,1)S(1)}, s16[1616,128]{1,0:T(8,128)(2,1)S(1)}, u32[]{:S(2)}, u32[]{:S(2)}) collective-permute-start(s16[1616,128]{1,0:T(8,128)(2,1)S(1)} %sum_step_04.1.rest_2_), channel_id=1, source_target_pairs={{0,8},{4,12},{24,16},{28,20},{1,9},{5,13},{25,17},{29,21},{2,10},{... | collective-permute-start | bytes 1241096 | tf_op jit(solution)/shard_map/ppermute | solution.py:436
  55.1 2.2 %sum_step_05.1 = (s16[1616,128]{1,0:T(8,128)(2,1)S(1)}, bf16[128,2048]{1,0:T(8,128)(2,1)S(1)}) custom-call(s32[53]{0:T(128)S(1)} %fusion.1.table, s32[8]{0:T(128)S(1)} %pad_add_fusion.1.rest_0_.counts, s32[2,512]{1,0:T(2,128)S(1)} %pad_add_fusion.pairs_ref, bf16[128,32768]{1,0:T(8,128)(2,1)} %bitcast.19, ...), custom_call_target="tpu_custom_call" | custom-call | flops 10000000000 | bytes 30000000 | tf_op jit(solution)/shard_map/sum_step_05/pallas_call | solution.py:245
  58.0 5.4 %collective-permute-start.13 = (s16[1616,128]{1,0:T(8,128)(2,1)S(1)}, s16[1616,128]{1,0:T(8,128)(2,1)S(1)}, u32[]{:S(2)}, u32[]{:S(2)}) collective-permute-start(s16[1616,128]{1,0:T(8,128)(2,1)S(1)} %get-tuple-element.35.rest_1_), channel_id=1, source_target_pairs={{0,8},{4,12},{24,16},{28,20},{1,9},{5,13},{25,17},{29,21},{2,10},{... | collective-permute-start | bytes 1241096 | tf_op jit(solution)/shard_map/ppermute | solution.py:436
  63.4 1.5 %collective-permute-start.12 = (bf16[128,2048]{1,0:T(8,128)(2,1)S(1)}, bf16[128,2048]{1,0:T(8,128)(2,1)S(1)}, u32[]{:S(2)}, u32[]{:S(2)}) collective-permute-start(bf16[128,2048]{1,0:T(8,128)(2,1)S(1)} %get-tuple-element.34), channel_id=1, source_target_pairs={{0,4},{4,0},{8,12},{12,8},{16,20},{20,16},{24,28},{28,24},{1,5},{5... | collective-permute-start | bytes 1572872 | tf_op jit(solution)/shard_map/ppermute | solution.py:385
  64.9 2.0 %sum_step_06.1.rest_3_ = s16[1616,128]{1,0:T(8,128)(2,1)S(1)} custom-call(s32[53]{0:T(128)S(1)} %fusion.1.table, s32[8]{0:T(128)S(1)} %pad_add_fusion.1.rest_0_.counts, s32[2,512]{1,0:T(2,128)S(1)} %pad_add_fusion.pairs_ref, bf16[128,32768]{1,0:T(8,128)(2,1)} %bitcast.21, bf16[128,2048]{1,0:T(8,128)(2,1)S(1)} %collective-permute-done.15.partner_ref, ...), custom_call_target="tpu_custom_call" | custom-call | flops 10000000000 | bytes 30000000 | tf_op jit(solution)/shard_map/sum_step_06/pallas_call | solution.py:245
  67.6 4.5 %collective-permute-start.18 = (s16[1616,128]{1,0:T(8,128)(2,1)S(1)}, s16[1616,128]{1,0:T(8,128)(2,1)S(1)}, u32[]{:S(2)}, u32[]{:S(2)}) collective-permute-start(s16[1616,128]{1,0:T(8,128)(2,1)S(1)} %sum_step_06.1.rest_3_), channel_id=1, source_target_pairs={{0,8},{4,12},{24,16},{28,20},{1,9},{5,13},{25,17},{29,21},{2,10},{... | collective-permute-start | bytes 1241096 | tf_op jit(solution)/shard_map/ppermute | solution.py:436
  72.2 0.9 collective-permute-done.13.rest_4_.rest_1_
  73.1 2.2 %sum_step_07.1 = (s16[1616,128]{1,0:T(8,128)(2,1)S(1)}, bf16[128,2048]{1,0:T(8,128)(2,1)S(1)}) custom-call(s32[53]{0:T(128)S(1)} %fusion.1.table, s32[8]{0:T(128)S(1)} %pad_add_fusion.1.rest_0_.counts, s32[2,512]{1,0:T(2,128)S(1)} %pad_add_fusion.pairs_ref, bf16[128,32768]{1,0:T(8,128)(2,1)} %bitcast.22, ...), custom_call_target="tpu_custom_call" | custom-call | flops 10000000000 | bytes 30000000 | tf_op jit(solution)/shard_map/sum_step_07/pallas_call | solution.py:245
  76.0 6.4 %collective-permute-start.20 = (s16[1616,128]{1,0:T(8,128)(2,1)S(1)}, s16[1616,128]{1,0:T(8,128)(2,1)S(1)}, u32[]{:S(2)}, u32[]{:S(2)}) collective-permute-start(s16[1616,128]{1,0:T(8,128)(2,1)S(1)} %get-tuple-element.37.rest_2_), channel_id=1, source_target_pairs={{0,8},{4,12},{24,16},{28,20},{1,9},{5,13},{25,17},{29,21},{2,10},{... | collective-permute-start | bytes 1241096 | tf_op jit(solution)/shard_map/ppermute | solution.py:436
  82.5 1.0 collective-permute-start.23
  83.5 2.2 %sum_step_08.1 = (s16[1616,128]{1,0:T(8,128)(2,1)S(1)}, bf16[128,2048]{1,0:T(8,128)(2,1)S(1)}) custom-call(s32[53]{0:T(128)S(1)} %fusion.1.table, s32[8]{0:T(128)S(1)} %pad_add_fusion.1.rest_0_.counts, s32[2,512]{1,0:T(2,128)S(1)} %pad_add_fusion.pairs_ref, bf16[128,32768]{1,0:T(8,128)(2,1)} %bitcast.24, ...), custom_call_target="tpu_custom_call" | custom-call | flops 10000000000 | bytes 30000000 | tf_op jit(solution)/shard_map/sum_step_08/pallas_call | solution.py:245
  85.7 1.2 collective-permute-start.24
  86.9 1.5 %collective-permute-start.26 = (bf16[128,2048]{1,0:T(8,128)(2,1)S(1)}, bf16[128,2048]{1,0:T(8,128)(2,1)S(1)}, u32[]{:S(2)}, u32[]{:S(2)}) collective-permute-start(bf16[128,2048]{1,0:T(8,128)(2,1)S(1)} %get-tuple-element.42), channel_id=1, source_target_pairs={{0,4},{4,0},{8,12},{12,8},{16,20},{20,16},{24,28},{28,24},{1,5},{5... | collective-permute-start | bytes 1572872 | tf_op jit(solution)/shard_map/ppermute | solution.py:385
  88.4 4.0 %collective-permute-done.20.rest_3_.rest_0_ = s16[1616,128]{1,0:T(8,128)(2,1)S(1)} collective-permute-done((s16[1616,128]{1,0:T(8,128)(2,1)S(1)}, s16[1616,128]{1,0:T(8,128)(2,1)S(1)}, u32[]{:S(2)}, u32[]{:S(2)}) %collective-permute-start.20) | collective-permute-done | bytes 413728 | tf_op jit(solution)/shard_map/ppermute | solution.py:436
  92.4 2.2 %sum_step_09.1 = (s16[1616,128]{1,0:T(8,128)(2,1)S(1)}, bf16[128,2048]{1,0:T(8,128)(2,1)S(1)}) custom-call(s32[53]{0:T(128)S(1)} %fusion.1.table, s32[8]{0:T(128)S(1)} %pad_add_fusion.1.rest_0_.counts, s32[2,512]{1,0:T(2,128)S(1)} %pad_add_fusion.pairs_ref, bf16[128,32768]{1,0:T(8,128)(2,1)} %bitcast.26, ...), custom_call_target="tpu_custom_call" | custom-call | flops 10000000000 | bytes 30000000 | tf_op jit(solution)/shard_map/sum_step_09/pallas_call | solution.py:245
  94.7 2.5 %collective-permute-start.25 = (s16[1616,128]{1,0:T(8,128)(2,1)S(1)}, s16[1616,128]{1,0:T(8,128)(2,1)S(1)}, u32[]{:S(2)}, u32[]{:S(2)}) collective-permute-start(s16[1616,128]{1,0:T(8,128)(2,1)S(1)} %get-tuple-element.41.rest_1_), channel_id=1, source_target_pairs={{0,8},{4,12},{8,24},{12,28},{16,0},{20,4},{24,16},{28,20},{1,9},{5... | collective-permute-start | bytes 1241096 | tf_op jit(solution)/shard_map/ppermute | solution.py:436
  97.2 0.9 collective-permute-start.22
  98.1 3.2 %collective-permute-done.24.rest_2_ = s16[1616,128]{1,0:T(8,128)(2,1)S(1)} collective-permute-done((s16[1616,128]{1,0:T(8,128)(2,1)S(1)}, s16[1616,128]{1,0:T(8,128)(2,1)S(1)}, u32[]{:S(2)}, u32[]{:S(2)}) %collective-permute-start.24) | collective-permute-done | bytes 413728 | tf_op jit(solution)/shard_map/ppermute | solution.py:436
  101.3 2.0 %sum_step_10.1.rest_1_ = s16[1616,128]{1,0:T(8,128)(2,1)S(1)} custom-call(s32[53]{0:T(128)S(1)} %fusion.1.table, s32[8]{0:T(128)S(1)} %pad_add_fusion.1.rest_0_.counts, s32[2,512]{1,0:T(2,128)S(1)} %pad_add_fusion.pairs_ref, bf16[128,32768]{1,0:T(8,128)(2,1)} %bitcast.28, bf16[128,2048]{1,0:T(8,128)(2,1)S(1)} %collective-permute-done.23.partner_ref, ...), custom_call_target="tpu_custom_call" | custom-call | flops 10000000000 | bytes 30000000 | tf_op jit(solution)/shard_map/sum_step_10/pallas_call | solution.py:245
  103.3 2.5 %collective-permute-start.28 = (s16[1616,128]{1,0:T(8,128)(2,1)S(1)}, s16[1616,128]{1,0:T(8,128)(2,1)S(1)}, u32[]{:S(2)}, u32[]{:S(2)}) collective-permute-start(s16[1616,128]{1,0:T(8,128)(2,1)S(1)} %sum_step_10.1.rest_1_), channel_id=1, source_target_pairs={{0,8},{4,12},{8,24},{12,28},{16,0},{20,4},{24,16},{28,20},{1,9},{5... | collective-permute-start | bytes 1241096 | tf_op jit(solution)/shard_map/ppermute | solution.py:436
  105.9 3.8 %finish_0.1 = (f32[200,4096]{1,0:T(8,128)}, f32[8,128]{1,0:T(8,128)S(1)}) custom-call(s32[53]{0:T(128)S(1)} %fusion.1.table, s32[8]{0:T(128)S(1)} %pad_add_fusion.1.rest_0_.counts, s32[2,512]{1,0:T(2,128)S(1)} %pad_add_fusion.pairs_ref, bf16[128,32768]{1,0:T(8,128)(2,1)} %bitcast.29, bf16[128,2048]{1,0:T(8,128)(2,1)S(1)} %collective-permute-done.26.partner_ref, ...), custom_call_target="tpu_custom_call" | custom-call | flops 1024 | bytes 1024 | tf_op jit(solution)/shard_map/finish_0/pallas_call | solution.py:336
  110.2 2.0 %sum_step_11.1 = s16[1616,128]{1,0:T(8,128)(2,1)S(1)} custom-call(s32[53]{0:T(128)S(1)} %fusion.1.table, s32[8]{0:T(128)S(1)} %pad_add_fusion.1.rest_0_.counts, s32[2,512]{1,0:T(2,128)S(1)} %pad_add_fusion.pairs_ref, bf16[128,32768]{1,0:T(8,128)(2,1)} %bitcast.30, bf16[128,2048]{1,0:T(8,128)(2,1)S(1)} %collective-permute-done.23.partner_ref, ...), custom_call_target="tpu_custom_call" | custom-call | flops 10000000000 | bytes 30000000 | tf_op jit(solution)/shard_map/sum_step_11/pallas_call | solution.py:245
  112.2 2.5 %collective-permute-start.27 = (s16[1616,128]{1,0:T(8,128)(2,1)S(1)}, s16[1616,128]{1,0:T(8,128)(2,1)S(1)}, u32[]{:S(2)}, u32[]{:S(2)}) collective-permute-start(s16[1616,128]{1,0:T(8,128)(2,1)S(1)} %sum_step_11.1), channel_id=1, source_target_pairs={{0,8},{4,12},{8,24},{12,28},{16,0},{20,4},{24,16},{28,20},{1,9},{5... | collective-permute-start | bytes 1241096 | tf_op jit(solution)/shard_map/ppermute | solution.py:436
  114.7 3.6 %finish_1.1.rest_3_ = f32[200,4096]{1,0:T(8,128)} custom-call(s32[53]{0:T(128)S(1)} %fusion.1.table, s32[8]{0:T(128)S(1)} %pad_add_fusion.1.rest_0_.counts, s32[2,512]{1,0:T(2,128)S(1)} %pad_add_fusion.pairs_ref, bf16[128,32768]{1,0:T(8,128)(2,1)} %bitcast.31, ...), custom_call_target="tpu_custom_call", output_to_operand_aliasing={{}: (9, {})} | custom-call | flops 1024 | bytes 1024 | tf_op jit(solution)/shard_map/finish_1/pallas_call | solution.py:336
  118.7 3.6 %finish_2.1.rest_4_ = f32[200,4096]{1,0:T(8,128)} custom-call(s32[53]{0:T(128)S(1)} %fusion.1.table, s32[8]{0:T(128)S(1)} %pad_add_fusion.1.rest_0_.counts, s32[2,512]{1,0:T(2,128)S(1)} %pad_add_fusion.pairs_ref, bf16[128,32768]{1,0:T(8,128)(2,1)} %bitcast.32, ...), custom_call_target="tpu_custom_call", output_to_operand_aliasing={{}: (9, {})} | custom-call | flops 1024 | bytes 1024 | tf_op jit(solution)/shard_map/finish_2/pallas_call | solution.py:336
  122.3 0.8 collective-permute-done.27.rest_3_
  123.1 3.9 %finish_3.1 = f32[200,4096]{1,0:T(8,128)} custom-call(s32[53]{0:T(128)S(1)} %fusion.1.table, s32[8]{0:T(128)S(1)} %pad_add_fusion.1.rest_0_.counts, s32[2,512]{1,0:T(2,128)S(1)} %pad_add_fusion.pairs_ref, bf16[128,32768]{1,0:T(8,128)(2,1)} %bitcast.33, bf16[128,2048]{1,0:T(8,128)(2,1)S(1)} %collective-permute-done.22.partner_ref, ...), custom_call_target="tpu_custom_call", output_to_operand_aliasing={{}: (10, {})} | custom-call | flops 1024 | bytes 1024 | tf_op jit(solution)/shard_map/finish_3/pallas_call | solution.py:336
  (39 shorter events, 6.6 us)
Async XLA Ops:
  0.0 1.1 copy-start
  2.1 11.9 %collective-permute-start.2 = (s32[2]{0:T(128)S(1)}, s32[2]{0:T(128)S(1)}, u32[]{:S(2)}, u32[]{:S(2)}) collective-permute-start(s32[2]{0:T(128)S(1)} %fusion.counts_ref), channel_id=1, source_target_pairs={{0,24},{4,28},{8,0},{12,4},{16,8},{20,12},{24,16},{28,20},{1,25},{... | collective-permute-start | bytes 32 | tf_op jit(solution)/shard_map/ppermute | solution.py:403
  7.1 7.0 %collective-permute-start.1 = (s32[2]{0:T(128)S(1)}, s32[2]{0:T(128)S(1)}, u32[]{:S(2)}, u32[]{:S(2)}) collective-permute-start(s32[2]{0:T(128)S(1)} %fusion.counts_ref), channel_id=1, source_target_pairs={{0,16},{4,20},{8,24},{12,28},{16,0},{20,4},{24,8},{28,12},{1,17},{... | collective-permute-start | bytes 32 | tf_op jit(solution)/shard_map/ppermute | solution.py:403
  7.2 7.0 %collective-permute-start = (s32[2]{0:T(128)S(1)}, s32[2]{0:T(128)S(1)}, u32[]{:S(2)}, u32[]{:S(2)}) collective-permute-start(s32[2]{0:T(128)S(1)} %fusion.counts_ref), channel_id=1, source_target_pairs={{0,8},{4,12},{8,16},{12,20},{16,24},{20,28},{24,0},{28,4},{1,9},{5... | collective-permute-start | bytes 32 | tf_op jit(solution)/shard_map/ppermute | solution.py:403
  8.2 15.0 %collective-permute-start.3 = (bf16[128,2048]{1,0:T(8,128)(2,1)S(1)}, bf16[128,2048]{1,0:T(8,128)(2,1)S(1)}, u32[]{:S(2)}, u32[]{:S(2)}) collective-permute-start(bf16[128,2048]{1,0:T(8,128)(2,1)S(1)} %dynamic-slice_bitcast_fusion), channel_id=1, source_target_pairs={{0,4},{4,0},{8,12},{12,8},{16,20},{20,16},{24,28},{28,24},{1,5},{5... | collective-permute-start | bytes 1572872 | tf_op jit(solution)/shard_map/ppermute | solution.py:385
  10.7 16.4 %collective-permute-start.5 = (bf16[128,1024]{1,0:T(8,128)(2,1)S(1)}, bf16[128,1024]{1,0:T(8,128)(2,1)S(1)}, u32[]{:S(2)}, u32[]{:S(2)}) collective-permute-start(bf16[128,1024]{1,0:T(8,128)(2,1)S(1)} %get-tuple-element.45), channel_id=1, source_target_pairs={{0,8},{4,12},{8,0},{12,4},{16,24},{20,28},{24,16},{28,20},{1,9},{5... | collective-permute-start | bytes 786440 | tf_op jit(solution)/shard_map/ppermute | solution.py:407
  14.0 13.1 %collective-permute-start.4 = (bf16[128,1024]{1,0:T(8,128)(2,1)S(1)}, bf16[128,1024]{1,0:T(8,128)(2,1)S(1)}, u32[]{:S(2)}, u32[]{:S(2)}) collective-permute-start(bf16[128,1024]{1,0:T(8,128)(2,1)S(1)} %get-tuple-element.46), channel_id=1, source_target_pairs={{0,8},{4,12},{8,0},{12,4},{16,24},{20,28},{24,16},{28,20},{1,9},{5... | collective-permute-start | bytes 786440 | tf_op jit(solution)/shard_map/ppermute | solution.py:408
  14.9 0.7 copy-start.1
  25.2 7.9 %collective-permute-start.9 = (bf16[128,1024]{1,0:T(8,128)(2,1)S(1)}, bf16[128,1024]{1,0:T(8,128)(2,1)S(1)}, u32[]{:S(2)}, u32[]{:S(2)}) collective-permute-start(bf16[128,1024]{1,0:T(8,128)(2,1)S(1)} %get-tuple-element.31), channel_id=1, source_target_pairs={{0,4},{4,0},{8,12},{12,8},{16,20},{20,16},{24,28},{28,24},{1,5},{5... | collective-permute-start | bytes 786440 | tf_op jit(solution)/shard_map/ppermute | solution.py:385
  25.8 12.5 %collective-permute-start.8 = (s16[1616,128]{1,0:T(8,128)(2,1)S(1)}, s16[1616,128]{1,0:T(8,128)(2,1)S(1)}, u32[]{:S(2)}, u32[]{:S(2)}) collective-permute-start(s16[1616,128]{1,0:T(8,128)(2,1)S(1)} %get-tuple-element.26.rest_1_), channel_id=1, source_target_pairs={{0,8},{4,12},{8,0},{12,4},{16,24},{20,28},{24,16},{28,20},{1,9},{5... | collective-permute-start | bytes 1241096 | tf_op jit(solution)/shard_map/ppermute | solution.py:436
  29.3 17.9 %collective-permute-start.7 = (s16[1616,128]{1,0:T(8,128)(2,1)S(1)}, s16[1616,128]{1,0:T(8,128)(2,1)S(1)}, u32[]{:S(2)}, u32[]{:S(2)}) collective-permute-start(s16[1616,128]{1,0:T(8,128)(2,1)S(1)} %get-tuple-element.30.rest_1_), channel_id=1, source_target_pairs={{0,8},{4,12},{8,0},{12,4},{16,24},{20,28},{24,16},{28,20},{1,9},{5... | collective-permute-start | bytes 1241096 | tf_op jit(solution)/shard_map/ppermute | solution.py:436
  30.1 17.1 %collective-permute-start.6 = (bf16[128,2048]{1,0:T(8,128)(2,1)S(1)}, bf16[128,2048]{1,0:T(8,128)(2,1)S(1)}, u32[]{:S(2)}, u32[]{:S(2)}) collective-permute-start(bf16[128,2048]{1,0:T(8,128)(2,1)S(1)} %get-tuple-element.29), channel_id=1, source_target_pairs={{0,4},{4,0},{8,12},{12,8},{16,20},{20,16},{24,28},{28,24},{1,5},{5... | collective-permute-start | bytes 1572872 | tf_op jit(solution)/shard_map/ppermute | solution.py:385
  40.5 14.6 %collective-permute-start.10 = (s16[1616,128]{1,0:T(8,128)(2,1)S(1)}, s16[1616,128]{1,0:T(8,128)(2,1)S(1)}, u32[]{:S(2)}, u32[]{:S(2)}) collective-permute-start(s16[1616,128]{1,0:T(8,128)(2,1)S(1)} %get-tuple-element.32.rest_1_), channel_id=1, source_target_pairs={{0,8},{4,12},{8,0},{12,4},{16,24},{20,28},{24,16},{28,20},{1,9},{5... | collective-permute-start | bytes 1241096 | tf_op jit(solution)/shard_map/ppermute | solution.py:436
  41.8 13.2 %collective-permute-start.11 = (bf16[128,1024]{1,0:T(8,128)(2,1)S(1)}, bf16[128,1024]{1,0:T(8,128)(2,1)S(1)}, u32[]{:S(2)}, u32[]{:S(2)}) collective-permute-start(bf16[128,1024]{1,0:T(8,128)(2,1)S(1)} %collective-permute-done.5.rest_3_), channel_id=1, source_target_pairs={{0,4},{4,0},{8,12},{12,8},{16,20},{20,16},{24,28},{28,24},{1,5},{5... | collective-permute-start | bytes 786440 | tf_op jit(solution)/shard_map/ppermute | solution.py:442
  43.3 20.1 %collective-permute-start.15 = (bf16[128,2048]{1,0:T(8,128)(2,1)S(1)}, bf16[128,2048]{1,0:T(8,128)(2,1)S(1)}, u32[]{:S(2)}, u32[]{:S(2)}) collective-permute-start(bf16[128,2048]{1,0:T(8,128)(2,1)S(1)} %get-tuple-element.36), channel_id=1, source_target_pairs={{0,4},{4,0},{8,12},{12,8},{16,20},{20,16},{24,28},{28,24},{1,5},{5... | collective-permute-start | bytes 1572872 | tf_op jit(solution)/shard_map/ppermute | solution.py:385
  49.2 15.7 %collective-permute-start.16 = (s16[1616,128]{1,0:T(8,128)(2,1)S(1)}, s16[1616,128]{1,0:T(8,128)(2,1)S(1)}, u32[]{:S(2)}, u32[]{:S(2)}) collective-permute-start(s16[1616,128]{1,0:T(8,128)(2,1)S(1)} %sum_step_04.1.rest_2_), channel_id=1, source_target_pairs={{8,16},{12,20},{16,8},{20,12},{9,17},{13,21},{17,9},{21,13},{10,18... | collective-permute-start | bytes 1241096 | tf_op jit(solution)/shard_map/ppermute | solution.py:436
  49.9 15.0 %collective-permute-start.14 = (s16[1616,128]{1,0:T(8,128)(2,1)S(1)}, s16[1616,128]{1,0:T(8,128)(2,1)S(1)}, u32[]{:S(2)}, u32[]{:S(2)}) collective-permute-start(s16[1616,128]{1,0:T(8,128)(2,1)S(1)} %sum_step_04.1.rest_2_), channel_id=1, source_target_pairs={{0,8},{4,12},{24,16},{28,20},{1,9},{5,13},{25,17},{29,21},{2,10},{... | collective-permute-start | bytes 1241096 | tf_op jit(solution)/shard_map/ppermute | solution.py:436
  57.3 14.9 %collective-permute-start.17 = (s16[1616,128]{1,0:T(8,128)(2,1)S(1)}, s16[1616,128]{1,0:T(8,128)(2,1)S(1)}, u32[]{:S(2)}, u32[]{:S(2)}) collective-permute-start(s16[1616,128]{1,0:T(8,128)(2,1)S(1)} %get-tuple-element.35.rest_1_), channel_id=1, source_target_pairs={{8,16},{12,20},{16,8},{20,12},{9,17},{13,21},{17,9},{21,13},{10,18... | collective-permute-start | bytes 1241096 | tf_op jit(solution)/shard_map/ppermute | solution.py:436
  58.0 15.1 %collective-permute-start.13 = (s16[1616,128]{1,0:T(8,128)(2,1)S(1)}, s16[1616,128]{1,0:T(8,128)(2,1)S(1)}, u32[]{:S(2)}, u32[]{:S(2)}) collective-permute-start(s16[1616,128]{1,0:T(8,128)(2,1)S(1)} %get-tuple-element.35.rest_1_), channel_id=1, source_target_pairs={{0,8},{4,12},{24,16},{28,20},{1,9},{5,13},{25,17},{29,21},{2,10},{... | collective-permute-start | bytes 1241096 | tf_op jit(solution)/shard_map/ppermute | solution.py:436
  63.4 20.1 %collective-permute-start.12 = (bf16[128,2048]{1,0:T(8,128)(2,1)S(1)}, bf16[128,2048]{1,0:T(8,128)(2,1)S(1)}, u32[]{:S(2)}, u32[]{:S(2)}) collective-permute-start(bf16[128,2048]{1,0:T(8,128)(2,1)S(1)} %get-tuple-element.34), channel_id=1, source_target_pairs={{0,4},{4,0},{8,12},{12,8},{16,20},{20,16},{24,28},{28,24},{1,5},{5... | collective-permute-start | bytes 1572872 | tf_op jit(solution)/shard_map/ppermute | solution.py:385
  66.9 15.6 %collective-permute-start.19 = (s16[1616,128]{1,0:T(8,128)(2,1)S(1)}, s16[1616,128]{1,0:T(8,128)(2,1)S(1)}, u32[]{:S(2)}, u32[]{:S(2)}) collective-permute-start(s16[1616,128]{1,0:T(8,128)(2,1)S(1)} %sum_step_06.1.rest_3_), channel_id=1, source_target_pairs={{8,16},{12,20},{16,8},{20,12},{9,17},{13,21},{17,9},{21,13},{10,18... | collective-permute-start | bytes 1241096 | tf_op jit(solution)/shard_map/ppermute | solution.py:436
  67.6 15.8 %collective-permute-start.18 = (s16[1616,128]{1,0:T(8,128)(2,1)S(1)}, s16[1616,128]{1,0:T(8,128)(2,1)S(1)}, u32[]{:S(2)}, u32[]{:S(2)}) collective-permute-start(s16[1616,128]{1,0:T(8,128)(2,1)S(1)} %sum_step_06.1.rest_3_), channel_id=1, source_target_pairs={{0,8},{4,12},{24,16},{28,20},{1,9},{5,13},{25,17},{29,21},{2,10},{... | collective-permute-start | bytes 1241096 | tf_op jit(solution)/shard_map/ppermute | solution.py:436
  75.3 13.1 %collective-permute-start.21 = (s16[1616,128]{1,0:T(8,128)(2,1)S(1)}, s16[1616,128]{1,0:T(8,128)(2,1)S(1)}, u32[]{:S(2)}, u32[]{:S(2)}) collective-permute-start(s16[1616,128]{1,0:T(8,128)(2,1)S(1)} %get-tuple-element.37.rest_2_), channel_id=1, source_target_pairs={{8,16},{12,20},{16,8},{20,12},{9,17},{13,21},{17,9},{21,13},{10,18... | collective-permute-start | bytes 1241096 | tf_op jit(solution)/shard_map/ppermute | solution.py:436
  76.0 16.4 %collective-permute-start.20 = (s16[1616,128]{1,0:T(8,128)(2,1)S(1)}, s16[1616,128]{1,0:T(8,128)(2,1)S(1)}, u32[]{:S(2)}, u32[]{:S(2)}) collective-permute-start(s16[1616,128]{1,0:T(8,128)(2,1)S(1)} %get-tuple-element.37.rest_2_), channel_id=1, source_target_pairs={{0,8},{4,12},{24,16},{28,20},{1,9},{5,13},{25,17},{29,21},{2,10},{... | collective-permute-start | bytes 1241096 | tf_op jit(solution)/shard_map/ppermute | solution.py:436
  82.5 15.6 %collective-permute-start.23 = (bf16[128,2048]{1,0:T(8,128)(2,1)S(1)}, bf16[128,2048]{1,0:T(8,128)(2,1)S(1)}, u32[]{:S(2)}, u32[]{:S(2)}) collective-permute-start(bf16[128,2048]{1,0:T(8,128)(2,1)S(1)} %get-tuple-element.40), channel_id=1, source_target_pairs={{0,4},{4,0},{8,12},{12,8},{16,20},{20,16},{24,28},{28,24},{1,5},{5... | collective-permute-start | bytes 1572872 | tf_op jit(solution)/shard_map/ppermute | solution.py:385
  85.7 15.6 %collective-permute-start.24 = (s16[1616,128]{1,0:T(8,128)(2,1)S(1)}, s16[1616,128]{1,0:T(8,128)(2,1)S(1)}, u32[]{:S(2)}, u32[]{:S(2)}) collective-permute-start(s16[1616,128]{1,0:T(8,128)(2,1)S(1)} %get-tuple-element.38.rest_2_), channel_id=1, source_target_pairs={{0,8},{4,12},{8,24},{12,28},{16,0},{20,4},{24,16},{28,20},{1,9},{5... | collective-permute-start | bytes 1241096 | tf_op jit(solution)/shard_map/ppermute | solution.py:436
  86.9 19.0 %collective-permute-start.26 = (bf16[128,2048]{1,0:T(8,128)(2,1)S(1)}, bf16[128,2048]{1,0:T(8,128)(2,1)S(1)}, u32[]{:S(2)}, u32[]{:S(2)}) collective-permute-start(bf16[128,2048]{1,0:T(8,128)(2,1)S(1)} %get-tuple-element.42), channel_id=1, source_target_pairs={{0,4},{4,0},{8,12},{12,8},{16,20},{20,16},{24,28},{28,24},{1,5},{5... | collective-permute-start | bytes 1572872 | tf_op jit(solution)/shard_map/ppermute | solution.py:385
  94.7 15.5 %collective-permute-start.25 = (s16[1616,128]{1,0:T(8,128)(2,1)S(1)}, s16[1616,128]{1,0:T(8,128)(2,1)S(1)}, u32[]{:S(2)}, u32[]{:S(2)}) collective-permute-start(s16[1616,128]{1,0:T(8,128)(2,1)S(1)} %get-tuple-element.41.rest_1_), channel_id=1, source_target_pairs={{0,8},{4,12},{8,24},{12,28},{16,0},{20,4},{24,16},{28,20},{1,9},{5... | collective-permute-start | bytes 1241096 | tf_op jit(solution)/shard_map/ppermute | solution.py:436
  97.2 21.5 %collective-permute-start.22 = (bf16[128,2048]{1,0:T(8,128)(2,1)S(1)}, bf16[128,2048]{1,0:T(8,128)(2,1)S(1)}, u32[]{:S(2)}, u32[]{:S(2)}) collective-permute-start(bf16[128,2048]{1,0:T(8,128)(2,1)S(1)} %get-tuple-element.39), channel_id=1, source_target_pairs={{0,4},{4,0},{8,12},{12,8},{16,20},{20,16},{24,28},{28,24},{1,5},{5... | collective-permute-start | bytes 1572872 | tf_op jit(solution)/shard_map/ppermute | solution.py:385
  103.3 15.4 %collective-permute-start.28 = (s16[1616,128]{1,0:T(8,128)(2,1)S(1)}, s16[1616,128]{1,0:T(8,128)(2,1)S(1)}, u32[]{:S(2)}, u32[]{:S(2)}) collective-permute-start(s16[1616,128]{1,0:T(8,128)(2,1)S(1)} %sum_step_10.1.rest_1_), channel_id=1, source_target_pairs={{0,8},{4,12},{8,24},{12,28},{16,0},{20,4},{24,16},{28,20},{1,9},{5... | collective-permute-start | bytes 1241096 | tf_op jit(solution)/shard_map/ppermute | solution.py:436
  112.2 11.0 %collective-permute-start.27 = (s16[1616,128]{1,0:T(8,128)(2,1)S(1)}, s16[1616,128]{1,0:T(8,128)(2,1)S(1)}, u32[]{:S(2)}, u32[]{:S(2)}) collective-permute-start(s16[1616,128]{1,0:T(8,128)(2,1)S(1)} %sum_step_11.1), channel_id=1, source_target_pairs={{0,8},{4,12},{8,24},{12,28},{16,0},{20,4},{24,16},{28,20},{1,9},{5... | collective-permute-start | bytes 1241096 | tf_op jit(solution)/shard_map/ppermute | solution.py:436

commit v7 on v6

--- a/solution.py
+++ b/solution.py
@@ -25,7 +25,7 @@
 SWAPS = {0: (2, 1), 1: (4, 2), 2: (6, 2), 5: (8, 2), 7: (10, 2), 8: (12, 2), 9: (14, 2)}
 SWAP_WAITS = {}
 RAW_STEP, RAW_WAIT = 2, 5
-INVERSE_STEP = 0
+INVERSE_STEPS = (0, 2)
 FINISHED_AHEAD = 1
 ME, PARTNER, NEAR, NEAR_PARTNER, INNER, FIXED = 0, 1, 2, 3, 4, 5
 LANES = 128
@@ -63,7 +63,7 @@
     return jnp.dot(left, right, precision=HIGHEST, preferred_element_type=F32)
 
 
-def inverse_kernel(counts_ref, pairs_ref, *rest):
+def inverse_kernel(first, counts_ref, pairs_ref, *rest):
     out_ref = rest[-1]
     runs = out_ref.shape[0]
     design = incidence(pairs_ref[0:1, :], pairs_ref[1:2, :], PAD)
@@ -74,7 +74,7 @@
     identity = (row == col).astype(F32)
     grams = []
     for run in range(runs):
-        kept = jnp.where(pair < counts_ref[run], design, 0.0).astype(jnp.bfloat16)
+        kept = jnp.where(pair < counts_ref[first + run], design, 0.0).astype(jnp.bfloat16)
         gram = lax.dot_general(kept, kept, contract_last, preferred_element_type=F32)
         grams.append(gram + DAMPING * identity)
     low = DAMPING
@@ -98,10 +98,10 @@
         out_ref[run] = guess
 
 
-def invert_classes(date_pairs, run_counts, after):
-    shape = (run_counts.shape[0], PAD, PAD)
+def invert_classes(first, runs, date_pairs, run_counts, after):
+    shape = (runs, PAD, PAD)
     return pl.pallas_call(
-        inverse_kernel,
+        functools.partial(inverse_kernel, first),
         out_shape=jax.ShapeDtypeStruct(shape, F32),
         grid_spec=pltpu.PrefetchScalarGridSpec(
             num_scalar_prefetch=1,
@@ -111,7 +111,7 @@
         ),
         compiler_params=pltpu.CompilerParams(vmem_limit_bytes=VMEM_BYTES),
         cost_estimate=LITTLE,
-        name="invert_classes_0",
+        name=f"invert_classes_{first}",
     )(run_counts, date_pairs, *after)
 
 
@@ -319,7 +319,7 @@
         pl.BlockSpec(pairs.shape, whole_block),
         pl.BlockSpec((local_pairs, piece), lambda i, t, c: (0, t[blocks + at])),
         pl.BlockSpec((local_pairs, piece), lambda i, t, c: (0, place_in)),
-        pl.BlockSpec((1, PAD, PAD), lambda i, t, c: (part // CUTS, 0, 0)),
+        pl.BlockSpec((1, PAD, PAD), lambda i, t, c: (0, 0, 0)),
     ]
     in_specs += [pl.BlockSpec(each.shape, whole_block) for each in [*raw, *arrived]]
     operands = [*scalars, pairs, phases, partner, inverse, *raw, *arrived]
@@ -409,12 +409,12 @@
     pairs = jnp.concatenate([lax.dynamic_slice(date_pairs, (0, (me ^ at) * local_pairs), (2, local_pairs)) for at in range(4)], axis=1)
     scalars = (row, counts)
 
-    received, sent, coded, series = {raw_part: [raw_own, raw_other]}, [raw_part], None, None
+    received, sent, coded, series, inverses = {raw_part: [raw_own, raw_other]}, [raw_part], None, None, []
 
     def finished(part, series, told):
         at = steps + part
         arrived = [received[place * parts + part][-1] for place in range(1 if part == raw_part else 0, line - 1)]
-        data = (layout, scalars, pairs, phases, partner_of[at], inverse, raw if part == raw_part else [], arrived)
+        data = (layout, scalars, pairs, phases, partner_of[at], inverses[part // CUTS], raw if part == raw_part else [], arrived)
         return finish(at, part, *data, series, told, owner_pixels, piece)
 
     for at in [each for each in range(steps) if each != raw_part]:
@@ -425,9 +425,10 @@
             after.append(partner_of[SWAP_WAITS[at]][0])
         if at == RAW_WAIT:
             after.append(raw[1])
-        if at == INVERSE_STEP:
-            inverse = invert_classes(date_pairs, run_counts, [counts if coded is None else coded])
-            after.append(inverse)
+        if at in INVERSE_STEPS:
+            run = len(inverses)
+            inverses.append(invert_classes(run, 1, date_pairs, run_counts, [counts if coded is None else coded]))
+            after.append(inverses[-1])
         if at == steps - 1:
             for part in range(FINISHED_AHEAD):
                 series, told = finished(part, series, True)
@@ -453,7 +454,7 @@
     run_counts = counts_of(None)
     outgoing = phases.reshape(local_pairs, owner_count, owner_pixels).transpose(1, 0, 2)
     received = lax.all_to_all(outgoing, "ifg", split_axis=0, concat_axis=0, tiled=True)
-    inverse = invert_classes(date_pairs, run_counts, [])
+    inverse = invert_classes(0, run_counts.shape[0], date_pairs, run_counts, [])
     return sum_solve(run_counts, date_pairs, received.reshape(-1, owner_pixels), inverse)
 
 

time: 129 us -> 130 us (level)
  Pallas kernels: 45.6 us -> 50.4 us
  waiting for transfers between devices: 20.1 us -> 17.3 us
    pallas_call x1 -> x2, Pallas kernels: 7.56 us -> 12.4 us  [invert_classes(): pl.pallas_call(functools.partial(inverse_kernel, first), out_shape=jax.Sh...]
    ppermute x15, waiting for transfers between devices: 18.5 us -> 14.2 us  [solve_by_sums(): lax.ppermute(coded, 'ifg', line_permutation(links))]
    ppermute x8, waiting for transfers between devices: 1.58 us -> 3.11 us  [swapped(): here = lax.ppermute(away, 'ifg', swap)]
  transfers between devices with their start and end apart: 29 -> 29, of which waited for: 9 -> 8; matrix products, arithmetic and copies ran while one was open for 2% -> 2% of each run, Pallas kernels for 33% -> 36%
where the time goes in v7:
time: 130 us; the launch traced here: 129 us
  starting transfers between devices  55.4 us (43%)
  Pallas kernels  50.4 us (39%)
  waiting for transfers between devices  17.3 us (13%)
  local copies, waits for them, and re-layouts  4.38 us (3%)
    ppermute x15, starting transfers between devices, solve_by_sums(): lax.ppermute(coded, 'ifg', line_permutation(links))  36.5 us
    pallas_call x11, Pallas kernels, step(): pl.pallas_call(functools.partial(step_kernel, at, layout, len(earlier), s...  23.3 us
    pallas_call x4, Pallas kernels, finish(): pl.pallas_call(functools.partial(finish_kernel, at, layout, HALVES, len(r...  14.8 us
    ppermute x15, waiting for transfers between devices, solve_by_sums(): lax.ppermute(coded, 'ifg', line_permutation(links))  14.2 us
    pallas_call x2, Pallas kernels, invert_classes(): pl.pallas_call(functools.partial(inverse_kernel, first), out_shape=jax.Sh...  12.4 us
    ppermute x8, starting transfers between devices, swapped(): here = lax.ppermute(away, 'ifg', swap)  8.63 us
    ppermute x3, starting transfers between devices, solve_by_sums(): counts.append(lax.ppermute(run_counts, 'ifg', line_permutation(links)))  6.11 us
    ppermute x8, waiting for transfers between devices, swapped(): here = lax.ppermute(away, 'ifg', swap)  3.11 us
  transfers between devices with their start and end apart: 29, of which 8 were waited for; matrix products, arithmetic and copies ran while one was open for 2% of the time, Pallas kernels for 36%

profile of v7, /device:TPU:0, one launch (start us, length us, event | category | flops | bytes accessed | tf_op | source)
XLA Modules:
  0.0 128.7 jit_solution(8809200764053664795)
XLA Ops:
  0.0 1.1 dynamic-slice_bitcast_fusion
  1.2 0.8 fusion.counts_ref
  2.1 5.1 %collective-permute-start.2 = (s32[2]{0:T(128)S(1)}, s32[2]{0:T(128)S(1)}, u32[]{:S(2)}, u32[]{:S(2)}) collective-permute-start(s32[2]{0:T(128)S(1)} %fusion.counts_ref), channel_id=1, source_target_pairs={{0,24},{4,28},{8,0},{12,4},{16,8},{20,12},{24,16},{28,20},{1,25},{... | collective-permute-start | bytes 32 | tf_op jit(solution)/shard_map/ppermute | solution.py:403
  7.2 1.0 collective-permute-start
  8.2 1.5 %collective-permute-start.3 = (bf16[128,2048]{1,0:T(8,128)(2,1)S(1)}, bf16[128,2048]{1,0:T(8,128)(2,1)S(1)}, u32[]{:S(2)}, u32[]{:S(2)}) collective-permute-start(bf16[128,2048]{1,0:T(8,128)(2,1)S(1)} %dynamic-slice_bitcast_fusion), channel_id=1, source_target_pairs={{0,4},{4,0},{8,12},{12,8},{16,20},{20,16},{24,28},{28,24},{1,5},{5... | collective-permute-start | bytes 1572872 | tf_op jit(solution)/shard_map/ppermute | solution.py:385
  9.7 1.1 dynamic-slice_bitcast_fusion.1
  10.7 2.5 %collective-permute-start.5 = (bf16[128,1024]{1,0:T(8,128)(2,1)S(1)}, bf16[128,1024]{1,0:T(8,128)(2,1)S(1)}, u32[]{:S(2)}, u32[]{:S(2)}) collective-permute-start(bf16[128,1024]{1,0:T(8,128)(2,1)S(1)} %get-tuple-element.45), channel_id=1, source_target_pairs={{0,8},{4,12},{8,0},{12,4},{16,24},{20,28},{24,16},{28,20},{1,9},{5... | collective-permute-start | bytes 786440 | tf_op jit(solution)/shard_map/ppermute | solution.py:407
  13.3 0.7 constant_dynamic-slice_fusion.3
  14.2 0.7 fusion.1.table
  14.9 0.7 copy-done.1
  15.6 6.5 %invert_classes_0.1.rest_1_.inverse_ref = f32[1,256,256]{2,1,0:T(8,128)S(1)} custom-call(s32[2]{0:T(128)S(1)} %fusion.counts_ref, s32[2,1024]{1,0:T(2,128)S(1)} %copy-done.1, s32[8]{0:T(128)S(1)} %pad_add_fusion.1.rest_0_.counts), custom_call_target="tpu_custom_call" | custom-call | flops 1024 | bytes 1024 | tf_op jit(solution)/shard_map/invert_classes_0/pallas_call | solution.py:103
  22.1 2.1 %sum_step_00.1 = (s16[1616,128]{1,0:T(8,128)(2,1)S(1)}, bf16[128,1024]{1,0:T(8,128)(2,1)S(1)}) custom-call(s32[53]{0:T(128)S(1)} %fusion.1.table, s32[8]{0:T(128)S(1)} %pad_add_fusion.1.rest_0_.counts, s32[2,512]{1,0:T(2,128)S(1)} %pad_add_fusion.pairs_ref, bf16[128,32768]{1,0:T(8,128)(2,1)} %bitcast.12, ...), custom_call_target="tpu_custom_call" | custom-call | flops 10000000000 | bytes 30000000 | tf_op jit(solution)/shard_map/sum_step_00/pallas_call | solution.py:245
  24.8 2.3 %collective-permute-start.8 = (s16[1616,128]{1,0:T(8,128)(2,1)S(1)}, s16[1616,128]{1,0:T(8,128)(2,1)S(1)}, u32[]{:S(2)}, u32[]{:S(2)}) collective-permute-start(s16[1616,128]{1,0:T(8,128)(2,1)S(1)} %get-tuple-element.26.rest_1_), channel_id=1, source_target_pairs={{0,8},{4,12},{8,0},{12,4},{16,24},{20,28},{24,16},{28,20},{1,9},{5... | collective-permute-start | bytes 1241096 | tf_op jit(solution)/shard_map/ppermute | solution.py:437
  27.1 2.2 %sum_step_01.1 = (s16[1616,128]{1,0:T(8,128)(2,1)S(1)}, bf16[128,2048]{1,0:T(8,128)(2,1)S(1)}) custom-call(s32[53]{0:T(128)S(1)} %fusion.1.table, s32[8]{0:T(128)S(1)} %pad_add_fusion.1.rest_0_.counts, s32[2,512]{1,0:T(2,128)S(1)} %pad_add_fusion.pairs_ref, bf16[128,32768]{1,0:T(8,128)(2,1)} %bitcast.14, ...), custom_call_target="tpu_custom_call" | custom-call | flops 10000000000 | bytes 30000000 | tf_op jit(solution)/shard_map/sum_step_01/pallas_call | solution.py:245
  29.3 5.8 %invert_classes_1.1.rest_3_.inverse_ref = f32[1,256,256]{2,1,0:T(8,128)S(1)} custom-call(s32[2]{0:T(128)S(1)} %fusion.counts_ref, s32[2,1024]{1,0:T(2,128)S(1)} %copy-done.2, s16[1616,128]{1,0:T(8,128)(2,1)S(1)} %get-tuple-element.30.rest_0_.rest_1_), custom_call_target="tpu_custom_call" | custom-call | flops 1024 | bytes 1024 | tf_op jit(solution)/shard_map/invert_classes_1/pallas_call | solution.py:103
  35.1 0.8 collective-permute-start.7
  36.4 2.2 %sum_step_02.1 = (s16[1616,128]{1,0:T(8,128)(2,1)S(1)}, bf16[128,2048]{1,0:T(8,128)(2,1)S(1)}) custom-call(s32[53]{0:T(128)S(1)} %fusion.1.table, s32[8]{0:T(128)S(1)} %pad_add_fusion.1.rest_0_.counts, s32[2,512]{1,0:T(2,128)S(1)} %pad_add_fusion.pairs_ref, bf16[128,32768]{1,0:T(8,128)(2,1)} %bitcast.16, ...), custom_call_target="tpu_custom_call" | custom-call | flops 10000000000 | bytes 30000000 | tf_op jit(solution)/shard_map/sum_step_02/pallas_call | solution.py:245
  38.6 1.4 %collective-permute-start.10 = (s16[1616,128]{1,0:T(8,128)(2,1)S(1)}, s16[1616,128]{1,0:T(8,128)(2,1)S(1)}, u32[]{:S(2)}, u32[]{:S(2)}) collective-permute-start(s16[1616,128]{1,0:T(8,128)(2,1)S(1)} %get-tuple-element.32.rest_1_), channel_id=1, source_target_pairs={{0,8},{4,12},{8,0},{12,4},{16,24},{20,28},{24,16},{28,20},{1,9},{5... | collective-permute-start | bytes 1241096 | tf_op jit(solution)/shard_map/ppermute | solution.py:437
  40.0 1.5 %collective-permute-start.11 = (bf16[128,1024]{1,0:T(8,128)(2,1)S(1)}, bf16[128,1024]{1,0:T(8,128)(2,1)S(1)}, u32[]{:S(2)}, u32[]{:S(2)}) collective-permute-start(bf16[128,1024]{1,0:T(8,128)(2,1)S(1)} %collective-permute-done.5.rest_3_), channel_id=1, source_target_pairs={{0,4},{4,0},{8,12},{12,8},{16,20},{20,16},{24,28},{28,24},{1,5},{5... | collective-permute-start | bytes 786440 | tf_op jit(solution)/shard_map/ppermute | solution.py:443
  42.0 5.6 %collective-permute-done.7.rest_2_.rest_1_.rest_0_ = s16[1616,128]{1,0:T(8,128)(2,1)S(1)} collective-permute-done((s16[1616,128]{1,0:T(8,128)(2,1)S(1)}, s16[1616,128]{1,0:T(8,128)(2,1)S(1)}, u32[]{:S(2)}, u32[]{:S(2)}) %collective-permute-start.7) | collective-permute-done | bytes 413728 | tf_op jit(solution)/shard_map/ppermute | solution.py:437
  47.7 3.1 %collective-permute-done.6.partner_ref = bf16[128,2048]{1,0:T(8,128)(2,1)S(1)} collective-permute-done((bf16[128,2048]{1,0:T(8,128)(2,1)S(1)}, bf16[128,2048]{1,0:T(8,128)(2,1)S(1)}, u32[]{:S(2)}, u32[]{:S(2)}) %collective-permute-start.6) | collective-permute-done | bytes 524320 | tf_op jit(solution)/shard_map/ppermute | solution.py:385
  50.8 2.0 %sum_step_04.1.rest_2_ = s16[1616,128]{1,0:T(8,128)(2,1)S(1)} custom-call(s32[53]{0:T(128)S(1)} %fusion.1.table, s32[8]{0:T(128)S(1)} %pad_add_fusion.1.rest_0_.counts, s32[2,512]{1,0:T(2,128)S(1)} %pad_add_fusion.pairs_ref, bf16[128,32768]{1,0:T(8,128)(2,1)} %bitcast.18, bf16[128,2048]{1,0:T(8,128)(2,1)S(1)} %collective-permute-done.6.partner_ref, ...), custom_call_target="tpu_custom_call" | custom-call | flops 10000000000 | bytes 30000000 | tf_op jit(solution)/shard_map/sum_step_04/pallas_call | solution.py:245
  53.5 5.4 %collective-permute-start.14 = (s16[1616,128]{1,0:T(8,128)(2,1)S(1)}, s16[1616,128]{1,0:T(8,128)(2,1)S(1)}, u32[]{:S(2)}, u32[]{:S(2)}) collective-permute-start(s16[1616,128]{1,0:T(8,128)(2,1)S(1)} %sum_step_04.1.rest_2_), channel_id=1, source_target_pairs={{0,8},{4,12},{24,16},{28,20},{1,9},{5,13},{25,17},{29,21},{2,10},{... | collective-permute-start | bytes 1241096 | tf_op jit(solution)/shard_map/ppermute | solution.py:437
  58.9 2.2 %sum_step_05.1 = (s16[1616,128]{1,0:T(8,128)(2,1)S(1)}, bf16[128,2048]{1,0:T(8,128)(2,1)S(1)}) custom-call(s32[53]{0:T(128)S(1)} %fusion.1.table, s32[8]{0:T(128)S(1)} %pad_add_fusion.1.rest_0_.counts, s32[2,512]{1,0:T(2,128)S(1)} %pad_add_fusion.pairs_ref, bf16[128,32768]{1,0:T(8,128)(2,1)} %bitcast.19, ...), custom_call_target="tpu_custom_call" | custom-call | flops 10000000000 | bytes 30000000 | tf_op jit(solution)/shard_map/sum_step_05/pallas_call | solution.py:245
  61.9 3.6 %collective-permute-start.13 = (s16[1616,128]{1,0:T(8,128)(2,1)S(1)}, s16[1616,128]{1,0:T(8,128)(2,1)S(1)}, u32[]{:S(2)}, u32[]{:S(2)}) collective-permute-start(s16[1616,128]{1,0:T(8,128)(2,1)S(1)} %get-tuple-element.35.rest_1_), channel_id=1, source_target_pairs={{0,8},{4,12},{24,16},{28,20},{1,9},{5,13},{25,17},{29,21},{2,10},{... | collective-permute-start | bytes 1241096 | tf_op jit(solution)/shard_map/ppermute | solution.py:437
  66.6 2.0 %sum_step_06.1.rest_3_ = s16[1616,128]{1,0:T(8,128)(2,1)S(1)} custom-call(s32[53]{0:T(128)S(1)} %fusion.1.table, s32[8]{0:T(128)S(1)} %pad_add_fusion.1.rest_0_.counts, s32[2,512]{1,0:T(2,128)S(1)} %pad_add_fusion.pairs_ref, bf16[128,32768]{1,0:T(8,128)(2,1)} %bitcast.21, bf16[128,2048]{1,0:T(8,128)(2,1)S(1)} %collective-permute-done.15.partner_ref, ...), custom_call_target="tpu_custom_call" | custom-call | flops 10000000000 | bytes 30000000 | tf_op jit(solution)/shard_map/sum_step_06/pallas_call | solution.py:245
  69.3 6.7 %collective-permute-start.18 = (s16[1616,128]{1,0:T(8,128)(2,1)S(1)}, s16[1616,128]{1,0:T(8,128)(2,1)S(1)}, u32[]{:S(2)}, u32[]{:S(2)}) collective-permute-start(s16[1616,128]{1,0:T(8,128)(2,1)S(1)} %sum_step_06.1.rest_3_), channel_id=1, source_target_pairs={{0,8},{4,12},{24,16},{28,20},{1,9},{5,13},{25,17},{29,21},{2,10},{... | collective-permute-start | bytes 1241096 | tf_op jit(solution)/shard_map/ppermute | solution.py:437
  76.1 2.2 %sum_step_07.1 = (s16[1616,128]{1,0:T(8,128)(2,1)S(1)}, bf16[128,2048]{1,0:T(8,128)(2,1)S(1)}) custom-call(s32[53]{0:T(128)S(1)} %fusion.1.table, s32[8]{0:T(128)S(1)} %pad_add_fusion.1.rest_0_.counts, s32[2,512]{1,0:T(2,128)S(1)} %pad_add_fusion.pairs_ref, bf16[128,32768]{1,0:T(8,128)(2,1)} %bitcast.22, ...), custom_call_target="tpu_custom_call" | custom-call | flops 10000000000 | bytes 30000000 | tf_op jit(solution)/shard_map/sum_step_07/pallas_call | solution.py:245
  78.3 0.7 collective-permute-start.21
  79.0 3.4 %collective-permute-start.20 = (s16[1616,128]{1,0:T(8,128)(2,1)S(1)}, s16[1616,128]{1,0:T(8,128)(2,1)S(1)}, u32[]{:S(2)}, u32[]{:S(2)}) collective-permute-start(s16[1616,128]{1,0:T(8,128)(2,1)S(1)} %get-tuple-element.37.rest_2_), channel_id=1, source_target_pairs={{0,8},{4,12},{24,16},{28,20},{1,9},{5,13},{25,17},{29,21},{2,10},{... | collective-permute-start | bytes 1241096 | tf_op jit(solution)/shard_map/ppermute | solution.py:437
  82.5 2.2 %collective-permute-start.23 = (bf16[128,2048]{1,0:T(8,128)(2,1)S(1)}, bf16[128,2048]{1,0:T(8,128)(2,1)S(1)}, u32[]{:S(2)}, u32[]{:S(2)}) collective-permute-start(bf16[128,2048]{1,0:T(8,128)(2,1)S(1)} %get-tuple-element.40), channel_id=1, source_target_pairs={{0,4},{4,0},{8,12},{12,8},{16,20},{20,16},{24,28},{28,24},{1,5},{5... | collective-permute-start | bytes 1572872 | tf_op jit(solution)/shard_map/ppermute | solution.py:385
  84.7 1.3 collective-permute-done.18.rest_3_.rest_0_
  86.0 2.2 %sum_step_08.1 = (s16[1616,128]{1,0:T(8,128)(2,1)S(1)}, bf16[128,2048]{1,0:T(8,128)(2,1)S(1)}) custom-call(s32[53]{0:T(128)S(1)} %fusion.1.table, s32[8]{0:T(128)S(1)} %pad_add_fusion.1.rest_0_.counts, s32[2,512]{1,0:T(2,128)S(1)} %pad_add_fusion.pairs_ref, bf16[128,32768]{1,0:T(8,128)(2,1)} %bitcast.24, ...), custom_call_target="tpu_custom_call" | custom-call | flops 10000000000 | bytes 30000000 | tf_op jit(solution)/shard_map/sum_step_08/pallas_call | solution.py:245
  88.2 2.5 %collective-permute-start.24 = (s16[1616,128]{1,0:T(8,128)(2,1)S(1)}, s16[1616,128]{1,0:T(8,128)(2,1)S(1)}, u32[]{:S(2)}, u32[]{:S(2)}) collective-permute-start(s16[1616,128]{1,0:T(8,128)(2,1)S(1)} %get-tuple-element.38.rest_2_), channel_id=1, source_target_pairs={{0,8},{4,12},{8,24},{12,28},{16,0},{20,4},{24,16},{28,20},{1,9},{5... | collective-permute-start | bytes 1241096 | tf_op jit(solution)/shard_map/ppermute | solution.py:437
  90.7 1.3 %collective-permute-start.26 = (bf16[128,2048]{1,0:T(8,128)(2,1)S(1)}, bf16[128,2048]{1,0:T(8,128)(2,1)S(1)}, u32[]{:S(2)}, u32[]{:S(2)}) collective-permute-start(bf16[128,2048]{1,0:T(8,128)(2,1)S(1)} %get-tuple-element.42), channel_id=1, source_target_pairs={{0,4},{4,0},{8,12},{12,8},{16,20},{20,16},{24,28},{28,24},{1,5},{5... | collective-permute-start | bytes 1572872 | tf_op jit(solution)/shard_map/ppermute | solution.py:385
  92.0 2.8 %collective-permute-done.20.rest_3_.rest_0_ = s16[1616,128]{1,0:T(8,128)(2,1)S(1)} collective-permute-done((s16[1616,128]{1,0:T(8,128)(2,1)S(1)}, s16[1616,128]{1,0:T(8,128)(2,1)S(1)}, u32[]{:S(2)}, u32[]{:S(2)}) %collective-permute-start.20) | collective-permute-done | bytes 413728 | tf_op jit(solution)/shard_map/ppermute | solution.py:437
  94.8 2.2 %sum_step_09.1 = (s16[1616,128]{1,0:T(8,128)(2,1)S(1)}, bf16[128,2048]{1,0:T(8,128)(2,1)S(1)}) custom-call(s32[53]{0:T(128)S(1)} %fusion.1.table, s32[8]{0:T(128)S(1)} %pad_add_fusion.1.rest_0_.counts, s32[2,512]{1,0:T(2,128)S(1)} %pad_add_fusion.pairs_ref, bf16[128,32768]{1,0:T(8,128)(2,1)} %bitcast.26, ...), custom_call_target="tpu_custom_call" | custom-call | flops 10000000000 | bytes 30000000 | tf_op jit(solution)/shard_map/sum_step_09/pallas_call | solution.py:245
  97.0 2.5 %collective-permute-start.25 = (s16[1616,128]{1,0:T(8,128)(2,1)S(1)}, s16[1616,128]{1,0:T(8,128)(2,1)S(1)}, u32[]{:S(2)}, u32[]{:S(2)}) collective-permute-start(s16[1616,128]{1,0:T(8,128)(2,1)S(1)} %get-tuple-element.41.rest_1_), channel_id=1, source_target_pairs={{0,8},{4,12},{8,24},{12,28},{16,0},{20,4},{24,16},{28,20},{1,9},{5... | collective-permute-start | bytes 1241096 | tf_op jit(solution)/shard_map/ppermute | solution.py:437
  99.6 1.3 %collective-permute-start.22 = (bf16[128,2048]{1,0:T(8,128)(2,1)S(1)}, bf16[128,2048]{1,0:T(8,128)(2,1)S(1)}, u32[]{:S(2)}, u32[]{:S(2)}) collective-permute-start(bf16[128,2048]{1,0:T(8,128)(2,1)S(1)} %get-tuple-element.39), channel_id=1, source_target_pairs={{0,4},{4,0},{8,12},{12,8},{16,20},{20,16},{24,28},{28,24},{1,5},{5... | collective-permute-start | bytes 1572872 | tf_op jit(solution)/shard_map/ppermute | solution.py:385
  100.9 2.8 %collective-permute-done.24.rest_2_ = s16[1616,128]{1,0:T(8,128)(2,1)S(1)} collective-permute-done((s16[1616,128]{1,0:T(8,128)(2,1)S(1)}, s16[1616,128]{1,0:T(8,128)(2,1)S(1)}, u32[]{:S(2)}, u32[]{:S(2)}) %collective-permute-start.24) | collective-permute-done | bytes 413728 | tf_op jit(solution)/shard_map/ppermute | solution.py:437
  103.7 2.0 %sum_step_10.1.rest_1_ = s16[1616,128]{1,0:T(8,128)(2,1)S(1)} custom-call(s32[53]{0:T(128)S(1)} %fusion.1.table, s32[8]{0:T(128)S(1)} %pad_add_fusion.1.rest_0_.counts, s32[2,512]{1,0:T(2,128)S(1)} %pad_add_fusion.pairs_ref, bf16[128,32768]{1,0:T(8,128)(2,1)} %bitcast.28, bf16[128,2048]{1,0:T(8,128)(2,1)S(1)} %collective-permute-done.23.partner_ref, ...), custom_call_target="tpu_custom_call" | custom-call | flops 10000000000 | bytes 30000000 | tf_op jit(solution)/shard_map/sum_step_10/pallas_call | solution.py:245
  105.7 2.5 %collective-permute-start.28 = (s16[1616,128]{1,0:T(8,128)(2,1)S(1)}, s16[1616,128]{1,0:T(8,128)(2,1)S(1)}, u32[]{:S(2)}, u32[]{:S(2)}) collective-permute-start(s16[1616,128]{1,0:T(8,128)(2,1)S(1)} %sum_step_10.1.rest_1_), channel_id=1, source_target_pairs={{0,8},{4,12},{8,24},{12,28},{16,0},{20,4},{24,16},{28,20},{1,9},{5... | collective-permute-start | bytes 1241096 | tf_op jit(solution)/shard_map/ppermute | solution.py:437
  108.2 3.8 %finish_0.1 = (f32[200,4096]{1,0:T(8,128)}, f32[8,128]{1,0:T(8,128)S(1)}) custom-call(s32[53]{0:T(128)S(1)} %fusion.1.table, s32[8]{0:T(128)S(1)} %pad_add_fusion.1.rest_0_.counts, s32[2,512]{1,0:T(2,128)S(1)} %pad_add_fusion.pairs_ref, bf16[128,32768]{1,0:T(8,128)(2,1)} %bitcast.29, bf16[128,2048]{1,0:T(8,128)(2,1)S(1)} %collective-permute-done.26.partner_ref, ...), custom_call_target="tpu_custom_call" | custom-call | flops 1024 | bytes 1024 | tf_op jit(solution)/shard_map/finish_0/pallas_call | solution.py:336
  112.6 2.0 %sum_step_11.1 = s16[1616,128]{1,0:T(8,128)(2,1)S(1)} custom-call(s32[53]{0:T(128)S(1)} %fusion.1.table, s32[8]{0:T(128)S(1)} %pad_add_fusion.1.rest_0_.counts, s32[2,512]{1,0:T(2,128)S(1)} %pad_add_fusion.pairs_ref, bf16[128,32768]{1,0:T(8,128)(2,1)} %bitcast.30, bf16[128,2048]{1,0:T(8,128)(2,1)S(1)} %collective-permute-done.23.partner_ref, ...), custom_call_target="tpu_custom_call" | custom-call | flops 10000000000 | bytes 30000000 | tf_op jit(solution)/shard_map/sum_step_11/pallas_call | solution.py:245
  114.6 2.5 %collective-permute-start.27 = (s16[1616,128]{1,0:T(8,128)(2,1)S(1)}, s16[1616,128]{1,0:T(8,128)(2,1)S(1)}, u32[]{:S(2)}, u32[]{:S(2)}) collective-permute-start(s16[1616,128]{1,0:T(8,128)(2,1)S(1)} %sum_step_11.1), channel_id=1, source_target_pairs={{0,8},{4,12},{8,24},{12,28},{16,0},{20,4},{24,16},{28,20},{1,9},{5... | collective-permute-start | bytes 1241096 | tf_op jit(solution)/shard_map/ppermute | solution.py:437
  117.1 3.6 %finish_1.1.rest_3_ = f32[200,4096]{1,0:T(8,128)} custom-call(s32[53]{0:T(128)S(1)} %fusion.1.table, s32[8]{0:T(128)S(1)} %pad_add_fusion.1.rest_0_.counts, s32[2,512]{1,0:T(2,128)S(1)} %pad_add_fusion.pairs_ref, bf16[128,32768]{1,0:T(8,128)(2,1)} %bitcast.31, ...), custom_call_target="tpu_custom_call", output_to_operand_aliasing={{}: (9, {})} | custom-call | flops 1024 | bytes 1024 | tf_op jit(solution)/shard_map/finish_1/pallas_call | solution.py:336
  120.7 3.6 %finish_2.1.rest_4_ = f32[200,4096]{1,0:T(8,128)} custom-call(s32[53]{0:T(128)S(1)} %fusion.1.table, s32[8]{0:T(128)S(1)} %pad_add_fusion.1.rest_0_.counts, s32[2,512]{1,0:T(2,128)S(1)} %pad_add_fusion.pairs_ref, bf16[128,32768]{1,0:T(8,128)(2,1)} %bitcast.32, ...), custom_call_target="tpu_custom_call", output_to_operand_aliasing={{}: (9, {})} | custom-call | flops 1024 | bytes 1024 | tf_op jit(solution)/shard_map/finish_2/pallas_call | solution.py:336
  124.8 3.8 %finish_3.1 = f32[200,4096]{1,0:T(8,128)} custom-call(s32[53]{0:T(128)S(1)} %fusion.1.table, s32[8]{0:T(128)S(1)} %pad_add_fusion.1.rest_0_.counts, s32[2,512]{1,0:T(2,128)S(1)} %pad_add_fusion.pairs_ref, bf16[128,32768]{1,0:T(8,128)(2,1)} %bitcast.33, bf16[128,2048]{1,0:T(8,128)(2,1)S(1)} %collective-permute-done.22.partner_ref, ...), custom_call_target="tpu_custom_call", output_to_operand_aliasing={{}: (10, {})} | custom-call | flops 1024 | bytes 1024 | tf_op jit(solution)/shard_map/finish_3/pallas_call | solution.py:336
  (42 shorter events, 6.4 us)
Async XLA Ops:
  0.0 1.1 copy-start
  2.1 11.9 %collective-permute-start.2 = (s32[2]{0:T(128)S(1)}, s32[2]{0:T(128)S(1)}, u32[]{:S(2)}, u32[]{:S(2)}) collective-permute-start(s32[2]{0:T(128)S(1)} %fusion.counts_ref), channel_id=1, source_target_pairs={{0,24},{4,28},{8,0},{12,4},{16,8},{20,12},{24,16},{28,20},{1,25},{... | collective-permute-start | bytes 32 | tf_op jit(solution)/shard_map/ppermute | solution.py:403
  7.1 7.0 %collective-permute-start.1 = (s32[2]{0:T(128)S(1)}, s32[2]{0:T(128)S(1)}, u32[]{:S(2)}, u32[]{:S(2)}) collective-permute-start(s32[2]{0:T(128)S(1)} %fusion.counts_ref), channel_id=1, source_target_pairs={{0,16},{4,20},{8,24},{12,28},{16,0},{20,4},{24,8},{28,12},{1,17},{... | collective-permute-start | bytes 32 | tf_op jit(solution)/shard_map/ppermute | solution.py:403
  7.2 7.0 %collective-permute-start = (s32[2]{0:T(128)S(1)}, s32[2]{0:T(128)S(1)}, u32[]{:S(2)}, u32[]{:S(2)}) collective-permute-start(s32[2]{0:T(128)S(1)} %fusion.counts_ref), channel_id=1, source_target_pairs={{0,8},{4,12},{8,16},{12,20},{16,24},{20,28},{24,0},{28,4},{1,9},{5... | collective-permute-start | bytes 32 | tf_op jit(solution)/shard_map/ppermute | solution.py:403
  8.2 14.0 %collective-permute-start.3 = (bf16[128,2048]{1,0:T(8,128)(2,1)S(1)}, bf16[128,2048]{1,0:T(8,128)(2,1)S(1)}, u32[]{:S(2)}, u32[]{:S(2)}) collective-permute-start(bf16[128,2048]{1,0:T(8,128)(2,1)S(1)} %dynamic-slice_bitcast_fusion), channel_id=1, source_target_pairs={{0,4},{4,0},{8,12},{12,8},{16,20},{20,16},{24,28},{28,24},{1,5},{5... | collective-permute-start | bytes 1572872 | tf_op jit(solution)/shard_map/ppermute | solution.py:385
  10.7 16.4 %collective-permute-start.5 = (bf16[128,1024]{1,0:T(8,128)(2,1)S(1)}, bf16[128,1024]{1,0:T(8,128)(2,1)S(1)}, u32[]{:S(2)}, u32[]{:S(2)}) collective-permute-start(bf16[128,1024]{1,0:T(8,128)(2,1)S(1)} %get-tuple-element.45), channel_id=1, source_target_pairs={{0,8},{4,12},{8,0},{12,4},{16,24},{20,28},{24,16},{28,20},{1,9},{5... | collective-permute-start | bytes 786440 | tf_op jit(solution)/shard_map/ppermute | solution.py:407
  14.0 13.1 %collective-permute-start.4 = (bf16[128,1024]{1,0:T(8,128)(2,1)S(1)}, bf16[128,1024]{1,0:T(8,128)(2,1)S(1)}, u32[]{:S(2)}, u32[]{:S(2)}) collective-permute-start(bf16[128,1024]{1,0:T(8,128)(2,1)S(1)} %get-tuple-element.46), channel_id=1, source_target_pairs={{0,8},{4,12},{8,0},{12,4},{16,24},{20,28},{24,16},{28,20},{1,9},{5... | collective-permute-start | bytes 786440 | tf_op jit(solution)/shard_map/ppermute | solution.py:408
  14.9 0.7 copy-start.1
  24.2 12.2 %collective-permute-start.9 = (bf16[128,1024]{1,0:T(8,128)(2,1)S(1)}, bf16[128,1024]{1,0:T(8,128)(2,1)S(1)}, u32[]{:S(2)}, u32[]{:S(2)}) collective-permute-start(bf16[128,1024]{1,0:T(8,128)(2,1)S(1)} %get-tuple-element.31), channel_id=1, source_target_pairs={{0,4},{4,0},{8,12},{12,8},{16,20},{20,16},{24,28},{28,24},{1,5},{5... | collective-permute-start | bytes 786440 | tf_op jit(solution)/shard_map/ppermute | solution.py:385
  24.8 4.5 %copy-start.2 = (s32[2,1024]{1,0:T(2,128)S(1)}, s32[2,1024]{1,0:T(2,128)}, u32[]{:S(2)}) copy-start(s32[2,1024]{1,0:T(2,128)} %pairs_ref.3) | copy-start | bytes 24580
  24.8 11.6 %collective-permute-start.8 = (s16[1616,128]{1,0:T(8,128)(2,1)S(1)}, s16[1616,128]{1,0:T(8,128)(2,1)S(1)}, u32[]{:S(2)}, u32[]{:S(2)}) collective-permute-start(s16[1616,128]{1,0:T(8,128)(2,1)S(1)} %get-tuple-element.26.rest_1_), channel_id=1, source_target_pairs={{0,8},{4,12},{8,0},{12,4},{16,24},{20,28},{24,16},{28,20},{1,9},{5... | collective-permute-start | bytes 1241096 | tf_op jit(solution)/shard_map/ppermute | solution.py:437
  35.1 12.6 %collective-permute-start.7 = (s16[1616,128]{1,0:T(8,128)(2,1)S(1)}, s16[1616,128]{1,0:T(8,128)(2,1)S(1)}, u32[]{:S(2)}, u32[]{:S(2)}) collective-permute-start(s16[1616,128]{1,0:T(8,128)(2,1)S(1)} %get-tuple-element.30.rest_0_.rest_1_), channel_id=1, source_target_pairs={{0,8},{4,12},{8,0},{12,4},{16,24},{20,28},{24,16},{28,20},{1,9},{5... | collective-permute-start | bytes 1241096 | tf_op jit(solution)/shard_map/ppermute | solution.py:437
  35.9 14.9 %collective-permute-start.6 = (bf16[128,2048]{1,0:T(8,128)(2,1)S(1)}, bf16[128,2048]{1,0:T(8,128)(2,1)S(1)}, u32[]{:S(2)}, u32[]{:S(2)}) collective-permute-start(bf16[128,2048]{1,0:T(8,128)(2,1)S(1)} %get-tuple-element.29), channel_id=1, source_target_pairs={{0,4},{4,0},{8,12},{12,8},{16,20},{20,16},{24,28},{28,24},{1,5},{5... | collective-permute-start | bytes 1572872 | tf_op jit(solution)/shard_map/ppermute | solution.py:385
  38.6 20.3 %collective-permute-start.10 = (s16[1616,128]{1,0:T(8,128)(2,1)S(1)}, s16[1616,128]{1,0:T(8,128)(2,1)S(1)}, u32[]{:S(2)}, u32[]{:S(2)}) collective-permute-start(s16[1616,128]{1,0:T(8,128)(2,1)S(1)} %get-tuple-element.32.rest_1_), channel_id=1, source_target_pairs={{0,8},{4,12},{8,0},{12,4},{16,24},{20,28},{24,16},{28,20},{1,9},{5... | collective-permute-start | bytes 1241096 | tf_op jit(solution)/shard_map/ppermute | solution.py:437
  40.0 18.9 %collective-permute-start.11 = (bf16[128,1024]{1,0:T(8,128)(2,1)S(1)}, bf16[128,1024]{1,0:T(8,128)(2,1)S(1)}, u32[]{:S(2)}, u32[]{:S(2)}) collective-permute-start(bf16[128,1024]{1,0:T(8,128)(2,1)S(1)} %collective-permute-done.5.rest_3_), channel_id=1, source_target_pairs={{0,4},{4,0},{8,12},{12,8},{16,20},{20,16},{24,28},{28,24},{1,5},{5... | collective-permute-start | bytes 786440 | tf_op jit(solution)/shard_map/ppermute | solution.py:443
  41.5 23.9 %collective-permute-start.15 = (bf16[128,2048]{1,0:T(8,128)(2,1)S(1)}, bf16[128,2048]{1,0:T(8,128)(2,1)S(1)}, u32[]{:S(2)}, u32[]{:S(2)}) collective-permute-start(bf16[128,2048]{1,0:T(8,128)(2,1)S(1)} %get-tuple-element.36), channel_id=1, source_target_pairs={{0,4},{4,0},{8,12},{12,8},{16,20},{20,16},{24,28},{28,24},{1,5},{5... | collective-permute-start | bytes 1572872 | tf_op jit(solution)/shard_map/ppermute | solution.py:385
  52.8 13.3 %collective-permute-start.16 = (s16[1616,128]{1,0:T(8,128)(2,1)S(1)}, s16[1616,128]{1,0:T(8,128)(2,1)S(1)}, u32[]{:S(2)}, u32[]{:S(2)}) collective-permute-start(s16[1616,128]{1,0:T(8,128)(2,1)S(1)} %sum_step_04.1.rest_2_), channel_id=1, source_target_pairs={{8,16},{12,20},{16,8},{20,12},{9,17},{13,21},{17,9},{21,13},{10,18... | collective-permute-start | bytes 1241096 | tf_op jit(solution)/shard_map/ppermute | solution.py:437
  53.5 13.1 %collective-permute-start.14 = (s16[1616,128]{1,0:T(8,128)(2,1)S(1)}, s16[1616,128]{1,0:T(8,128)(2,1)S(1)}, u32[]{:S(2)}, u32[]{:S(2)}) collective-permute-start(s16[1616,128]{1,0:T(8,128)(2,1)S(1)} %sum_step_04.1.rest_2_), channel_id=1, source_target_pairs={{0,8},{4,12},{24,16},{28,20},{1,9},{5,13},{25,17},{29,21},{2,10},{... | collective-permute-start | bytes 1241096 | tf_op jit(solution)/shard_map/ppermute | solution.py:437
  61.2 14.9 %collective-permute-start.17 = (s16[1616,128]{1,0:T(8,128)(2,1)S(1)}, s16[1616,128]{1,0:T(8,128)(2,1)S(1)}, u32[]{:S(2)}, u32[]{:S(2)}) collective-permute-start(s16[1616,128]{1,0:T(8,128)(2,1)S(1)} %get-tuple-element.35.rest_1_), channel_id=1, source_target_pairs={{8,16},{12,20},{16,8},{20,12},{9,17},{13,21},{17,9},{21,13},{10,18... | collective-permute-start | bytes 1241096 | tf_op jit(solution)/shard_map/ppermute | solution.py:437
  61.9 14.2 %collective-permute-start.13 = (s16[1616,128]{1,0:T(8,128)(2,1)S(1)}, s16[1616,128]{1,0:T(8,128)(2,1)S(1)}, u32[]{:S(2)}, u32[]{:S(2)}) collective-permute-start(s16[1616,128]{1,0:T(8,128)(2,1)S(1)} %get-tuple-element.35.rest_1_), channel_id=1, source_target_pairs={{0,8},{4,12},{24,16},{28,20},{1,9},{5,13},{25,17},{29,21},{2,10},{... | collective-permute-start | bytes 1241096 | tf_op jit(solution)/shard_map/ppermute | solution.py:437
  65.4 20.5 %collective-permute-start.12 = (bf16[128,2048]{1,0:T(8,128)(2,1)S(1)}, bf16[128,2048]{1,0:T(8,128)(2,1)S(1)}, u32[]{:S(2)}, u32[]{:S(2)}) collective-permute-start(bf16[128,2048]{1,0:T(8,128)(2,1)S(1)} %get-tuple-element.34), channel_id=1, source_target_pairs={{0,4},{4,0},{8,12},{12,8},{16,20},{20,16},{24,28},{28,24},{1,5},{5... | collective-permute-start | bytes 1572872 | tf_op jit(solution)/shard_map/ppermute | solution.py:385
  68.6 13.9 %collective-permute-start.19 = (s16[1616,128]{1,0:T(8,128)(2,1)S(1)}, s16[1616,128]{1,0:T(8,128)(2,1)S(1)}, u32[]{:S(2)}, u32[]{:S(2)}) collective-permute-start(s16[1616,128]{1,0:T(8,128)(2,1)S(1)} %sum_step_06.1.rest_3_), channel_id=1, source_target_pairs={{8,16},{12,20},{16,8},{20,12},{9,17},{13,21},{17,9},{21,13},{10,18... | collective-permute-start | bytes 1241096 | tf_op jit(solution)/shard_map/ppermute | solution.py:437
  69.3 16.6 %collective-permute-start.18 = (s16[1616,128]{1,0:T(8,128)(2,1)S(1)}, s16[1616,128]{1,0:T(8,128)(2,1)S(1)}, u32[]{:S(2)}, u32[]{:S(2)}) collective-permute-start(s16[1616,128]{1,0:T(8,128)(2,1)S(1)} %sum_step_06.1.rest_3_), channel_id=1, source_target_pairs={{0,8},{4,12},{24,16},{28,20},{1,9},{5,13},{25,17},{29,21},{2,10},{... | collective-permute-start | bytes 1241096 | tf_op jit(solution)/shard_map/ppermute | solution.py:437
  78.3 13.7 %collective-permute-start.21 = (s16[1616,128]{1,0:T(8,128)(2,1)S(1)}, s16[1616,128]{1,0:T(8,128)(2,1)S(1)}, u32[]{:S(2)}, u32[]{:S(2)}) collective-permute-start(s16[1616,128]{1,0:T(8,128)(2,1)S(1)} %get-tuple-element.37.rest_2_), channel_id=1, source_target_pairs={{8,16},{12,20},{16,8},{20,12},{9,17},{13,21},{17,9},{21,13},{10,18... | collective-permute-start | bytes 1241096 | tf_op jit(solution)/shard_map/ppermute | solution.py:437
  79.0 15.8 %collective-permute-start.20 = (s16[1616,128]{1,0:T(8,128)(2,1)S(1)}, s16[1616,128]{1,0:T(8,128)(2,1)S(1)}, u32[]{:S(2)}, u32[]{:S(2)}) collective-permute-start(s16[1616,128]{1,0:T(8,128)(2,1)S(1)} %get-tuple-element.37.rest_2_), channel_id=1, source_target_pairs={{0,8},{4,12},{24,16},{28,20},{1,9},{5,13},{25,17},{29,21},{2,10},{... | collective-permute-start | bytes 1241096 | tf_op jit(solution)/shard_map/ppermute | solution.py:437
  82.5 18.4 %collective-permute-start.23 = (bf16[128,2048]{1,0:T(8,128)(2,1)S(1)}, bf16[128,2048]{1,0:T(8,128)(2,1)S(1)}, u32[]{:S(2)}, u32[]{:S(2)}) collective-permute-start(bf16[128,2048]{1,0:T(8,128)(2,1)S(1)} %get-tuple-element.40), channel_id=1, source_target_pairs={{0,4},{4,0},{8,12},{12,8},{16,20},{20,16},{24,28},{28,24},{1,5},{5... | collective-permute-start | bytes 1572872 | tf_op jit(solution)/shard_map/ppermute | solution.py:385
  88.2 15.5 %collective-permute-start.24 = (s16[1616,128]{1,0:T(8,128)(2,1)S(1)}, s16[1616,128]{1,0:T(8,128)(2,1)S(1)}, u32[]{:S(2)}, u32[]{:S(2)}) collective-permute-start(s16[1616,128]{1,0:T(8,128)(2,1)S(1)} %get-tuple-element.38.rest_2_), channel_id=1, source_target_pairs={{0,8},{4,12},{8,24},{12,28},{16,0},{20,4},{24,16},{28,20},{1,9},{5... | collective-permute-start | bytes 1241096 | tf_op jit(solution)/shard_map/ppermute | solution.py:437
  90.7 17.5 %collective-permute-start.26 = (bf16[128,2048]{1,0:T(8,128)(2,1)S(1)}, bf16[128,2048]{1,0:T(8,128)(2,1)S(1)}, u32[]{:S(2)}, u32[]{:S(2)}) collective-permute-start(bf16[128,2048]{1,0:T(8,128)(2,1)S(1)} %get-tuple-element.42), channel_id=1, source_target_pairs={{0,4},{4,0},{8,12},{12,8},{16,20},{20,16},{24,28},{28,24},{1,5},{5... | collective-permute-start | bytes 1572872 | tf_op jit(solution)/shard_map/ppermute | solution.py:385
  97.0 15.5 %collective-permute-start.25 = (s16[1616,128]{1,0:T(8,128)(2,1)S(1)}, s16[1616,128]{1,0:T(8,128)(2,1)S(1)}, u32[]{:S(2)}, u32[]{:S(2)}) collective-permute-start(s16[1616,128]{1,0:T(8,128)(2,1)S(1)} %get-tuple-element.41.rest_1_), channel_id=1, source_target_pairs={{0,8},{4,12},{8,24},{12,28},{16,0},{20,4},{24,16},{28,20},{1,9},{5... | collective-permute-start | bytes 1241096 | tf_op jit(solution)/shard_map/ppermute | solution.py:437
  99.6 21.1 %collective-permute-start.22 = (bf16[128,2048]{1,0:T(8,128)(2,1)S(1)}, bf16[128,2048]{1,0:T(8,128)(2,1)S(1)}, u32[]{:S(2)}, u32[]{:S(2)}) collective-permute-start(bf16[128,2048]{1,0:T(8,128)(2,1)S(1)} %get-tuple-element.39), channel_id=1, source_target_pairs={{0,4},{4,0},{8,12},{12,8},{16,20},{20,16},{24,28},{28,24},{1,5},{5... | collective-permute-start | bytes 1572872 | tf_op jit(solution)/shard_map/ppermute | solution.py:385
  105.7 15.0 %collective-permute-start.28 = (s16[1616,128]{1,0:T(8,128)(2,1)S(1)}, s16[1616,128]{1,0:T(8,128)(2,1)S(1)}, u32[]{:S(2)}, u32[]{:S(2)}) collective-permute-start(s16[1616,128]{1,0:T(8,128)(2,1)S(1)} %sum_step_10.1.rest_1_), channel_id=1, source_target_pairs={{0,8},{4,12},{8,24},{12,28},{16,0},{20,4},{24,16},{28,20},{1,9},{5... | collective-permute-start | bytes 1241096 | tf_op jit(solution)/shard_map/ppermute | solution.py:437
  114.6 10.3 %collective-permute-start.27 = (s16[1616,128]{1,0:T(8,128)(2,1)S(1)}, s16[1616,128]{1,0:T(8,128)(2,1)S(1)}, u32[]{:S(2)}, u32[]{:S(2)}) collective-permute-start(s16[1616,128]{1,0:T(8,128)(2,1)S(1)} %sum_step_11.1), channel_id=1, source_target_pairs={{0,8},{4,12},{8,24},{12,28},{16,0},{20,4},{24,16},{28,20},{1,9},{5... | collective-permute-start | bytes 1241096 | tf_op jit(solution)/shard_map/ppermute | solution.py:437

commit v8 on v6

--- a/solution.py
+++ b/solution.py
@@ -19,7 +19,7 @@
 STEADY = pl.CostEstimate(flops=10_000_000_000, bytes_accessed=30_000_000, transcendentals=0)
 LITTLE = pl.CostEstimate(flops=1024, bytes_accessed=1024, transcendentals=0)
 CUTS = 2
-HALVES = 2
+HALVES = 1
 FLIGHT = 2
 FIRST_SWAP = (0, 2)
 SWAPS = {0: (2, 1), 1: (4, 2), 2: (6, 2), 5: (8, 2), 7: (10, 2), 8: (12, 2), 9: (14, 2)}

time: 129 us -> 128 us (level)
  waiting for transfers between devices: 20.1 us -> 23.1 us
  Pallas kernels: 45.6 us -> 43.7 us
  starting transfers between devices: 55.7 us -> 54.3 us
    ppermute x15, starting transfers between devices: 36.5 us -> 34.3 us  [solve_by_sums(): lax.ppermute(coded, 'ifg', line_permutation(links))]
    ppermute x15, waiting for transfers between devices: 18.5 us -> 20.1 us  [solve_by_sums(): lax.ppermute(coded, 'ifg', line_permutation(links))]
    ppermute x8, waiting for transfers between devices: 1.58 us -> 2.91 us  [swapped(): here = lax.ppermute(away, 'ifg', swap)]
  transfers between devices with their start and end apart: 29 -> 29, of which waited for: 9 -> 8; matrix products, arithmetic and copies ran while one was open for 2% -> 2% of each run, Pallas kernels for 33% -> 32%
where the time goes in v8:
time: 128 us; the launch traced here: 127 us
  starting transfers between devices  54.3 us (42%)
  Pallas kernels  43.7 us (34%)
  waiting for transfers between devices  23.1 us (18%)
  local copies, waits for them, and re-layouts  4.38 us (3%)
    ppermute x15, starting transfers between devices, solve_by_sums(): lax.ppermute(coded, 'ifg', line_permutation(links))  34.3 us
    pallas_call x11, Pallas kernels, step(): pl.pallas_call(functools.partial(step_kernel, at, layout, len(earlier), s...  23.3 us
    ppermute x15, waiting for transfers between devices, solve_by_sums(): lax.ppermute(coded, 'ifg', line_permutation(links))  20.1 us
    pallas_call x4, Pallas kernels, finish(): pl.pallas_call(functools.partial(finish_kernel, at, layout, HALVES, len(r...  13.7 us
    ppermute x8, starting transfers between devices, swapped(): here = lax.ppermute(away, 'ifg', swap)  9.77 us
    pallas_call x1, Pallas kernels, invert_classes(): pl.pallas_call(inverse_kernel, out_shape=jax.ShapeDtypeStruct(shape, F32)...  6.77 us
    ppermute x3, starting transfers between devices, solve_by_sums(): counts.append(lax.ppermute(run_counts, 'ifg', line_permutation(links)))  6.11 us
    ppermute x8, waiting for transfers between devices, swapped(): here = lax.ppermute(away, 'ifg', swap)  2.91 us
  transfers between devices with their start and end apart: 29, of which 8 were waited for; matrix products, arithmetic and copies ran while one was open for 2% of the time, Pallas kernels for 32%

profile of v8, /device:TPU:0, one launch (start us, length us, event | category | flops | bytes accessed | tf_op | source)
XLA Modules:
  0.0 126.7 jit_solution(18007032835010816709)
XLA Ops:
  0.0 1.1 dynamic-slice_bitcast_fusion
  1.2 0.8 fusion.counts_ref
  2.1 5.1 %collective-permute-start.2 = (s32[2]{0:T(128)S(1)}, s32[2]{0:T(128)S(1)}, u32[]{:S(2)}, u32[]{:S(2)}) collective-permute-start(s32[2]{0:T(128)S(1)} %fusion.counts_ref), channel_id=1, source_target_pairs={{0,24},{4,28},{8,0},{12,4},{16,8},{20,12},{24,16},{28,20},{1,25},{... | collective-permute-start | bytes 32 | tf_op jit(solution)/shard_map/ppermute | solution.py:403
  7.2 1.0 collective-permute-start
  8.2 1.5 %collective-permute-start.3 = (bf16[128,2048]{1,0:T(8,128)(2,1)S(1)}, bf16[128,2048]{1,0:T(8,128)(2,1)S(1)}, u32[]{:S(2)}, u32[]{:S(2)}) collective-permute-start(bf16[128,2048]{1,0:T(8,128)(2,1)S(1)} %dynamic-slice_bitcast_fusion), channel_id=1, source_target_pairs={{0,4},{4,0},{8,12},{12,8},{16,20},{20,16},{24,28},{28,24},{1,5},{5... | collective-permute-start | bytes 1572872 | tf_op jit(solution)/shard_map/ppermute | solution.py:385
  9.7 1.1 dynamic-slice_bitcast_fusion.1
  10.7 2.5 %collective-permute-start.5 = (bf16[128,1024]{1,0:T(8,128)(2,1)S(1)}, bf16[128,1024]{1,0:T(8,128)(2,1)S(1)}, u32[]{:S(2)}, u32[]{:S(2)}) collective-permute-start(bf16[128,1024]{1,0:T(8,128)(2,1)S(1)} %get-tuple-element.45), channel_id=1, source_target_pairs={{0,8},{4,12},{8,0},{12,4},{16,24},{20,28},{24,16},{28,20},{1,9},{5... | collective-permute-start | bytes 786440 | tf_op jit(solution)/shard_map/ppermute | solution.py:407
  13.3 0.7 constant_dynamic-slice_fusion.3
  14.2 0.7 fusion.1.table
  14.9 0.7 copy-done.1
  15.6 6.8 %invert_classes_0.1.rest_1_.inverse_ref = f32[2,256,256]{2,1,0:T(8,128)S(1)} custom-call(s32[2]{0:T(128)S(1)} %fusion.counts_ref, s32[2,1024]{1,0:T(2,128)S(1)} %copy-done.1, s32[8]{0:T(128)S(1)} %pad_add_fusion.1.rest_0_.counts), custom_call_target="tpu_custom_call" | custom-call | flops 1024 | bytes 1024 | tf_op jit(solution)/shard_map/invert_classes_0/pallas_call | solution.py:103
  22.4 2.1 %sum_step_00.1 = (s16[1616,128]{1,0:T(8,128)(2,1)S(1)}, bf16[128,1024]{1,0:T(8,128)(2,1)S(1)}) custom-call(s32[53]{0:T(128)S(1)} %fusion.1.table, s32[8]{0:T(128)S(1)} %pad_add_fusion.1.rest_0_.counts, s32[2,512]{1,0:T(2,128)S(1)} %pad_add_fusion.pairs_ref, bf16[128,32768]{1,0:T(8,128)(2,1)} %bitcast.12, ...), custom_call_target="tpu_custom_call" | custom-call | flops 10000000000 | bytes 30000000 | tf_op jit(solution)/shard_map/sum_step_00/pallas_call | solution.py:245
  24.4 2.2 %collective-permute-start.9 = (bf16[128,1024]{1,0:T(8,128)(2,1)S(1)}, bf16[128,1024]{1,0:T(8,128)(2,1)S(1)}, u32[]{:S(2)}, u32[]{:S(2)}) collective-permute-start(bf16[128,1024]{1,0:T(8,128)(2,1)S(1)} %get-tuple-element.31), channel_id=1, source_target_pairs={{0,4},{4,0},{8,12},{12,8},{16,20},{20,16},{24,28},{28,24},{1,5},{5... | collective-permute-start | bytes 786440 | tf_op jit(solution)/shard_map/ppermute | solution.py:385
  26.6 1.2 collective-permute-start.8
  27.8 2.2 %sum_step_01.1 = (s16[1616,128]{1,0:T(8,128)(2,1)S(1)}, bf16[128,2048]{1,0:T(8,128)(2,1)S(1)}) custom-call(s32[53]{0:T(128)S(1)} %fusion.1.table, s32[8]{0:T(128)S(1)} %pad_add_fusion.1.rest_0_.counts, s32[2,512]{1,0:T(2,128)S(1)} %pad_add_fusion.pairs_ref, bf16[128,32768]{1,0:T(8,128)(2,1)} %bitcast.14, ...), custom_call_target="tpu_custom_call" | custom-call | flops 10000000000 | bytes 30000000 | tf_op jit(solution)/shard_map/sum_step_01/pallas_call | solution.py:245
  30.0 0.9 collective-permute-start.7
  30.9 0.7 collective-permute-start.6
  32.2 6.9 %collective-permute-done.8.rest_2_.rest_0_ = s16[1616,128]{1,0:T(8,128)(2,1)S(1)} collective-permute-done((s16[1616,128]{1,0:T(8,128)(2,1)S(1)}, s16[1616,128]{1,0:T(8,128)(2,1)S(1)}, u32[]{:S(2)}, u32[]{:S(2)}) %collective-permute-start.8) | collective-permute-done | bytes 413728 | tf_op jit(solution)/shard_map/ppermute | solution.py:436
  39.1 2.2 %sum_step_02.1 = (s16[1616,128]{1,0:T(8,128)(2,1)S(1)}, bf16[128,2048]{1,0:T(8,128)(2,1)S(1)}) custom-call(s32[53]{0:T(128)S(1)} %fusion.1.table, s32[8]{0:T(128)S(1)} %pad_add_fusion.1.rest_0_.counts, s32[2,512]{1,0:T(2,128)S(1)} %pad_add_fusion.pairs_ref, bf16[128,32768]{1,0:T(8,128)(2,1)} %bitcast.16, ...), custom_call_target="tpu_custom_call" | custom-call | flops 10000000000 | bytes 30000000 | tf_op jit(solution)/shard_map/sum_step_02/pallas_call | solution.py:245
  41.3 1.3 collective-permute-start.10
  42.5 1.5 %collective-permute-start.11 = (bf16[128,1024]{1,0:T(8,128)(2,1)S(1)}, bf16[128,1024]{1,0:T(8,128)(2,1)S(1)}, u32[]{:S(2)}, u32[]{:S(2)}) collective-permute-start(bf16[128,1024]{1,0:T(8,128)(2,1)S(1)} %collective-permute-done.5.rest_3_), channel_id=1, source_target_pairs={{0,4},{4,0},{8,12},{12,8},{16,20},{20,16},{24,28},{28,24},{1,5},{5... | collective-permute-start | bytes 786440 | tf_op jit(solution)/shard_map/ppermute | solution.py:442
  44.6 3.4 %collective-permute-done.7.rest_2_.rest_1_.rest_0_ = s16[1616,128]{1,0:T(8,128)(2,1)S(1)} collective-permute-done((s16[1616,128]{1,0:T(8,128)(2,1)S(1)}, s16[1616,128]{1,0:T(8,128)(2,1)S(1)}, u32[]{:S(2)}, u32[]{:S(2)}) %collective-permute-start.7) | collective-permute-done | bytes 413728 | tf_op jit(solution)/shard_map/ppermute | solution.py:436
  48.0 2.0 %sum_step_04.1.rest_2_ = s16[1616,128]{1,0:T(8,128)(2,1)S(1)} custom-call(s32[53]{0:T(128)S(1)} %fusion.1.table, s32[8]{0:T(128)S(1)} %pad_add_fusion.1.rest_0_.counts, s32[2,512]{1,0:T(2,128)S(1)} %pad_add_fusion.pairs_ref, bf16[128,32768]{1,0:T(8,128)(2,1)} %bitcast.18, bf16[128,2048]{1,0:T(8,128)(2,1)S(1)} %collective-permute-done.6.partner_ref, ...), custom_call_target="tpu_custom_call" | custom-call | flops 10000000000 | bytes 30000000 | tf_op jit(solution)/shard_map/sum_step_04/pallas_call | solution.py:245
  50.7 4.4 %collective-permute-start.14 = (s16[1616,128]{1,0:T(8,128)(2,1)S(1)}, s16[1616,128]{1,0:T(8,128)(2,1)S(1)}, u32[]{:S(2)}, u32[]{:S(2)}) collective-permute-start(s16[1616,128]{1,0:T(8,128)(2,1)S(1)} %sum_step_04.1.rest_2_), channel_id=1, source_target_pairs={{0,8},{4,12},{24,16},{28,20},{1,9},{5,13},{25,17},{29,21},{2,10},{... | collective-permute-start | bytes 1241096 | tf_op jit(solution)/shard_map/ppermute | solution.py:436
  55.1 2.2 %sum_step_05.1 = (s16[1616,128]{1,0:T(8,128)(2,1)S(1)}, bf16[128,2048]{1,0:T(8,128)(2,1)S(1)}) custom-call(s32[53]{0:T(128)S(1)} %fusion.1.table, s32[8]{0:T(128)S(1)} %pad_add_fusion.1.rest_0_.counts, s32[2,512]{1,0:T(2,128)S(1)} %pad_add_fusion.pairs_ref, bf16[128,32768]{1,0:T(8,128)(2,1)} %bitcast.19, ...), custom_call_target="tpu_custom_call" | custom-call | flops 10000000000 | bytes 30000000 | tf_op jit(solution)/shard_map/sum_step_05/pallas_call | solution.py:245
  58.0 5.7 %collective-permute-start.13 = (s16[1616,128]{1,0:T(8,128)(2,1)S(1)}, s16[1616,128]{1,0:T(8,128)(2,1)S(1)}, u32[]{:S(2)}, u32[]{:S(2)}) collective-permute-start(s16[1616,128]{1,0:T(8,128)(2,1)S(1)} %get-tuple-element.35.rest_1_), channel_id=1, source_target_pairs={{0,8},{4,12},{24,16},{28,20},{1,9},{5,13},{25,17},{29,21},{2,10},{... | collective-permute-start | bytes 1241096 | tf_op jit(solution)/shard_map/ppermute | solution.py:436
  63.7 1.2 collective-permute-start.12
  64.9 2.0 %sum_step_06.1.rest_3_ = s16[1616,128]{1,0:T(8,128)(2,1)S(1)} custom-call(s32[53]{0:T(128)S(1)} %fusion.1.table, s32[8]{0:T(128)S(1)} %pad_add_fusion.1.rest_0_.counts, s32[2,512]{1,0:T(2,128)S(1)} %pad_add_fusion.pairs_ref, bf16[128,32768]{1,0:T(8,128)(2,1)} %bitcast.21, bf16[128,2048]{1,0:T(8,128)(2,1)S(1)} %collective-permute-done.15.partner_ref, ...), custom_call_target="tpu_custom_call" | custom-call | flops 10000000000 | bytes 30000000 | tf_op jit(solution)/shard_map/sum_step_06/pallas_call | solution.py:245
  67.6 5.2 %collective-permute-start.18 = (s16[1616,128]{1,0:T(8,128)(2,1)S(1)}, s16[1616,128]{1,0:T(8,128)(2,1)S(1)}, u32[]{:S(2)}, u32[]{:S(2)}) collective-permute-start(s16[1616,128]{1,0:T(8,128)(2,1)S(1)} %sum_step_06.1.rest_3_), channel_id=1, source_target_pairs={{0,8},{4,12},{24,16},{28,20},{1,9},{5,13},{25,17},{29,21},{2,10},{... | collective-permute-start | bytes 1241096 | tf_op jit(solution)/shard_map/ppermute | solution.py:436
  72.8 2.3 %sum_step_07.1 = (s16[1616,128]{1,0:T(8,128)(2,1)S(1)}, bf16[128,2048]{1,0:T(8,128)(2,1)S(1)}) custom-call(s32[53]{0:T(128)S(1)} %fusion.1.table, s32[8]{0:T(128)S(1)} %pad_add_fusion.1.rest_0_.counts, s32[2,512]{1,0:T(2,128)S(1)} %pad_add_fusion.pairs_ref, bf16[128,32768]{1,0:T(8,128)(2,1)} %bitcast.22, ...), custom_call_target="tpu_custom_call" | custom-call | flops 10000000000 | bytes 30000000 | tf_op jit(solution)/shard_map/sum_step_07/pallas_call | solution.py:245
  75.8 6.5 %collective-permute-start.20 = (s16[1616,128]{1,0:T(8,128)(2,1)S(1)}, s16[1616,128]{1,0:T(8,128)(2,1)S(1)}, u32[]{:S(2)}, u32[]{:S(2)}) collective-permute-start(s16[1616,128]{1,0:T(8,128)(2,1)S(1)} %get-tuple-element.37.rest_2_), channel_id=1, source_target_pairs={{0,8},{4,12},{24,16},{28,20},{1,9},{5,13},{25,17},{29,21},{2,10},{... | collective-permute-start | bytes 1241096 | tf_op jit(solution)/shard_map/ppermute | solution.py:436
  82.3 1.5 %collective-permute-start.23 = (bf16[128,2048]{1,0:T(8,128)(2,1)S(1)}, bf16[128,2048]{1,0:T(8,128)(2,1)S(1)}, u32[]{:S(2)}, u32[]{:S(2)}) collective-permute-start(bf16[128,2048]{1,0:T(8,128)(2,1)S(1)} %get-tuple-element.40), channel_id=1, source_target_pairs={{0,4},{4,0},{8,12},{12,8},{16,20},{20,16},{24,28},{28,24},{1,5},{5... | collective-permute-start | bytes 1572872 | tf_op jit(solution)/shard_map/ppermute | solution.py:385
  83.9 2.2 %sum_step_08.1 = (s16[1616,128]{1,0:T(8,128)(2,1)S(1)}, bf16[128,2048]{1,0:T(8,128)(2,1)S(1)}) custom-call(s32[53]{0:T(128)S(1)} %fusion.1.table, s32[8]{0:T(128)S(1)} %pad_add_fusion.1.rest_0_.counts, s32[2,512]{1,0:T(2,128)S(1)} %pad_add_fusion.pairs_ref, bf16[128,32768]{1,0:T(8,128)(2,1)} %bitcast.24, ...), custom_call_target="tpu_custom_call" | custom-call | flops 10000000000 | bytes 30000000 | tf_op jit(solution)/shard_map/sum_step_08/pallas_call | solution.py:245
  86.8 5.5 %collective-permute-done.20.rest_3_.rest_0_ = s16[1616,128]{1,0:T(8,128)(2,1)S(1)} collective-permute-done((s16[1616,128]{1,0:T(8,128)(2,1)S(1)}, s16[1616,128]{1,0:T(8,128)(2,1)S(1)}, u32[]{:S(2)}, u32[]{:S(2)}) %collective-permute-start.20) | collective-permute-done | bytes 413728 | tf_op jit(solution)/shard_map/ppermute | solution.py:436
  92.3 2.2 %sum_step_09.1 = (s16[1616,128]{1,0:T(8,128)(2,1)S(1)}, bf16[128,2048]{1,0:T(8,128)(2,1)S(1)}) custom-call(s32[53]{0:T(128)S(1)} %fusion.1.table, s32[8]{0:T(128)S(1)} %pad_add_fusion.1.rest_0_.counts, s32[2,512]{1,0:T(2,128)S(1)} %pad_add_fusion.pairs_ref, bf16[128,32768]{1,0:T(8,128)(2,1)} %bitcast.26, ...), custom_call_target="tpu_custom_call" | custom-call | flops 10000000000 | bytes 30000000 | tf_op jit(solution)/shard_map/sum_step_09/pallas_call | solution.py:245
  94.5 2.5 %collective-permute-start.25 = (s16[1616,128]{1,0:T(8,128)(2,1)S(1)}, s16[1616,128]{1,0:T(8,128)(2,1)S(1)}, u32[]{:S(2)}, u32[]{:S(2)}) collective-permute-start(s16[1616,128]{1,0:T(8,128)(2,1)S(1)} %get-tuple-element.41.rest_1_), channel_id=1, source_target_pairs={{0,8},{4,12},{8,24},{12,28},{16,0},{20,4},{24,16},{28,20},{1,9},{5... | collective-permute-start | bytes 1241096 | tf_op jit(solution)/shard_map/ppermute | solution.py:436
  97.0 1.5 %collective-permute-start.22 = (bf16[128,2048]{1,0:T(8,128)(2,1)S(1)}, bf16[128,2048]{1,0:T(8,128)(2,1)S(1)}, u32[]{:S(2)}, u32[]{:S(2)}) collective-permute-start(bf16[128,2048]{1,0:T(8,128)(2,1)S(1)} %get-tuple-element.39), channel_id=1, source_target_pairs={{0,4},{4,0},{8,12},{12,8},{16,20},{20,16},{24,28},{28,24},{1,5},{5... | collective-permute-start | bytes 1572872 | tf_op jit(solution)/shard_map/ppermute | solution.py:385
  98.5 2.6 %collective-permute-done.24.rest_2_ = s16[1616,128]{1,0:T(8,128)(2,1)S(1)} collective-permute-done((s16[1616,128]{1,0:T(8,128)(2,1)S(1)}, s16[1616,128]{1,0:T(8,128)(2,1)S(1)}, u32[]{:S(2)}, u32[]{:S(2)}) %collective-permute-start.24) | collective-permute-done | bytes 413728 | tf_op jit(solution)/shard_map/ppermute | solution.py:436
  101.1 2.0 %sum_step_10.1.rest_1_ = s16[1616,128]{1,0:T(8,128)(2,1)S(1)} custom-call(s32[53]{0:T(128)S(1)} %fusion.1.table, s32[8]{0:T(128)S(1)} %pad_add_fusion.1.rest_0_.counts, s32[2,512]{1,0:T(2,128)S(1)} %pad_add_fusion.pairs_ref, bf16[128,32768]{1,0:T(8,128)(2,1)} %bitcast.28, bf16[128,2048]{1,0:T(8,128)(2,1)S(1)} %collective-permute-done.23.partner_ref, ...), custom_call_target="tpu_custom_call" | custom-call | flops 10000000000 | bytes 30000000 | tf_op jit(solution)/shard_map/sum_step_10/pallas_call | solution.py:245
  103.2 2.5 %collective-permute-start.28 = (s16[1616,128]{1,0:T(8,128)(2,1)S(1)}, s16[1616,128]{1,0:T(8,128)(2,1)S(1)}, u32[]{:S(2)}, u32[]{:S(2)}) collective-permute-start(s16[1616,128]{1,0:T(8,128)(2,1)S(1)} %sum_step_10.1.rest_1_), channel_id=1, source_target_pairs={{0,8},{4,12},{8,24},{12,28},{16,0},{20,4},{24,16},{28,20},{1,9},{5... | collective-permute-start | bytes 1241096 | tf_op jit(solution)/shard_map/ppermute | solution.py:436
  105.7 2.4 %collective-permute-done.26.partner_ref = bf16[128,2048]{1,0:T(8,128)(2,1)S(1)} collective-permute-done((bf16[128,2048]{1,0:T(8,128)(2,1)S(1)}, bf16[128,2048]{1,0:T(8,128)(2,1)S(1)}, u32[]{:S(2)}, u32[]{:S(2)}) %collective-permute-start.26) | collective-permute-done | bytes 524320 | tf_op jit(solution)/shard_map/ppermute | solution.py:385
  108.0 3.4 %finish_0.1 = (f32[200,4096]{1,0:T(8,128)}, f32[8,128]{1,0:T(8,128)S(1)}) custom-call(s32[53]{0:T(128)S(1)} %fusion.1.table, s32[8]{0:T(128)S(1)} %pad_add_fusion.1.rest_0_.counts, s32[2,512]{1,0:T(2,128)S(1)} %pad_add_fusion.pairs_ref, bf16[128,32768]{1,0:T(8,128)(2,1)} %bitcast.29, bf16[128,2048]{1,0:T(8,128)(2,1)S(1)} %collective-permute-done.26.partner_ref, ...), custom_call_target="tpu_custom_call" | custom-call | flops 1024 | bytes 1024 | tf_op jit(solution)/shard_map/finish_0/pallas_call | solution.py:336
  111.4 2.0 %sum_step_11.1 = s16[1616,128]{1,0:T(8,128)(2,1)S(1)} custom-call(s32[53]{0:T(128)S(1)} %fusion.1.table, s32[8]{0:T(128)S(1)} %pad_add_fusion.1.rest_0_.counts, s32[2,512]{1,0:T(2,128)S(1)} %pad_add_fusion.pairs_ref, bf16[128,32768]{1,0:T(8,128)(2,1)} %bitcast.30, bf16[128,2048]{1,0:T(8,128)(2,1)S(1)} %collective-permute-done.23.partner_ref, ...), custom_call_target="tpu_custom_call" | custom-call | flops 10000000000 | bytes 30000000 | tf_op jit(solution)/shard_map/sum_step_11/pallas_call | solution.py:245
  113.4 1.3 %collective-permute-start.27 = (s16[1616,128]{1,0:T(8,128)(2,1)S(1)}, s16[1616,128]{1,0:T(8,128)(2,1)S(1)}, u32[]{:S(2)}, u32[]{:S(2)}) collective-permute-start(s16[1616,128]{1,0:T(8,128)(2,1)S(1)} %sum_step_11.1), channel_id=1, source_target_pairs={{0,8},{4,12},{8,24},{12,28},{16,0},{20,4},{24,16},{28,20},{1,9},{5... | collective-permute-start | bytes 1241096 | tf_op jit(solution)/shard_map/ppermute | solution.py:436
  114.7 3.4 %finish_1.1.rest_3_ = f32[200,4096]{1,0:T(8,128)} custom-call(s32[53]{0:T(128)S(1)} %fusion.1.table, s32[8]{0:T(128)S(1)} %pad_add_fusion.1.rest_0_.counts, s32[2,512]{1,0:T(2,128)S(1)} %pad_add_fusion.pairs_ref, bf16[128,32768]{1,0:T(8,128)(2,1)} %bitcast.31, ...), custom_call_target="tpu_custom_call", output_to_operand_aliasing={{}: (9, {})} | custom-call | flops 1024 | bytes 1024 | tf_op jit(solution)/shard_map/finish_1/pallas_call | solution.py:336
  118.7 3.4 %finish_2.1.rest_4_ = f32[200,4096]{1,0:T(8,128)} custom-call(s32[53]{0:T(128)S(1)} %fusion.1.table, s32[8]{0:T(128)S(1)} %pad_add_fusion.1.rest_0_.counts, s32[2,512]{1,0:T(2,128)S(1)} %pad_add_fusion.pairs_ref, bf16[128,32768]{1,0:T(8,128)(2,1)} %bitcast.32, ...), custom_call_target="tpu_custom_call", output_to_operand_aliasing={{}: (9, {})} | custom-call | flops 1024 | bytes 1024 | tf_op jit(solution)/shard_map/finish_2/pallas_call | solution.py:336
  122.1 1.0 collective-permute-done.27.rest_3_
  123.1 3.5 %finish_3.1 = f32[200,4096]{1,0:T(8,128)} custom-call(s32[53]{0:T(128)S(1)} %fusion.1.table, s32[8]{0:T(128)S(1)} %pad_add_fusion.1.rest_0_.counts, s32[2,512]{1,0:T(2,128)S(1)} %pad_add_fusion.pairs_ref, bf16[128,32768]{1,0:T(8,128)(2,1)} %bitcast.33, bf16[128,2048]{1,0:T(8,128)(2,1)S(1)} %collective-permute-done.22.partner_ref, ...), custom_call_target="tpu_custom_call", output_to_operand_aliasing={{}: (10, {})} | custom-call | flops 1024 | bytes 1024 | tf_op jit(solution)/shard_map/finish_3/pallas_call | solution.py:336
  (39 shorter events, 5.4 us)
Async XLA Ops:
  0.0 1.1 copy-start
  2.1 11.9 %collective-permute-start.2 = (s32[2]{0:T(128)S(1)}, s32[2]{0:T(128)S(1)}, u32[]{:S(2)}, u32[]{:S(2)}) collective-permute-start(s32[2]{0:T(128)S(1)} %fusion.counts_ref), channel_id=1, source_target_pairs={{0,24},{4,28},{8,0},{12,4},{16,8},{20,12},{24,16},{28,20},{1,25},{... | collective-permute-start | bytes 32 | tf_op jit(solution)/shard_map/ppermute | solution.py:403
  7.1 7.0 %collective-permute-start.1 = (s32[2]{0:T(128)S(1)}, s32[2]{0:T(128)S(1)}, u32[]{:S(2)}, u32[]{:S(2)}) collective-permute-start(s32[2]{0:T(128)S(1)} %fusion.counts_ref), channel_id=1, source_target_pairs={{0,16},{4,20},{8,24},{12,28},{16,0},{20,4},{24,8},{28,12},{1,17},{... | collective-permute-start | bytes 32 | tf_op jit(solution)/shard_map/ppermute | solution.py:403
  7.2 7.0 %collective-permute-start = (s32[2]{0:T(128)S(1)}, s32[2]{0:T(128)S(1)}, u32[]{:S(2)}, u32[]{:S(2)}) collective-permute-start(s32[2]{0:T(128)S(1)} %fusion.counts_ref), channel_id=1, source_target_pairs={{0,8},{4,12},{8,16},{12,20},{16,24},{20,28},{24,0},{28,4},{1,9},{5... | collective-permute-start | bytes 32 | tf_op jit(solution)/shard_map/ppermute | solution.py:403
  8.2 14.2 %collective-permute-start.3 = (bf16[128,2048]{1,0:T(8,128)(2,1)S(1)}, bf16[128,2048]{1,0:T(8,128)(2,1)S(1)}, u32[]{:S(2)}, u32[]{:S(2)}) collective-permute-start(bf16[128,2048]{1,0:T(8,128)(2,1)S(1)} %dynamic-slice_bitcast_fusion), channel_id=1, source_target_pairs={{0,4},{4,0},{8,12},{12,8},{16,20},{20,16},{24,28},{28,24},{1,5},{5... | collective-permute-start | bytes 1572872 | tf_op jit(solution)/shard_map/ppermute | solution.py:385
  10.7 17.1 %collective-permute-start.5 = (bf16[128,1024]{1,0:T(8,128)(2,1)S(1)}, bf16[128,1024]{1,0:T(8,128)(2,1)S(1)}, u32[]{:S(2)}, u32[]{:S(2)}) collective-permute-start(bf16[128,1024]{1,0:T(8,128)(2,1)S(1)} %get-tuple-element.45), channel_id=1, source_target_pairs={{0,8},{4,12},{8,0},{12,4},{16,24},{20,28},{24,16},{28,20},{1,9},{5... | collective-permute-start | bytes 786440 | tf_op jit(solution)/shard_map/ppermute | solution.py:407
  14.0 13.8 %collective-permute-start.4 = (bf16[128,1024]{1,0:T(8,128)(2,1)S(1)}, bf16[128,1024]{1,0:T(8,128)(2,1)S(1)}, u32[]{:S(2)}, u32[]{:S(2)}) collective-permute-start(bf16[128,1024]{1,0:T(8,128)(2,1)S(1)} %get-tuple-element.46), channel_id=1, source_target_pairs={{0,8},{4,12},{8,0},{12,4},{16,24},{20,28},{24,16},{28,20},{1,9},{5... | collective-permute-start | bytes 786440 | tf_op jit(solution)/shard_map/ppermute | solution.py:408
  14.9 0.7 copy-start.1
  24.4 7.7 %collective-permute-start.9 = (bf16[128,1024]{1,0:T(8,128)(2,1)S(1)}, bf16[128,1024]{1,0:T(8,128)(2,1)S(1)}, u32[]{:S(2)}, u32[]{:S(2)}) collective-permute-start(bf16[128,1024]{1,0:T(8,128)(2,1)S(1)} %get-tuple-element.31), channel_id=1, source_target_pairs={{0,4},{4,0},{8,12},{12,8},{16,20},{20,16},{24,28},{28,24},{1,5},{5... | collective-permute-start | bytes 786440 | tf_op jit(solution)/shard_map/ppermute | solution.py:385
  26.6 12.5 %collective-permute-start.8 = (s16[1616,128]{1,0:T(8,128)(2,1)S(1)}, s16[1616,128]{1,0:T(8,128)(2,1)S(1)}, u32[]{:S(2)}, u32[]{:S(2)}) collective-permute-start(s16[1616,128]{1,0:T(8,128)(2,1)S(1)} %get-tuple-element.26.rest_1_), channel_id=1, source_target_pairs={{0,8},{4,12},{8,0},{12,4},{16,24},{20,28},{24,16},{28,20},{1,9},{5... | collective-permute-start | bytes 1241096 | tf_op jit(solution)/shard_map/ppermute | solution.py:436
  30.0 18.0 %collective-permute-start.7 = (s16[1616,128]{1,0:T(8,128)(2,1)S(1)}, s16[1616,128]{1,0:T(8,128)(2,1)S(1)}, u32[]{:S(2)}, u32[]{:S(2)}) collective-permute-start(s16[1616,128]{1,0:T(8,128)(2,1)S(1)} %get-tuple-element.30.rest_1_), channel_id=1, source_target_pairs={{0,8},{4,12},{8,0},{12,4},{16,24},{20,28},{24,16},{28,20},{1,9},{5... | collective-permute-start | bytes 1241096 | tf_op jit(solution)/shard_map/ppermute | solution.py:436
  30.9 17.1 %collective-permute-start.6 = (bf16[128,2048]{1,0:T(8,128)(2,1)S(1)}, bf16[128,2048]{1,0:T(8,128)(2,1)S(1)}, u32[]{:S(2)}, u32[]{:S(2)}) collective-permute-start(bf16[128,2048]{1,0:T(8,128)(2,1)S(1)} %get-tuple-element.29), channel_id=1, source_target_pairs={{0,4},{4,0},{8,12},{12,8},{16,20},{20,16},{24,28},{28,24},{1,5},{5... | collective-permute-start | bytes 1572872 | tf_op jit(solution)/shard_map/ppermute | solution.py:385
  41.3 13.8 %collective-permute-start.10 = (s16[1616,128]{1,0:T(8,128)(2,1)S(1)}, s16[1616,128]{1,0:T(8,128)(2,1)S(1)}, u32[]{:S(2)}, u32[]{:S(2)}) collective-permute-start(s16[1616,128]{1,0:T(8,128)(2,1)S(1)} %get-tuple-element.32.rest_1_), channel_id=1, source_target_pairs={{0,8},{4,12},{8,0},{12,4},{16,24},{20,28},{24,16},{28,20},{1,9},{5... | collective-permute-start | bytes 1241096 | tf_op jit(solution)/shard_map/ppermute | solution.py:436
  42.5 12.5 %collective-permute-start.11 = (bf16[128,1024]{1,0:T(8,128)(2,1)S(1)}, bf16[128,1024]{1,0:T(8,128)(2,1)S(1)}, u32[]{:S(2)}, u32[]{:S(2)}) collective-permute-start(bf16[128,1024]{1,0:T(8,128)(2,1)S(1)} %collective-permute-done.5.rest_3_), channel_id=1, source_target_pairs={{0,4},{4,0},{8,12},{12,8},{16,20},{20,16},{24,28},{28,24},{1,5},{5... | collective-permute-start | bytes 786440 | tf_op jit(solution)/shard_map/ppermute | solution.py:442
  44.0 19.6 %collective-permute-start.15 = (bf16[128,2048]{1,0:T(8,128)(2,1)S(1)}, bf16[128,2048]{1,0:T(8,128)(2,1)S(1)}, u32[]{:S(2)}, u32[]{:S(2)}) collective-permute-start(bf16[128,2048]{1,0:T(8,128)(2,1)S(1)} %get-tuple-element.36), channel_id=1, source_target_pairs={{0,4},{4,0},{8,12},{12,8},{16,20},{20,16},{24,28},{28,24},{1,5},{5... | collective-permute-start | bytes 1572872 | tf_op jit(solution)/shard_map/ppermute | solution.py:385
  50.0 14.9 %collective-permute-start.16 = (s16[1616,128]{1,0:T(8,128)(2,1)S(1)}, s16[1616,128]{1,0:T(8,128)(2,1)S(1)}, u32[]{:S(2)}, u32[]{:S(2)}) collective-permute-start(s16[1616,128]{1,0:T(8,128)(2,1)S(1)} %sum_step_04.1.rest_2_), channel_id=1, source_target_pairs={{8,16},{12,20},{16,8},{20,12},{9,17},{13,21},{17,9},{21,13},{10,18... | collective-permute-start | bytes 1241096 | tf_op jit(solution)/shard_map/ppermute | solution.py:436
  50.7 14.2 %collective-permute-start.14 = (s16[1616,128]{1,0:T(8,128)(2,1)S(1)}, s16[1616,128]{1,0:T(8,128)(2,1)S(1)}, u32[]{:S(2)}, u32[]{:S(2)}) collective-permute-start(s16[1616,128]{1,0:T(8,128)(2,1)S(1)} %sum_step_04.1.rest_2_), channel_id=1, source_target_pairs={{0,8},{4,12},{24,16},{28,20},{1,9},{5,13},{25,17},{29,21},{2,10},{... | collective-permute-start | bytes 1241096 | tf_op jit(solution)/shard_map/ppermute | solution.py:436
  57.3 15.5 %collective-permute-start.17 = (s16[1616,128]{1,0:T(8,128)(2,1)S(1)}, s16[1616,128]{1,0:T(8,128)(2,1)S(1)}, u32[]{:S(2)}, u32[]{:S(2)}) collective-permute-start(s16[1616,128]{1,0:T(8,128)(2,1)S(1)} %get-tuple-element.35.rest_1_), channel_id=1, source_target_pairs={{8,16},{12,20},{16,8},{20,12},{9,17},{13,21},{17,9},{21,13},{10,18... | collective-permute-start | bytes 1241096 | tf_op jit(solution)/shard_map/ppermute | solution.py:436
  58.0 14.8 %collective-permute-start.13 = (s16[1616,128]{1,0:T(8,128)(2,1)S(1)}, s16[1616,128]{1,0:T(8,128)(2,1)S(1)}, u32[]{:S(2)}, u32[]{:S(2)}) collective-permute-start(s16[1616,128]{1,0:T(8,128)(2,1)S(1)} %get-tuple-element.35.rest_1_), channel_id=1, source_target_pairs={{0,8},{4,12},{24,16},{28,20},{1,9},{5,13},{25,17},{29,21},{2,10},{... | collective-permute-start | bytes 1241096 | tf_op jit(solution)/shard_map/ppermute | solution.py:436
  63.7 20.2 %collective-permute-start.12 = (bf16[128,2048]{1,0:T(8,128)(2,1)S(1)}, bf16[128,2048]{1,0:T(8,128)(2,1)S(1)}, u32[]{:S(2)}, u32[]{:S(2)}) collective-permute-start(bf16[128,2048]{1,0:T(8,128)(2,1)S(1)} %get-tuple-element.34), channel_id=1, source_target_pairs={{0,4},{4,0},{8,12},{12,8},{16,20},{20,16},{24,28},{28,24},{1,5},{5... | collective-permute-start | bytes 1572872 | tf_op jit(solution)/shard_map/ppermute | solution.py:385
  66.9 15.5 %collective-permute-start.19 = (s16[1616,128]{1,0:T(8,128)(2,1)S(1)}, s16[1616,128]{1,0:T(8,128)(2,1)S(1)}, u32[]{:S(2)}, u32[]{:S(2)}) collective-permute-start(s16[1616,128]{1,0:T(8,128)(2,1)S(1)} %sum_step_06.1.rest_3_), channel_id=1, source_target_pairs={{8,16},{12,20},{16,8},{20,12},{9,17},{13,21},{17,9},{21,13},{10,18... | collective-permute-start | bytes 1241096 | tf_op jit(solution)/shard_map/ppermute | solution.py:436
  67.6 16.3 %collective-permute-start.18 = (s16[1616,128]{1,0:T(8,128)(2,1)S(1)}, s16[1616,128]{1,0:T(8,128)(2,1)S(1)}, u32[]{:S(2)}, u32[]{:S(2)}) collective-permute-start(s16[1616,128]{1,0:T(8,128)(2,1)S(1)} %sum_step_06.1.rest_3_), channel_id=1, source_target_pairs={{0,8},{4,12},{24,16},{28,20},{1,9},{5,13},{25,17},{29,21},{2,10},{... | collective-permute-start | bytes 1241096 | tf_op jit(solution)/shard_map/ppermute | solution.py:436
  75.1 11.7 %collective-permute-start.21 = (s16[1616,128]{1,0:T(8,128)(2,1)S(1)}, s16[1616,128]{1,0:T(8,128)(2,1)S(1)}, u32[]{:S(2)}, u32[]{:S(2)}) collective-permute-start(s16[1616,128]{1,0:T(8,128)(2,1)S(1)} %get-tuple-element.37.rest_2_), channel_id=1, source_target_pairs={{8,16},{12,20},{16,8},{20,12},{9,17},{13,21},{17,9},{21,13},{10,18... | collective-permute-start | bytes 1241096 | tf_op jit(solution)/shard_map/ppermute | solution.py:436
  75.8 16.5 %collective-permute-start.20 = (s16[1616,128]{1,0:T(8,128)(2,1)S(1)}, s16[1616,128]{1,0:T(8,128)(2,1)S(1)}, u32[]{:S(2)}, u32[]{:S(2)}) collective-permute-start(s16[1616,128]{1,0:T(8,128)(2,1)S(1)} %get-tuple-element.37.rest_2_), channel_id=1, source_target_pairs={{0,8},{4,12},{24,16},{28,20},{1,9},{5,13},{25,17},{29,21},{2,10},{... | collective-permute-start | bytes 1241096 | tf_op jit(solution)/shard_map/ppermute | solution.py:436
  82.3 16.2 %collective-permute-start.23 = (bf16[128,2048]{1,0:T(8,128)(2,1)S(1)}, bf16[128,2048]{1,0:T(8,128)(2,1)S(1)}, u32[]{:S(2)}, u32[]{:S(2)}) collective-permute-start(bf16[128,2048]{1,0:T(8,128)(2,1)S(1)} %get-tuple-element.40), channel_id=1, source_target_pairs={{0,4},{4,0},{8,12},{12,8},{16,20},{20,16},{24,28},{28,24},{1,5},{5... | collective-permute-start | bytes 1572872 | tf_op jit(solution)/shard_map/ppermute | solution.py:385
  86.1 15.1 %collective-permute-start.24 = (s16[1616,128]{1,0:T(8,128)(2,1)S(1)}, s16[1616,128]{1,0:T(8,128)(2,1)S(1)}, u32[]{:S(2)}, u32[]{:S(2)}) collective-permute-start(s16[1616,128]{1,0:T(8,128)(2,1)S(1)} %get-tuple-element.38.rest_2_), channel_id=1, source_target_pairs={{0,8},{4,12},{8,24},{12,28},{16,0},{20,4},{24,16},{28,20},{1,9},{5... | collective-permute-start | bytes 1241096 | tf_op jit(solution)/shard_map/ppermute | solution.py:436
  86.1 21.9 %collective-permute-start.26 = (bf16[128,2048]{1,0:T(8,128)(2,1)S(1)}, bf16[128,2048]{1,0:T(8,128)(2,1)S(1)}, u32[]{:S(2)}, u32[]{:S(2)}) collective-permute-start(bf16[128,2048]{1,0:T(8,128)(2,1)S(1)} %get-tuple-element.42), channel_id=1, source_target_pairs={{0,4},{4,0},{8,12},{12,8},{16,20},{20,16},{24,28},{28,24},{1,5},{5... | collective-permute-start | bytes 1572872 | tf_op jit(solution)/shard_map/ppermute | solution.py:385
  94.5 16.9 %collective-permute-start.25 = (s16[1616,128]{1,0:T(8,128)(2,1)S(1)}, s16[1616,128]{1,0:T(8,128)(2,1)S(1)}, u32[]{:S(2)}, u32[]{:S(2)}) collective-permute-start(s16[1616,128]{1,0:T(8,128)(2,1)S(1)} %get-tuple-element.41.rest_1_), channel_id=1, source_target_pairs={{0,8},{4,12},{8,24},{12,28},{16,0},{20,4},{24,16},{28,20},{1,9},{5... | collective-permute-start | bytes 1241096 | tf_op jit(solution)/shard_map/ppermute | solution.py:436
  97.0 21.7 %collective-permute-start.22 = (bf16[128,2048]{1,0:T(8,128)(2,1)S(1)}, bf16[128,2048]{1,0:T(8,128)(2,1)S(1)}, u32[]{:S(2)}, u32[]{:S(2)}) collective-permute-start(bf16[128,2048]{1,0:T(8,128)(2,1)S(1)} %get-tuple-element.39), channel_id=1, source_target_pairs={{0,4},{4,0},{8,12},{12,8},{16,20},{20,16},{24,28},{28,24},{1,5},{5... | collective-permute-start | bytes 1572872 | tf_op jit(solution)/shard_map/ppermute | solution.py:385
  103.2 15.5 %collective-permute-start.28 = (s16[1616,128]{1,0:T(8,128)(2,1)S(1)}, s16[1616,128]{1,0:T(8,128)(2,1)S(1)}, u32[]{:S(2)}, u32[]{:S(2)}) collective-permute-start(s16[1616,128]{1,0:T(8,128)(2,1)S(1)} %sum_step_10.1.rest_1_), channel_id=1, source_target_pairs={{0,8},{4,12},{8,24},{12,28},{16,0},{20,4},{24,16},{28,20},{1,9},{5... | collective-permute-start | bytes 1241096 | tf_op jit(solution)/shard_map/ppermute | solution.py:436
  113.4 9.7 %collective-permute-start.27 = (s16[1616,128]{1,0:T(8,128)(2,1)S(1)}, s16[1616,128]{1,0:T(8,128)(2,1)S(1)}, u32[]{:S(2)}, u32[]{:S(2)}) collective-permute-start(s16[1616,128]{1,0:T(8,128)(2,1)S(1)} %sum_step_11.1), channel_id=1, source_target_pairs={{0,8},{4,12},{8,24},{12,28},{16,0},{20,4},{24,16},{28,20},{1,9},{5... | collective-permute-start | bytes 1241096 | tf_op jit(solution)/shard_map/ppermute | solution.py:436

commit v9 on v8

--- a/solution.py
+++ b/solution.py
@@ -404,12 +404,12 @@
     counts = jnp.concatenate(counts)
     raw_part = parts - 1
     near = line_permutation(SENDS[0][0])
-    raw_other = lax.ppermute(first_away(1 - side, raw_part, 1, run_counts), "ifg", near)
-    raw_own = lax.ppermute(first_away(side, raw_part, 1, run_counts), "ifg", near)
+    both_sides = jnp.concatenate([first_away(column, raw_part, 1, run_counts) for column in (1 - side, side)])
+    raws = lax.ppermute(both_sides, "ifg", near)
     pairs = jnp.concatenate([lax.dynamic_slice(date_pairs, (0, (me ^ at) * local_pairs), (2, local_pairs)) for at in range(4)], axis=1)
     scalars = (row, counts)
 
-    received, sent, coded, series = {raw_part: [raw_own, raw_other]}, [raw_part], None, None
+    received, sent, coded, series = {raw_part: [raws]}, [raw_part], None, None
 
     def finished(part, series, told):
         at = steps + part
@@ -426,7 +426,7 @@
         if at == RAW_WAIT:
             after.append(raw[1])
         if at == INVERSE_STEP:
-            inverse = invert_classes(date_pairs, run_counts, [counts if coded is None else coded])
+            inverse = invert_classes(date_pairs, run_counts, [] if coded is None else [coded])
             after.append(inverse)
         if at == steps - 1:
             for part in range(FINISHED_AHEAD):
@@ -438,8 +438,8 @@
         if at in SWAPS:
             swapped(away, *SWAPS[at])
         if at == RAW_STEP:
-            raw_other, _ = lax.optimization_barrier((raw_other, coded))
-            raw = [raw_own, lax.ppermute(raw_other, "ifg", swap)]
+            raws, _ = lax.optimization_barrier((raws, coded))
+            raw = [raws[local_pairs:], lax.ppermute(raws[:local_pairs], "ifg", swap)]
 
     for part in range(FINISHED_AHEAD, parts):
         series = finished(part, series, False)[0]

time: 128 us -> 127 us (level)
  starting transfers between devices: 54.3 us -> 57.5 us
  waiting for transfers between devices: 23.1 us -> 20.2 us
    ppermute x15, starting transfers between devices: 34.3 us -> 39.9 us  [solve_by_sums(): lax.ppermute(coded, 'ifg', line_permutation(links))]
    ppermute x8, waiting for transfers between devices: 2.91 us -> 1.18 us  [swapped(): here = lax.ppermute(away, 'ifg', swap)]
    ppermute x8, starting transfers between devices: 9.77 us -> 8.37 us  [swapped(): here = lax.ppermute(away, 'ifg', swap)]
    ppermute x3 -> x2, starting transfers between devices: 4.13 us -> 3.14 us  [the longest x1 2.54 us: solve_by_sums(): raws = lax.ppermute(both_sides, 'ifg', near)]
  transfers between devices with their start and end apart: 29 -> 28, of which waited for: 8 -> 7; matrix products, arithmetic and copies ran while one was open for 2% -> 2% of each run, Pallas kernels for 32% -> 32%
where the time goes in v9:
time: 127 us; the launch traced here: 126 us
  starting transfers between devices  57.5 us (45%)
  Pallas kernels  43.7 us (34%)
  waiting for transfers between devices  20.2 us (16%)
  local copies, waits for them, and re-layouts  3.72 us (3%)
    ppermute x15, starting transfers between devices, solve_by_sums(): lax.ppermute(coded, 'ifg', line_permutation(links))  39.9 us
    pallas_call x11, Pallas kernels, step(): pl.pallas_call(functools.partial(step_kernel, at, layout, len(earlier), s...  23.3 us
    ppermute x15, waiting for transfers between devices, solve_by_sums(): lax.ppermute(coded, 'ifg', line_permutation(links))  19 us
    pallas_call x4, Pallas kernels, finish(): pl.pallas_call(functools.partial(finish_kernel, at, layout, HALVES, len(r...  13.7 us
    ppermute x8, starting transfers between devices, swapped(): here = lax.ppermute(away, 'ifg', swap)  8.37 us
    pallas_call x1, Pallas kernels, invert_classes(): pl.pallas_call(inverse_kernel, out_shape=jax.ShapeDtypeStruct(shape, F32)...  6.77 us
    ppermute x3, starting transfers between devices, solve_by_sums(): counts.append(lax.ppermute(run_counts, 'ifg', line_permutation(links)))  6.11 us
    ppermute x1, starting transfers between devices, solve_by_sums(): raws = lax.ppermute(both_sides, 'ifg', near)  2.54 us
  transfers between devices with their start and end apart: 28, of which 7 were waited for; matrix products, arithmetic and copies ran while one was open for 2% of the time, Pallas kernels for 32%

profile of v9, /device:TPU:0, one launch (start us, length us, event | category | flops | bytes accessed | tf_op | source)
XLA Modules:
  0.0 126.4 jit_solution(9252843483015043721)
XLA Ops:
  0.0 1.1 dynamic-slice_bitcast_fusion
  1.2 0.8 fusion.counts_ref
  2.1 5.1 %collective-permute-start.2 = (s32[2]{0:T(128)S(1)}, s32[2]{0:T(128)S(1)}, u32[]{:S(2)}, u32[]{:S(2)}) collective-permute-start(s32[2]{0:T(128)S(1)} %fusion.counts_ref), channel_id=1, source_target_pairs={{0,24},{4,28},{8,0},{12,4},{16,8},{20,12},{24,16},{28,20},{1,25},{... | collective-permute-start | bytes 32 | tf_op jit(solution)/shard_map/ppermute | solution.py:403
  7.2 1.0 collective-permute-start
  8.2 1.5 %collective-permute-start.3 = (bf16[128,2048]{1,0:T(8,128)(2,1)S(1)}, bf16[128,2048]{1,0:T(8,128)(2,1)S(1)}, u32[]{:S(2)}, u32[]{:S(2)}) collective-permute-start(bf16[128,2048]{1,0:T(8,128)(2,1)S(1)} %dynamic-slice_bitcast_fusion), channel_id=1, source_target_pairs={{0,4},{4,0},{8,12},{12,8},{16,20},{20,16},{24,28},{28,24},{1,5},{5... | collective-permute-start | bytes 1572872 | tf_op jit(solution)/shard_map/ppermute | solution.py:385
  9.7 1.1 dynamic-slice_bitcast_fusion.2
  10.8 2.5 %collective-permute-start.4 = (bf16[256,1024]{1,0:T(8,128)(2,1)S(1)}, bf16[256,1024]{1,0:T(8,128)(2,1)S(1)}, u32[]{:S(2)}, u32[]{:S(2)}) collective-permute-start(bf16[256,1024]{1,0:T(8,128)(2,1)S(1)} %pad_maximum_fusion), channel_id=1, source_target_pairs={{0,8},{4,12},{8,0},{12,4},{16,24},{20,28},{24,16},{28,20},{1,9},{5... | collective-permute-start | bytes 1572872 | tf_op jit(solution)/shard_map/ppermute | solution.py:408
  13.3 0.7 copy-done.1
  14.0 6.8 %invert_classes_0.1.rest_1_.inverse_ref = f32[2,256,256]{2,1,0:T(8,128)S(1)} custom-call(s32[2]{0:T(128)S(1)} %fusion.counts_ref, s32[2,1024]{1,0:T(2,128)S(1)} %copy-done.1), custom_call_target="tpu_custom_call" | custom-call | flops 1024 | bytes 1024 | tf_op jit(solution)/shard_map/invert_classes_0/pallas_call | solution.py:103
  20.8 0.7 fusion.1.table
  21.7 2.1 %sum_step_00.1 = (s16[1616,128]{1,0:T(8,128)(2,1)S(1)}, bf16[128,1024]{1,0:T(8,128)(2,1)S(1)}) custom-call(s32[53]{0:T(128)S(1)} %fusion.1.table, s32[8]{0:T(128)S(1)} %pad_add_fusion.1.counts, s32[2,512]{1,0:T(2,128)S(1)} %pad_add_fusion.pairs_ref, bf16[128,32768]{1,0:T(8,128)(2,1)} %bitcast.12, bf16[128,2048]{1,0:T(8,128)(2,1)S(1)} %collective-permute-done.3.partner_ref, ...), custom_call_target="tpu_custom_call" | custom-call | flops 10000000000 | bytes 30000000 | tf_op jit(solution)/shard_map/sum_step_00/pallas_call | solution.py:245
  23.7 1.4 %collective-permute-start.8 = (bf16[128,1024]{1,0:T(8,128)(2,1)S(1)}, bf16[128,1024]{1,0:T(8,128)(2,1)S(1)}, u32[]{:S(2)}, u32[]{:S(2)}) collective-permute-start(bf16[128,1024]{1,0:T(8,128)(2,1)S(1)} %get-tuple-element.31), channel_id=1, source_target_pairs={{0,4},{4,0},{8,12},{12,8},{16,20},{20,16},{24,28},{28,24},{1,5},{5... | collective-permute-start | bytes 786440 | tf_op jit(solution)/shard_map/ppermute | solution.py:385
  25.1 2.0 %collective-permute-start.7 = (s16[1616,128]{1,0:T(8,128)(2,1)S(1)}, s16[1616,128]{1,0:T(8,128)(2,1)S(1)}, u32[]{:S(2)}, u32[]{:S(2)}) collective-permute-start(s16[1616,128]{1,0:T(8,128)(2,1)S(1)} %get-tuple-element.26.rest_1_), channel_id=1, source_target_pairs={{0,8},{4,12},{8,0},{12,4},{16,24},{20,28},{24,16},{28,20},{1,9},{5... | collective-permute-start | bytes 1241096 | tf_op jit(solution)/shard_map/ppermute | solution.py:436
  27.1 2.2 %sum_step_01.1 = (s16[1616,128]{1,0:T(8,128)(2,1)S(1)}, bf16[128,2048]{1,0:T(8,128)(2,1)S(1)}) custom-call(s32[53]{0:T(128)S(1)} %fusion.1.table, s32[8]{0:T(128)S(1)} %pad_add_fusion.1.counts, s32[2,512]{1,0:T(2,128)S(1)} %pad_add_fusion.pairs_ref, bf16[128,32768]{1,0:T(8,128)(2,1)} %bitcast.14, bf16[128,2048]{1,0:T(8,128)(2,1)S(1)} %collective-permute-done.3.partner_ref, ...), custom_call_target="tpu_custom_call" | custom-call | flops 10000000000 | bytes 30000000 | tf_op jit(solution)/shard_map/sum_step_01/pallas_call | solution.py:245
  29.4 0.7 collective-permute-start.5
  30.1 1.2 collective-permute-done.8.partner_ref
  31.2 6.4 %collective-permute-done.7.rest_2_.rest_0_ = s16[1616,128]{1,0:T(8,128)(2,1)S(1)} collective-permute-done((s16[1616,128]{1,0:T(8,128)(2,1)S(1)}, s16[1616,128]{1,0:T(8,128)(2,1)S(1)}, u32[]{:S(2)}, u32[]{:S(2)}) %collective-permute-start.7) | collective-permute-done | bytes 413728 | tf_op jit(solution)/shard_map/ppermute | solution.py:436
  37.6 2.2 %sum_step_02.1 = (s16[1616,128]{1,0:T(8,128)(2,1)S(1)}, bf16[128,2048]{1,0:T(8,128)(2,1)S(1)}) custom-call(s32[53]{0:T(128)S(1)} %fusion.1.table, s32[8]{0:T(128)S(1)} %pad_add_fusion.1.counts, s32[2,512]{1,0:T(2,128)S(1)} %pad_add_fusion.pairs_ref, bf16[128,32768]{1,0:T(8,128)(2,1)} %bitcast.16, bf16[128,1024]{1,0:T(8,128)(2,1)S(1)} %collective-permute-done.8.partner_ref, ...), custom_call_target="tpu_custom_call" | custom-call | flops 10000000000 | bytes 30000000 | tf_op jit(solution)/shard_map/sum_step_02/pallas_call | solution.py:245
  39.8 2.0 %collective-permute-start.9 = (s16[1616,128]{1,0:T(8,128)(2,1)S(1)}, s16[1616,128]{1,0:T(8,128)(2,1)S(1)}, u32[]{:S(2)}, u32[]{:S(2)}) collective-permute-start(s16[1616,128]{1,0:T(8,128)(2,1)S(1)} %get-tuple-element.32.rest_1_), channel_id=1, source_target_pairs={{0,8},{4,12},{8,0},{12,4},{16,24},{20,28},{24,16},{28,20},{1,9},{5... | collective-permute-start | bytes 1241096 | tf_op jit(solution)/shard_map/ppermute | solution.py:436
  42.5 1.5 %collective-permute-start.14 = (bf16[128,2048]{1,0:T(8,128)(2,1)S(1)}, bf16[128,2048]{1,0:T(8,128)(2,1)S(1)}, u32[]{:S(2)}, u32[]{:S(2)}) collective-permute-start(bf16[128,2048]{1,0:T(8,128)(2,1)S(1)} %get-tuple-element.36), channel_id=1, source_target_pairs={{0,4},{4,0},{8,12},{12,8},{16,20},{20,16},{24,28},{28,24},{1,5},{5... | collective-permute-start | bytes 1572872 | tf_op jit(solution)/shard_map/ppermute | solution.py:385
  44.0 2.5 %collective-permute-done.6.rest_2_.rest_1_.rest_0_ = s16[1616,128]{1,0:T(8,128)(2,1)S(1)} collective-permute-done((s16[1616,128]{1,0:T(8,128)(2,1)S(1)}, s16[1616,128]{1,0:T(8,128)(2,1)S(1)}, u32[]{:S(2)}, u32[]{:S(2)}) %collective-permute-start.6) | collective-permute-done | bytes 413728 | tf_op jit(solution)/shard_map/ppermute | solution.py:436
  46.5 2.0 %sum_step_04.1.rest_2_ = s16[1616,128]{1,0:T(8,128)(2,1)S(1)} custom-call(s32[53]{0:T(128)S(1)} %fusion.1.table, s32[8]{0:T(128)S(1)} %pad_add_fusion.1.counts, s32[2,512]{1,0:T(2,128)S(1)} %pad_add_fusion.pairs_ref, bf16[128,32768]{1,0:T(8,128)(2,1)} %bitcast.18, bf16[128,2048]{1,0:T(8,128)(2,1)S(1)} %collective-permute-done.5.partner_ref, ...), custom_call_target="tpu_custom_call" | custom-call | flops 10000000000 | bytes 30000000 | tf_op jit(solution)/shard_map/sum_step_04/pallas_call | solution.py:245
  48.5 0.7 collective-permute-start.15
  49.2 5.4 %collective-permute-start.13 = (s16[1616,128]{1,0:T(8,128)(2,1)S(1)}, s16[1616,128]{1,0:T(8,128)(2,1)S(1)}, u32[]{:S(2)}, u32[]{:S(2)}) collective-permute-start(s16[1616,128]{1,0:T(8,128)(2,1)S(1)} %sum_step_04.1.rest_2_), channel_id=1, source_target_pairs={{0,8},{4,12},{24,16},{28,20},{1,9},{5,13},{25,17},{29,21},{2,10},{... | collective-permute-start | bytes 1241096 | tf_op jit(solution)/shard_map/ppermute | solution.py:436
  54.6 2.2 %sum_step_05.1 = (s16[1616,128]{1,0:T(8,128)(2,1)S(1)}, bf16[128,2048]{1,0:T(8,128)(2,1)S(1)}) custom-call(s32[53]{0:T(128)S(1)} %fusion.1.table, s32[8]{0:T(128)S(1)} %pad_add_fusion.1.counts, s32[2,512]{1,0:T(2,128)S(1)} %pad_add_fusion.pairs_ref, bf16[128,32768]{1,0:T(8,128)(2,1)} %bitcast.19, bf16[128,2048]{1,0:T(8,128)(2,1)S(1)} %collective-permute-done.5.partner_ref, ...), custom_call_target="tpu_custom_call" | custom-call | flops 10000000000 | bytes 30000000 | tf_op jit(solution)/shard_map/sum_step_05/pallas_call | solution.py:245
  57.5 5.6 %collective-permute-start.12 = (s16[1616,128]{1,0:T(8,128)(2,1)S(1)}, s16[1616,128]{1,0:T(8,128)(2,1)S(1)}, u32[]{:S(2)}, u32[]{:S(2)}) collective-permute-start(s16[1616,128]{1,0:T(8,128)(2,1)S(1)} %get-tuple-element.35.rest_1_), channel_id=1, source_target_pairs={{0,8},{4,12},{24,16},{28,20},{1,9},{5,13},{25,17},{29,21},{2,10},{... | collective-permute-start | bytes 1241096 | tf_op jit(solution)/shard_map/ppermute | solution.py:436
  63.1 0.7 collective-permute-start.11
  63.9 2.0 %sum_step_06.1.rest_3_ = s16[1616,128]{1,0:T(8,128)(2,1)S(1)} custom-call(s32[53]{0:T(128)S(1)} %fusion.1.table, s32[8]{0:T(128)S(1)} %pad_add_fusion.1.counts, s32[2,512]{1,0:T(2,128)S(1)} %pad_add_fusion.pairs_ref, bf16[128,32768]{1,0:T(8,128)(2,1)} %bitcast.21, bf16[128,2048]{1,0:T(8,128)(2,1)S(1)} %collective-permute-done.14.partner_ref, ...), custom_call_target="tpu_custom_call" | custom-call | flops 10000000000 | bytes 30000000 | tf_op jit(solution)/shard_map/sum_step_06/pallas_call | solution.py:245
  66.6 6.5 %collective-permute-start.17 = (s16[1616,128]{1,0:T(8,128)(2,1)S(1)}, s16[1616,128]{1,0:T(8,128)(2,1)S(1)}, u32[]{:S(2)}, u32[]{:S(2)}) collective-permute-start(s16[1616,128]{1,0:T(8,128)(2,1)S(1)} %sum_step_06.1.rest_3_), channel_id=1, source_target_pairs={{0,8},{4,12},{24,16},{28,20},{1,9},{5,13},{25,17},{29,21},{2,10},{... | collective-permute-start | bytes 1241096 | tf_op jit(solution)/shard_map/ppermute | solution.py:436
  73.1 2.3 %sum_step_07.1 = (s16[1616,128]{1,0:T(8,128)(2,1)S(1)}, bf16[128,2048]{1,0:T(8,128)(2,1)S(1)}) custom-call(s32[53]{0:T(128)S(1)} %fusion.1.table, s32[8]{0:T(128)S(1)} %pad_add_fusion.1.counts, s32[2,512]{1,0:T(2,128)S(1)} %pad_add_fusion.pairs_ref, bf16[128,32768]{1,0:T(8,128)(2,1)} %bitcast.22, bf16[128,2048]{1,0:T(8,128)(2,1)S(1)} %collective-permute-done.14.partner_ref, ...), custom_call_target="tpu_custom_call" | custom-call | flops 10000000000 | bytes 30000000 | tf_op jit(solution)/shard_map/sum_step_07/pallas_call | solution.py:245
  76.1 6.9 %collective-permute-start.19 = (s16[1616,128]{1,0:T(8,128)(2,1)S(1)}, s16[1616,128]{1,0:T(8,128)(2,1)S(1)}, u32[]{:S(2)}, u32[]{:S(2)}) collective-permute-start(s16[1616,128]{1,0:T(8,128)(2,1)S(1)} %get-tuple-element.37.rest_2_), channel_id=1, source_target_pairs={{0,8},{4,12},{24,16},{28,20},{1,9},{5,13},{25,17},{29,21},{2,10},{... | collective-permute-start | bytes 1241096 | tf_op jit(solution)/shard_map/ppermute | solution.py:436
  83.0 1.0 collective-permute-start.22
  84.0 2.2 %sum_step_08.1 = (s16[1616,128]{1,0:T(8,128)(2,1)S(1)}, bf16[128,2048]{1,0:T(8,128)(2,1)S(1)}) custom-call(s32[53]{0:T(128)S(1)} %fusion.1.table, s32[8]{0:T(128)S(1)} %pad_add_fusion.1.counts, s32[2,512]{1,0:T(2,128)S(1)} %pad_add_fusion.pairs_ref, bf16[128,32768]{1,0:T(8,128)(2,1)} %bitcast.24, bf16[128,2048]{1,0:T(8,128)(2,1)S(1)} %collective-permute-done.11.partner_ref, ...), custom_call_target="tpu_custom_call" | custom-call | flops 10000000000 | bytes 30000000 | tf_op jit(solution)/shard_map/sum_step_08/pallas_call | solution.py:245
  86.3 0.9 collective-permute-start.23
  87.7 5.3 %collective-permute-done.19.rest_3_.rest_0_ = s16[1616,128]{1,0:T(8,128)(2,1)S(1)} collective-permute-done((s16[1616,128]{1,0:T(8,128)(2,1)S(1)}, s16[1616,128]{1,0:T(8,128)(2,1)S(1)}, u32[]{:S(2)}, u32[]{:S(2)}) %collective-permute-start.19) | collective-permute-done | bytes 413728 | tf_op jit(solution)/shard_map/ppermute | solution.py:436
  93.0 2.2 %sum_step_09.1 = (s16[1616,128]{1,0:T(8,128)(2,1)S(1)}, bf16[128,2048]{1,0:T(8,128)(2,1)S(1)}) custom-call(s32[53]{0:T(128)S(1)} %fusion.1.table, s32[8]{0:T(128)S(1)} %pad_add_fusion.1.counts, s32[2,512]{1,0:T(2,128)S(1)} %pad_add_fusion.pairs_ref, bf16[128,32768]{1,0:T(8,128)(2,1)} %bitcast.26, bf16[128,2048]{1,0:T(8,128)(2,1)S(1)} %collective-permute-done.11.partner_ref, ...), custom_call_target="tpu_custom_call" | custom-call | flops 10000000000 | bytes 30000000 | tf_op jit(solution)/shard_map/sum_step_09/pallas_call | solution.py:245
  95.2 2.5 %collective-permute-start.24 = (s16[1616,128]{1,0:T(8,128)(2,1)S(1)}, s16[1616,128]{1,0:T(8,128)(2,1)S(1)}, u32[]{:S(2)}, u32[]{:S(2)}) collective-permute-start(s16[1616,128]{1,0:T(8,128)(2,1)S(1)} %get-tuple-element.41.rest_1_), channel_id=1, source_target_pairs={{0,8},{4,12},{8,24},{12,28},{16,0},{20,4},{24,16},{28,20},{1,9},{5... | collective-permute-start | bytes 1241096 | tf_op jit(solution)/shard_map/ppermute | solution.py:436
  97.7 1.0 collective-permute-start.21
  98.7 3.1 %collective-permute-done.23.rest_2_ = s16[1616,128]{1,0:T(8,128)(2,1)S(1)} collective-permute-done((s16[1616,128]{1,0:T(8,128)(2,1)S(1)}, s16[1616,128]{1,0:T(8,128)(2,1)S(1)}, u32[]{:S(2)}, u32[]{:S(2)}) %collective-permute-start.23) | collective-permute-done | bytes 413728 | tf_op jit(solution)/shard_map/ppermute | solution.py:436
  101.8 2.0 %sum_step_10.1.rest_1_ = s16[1616,128]{1,0:T(8,128)(2,1)S(1)} custom-call(s32[53]{0:T(128)S(1)} %fusion.1.table, s32[8]{0:T(128)S(1)} %pad_add_fusion.1.counts, s32[2,512]{1,0:T(2,128)S(1)} %pad_add_fusion.pairs_ref, bf16[128,32768]{1,0:T(8,128)(2,1)} %bitcast.28, bf16[128,2048]{1,0:T(8,128)(2,1)S(1)} %collective-permute-done.22.partner_ref, ...), custom_call_target="tpu_custom_call" | custom-call | flops 10000000000 | bytes 30000000 | tf_op jit(solution)/shard_map/sum_step_10/pallas_call | solution.py:245
  103.8 2.5 %collective-permute-start.27 = (s16[1616,128]{1,0:T(8,128)(2,1)S(1)}, s16[1616,128]{1,0:T(8,128)(2,1)S(1)}, u32[]{:S(2)}, u32[]{:S(2)}) collective-permute-start(s16[1616,128]{1,0:T(8,128)(2,1)S(1)} %sum_step_10.1.rest_1_), channel_id=1, source_target_pairs={{0,8},{4,12},{8,24},{12,28},{16,0},{20,4},{24,16},{28,20},{1,9},{5... | collective-permute-start | bytes 1241096 | tf_op jit(solution)/shard_map/ppermute | solution.py:436
  106.4 3.4 %finish_0.1 = (f32[200,4096]{1,0:T(8,128)}, f32[8,128]{1,0:T(8,128)S(1)}) custom-call(s32[53]{0:T(128)S(1)} %fusion.1.table, s32[8]{0:T(128)S(1)} %pad_add_fusion.1.counts, s32[2,512]{1,0:T(2,128)S(1)} %pad_add_fusion.pairs_ref, bf16[128,32768]{1,0:T(8,128)(2,1)} %bitcast.29, bf16[128,2048]{1,0:T(8,128)(2,1)S(1)} %collective-permute-done.25.partner_ref, ...), custom_call_target="tpu_custom_call" | custom-call | flops 1024 | bytes 1024 | tf_op jit(solution)/shard_map/finish_0/pallas_call | solution.py:336
  109.8 0.9 collective-permute-done.24.rest_2_
  110.7 2.0 %sum_step_11.1 = s16[1616,128]{1,0:T(8,128)(2,1)S(1)} custom-call(s32[53]{0:T(128)S(1)} %fusion.1.table, s32[8]{0:T(128)S(1)} %pad_add_fusion.1.counts, s32[2,512]{1,0:T(2,128)S(1)} %pad_add_fusion.pairs_ref, bf16[128,32768]{1,0:T(8,128)(2,1)} %bitcast.30, bf16[128,2048]{1,0:T(8,128)(2,1)S(1)} %collective-permute-done.22.partner_ref, ...), custom_call_target="tpu_custom_call" | custom-call | flops 10000000000 | bytes 30000000 | tf_op jit(solution)/shard_map/sum_step_11/pallas_call | solution.py:245
  112.7 2.7 %collective-permute-start.26 = (s16[1616,128]{1,0:T(8,128)(2,1)S(1)}, s16[1616,128]{1,0:T(8,128)(2,1)S(1)}, u32[]{:S(2)}, u32[]{:S(2)}) collective-permute-start(s16[1616,128]{1,0:T(8,128)(2,1)S(1)} %sum_step_11.1), channel_id=1, source_target_pairs={{0,8},{4,12},{8,24},{12,28},{16,0},{20,4},{24,16},{28,20},{1,9},{5... | collective-permute-start | bytes 1241096 | tf_op jit(solution)/shard_map/ppermute | solution.py:436
  115.4 3.4 %finish_1.1.rest_3_ = f32[200,4096]{1,0:T(8,128)} custom-call(s32[53]{0:T(128)S(1)} %fusion.1.table, s32[8]{0:T(128)S(1)} %pad_add_fusion.1.counts, s32[2,512]{1,0:T(2,128)S(1)} %pad_add_fusion.pairs_ref, bf16[128,32768]{1,0:T(8,128)(2,1)} %bitcast.31, bf16[128,2048]{1,0:T(8,128)(2,1)S(1)} %collective-permute-done.25.partner_ref, ...), custom_call_target="tpu_custom_call", output_to_operand_aliasing={{}: (9, {})} | custom-call | flops 1024 | bytes 1024 | tf_op jit(solution)/shard_map/finish_1/pallas_call | solution.py:336
  118.8 3.4 %finish_2.1.rest_4_ = f32[200,4096]{1,0:T(8,128)} custom-call(s32[53]{0:T(128)S(1)} %fusion.1.table, s32[8]{0:T(128)S(1)} %pad_add_fusion.1.counts, s32[2,512]{1,0:T(2,128)S(1)} %pad_add_fusion.pairs_ref, bf16[128,32768]{1,0:T(8,128)(2,1)} %bitcast.32, bf16[128,2048]{1,0:T(8,128)(2,1)S(1)} %collective-permute-done.21.partner_ref, ...), custom_call_target="tpu_custom_call", output_to_operand_aliasing={{}: (9, {})} | custom-call | flops 1024 | bytes 1024 | tf_op jit(solution)/shard_map/finish_2/pallas_call | solution.py:336
  122.9 3.5 %finish_3.1 = f32[200,4096]{1,0:T(8,128)} custom-call(s32[53]{0:T(128)S(1)} %fusion.1.table, s32[8]{0:T(128)S(1)} %pad_add_fusion.1.counts, s32[2,512]{1,0:T(2,128)S(1)} %pad_add_fusion.pairs_ref, bf16[128,32768]{1,0:T(8,128)(2,1)} %bitcast.33, bf16[128,2048]{1,0:T(8,128)(2,1)S(1)} %collective-permute-done.21.partner_ref, ...), custom_call_target="tpu_custom_call", output_to_operand_aliasing={{}: (10, {})} | custom-call | flops 1024 | bytes 1024 | tf_op jit(solution)/shard_map/finish_3/pallas_call | solution.py:336
  (41 shorter events, 4.3 us)
Async XLA Ops:
  0.0 1.1 copy-start
  0.0 21.5 %copy-start.2 = (s32[2,1024]{1,0:T(2,128)S(1)}, s32[2,1024]{1,0:T(2,128)}, u32[]{:S(2)}) copy-start(s32[2,1024]{1,0:T(2,128)} %pairs_ref.1) | copy-start | bytes 24580
  2.1 19.5 %collective-permute-start.2 = (s32[2]{0:T(128)S(1)}, s32[2]{0:T(128)S(1)}, u32[]{:S(2)}, u32[]{:S(2)}) collective-permute-start(s32[2]{0:T(128)S(1)} %fusion.counts_ref), channel_id=1, source_target_pairs={{0,24},{4,28},{8,0},{12,4},{16,8},{20,12},{24,16},{28,20},{1,25},{... | collective-permute-start | bytes 32 | tf_op jit(solution)/shard_map/ppermute | solution.py:403
  7.2 14.4 %collective-permute-start.1 = (s32[2]{0:T(128)S(1)}, s32[2]{0:T(128)S(1)}, u32[]{:S(2)}, u32[]{:S(2)}) collective-permute-start(s32[2]{0:T(128)S(1)} %fusion.counts_ref), channel_id=1, source_target_pairs={{0,16},{4,20},{8,24},{12,28},{16,0},{20,4},{24,8},{28,12},{1,17},{... | collective-permute-start | bytes 32 | tf_op jit(solution)/shard_map/ppermute | solution.py:403
  7.2 14.4 %collective-permute-start = (s32[2]{0:T(128)S(1)}, s32[2]{0:T(128)S(1)}, u32[]{:S(2)}, u32[]{:S(2)}) collective-permute-start(s32[2]{0:T(128)S(1)} %fusion.counts_ref), channel_id=1, source_target_pairs={{0,8},{4,12},{8,16},{12,20},{16,24},{20,28},{24,0},{28,4},{1,9},{5... | collective-permute-start | bytes 32 | tf_op jit(solution)/shard_map/ppermute | solution.py:403
  8.2 13.5 %collective-permute-start.3 = (bf16[128,2048]{1,0:T(8,128)(2,1)S(1)}, bf16[128,2048]{1,0:T(8,128)(2,1)S(1)}, u32[]{:S(2)}, u32[]{:S(2)}) collective-permute-start(bf16[128,2048]{1,0:T(8,128)(2,1)S(1)} %dynamic-slice_bitcast_fusion), channel_id=1, source_target_pairs={{0,4},{4,0},{8,12},{12,8},{16,20},{20,16},{24,28},{28,24},{1,5},{5... | collective-permute-start | bytes 1572872 | tf_op jit(solution)/shard_map/ppermute | solution.py:385
  10.8 16.3 %collective-permute-start.4 = (bf16[256,1024]{1,0:T(8,128)(2,1)S(1)}, bf16[256,1024]{1,0:T(8,128)(2,1)S(1)}, u32[]{:S(2)}, u32[]{:S(2)}) collective-permute-start(bf16[256,1024]{1,0:T(8,128)(2,1)S(1)} %pad_maximum_fusion), channel_id=1, source_target_pairs={{0,8},{4,12},{8,0},{12,4},{16,24},{20,28},{24,16},{28,20},{1,9},{5... | collective-permute-start | bytes 1572872 | tf_op jit(solution)/shard_map/ppermute | solution.py:408
  13.3 0.7 copy-start.1
  23.7 7.5 %collective-permute-start.8 = (bf16[128,1024]{1,0:T(8,128)(2,1)S(1)}, bf16[128,1024]{1,0:T(8,128)(2,1)S(1)}, u32[]{:S(2)}, u32[]{:S(2)}) collective-permute-start(bf16[128,1024]{1,0:T(8,128)(2,1)S(1)} %get-tuple-element.31), channel_id=1, source_target_pairs={{0,4},{4,0},{8,12},{12,8},{16,20},{20,16},{24,28},{28,24},{1,5},{5... | collective-permute-start | bytes 786440 | tf_op jit(solution)/shard_map/ppermute | solution.py:385
  25.1 12.5 %collective-permute-start.7 = (s16[1616,128]{1,0:T(8,128)(2,1)S(1)}, s16[1616,128]{1,0:T(8,128)(2,1)S(1)}, u32[]{:S(2)}, u32[]{:S(2)}) collective-permute-start(s16[1616,128]{1,0:T(8,128)(2,1)S(1)} %get-tuple-element.26.rest_1_), channel_id=1, source_target_pairs={{0,8},{4,12},{8,0},{12,4},{16,24},{20,28},{24,16},{28,20},{1,9},{5... | collective-permute-start | bytes 1241096 | tf_op jit(solution)/shard_map/ppermute | solution.py:436
  29.3 17.2 %collective-permute-start.6 = (s16[1616,128]{1,0:T(8,128)(2,1)S(1)}, s16[1616,128]{1,0:T(8,128)(2,1)S(1)}, u32[]{:S(2)}, u32[]{:S(2)}) collective-permute-start(s16[1616,128]{1,0:T(8,128)(2,1)S(1)} %get-tuple-element.30.rest_1_), channel_id=1, source_target_pairs={{0,8},{4,12},{8,0},{12,4},{16,24},{20,28},{24,16},{28,20},{1,9},{5... | collective-permute-start | bytes 1241096 | tf_op jit(solution)/shard_map/ppermute | solution.py:436
  29.4 17.1 %collective-permute-start.5 = (bf16[128,2048]{1,0:T(8,128)(2,1)S(1)}, bf16[128,2048]{1,0:T(8,128)(2,1)S(1)}, u32[]{:S(2)}, u32[]{:S(2)}) collective-permute-start(bf16[128,2048]{1,0:T(8,128)(2,1)S(1)} %get-tuple-element.29), channel_id=1, source_target_pairs={{0,4},{4,0},{8,12},{12,8},{16,20},{20,16},{24,28},{28,24},{1,5},{5... | collective-permute-start | bytes 1572872 | tf_op jit(solution)/shard_map/ppermute | solution.py:385
  39.8 14.8 %collective-permute-start.9 = (s16[1616,128]{1,0:T(8,128)(2,1)S(1)}, s16[1616,128]{1,0:T(8,128)(2,1)S(1)}, u32[]{:S(2)}, u32[]{:S(2)}) collective-permute-start(s16[1616,128]{1,0:T(8,128)(2,1)S(1)} %get-tuple-element.32.rest_1_), channel_id=1, source_target_pairs={{0,8},{4,12},{8,0},{12,4},{16,24},{20,28},{24,16},{28,20},{1,9},{5... | collective-permute-start | bytes 1241096 | tf_op jit(solution)/shard_map/ppermute | solution.py:436
  41.9 12.7 %collective-permute-start.10 = (bf16[128,1024]{1,0:T(8,128)(2,1)S(1)}, bf16[128,1024]{1,0:T(8,128)(2,1)S(1)}, u32[]{:S(2)}, u32[]{:S(2)}) collective-permute-start(bf16[128,1024]{1,0:T(8,128)(2,1)S(1)} %get-tuple-element.48), channel_id=1, source_target_pairs={{0,4},{4,0},{8,12},{12,8},{16,20},{20,16},{24,28},{28,24},{1,5},{5... | collective-permute-start | bytes 786440 | tf_op jit(solution)/shard_map/ppermute | solution.py:442
  42.5 20.6 %collective-permute-start.14 = (bf16[128,2048]{1,0:T(8,128)(2,1)S(1)}, bf16[128,2048]{1,0:T(8,128)(2,1)S(1)}, u32[]{:S(2)}, u32[]{:S(2)}) collective-permute-start(bf16[128,2048]{1,0:T(8,128)(2,1)S(1)} %get-tuple-element.36), channel_id=1, source_target_pairs={{0,4},{4,0},{8,12},{12,8},{16,20},{20,16},{24,28},{28,24},{1,5},{5... | collective-permute-start | bytes 1572872 | tf_op jit(solution)/shard_map/ppermute | solution.py:385
  48.5 15.4 %collective-permute-start.15 = (s16[1616,128]{1,0:T(8,128)(2,1)S(1)}, s16[1616,128]{1,0:T(8,128)(2,1)S(1)}, u32[]{:S(2)}, u32[]{:S(2)}) collective-permute-start(s16[1616,128]{1,0:T(8,128)(2,1)S(1)} %sum_step_04.1.rest_2_), channel_id=1, source_target_pairs={{8,16},{12,20},{16,8},{20,12},{9,17},{13,21},{17,9},{21,13},{10,18... | collective-permute-start | bytes 1241096 | tf_op jit(solution)/shard_map/ppermute | solution.py:436
  49.2 14.7 %collective-permute-start.13 = (s16[1616,128]{1,0:T(8,128)(2,1)S(1)}, s16[1616,128]{1,0:T(8,128)(2,1)S(1)}, u32[]{:S(2)}, u32[]{:S(2)}) collective-permute-start(s16[1616,128]{1,0:T(8,128)(2,1)S(1)} %sum_step_04.1.rest_2_), channel_id=1, source_target_pairs={{0,8},{4,12},{24,16},{28,20},{1,9},{5,13},{25,17},{29,21},{2,10},{... | collective-permute-start | bytes 1241096 | tf_op jit(solution)/shard_map/ppermute | solution.py:436
  56.8 16.2 %collective-permute-start.16 = (s16[1616,128]{1,0:T(8,128)(2,1)S(1)}, s16[1616,128]{1,0:T(8,128)(2,1)S(1)}, u32[]{:S(2)}, u32[]{:S(2)}) collective-permute-start(s16[1616,128]{1,0:T(8,128)(2,1)S(1)} %get-tuple-element.35.rest_1_), channel_id=1, source_target_pairs={{8,16},{12,20},{16,8},{20,12},{9,17},{13,21},{17,9},{21,13},{10,18... | collective-permute-start | bytes 1241096 | tf_op jit(solution)/shard_map/ppermute | solution.py:436
  57.5 15.6 %collective-permute-start.12 = (s16[1616,128]{1,0:T(8,128)(2,1)S(1)}, s16[1616,128]{1,0:T(8,128)(2,1)S(1)}, u32[]{:S(2)}, u32[]{:S(2)}) collective-permute-start(s16[1616,128]{1,0:T(8,128)(2,1)S(1)} %get-tuple-element.35.rest_1_), channel_id=1, source_target_pairs={{0,8},{4,12},{24,16},{28,20},{1,9},{5,13},{25,17},{29,21},{2,10},{... | collective-permute-start | bytes 1241096 | tf_op jit(solution)/shard_map/ppermute | solution.py:436
  63.1 20.9 %collective-permute-start.11 = (bf16[128,2048]{1,0:T(8,128)(2,1)S(1)}, bf16[128,2048]{1,0:T(8,128)(2,1)S(1)}, u32[]{:S(2)}, u32[]{:S(2)}) collective-permute-start(bf16[128,2048]{1,0:T(8,128)(2,1)S(1)} %get-tuple-element.34), channel_id=1, source_target_pairs={{0,4},{4,0},{8,12},{12,8},{16,20},{20,16},{24,28},{28,24},{1,5},{5... | collective-permute-start | bytes 1572872 | tf_op jit(solution)/shard_map/ppermute | solution.py:385
  65.9 17.1 %collective-permute-start.18 = (s16[1616,128]{1,0:T(8,128)(2,1)S(1)}, s16[1616,128]{1,0:T(8,128)(2,1)S(1)}, u32[]{:S(2)}, u32[]{:S(2)}) collective-permute-start(s16[1616,128]{1,0:T(8,128)(2,1)S(1)} %sum_step_06.1.rest_3_), channel_id=1, source_target_pairs={{8,16},{12,20},{16,8},{20,12},{9,17},{13,21},{17,9},{21,13},{10,18... | collective-permute-start | bytes 1241096 | tf_op jit(solution)/shard_map/ppermute | solution.py:436
  66.6 17.5 %collective-permute-start.17 = (s16[1616,128]{1,0:T(8,128)(2,1)S(1)}, s16[1616,128]{1,0:T(8,128)(2,1)S(1)}, u32[]{:S(2)}, u32[]{:S(2)}) collective-permute-start(s16[1616,128]{1,0:T(8,128)(2,1)S(1)} %sum_step_06.1.rest_3_), channel_id=1, source_target_pairs={{0,8},{4,12},{24,16},{28,20},{1,9},{5,13},{25,17},{29,21},{2,10},{... | collective-permute-start | bytes 1241096 | tf_op jit(solution)/shard_map/ppermute | solution.py:436
  75.4 12.3 %collective-permute-start.20 = (s16[1616,128]{1,0:T(8,128)(2,1)S(1)}, s16[1616,128]{1,0:T(8,128)(2,1)S(1)}, u32[]{:S(2)}, u32[]{:S(2)}) collective-permute-start(s16[1616,128]{1,0:T(8,128)(2,1)S(1)} %get-tuple-element.37.rest_2_), channel_id=1, source_target_pairs={{8,16},{12,20},{16,8},{20,12},{9,17},{13,21},{17,9},{21,13},{10,18... | collective-permute-start | bytes 1241096 | tf_op jit(solution)/shard_map/ppermute | solution.py:436
  76.1 16.9 %collective-permute-start.19 = (s16[1616,128]{1,0:T(8,128)(2,1)S(1)}, s16[1616,128]{1,0:T(8,128)(2,1)S(1)}, u32[]{:S(2)}, u32[]{:S(2)}) collective-permute-start(s16[1616,128]{1,0:T(8,128)(2,1)S(1)} %get-tuple-element.37.rest_2_), channel_id=1, source_target_pairs={{0,8},{4,12},{24,16},{28,20},{1,9},{5,13},{25,17},{29,21},{2,10},{... | collective-permute-start | bytes 1241096 | tf_op jit(solution)/shard_map/ppermute | solution.py:436
  83.0 15.7 %collective-permute-start.22 = (bf16[128,2048]{1,0:T(8,128)(2,1)S(1)}, bf16[128,2048]{1,0:T(8,128)(2,1)S(1)}, u32[]{:S(2)}, u32[]{:S(2)}) collective-permute-start(bf16[128,2048]{1,0:T(8,128)(2,1)S(1)} %get-tuple-element.40), channel_id=1, source_target_pairs={{0,4},{4,0},{8,12},{12,8},{16,20},{20,16},{24,28},{28,24},{1,5},{5... | collective-permute-start | bytes 1572872 | tf_op jit(solution)/shard_map/ppermute | solution.py:385
  86.3 15.6 %collective-permute-start.23 = (s16[1616,128]{1,0:T(8,128)(2,1)S(1)}, s16[1616,128]{1,0:T(8,128)(2,1)S(1)}, u32[]{:S(2)}, u32[]{:S(2)}) collective-permute-start(s16[1616,128]{1,0:T(8,128)(2,1)S(1)} %get-tuple-element.38.rest_2_), channel_id=1, source_target_pairs={{0,8},{4,12},{8,24},{12,28},{16,0},{20,4},{24,16},{28,20},{1,9},{5... | collective-permute-start | bytes 1241096 | tf_op jit(solution)/shard_map/ppermute | solution.py:436
  87.1 19.3 %collective-permute-start.25 = (bf16[128,2048]{1,0:T(8,128)(2,1)S(1)}, bf16[128,2048]{1,0:T(8,128)(2,1)S(1)}, u32[]{:S(2)}, u32[]{:S(2)}) collective-permute-start(bf16[128,2048]{1,0:T(8,128)(2,1)S(1)} %get-tuple-element.42), channel_id=1, source_target_pairs={{0,4},{4,0},{8,12},{12,8},{16,20},{20,16},{24,28},{28,24},{1,5},{5... | collective-permute-start | bytes 1572872 | tf_op jit(solution)/shard_map/ppermute | solution.py:385
  95.2 15.5 %collective-permute-start.24 = (s16[1616,128]{1,0:T(8,128)(2,1)S(1)}, s16[1616,128]{1,0:T(8,128)(2,1)S(1)}, u32[]{:S(2)}, u32[]{:S(2)}) collective-permute-start(s16[1616,128]{1,0:T(8,128)(2,1)S(1)} %get-tuple-element.41.rest_1_), channel_id=1, source_target_pairs={{0,8},{4,12},{8,24},{12,28},{16,0},{20,4},{24,16},{28,20},{1,9},{5... | collective-permute-start | bytes 1241096 | tf_op jit(solution)/shard_map/ppermute | solution.py:436
  97.7 21.1 %collective-permute-start.21 = (bf16[128,2048]{1,0:T(8,128)(2,1)S(1)}, bf16[128,2048]{1,0:T(8,128)(2,1)S(1)}, u32[]{:S(2)}, u32[]{:S(2)}) collective-permute-start(bf16[128,2048]{1,0:T(8,128)(2,1)S(1)} %get-tuple-element.39), channel_id=1, source_target_pairs={{0,4},{4,0},{8,12},{12,8},{16,20},{20,16},{24,28},{28,24},{1,5},{5... | collective-permute-start | bytes 1572872 | tf_op jit(solution)/shard_map/ppermute | solution.py:385
  103.8 15.0 %collective-permute-start.27 = (s16[1616,128]{1,0:T(8,128)(2,1)S(1)}, s16[1616,128]{1,0:T(8,128)(2,1)S(1)}, u32[]{:S(2)}, u32[]{:S(2)}) collective-permute-start(s16[1616,128]{1,0:T(8,128)(2,1)S(1)} %sum_step_10.1.rest_1_), channel_id=1, source_target_pairs={{0,8},{4,12},{8,24},{12,28},{16,0},{20,4},{24,16},{28,20},{1,9},{5... | collective-permute-start | bytes 1241096 | tf_op jit(solution)/shard_map/ppermute | solution.py:436
  112.7 10.2 %collective-permute-start.26 = (s16[1616,128]{1,0:T(8,128)(2,1)S(1)}, s16[1616,128]{1,0:T(8,128)(2,1)S(1)}, u32[]{:S(2)}, u32[]{:S(2)}) collective-permute-start(s16[1616,128]{1,0:T(8,128)(2,1)S(1)} %sum_step_11.1), channel_id=1, source_target_pairs={{0,8},{4,12},{8,24},{12,28},{16,0},{20,4},{24,16},{28,20},{1,9},{5... | collective-permute-start | bytes 1241096 | tf_op jit(solution)/shard_map/ppermute | solution.py:436

commit v10 on v9

--- a/solution.py
+++ b/solution.py
@@ -420,7 +420,7 @@
     for at in [each for each in range(steps) if each != raw_part]:
         earlier = [] if at < parts else raw if at == parts + raw_part else [received[at - parts][0]]
         after = [] if coded is None else [coded]
-        after += received[sent[-FLIGHT]] if len(sent) >= FLIGHT else []
+        after += received[sent[-FLIGHT]][::-1] if len(sent) >= FLIGHT else []
         if at in SWAP_WAITS:
             after.append(partner_of[SWAP_WAITS[at]][0])
         if at == RAW_WAIT:

time: 127 us -> 127 us (level)
  starting transfers between devices: 57.5 us -> 50.3 us
  waiting for transfers between devices: 20.2 us -> 26.4 us
    ppermute x15, starting transfers between devices: 39.9 us -> 32 us  [solve_by_sums(): lax.ppermute(coded, 'ifg', line_permutation(links))]
    ppermute x15, waiting for transfers between devices: 19 us -> 23.2 us  [solve_by_sums(): lax.ppermute(coded, 'ifg', line_permutation(links))]
    ppermute x8, waiting for transfers between devices: 1.18 us -> 3.2 us  [swapped(): here = lax.ppermute(away, 'ifg', swap)]
  transfers between devices with their start and end apart: 28 -> 28, of which waited for: 7 -> 12; matrix products, arithmetic and copies ran while one was open for 2% -> 2% of each run, Pallas kernels for 32% -> 32%
where the time goes in v10:
time: 127 us; the launch traced here: 126 us
  starting transfers between devices  50.3 us (40%)
  Pallas kernels  44.5 us (35%)
  waiting for transfers between devices  26.4 us (21%)
  local copies, waits for them, and re-layouts  3.72 us (3%)
    ppermute x15, starting transfers between devices, solve_by_sums(): lax.ppermute(coded, 'ifg', line_permutation(links))  32 us
    pallas_call x11, Pallas kernels, step(): pl.pallas_call(functools.partial(step_kernel, at, layout, len(earlier), s...  23.3 us
    ppermute x15, waiting for transfers between devices, solve_by_sums(): lax.ppermute(coded, 'ifg', line_permutation(links))  23.2 us
    pallas_call x4, Pallas kernels, finish(): pl.pallas_call(functools.partial(finish_kernel, at, layout, HALVES, len(r...  13.7 us
    ppermute x8, starting transfers between devices, swapped(): here = lax.ppermute(away, 'ifg', swap)  9.08 us
    pallas_call x1, Pallas kernels, invert_classes(): pl.pallas_call(inverse_kernel, out_shape=jax.ShapeDtypeStruct(shape, F32)...  7.56 us
    ppermute x3, starting transfers between devices, solve_by_sums(): counts.append(lax.ppermute(run_counts, 'ifg', line_permutation(links)))  6.11 us
    ppermute x8, waiting for transfers between devices, swapped(): here = lax.ppermute(away, 'ifg', swap)  3.2 us
  transfers between devices with their start and end apart: 28, of which 12 were waited for; matrix products, arithmetic and copies ran while one was open for 2% of the time, Pallas kernels for 32%

profile of v10, /device:TPU:0, one launch (start us, length us, event | category | flops | bytes accessed | tf_op | source)
XLA Modules:
  0.0 126.2 jit_solution(6588278299829298253)
XLA Ops:
  0.0 1.1 dynamic-slice_bitcast_fusion
  1.2 0.8 fusion.counts_ref
  2.1 5.1 %collective-permute-start.2 = (s32[2]{0:T(128)S(1)}, s32[2]{0:T(128)S(1)}, u32[]{:S(2)}, u32[]{:S(2)}) collective-permute-start(s32[2]{0:T(128)S(1)} %fusion.counts_ref), channel_id=1, source_target_pairs={{0,24},{4,28},{8,0},{12,4},{16,8},{20,12},{24,16},{28,20},{1,25},{... | collective-permute-start | bytes 32 | tf_op jit(solution)/shard_map/ppermute | solution.py:403
  7.2 1.0 collective-permute-start
  8.2 1.5 %collective-permute-start.3 = (bf16[128,2048]{1,0:T(8,128)(2,1)S(1)}, bf16[128,2048]{1,0:T(8,128)(2,1)S(1)}, u32[]{:S(2)}, u32[]{:S(2)}) collective-permute-start(bf16[128,2048]{1,0:T(8,128)(2,1)S(1)} %dynamic-slice_bitcast_fusion), channel_id=1, source_target_pairs={{0,4},{4,0},{8,12},{12,8},{16,20},{20,16},{24,28},{28,24},{1,5},{5... | collective-permute-start | bytes 1572872 | tf_op jit(solution)/shard_map/ppermute | solution.py:385
  9.7 1.1 dynamic-slice_bitcast_fusion.2
  10.8 2.5 %collective-permute-start.4 = (bf16[256,1024]{1,0:T(8,128)(2,1)S(1)}, bf16[256,1024]{1,0:T(8,128)(2,1)S(1)}, u32[]{:S(2)}, u32[]{:S(2)}) collective-permute-start(bf16[256,1024]{1,0:T(8,128)(2,1)S(1)} %pad_maximum_fusion), channel_id=1, source_target_pairs={{0,8},{4,12},{8,0},{12,4},{16,24},{20,28},{24,16},{28,20},{1,9},{5... | collective-permute-start | bytes 1572872 | tf_op jit(solution)/shard_map/ppermute | solution.py:408
  14.0 7.6 %invert_classes_0.1.rest_1_.inverse_ref = f32[2,256,256]{2,1,0:T(8,128)S(1)} custom-call(s32[2]{0:T(128)S(1)} %fusion.counts_ref, s32[2,1024]{1,0:T(2,128)S(1)} %copy-done.1), custom_call_target="tpu_custom_call" | custom-call | flops 1024 | bytes 1024 | tf_op jit(solution)/shard_map/invert_classes_0/pallas_call | solution.py:103
  22.5 2.1 %sum_step_00.1 = (s16[1616,128]{1,0:T(8,128)(2,1)S(1)}, bf16[128,1024]{1,0:T(8,128)(2,1)S(1)}) custom-call(s32[53]{0:T(128)S(1)} %fusion.1.table, s32[8]{0:T(128)S(1)} %pad_add_fusion.1.counts, s32[2,512]{1,0:T(2,128)S(1)} %pad_add_fusion.pairs_ref, bf16[128,32768]{1,0:T(8,128)(2,1)} %bitcast.12, bf16[128,2048]{1,0:T(8,128)(2,1)S(1)} %collective-permute-done.3.partner_ref, ...), custom_call_target="tpu_custom_call" | custom-call | flops 10000000000 | bytes 30000000 | tf_op jit(solution)/shard_map/sum_step_00/pallas_call | solution.py:245
  25.1 2.0 %collective-permute-start.7 = (s16[1616,128]{1,0:T(8,128)(2,1)S(1)}, s16[1616,128]{1,0:T(8,128)(2,1)S(1)}, u32[]{:S(2)}, u32[]{:S(2)}) collective-permute-start(s16[1616,128]{1,0:T(8,128)(2,1)S(1)} %get-tuple-element.26.rest_1_), channel_id=1, source_target_pairs={{0,8},{4,12},{8,0},{12,4},{16,24},{20,28},{24,16},{28,20},{1,9},{5... | collective-permute-start | bytes 1241096 | tf_op jit(solution)/shard_map/ppermute | solution.py:436
  27.1 2.2 %sum_step_01.1 = (s16[1616,128]{1,0:T(8,128)(2,1)S(1)}, bf16[128,2048]{1,0:T(8,128)(2,1)S(1)}) custom-call(s32[53]{0:T(128)S(1)} %fusion.1.table, s32[8]{0:T(128)S(1)} %pad_add_fusion.1.counts, s32[2,512]{1,0:T(2,128)S(1)} %pad_add_fusion.pairs_ref, bf16[128,32768]{1,0:T(8,128)(2,1)} %bitcast.14, bf16[128,2048]{1,0:T(8,128)(2,1)S(1)} %collective-permute-done.3.partner_ref, ...), custom_call_target="tpu_custom_call" | custom-call | flops 10000000000 | bytes 30000000 | tf_op jit(solution)/shard_map/sum_step_01/pallas_call | solution.py:245
  29.4 1.5 %collective-permute-start.5 = (bf16[128,2048]{1,0:T(8,128)(2,1)S(1)}, bf16[128,2048]{1,0:T(8,128)(2,1)S(1)}, u32[]{:S(2)}, u32[]{:S(2)}) collective-permute-start(bf16[128,2048]{1,0:T(8,128)(2,1)S(1)} %get-tuple-element.29), channel_id=1, source_target_pairs={{0,4},{4,0},{8,12},{12,8},{16,20},{20,16},{24,28},{28,24},{1,5},{5... | collective-permute-start | bytes 1572872 | tf_op jit(solution)/shard_map/ppermute | solution.py:385
  30.9 2.0 %collective-permute-done.8.partner_ref = bf16[128,1024]{1,0:T(8,128)(2,1)S(1)} collective-permute-done((bf16[128,1024]{1,0:T(8,128)(2,1)S(1)}, bf16[128,1024]{1,0:T(8,128)(2,1)S(1)}, u32[]{:S(2)}, u32[]{:S(2)}) %collective-permute-start.8) | collective-permute-done | bytes 262176 | tf_op jit(solution)/shard_map/ppermute | solution.py:385
  32.9 4.7 %collective-permute-done.7.rest_2_.rest_0_ = s16[1616,128]{1,0:T(8,128)(2,1)S(1)} collective-permute-done((s16[1616,128]{1,0:T(8,128)(2,1)S(1)}, s16[1616,128]{1,0:T(8,128)(2,1)S(1)}, u32[]{:S(2)}, u32[]{:S(2)}) %collective-permute-start.7) | collective-permute-done | bytes 413728 | tf_op jit(solution)/shard_map/ppermute | solution.py:436
  37.6 2.2 %sum_step_02.1 = (s16[1616,128]{1,0:T(8,128)(2,1)S(1)}, bf16[128,2048]{1,0:T(8,128)(2,1)S(1)}) custom-call(s32[53]{0:T(128)S(1)} %fusion.1.table, s32[8]{0:T(128)S(1)} %pad_add_fusion.1.counts, s32[2,512]{1,0:T(2,128)S(1)} %pad_add_fusion.pairs_ref, bf16[128,32768]{1,0:T(8,128)(2,1)} %bitcast.16, bf16[128,1024]{1,0:T(8,128)(2,1)S(1)} %collective-permute-done.8.partner_ref, ...), custom_call_target="tpu_custom_call" | custom-call | flops 10000000000 | bytes 30000000 | tf_op jit(solution)/shard_map/sum_step_02/pallas_call | solution.py:245
  39.8 2.0 %collective-permute-start.9 = (s16[1616,128]{1,0:T(8,128)(2,1)S(1)}, s16[1616,128]{1,0:T(8,128)(2,1)S(1)}, u32[]{:S(2)}, u32[]{:S(2)}) collective-permute-start(s16[1616,128]{1,0:T(8,128)(2,1)S(1)} %get-tuple-element.32.rest_1_), channel_id=1, source_target_pairs={{0,8},{4,12},{8,0},{12,4},{16,24},{20,28},{24,16},{28,20},{1,9},{5... | collective-permute-start | bytes 1241096 | tf_op jit(solution)/shard_map/ppermute | solution.py:436
  42.5 1.5 %collective-permute-start.14 = (bf16[128,2048]{1,0:T(8,128)(2,1)S(1)}, bf16[128,2048]{1,0:T(8,128)(2,1)S(1)}, u32[]{:S(2)}, u32[]{:S(2)}) collective-permute-start(bf16[128,2048]{1,0:T(8,128)(2,1)S(1)} %get-tuple-element.36), channel_id=1, source_target_pairs={{0,4},{4,0},{8,12},{12,8},{16,20},{20,16},{24,28},{28,24},{1,5},{5... | collective-permute-start | bytes 1572872 | tf_op jit(solution)/shard_map/ppermute | solution.py:385
  44.0 2.5 %collective-permute-done.6.rest_2_.rest_1_.rest_0_ = s16[1616,128]{1,0:T(8,128)(2,1)S(1)} collective-permute-done((s16[1616,128]{1,0:T(8,128)(2,1)S(1)}, s16[1616,128]{1,0:T(8,128)(2,1)S(1)}, u32[]{:S(2)}, u32[]{:S(2)}) %collective-permute-start.6) | collective-permute-done | bytes 413728 | tf_op jit(solution)/shard_map/ppermute | solution.py:436
  46.5 2.0 %sum_step_04.1.rest_2_ = s16[1616,128]{1,0:T(8,128)(2,1)S(1)} custom-call(s32[53]{0:T(128)S(1)} %fusion.1.table, s32[8]{0:T(128)S(1)} %pad_add_fusion.1.counts, s32[2,512]{1,0:T(2,128)S(1)} %pad_add_fusion.pairs_ref, bf16[128,32768]{1,0:T(8,128)(2,1)} %bitcast.18, bf16[128,2048]{1,0:T(8,128)(2,1)S(1)} %collective-permute-done.5.partner_ref, ...), custom_call_target="tpu_custom_call" | custom-call | flops 10000000000 | bytes 30000000 | tf_op jit(solution)/shard_map/sum_step_04/pallas_call | solution.py:245
  49.2 5.4 %collective-permute-start.13 = (s16[1616,128]{1,0:T(8,128)(2,1)S(1)}, s16[1616,128]{1,0:T(8,128)(2,1)S(1)}, u32[]{:S(2)}, u32[]{:S(2)}) collective-permute-start(s16[1616,128]{1,0:T(8,128)(2,1)S(1)} %sum_step_04.1.rest_2_), channel_id=1, source_target_pairs={{0,8},{4,12},{24,16},{28,20},{1,9},{5,13},{25,17},{29,21},{2,10},{... | collective-permute-start | bytes 1241096 | tf_op jit(solution)/shard_map/ppermute | solution.py:436
  54.6 2.2 %sum_step_05.1 = (s16[1616,128]{1,0:T(8,128)(2,1)S(1)}, bf16[128,2048]{1,0:T(8,128)(2,1)S(1)}) custom-call(s32[53]{0:T(128)S(1)} %fusion.1.table, s32[8]{0:T(128)S(1)} %pad_add_fusion.1.counts, s32[2,512]{1,0:T(2,128)S(1)} %pad_add_fusion.pairs_ref, bf16[128,32768]{1,0:T(8,128)(2,1)} %bitcast.19, bf16[128,2048]{1,0:T(8,128)(2,1)S(1)} %collective-permute-done.5.partner_ref, ...), custom_call_target="tpu_custom_call" | custom-call | flops 10000000000 | bytes 30000000 | tf_op jit(solution)/shard_map/sum_step_05/pallas_call | solution.py:245
  57.5 5.6 %collective-permute-start.12 = (s16[1616,128]{1,0:T(8,128)(2,1)S(1)}, s16[1616,128]{1,0:T(8,128)(2,1)S(1)}, u32[]{:S(2)}, u32[]{:S(2)}) collective-permute-start(s16[1616,128]{1,0:T(8,128)(2,1)S(1)} %get-tuple-element.35.rest_1_), channel_id=1, source_target_pairs={{0,8},{4,12},{24,16},{28,20},{1,9},{5,13},{25,17},{29,21},{2,10},{... | collective-permute-start | bytes 1241096 | tf_op jit(solution)/shard_map/ppermute | solution.py:436
  63.1 1.2 collective-permute-start.11
  64.3 2.0 %sum_step_06.1.rest_3_ = s16[1616,128]{1,0:T(8,128)(2,1)S(1)} custom-call(s32[53]{0:T(128)S(1)} %fusion.1.table, s32[8]{0:T(128)S(1)} %pad_add_fusion.1.counts, s32[2,512]{1,0:T(2,128)S(1)} %pad_add_fusion.pairs_ref, bf16[128,32768]{1,0:T(8,128)(2,1)} %bitcast.21, bf16[128,2048]{1,0:T(8,128)(2,1)S(1)} %collective-permute-done.14.partner_ref, ...), custom_call_target="tpu_custom_call" | custom-call | flops 10000000000 | bytes 30000000 | tf_op jit(solution)/shard_map/sum_step_06/pallas_call | solution.py:245
  66.3 3.3 %collective-permute-start.18 = (s16[1616,128]{1,0:T(8,128)(2,1)S(1)}, s16[1616,128]{1,0:T(8,128)(2,1)S(1)}, u32[]{:S(2)}, u32[]{:S(2)}) collective-permute-start(s16[1616,128]{1,0:T(8,128)(2,1)S(1)} %sum_step_06.1.rest_3_), channel_id=1, source_target_pairs={{0,8},{4,12},{24,16},{28,20},{1,9},{5,13},{25,17},{29,21},{2,10},{... | collective-permute-start | bytes 1241096 | tf_op jit(solution)/shard_map/ppermute | solution.py:436
  70.4 2.7 %collective-permute-done.12.rest_5_.rest_1_ = s16[1616,128]{1,0:T(8,128)(2,1)S(1)} collective-permute-done((s16[1616,128]{1,0:T(8,128)(2,1)S(1)}, s16[1616,128]{1,0:T(8,128)(2,1)S(1)}, u32[]{:S(2)}, u32[]{:S(2)}) %collective-permute-start.12) | collective-permute-done | bytes 413728 | tf_op jit(solution)/shard_map/ppermute | solution.py:436
  73.1 2.3 %sum_step_07.1 = (s16[1616,128]{1,0:T(8,128)(2,1)S(1)}, bf16[128,2048]{1,0:T(8,128)(2,1)S(1)}) custom-call(s32[53]{0:T(128)S(1)} %fusion.1.table, s32[8]{0:T(128)S(1)} %pad_add_fusion.1.counts, s32[2,512]{1,0:T(2,128)S(1)} %pad_add_fusion.pairs_ref, bf16[128,32768]{1,0:T(8,128)(2,1)} %bitcast.22, bf16[128,2048]{1,0:T(8,128)(2,1)S(1)} %collective-permute-done.14.partner_ref, ...), custom_call_target="tpu_custom_call" | custom-call | flops 10000000000 | bytes 30000000 | tf_op jit(solution)/shard_map/sum_step_07/pallas_call | solution.py:245
  75.4 4.4 %collective-permute-start.20 = (s16[1616,128]{1,0:T(8,128)(2,1)S(1)}, s16[1616,128]{1,0:T(8,128)(2,1)S(1)}, u32[]{:S(2)}, u32[]{:S(2)}) collective-permute-start(s16[1616,128]{1,0:T(8,128)(2,1)S(1)} %get-tuple-element.37.rest_2_), channel_id=1, source_target_pairs={{0,8},{4,12},{24,16},{28,20},{1,9},{5,13},{25,17},{29,21},{2,10},{... | collective-permute-start | bytes 1241096 | tf_op jit(solution)/shard_map/ppermute | solution.py:436
  80.5 1.5 %collective-permute-done.18.rest_4_.rest_0_ = s16[1616,128]{1,0:T(8,128)(2,1)S(1)} collective-permute-done((s16[1616,128]{1,0:T(8,128)(2,1)S(1)}, s16[1616,128]{1,0:T(8,128)(2,1)S(1)}, u32[]{:S(2)}, u32[]{:S(2)}) %collective-permute-start.18) | collective-permute-done | bytes 413728 | tf_op jit(solution)/shard_map/ppermute | solution.py:436
  81.9 1.1 collective-permute-start.22
  83.0 2.2 %sum_step_08.1 = (s16[1616,128]{1,0:T(8,128)(2,1)S(1)}, bf16[128,2048]{1,0:T(8,128)(2,1)S(1)}) custom-call(s32[53]{0:T(128)S(1)} %fusion.1.table, s32[8]{0:T(128)S(1)} %pad_add_fusion.1.counts, s32[2,512]{1,0:T(2,128)S(1)} %pad_add_fusion.pairs_ref, bf16[128,32768]{1,0:T(8,128)(2,1)} %bitcast.24, bf16[128,2048]{1,0:T(8,128)(2,1)S(1)} %collective-permute-done.11.partner_ref, ...), custom_call_target="tpu_custom_call" | custom-call | flops 10000000000 | bytes 30000000 | tf_op jit(solution)/shard_map/sum_step_08/pallas_call | solution.py:245
  85.3 2.6 %collective-permute-start.23 = (s16[1616,128]{1,0:T(8,128)(2,1)S(1)}, s16[1616,128]{1,0:T(8,128)(2,1)S(1)}, u32[]{:S(2)}, u32[]{:S(2)}) collective-permute-start(s16[1616,128]{1,0:T(8,128)(2,1)S(1)} %get-tuple-element.38.rest_2_), channel_id=1, source_target_pairs={{0,8},{4,12},{8,24},{12,28},{16,0},{20,4},{24,16},{28,20},{1,9},{5... | collective-permute-start | bytes 1241096 | tf_op jit(solution)/shard_map/ppermute | solution.py:436
  87.8 0.9 collective-permute-start.25
  88.7 2.1 %collective-permute-done.20.rest_4_.rest_0_ = s16[1616,128]{1,0:T(8,128)(2,1)S(1)} collective-permute-done((s16[1616,128]{1,0:T(8,128)(2,1)S(1)}, s16[1616,128]{1,0:T(8,128)(2,1)S(1)}, u32[]{:S(2)}, u32[]{:S(2)}) %collective-permute-start.20) | collective-permute-done | bytes 413728 | tf_op jit(solution)/shard_map/ppermute | solution.py:436
  90.8 2.2 %sum_step_09.1 = (s16[1616,128]{1,0:T(8,128)(2,1)S(1)}, bf16[128,2048]{1,0:T(8,128)(2,1)S(1)}) custom-call(s32[53]{0:T(128)S(1)} %fusion.1.table, s32[8]{0:T(128)S(1)} %pad_add_fusion.1.counts, s32[2,512]{1,0:T(2,128)S(1)} %pad_add_fusion.pairs_ref, bf16[128,32768]{1,0:T(8,128)(2,1)} %bitcast.26, bf16[128,2048]{1,0:T(8,128)(2,1)S(1)} %collective-permute-done.11.partner_ref, ...), custom_call_target="tpu_custom_call" | custom-call | flops 10000000000 | bytes 30000000 | tf_op jit(solution)/shard_map/sum_step_09/pallas_call | solution.py:245
  93.0 2.8 %collective-permute-start.24 = (s16[1616,128]{1,0:T(8,128)(2,1)S(1)}, s16[1616,128]{1,0:T(8,128)(2,1)S(1)}, u32[]{:S(2)}, u32[]{:S(2)}) collective-permute-start(s16[1616,128]{1,0:T(8,128)(2,1)S(1)} %get-tuple-element.41.rest_1_), channel_id=1, source_target_pairs={{0,8},{4,12},{8,24},{12,28},{16,0},{20,4},{24,16},{28,20},{1,9},{5... | collective-permute-start | bytes 1241096 | tf_op jit(solution)/shard_map/ppermute | solution.py:436
  95.8 0.8 collective-permute-start.21
  96.8 5.0 %collective-permute-done.23.rest_2_ = s16[1616,128]{1,0:T(8,128)(2,1)S(1)} collective-permute-done((s16[1616,128]{1,0:T(8,128)(2,1)S(1)}, s16[1616,128]{1,0:T(8,128)(2,1)S(1)}, u32[]{:S(2)}, u32[]{:S(2)}) %collective-permute-start.23) | collective-permute-done | bytes 413728 | tf_op jit(solution)/shard_map/ppermute | solution.py:436
  101.8 2.0 %sum_step_10.1.rest_1_ = s16[1616,128]{1,0:T(8,128)(2,1)S(1)} custom-call(s32[53]{0:T(128)S(1)} %fusion.1.table, s32[8]{0:T(128)S(1)} %pad_add_fusion.1.counts, s32[2,512]{1,0:T(2,128)S(1)} %pad_add_fusion.pairs_ref, bf16[128,32768]{1,0:T(8,128)(2,1)} %bitcast.28, bf16[128,2048]{1,0:T(8,128)(2,1)S(1)} %collective-permute-done.22.partner_ref, ...), custom_call_target="tpu_custom_call" | custom-call | flops 10000000000 | bytes 30000000 | tf_op jit(solution)/shard_map/sum_step_10/pallas_call | solution.py:245
  104.2 1.0 collective-permute-done.25.partner_ref
  105.2 3.4 %finish_0.1 = (f32[200,4096]{1,0:T(8,128)}, f32[8,128]{1,0:T(8,128)S(1)}) custom-call(s32[53]{0:T(128)S(1)} %fusion.1.table, s32[8]{0:T(128)S(1)} %pad_add_fusion.1.counts, s32[2,512]{1,0:T(2,128)S(1)} %pad_add_fusion.pairs_ref, bf16[128,32768]{1,0:T(8,128)(2,1)} %bitcast.29, bf16[128,2048]{1,0:T(8,128)(2,1)S(1)} %collective-permute-done.25.partner_ref, ...), custom_call_target="tpu_custom_call" | custom-call | flops 1024 | bytes 1024 | tf_op jit(solution)/shard_map/finish_0/pallas_call | solution.py:336
  108.6 2.1 %collective-permute-done.24.rest_2_ = s16[1616,128]{1,0:T(8,128)(2,1)S(1)} collective-permute-done((s16[1616,128]{1,0:T(8,128)(2,1)S(1)}, s16[1616,128]{1,0:T(8,128)(2,1)S(1)}, u32[]{:S(2)}, u32[]{:S(2)}) %collective-permute-start.24) | collective-permute-done | bytes 413728 | tf_op jit(solution)/shard_map/ppermute | solution.py:436
  110.7 2.0 %sum_step_11.1 = s16[1616,128]{1,0:T(8,128)(2,1)S(1)} custom-call(s32[53]{0:T(128)S(1)} %fusion.1.table, s32[8]{0:T(128)S(1)} %pad_add_fusion.1.counts, s32[2,512]{1,0:T(2,128)S(1)} %pad_add_fusion.pairs_ref, bf16[128,32768]{1,0:T(8,128)(2,1)} %bitcast.30, bf16[128,2048]{1,0:T(8,128)(2,1)S(1)} %collective-permute-done.22.partner_ref, ...), custom_call_target="tpu_custom_call" | custom-call | flops 10000000000 | bytes 30000000 | tf_op jit(solution)/shard_map/sum_step_11/pallas_call | solution.py:245
  113.4 3.4 %finish_1.1.rest_3_ = f32[200,4096]{1,0:T(8,128)} custom-call(s32[53]{0:T(128)S(1)} %fusion.1.table, s32[8]{0:T(128)S(1)} %pad_add_fusion.1.counts, s32[2,512]{1,0:T(2,128)S(1)} %pad_add_fusion.pairs_ref, bf16[128,32768]{1,0:T(8,128)(2,1)} %bitcast.31, bf16[128,2048]{1,0:T(8,128)(2,1)S(1)} %collective-permute-done.25.partner_ref, ...), custom_call_target="tpu_custom_call", output_to_operand_aliasing={{}: (9, {})} | custom-call | flops 1024 | bytes 1024 | tf_op jit(solution)/shard_map/finish_1/pallas_call | solution.py:336
  116.8 1.5 %collective-permute-done.27.rest_2_ = s16[1616,128]{1,0:T(8,128)(2,1)S(1)} collective-permute-done((s16[1616,128]{1,0:T(8,128)(2,1)S(1)}, s16[1616,128]{1,0:T(8,128)(2,1)S(1)}, u32[]{:S(2)}, u32[]{:S(2)}) %collective-permute-start.27) | collective-permute-done | bytes 413728 | tf_op jit(solution)/shard_map/ppermute | solution.py:436
  118.2 3.4 %finish_2.1.rest_4_ = f32[200,4096]{1,0:T(8,128)} custom-call(s32[53]{0:T(128)S(1)} %fusion.1.table, s32[8]{0:T(128)S(1)} %pad_add_fusion.1.counts, s32[2,512]{1,0:T(2,128)S(1)} %pad_add_fusion.pairs_ref, bf16[128,32768]{1,0:T(8,128)(2,1)} %bitcast.32, bf16[128,2048]{1,0:T(8,128)(2,1)S(1)} %collective-permute-done.21.partner_ref, ...), custom_call_target="tpu_custom_call", output_to_operand_aliasing={{}: (9, {})} | custom-call | flops 1024 | bytes 1024 | tf_op jit(solution)/shard_map/finish_2/pallas_call | solution.py:336
  121.6 1.0 collective-permute-done.26.rest_3_
  122.7 3.5 %finish_3.1 = f32[200,4096]{1,0:T(8,128)} custom-call(s32[53]{0:T(128)S(1)} %fusion.1.table, s32[8]{0:T(128)S(1)} %pad_add_fusion.1.counts, s32[2,512]{1,0:T(2,128)S(1)} %pad_add_fusion.pairs_ref, bf16[128,32768]{1,0:T(8,128)(2,1)} %bitcast.33, bf16[128,2048]{1,0:T(8,128)(2,1)S(1)} %collective-permute-done.21.partner_ref, ...), custom_call_target="tpu_custom_call", output_to_operand_aliasing={{}: (10, {})} | custom-call | flops 1024 | bytes 1024 | tf_op jit(solution)/shard_map/finish_3/pallas_call | solution.py:336
  (41 shorter events, 6.9 us)
Async XLA Ops:
  0.0 1.1 copy-start
  0.0 22.3 %copy-start.2 = (s32[2,1024]{1,0:T(2,128)S(1)}, s32[2,1024]{1,0:T(2,128)}, u32[]{:S(2)}) copy-start(s32[2,1024]{1,0:T(2,128)} %pairs_ref.1) | copy-start | bytes 24580
  2.1 20.3 %collective-permute-start.2 = (s32[2]{0:T(128)S(1)}, s32[2]{0:T(128)S(1)}, u32[]{:S(2)}, u32[]{:S(2)}) collective-permute-start(s32[2]{0:T(128)S(1)} %fusion.counts_ref), channel_id=1, source_target_pairs={{0,24},{4,28},{8,0},{12,4},{16,8},{20,12},{24,16},{28,20},{1,25},{... | collective-permute-start | bytes 32 | tf_op jit(solution)/shard_map/ppermute | solution.py:403
  7.2 15.2 %collective-permute-start.1 = (s32[2]{0:T(128)S(1)}, s32[2]{0:T(128)S(1)}, u32[]{:S(2)}, u32[]{:S(2)}) collective-permute-start(s32[2]{0:T(128)S(1)} %fusion.counts_ref), channel_id=1, source_target_pairs={{0,16},{4,20},{8,24},{12,28},{16,0},{20,4},{24,8},{28,12},{1,17},{... | collective-permute-start | bytes 32 | tf_op jit(solution)/shard_map/ppermute | solution.py:403
  7.2 15.2 %collective-permute-start = (s32[2]{0:T(128)S(1)}, s32[2]{0:T(128)S(1)}, u32[]{:S(2)}, u32[]{:S(2)}) collective-permute-start(s32[2]{0:T(128)S(1)} %fusion.counts_ref), channel_id=1, source_target_pairs={{0,8},{4,12},{8,16},{12,20},{16,24},{20,28},{24,0},{28,4},{1,9},{5... | collective-permute-start | bytes 32 | tf_op jit(solution)/shard_map/ppermute | solution.py:403
  8.2 14.3 %collective-permute-start.3 = (bf16[128,2048]{1,0:T(8,128)(2,1)S(1)}, bf16[128,2048]{1,0:T(8,128)(2,1)S(1)}, u32[]{:S(2)}, u32[]{:S(2)}) collective-permute-start(bf16[128,2048]{1,0:T(8,128)(2,1)S(1)} %dynamic-slice_bitcast_fusion), channel_id=1, source_target_pairs={{0,4},{4,0},{8,12},{12,8},{16,20},{20,16},{24,28},{28,24},{1,5},{5... | collective-permute-start | bytes 1572872 | tf_op jit(solution)/shard_map/ppermute | solution.py:385
  10.8 16.3 %collective-permute-start.4 = (bf16[256,1024]{1,0:T(8,128)(2,1)S(1)}, bf16[256,1024]{1,0:T(8,128)(2,1)S(1)}, u32[]{:S(2)}, u32[]{:S(2)}) collective-permute-start(bf16[256,1024]{1,0:T(8,128)(2,1)S(1)} %pad_maximum_fusion), channel_id=1, source_target_pairs={{0,8},{4,12},{8,0},{12,4},{16,24},{20,28},{24,16},{28,20},{1,9},{5... | collective-permute-start | bytes 1572872 | tf_op jit(solution)/shard_map/ppermute | solution.py:408
  13.3 0.7 copy-start.1
  24.5 8.4 %collective-permute-start.8 = (bf16[128,1024]{1,0:T(8,128)(2,1)S(1)}, bf16[128,1024]{1,0:T(8,128)(2,1)S(1)}, u32[]{:S(2)}, u32[]{:S(2)}) collective-permute-start(bf16[128,1024]{1,0:T(8,128)(2,1)S(1)} %get-tuple-element.31), channel_id=1, source_target_pairs={{0,4},{4,0},{8,12},{12,8},{16,20},{20,16},{24,28},{28,24},{1,5},{5... | collective-permute-start | bytes 786440 | tf_op jit(solution)/shard_map/ppermute | solution.py:385
  25.1 12.5 %collective-permute-start.7 = (s16[1616,128]{1,0:T(8,128)(2,1)S(1)}, s16[1616,128]{1,0:T(8,128)(2,1)S(1)}, u32[]{:S(2)}, u32[]{:S(2)}) collective-permute-start(s16[1616,128]{1,0:T(8,128)(2,1)S(1)} %get-tuple-element.26.rest_1_), channel_id=1, source_target_pairs={{0,8},{4,12},{8,0},{12,4},{16,24},{20,28},{24,16},{28,20},{1,9},{5... | collective-permute-start | bytes 1241096 | tf_op jit(solution)/shard_map/ppermute | solution.py:436
  29.3 17.2 %collective-permute-start.6 = (s16[1616,128]{1,0:T(8,128)(2,1)S(1)}, s16[1616,128]{1,0:T(8,128)(2,1)S(1)}, u32[]{:S(2)}, u32[]{:S(2)}) collective-permute-start(s16[1616,128]{1,0:T(8,128)(2,1)S(1)} %get-tuple-element.30.rest_1_), channel_id=1, source_target_pairs={{0,8},{4,12},{8,0},{12,4},{16,24},{20,28},{24,16},{28,20},{1,9},{5... | collective-permute-start | bytes 1241096 | tf_op jit(solution)/shard_map/ppermute | solution.py:436
  29.4 17.1 %collective-permute-start.5 = (bf16[128,2048]{1,0:T(8,128)(2,1)S(1)}, bf16[128,2048]{1,0:T(8,128)(2,1)S(1)}, u32[]{:S(2)}, u32[]{:S(2)}) collective-permute-start(bf16[128,2048]{1,0:T(8,128)(2,1)S(1)} %get-tuple-element.29), channel_id=1, source_target_pairs={{0,4},{4,0},{8,12},{12,8},{16,20},{20,16},{24,28},{28,24},{1,5},{5... | collective-permute-start | bytes 1572872 | tf_op jit(solution)/shard_map/ppermute | solution.py:385
  39.8 14.8 %collective-permute-start.9 = (s16[1616,128]{1,0:T(8,128)(2,1)S(1)}, s16[1616,128]{1,0:T(8,128)(2,1)S(1)}, u32[]{:S(2)}, u32[]{:S(2)}) collective-permute-start(s16[1616,128]{1,0:T(8,128)(2,1)S(1)} %get-tuple-element.32.rest_1_), channel_id=1, source_target_pairs={{0,8},{4,12},{8,0},{12,4},{16,24},{20,28},{24,16},{28,20},{1,9},{5... | collective-permute-start | bytes 1241096 | tf_op jit(solution)/shard_map/ppermute | solution.py:436
  41.9 12.7 %collective-permute-start.10 = (bf16[128,1024]{1,0:T(8,128)(2,1)S(1)}, bf16[128,1024]{1,0:T(8,128)(2,1)S(1)}, u32[]{:S(2)}, u32[]{:S(2)}) collective-permute-start(bf16[128,1024]{1,0:T(8,128)(2,1)S(1)} %get-tuple-element.48), channel_id=1, source_target_pairs={{0,4},{4,0},{8,12},{12,8},{16,20},{20,16},{24,28},{28,24},{1,5},{5... | collective-permute-start | bytes 786440 | tf_op jit(solution)/shard_map/ppermute | solution.py:442
  42.5 20.6 %collective-permute-start.14 = (bf16[128,2048]{1,0:T(8,128)(2,1)S(1)}, bf16[128,2048]{1,0:T(8,128)(2,1)S(1)}, u32[]{:S(2)}, u32[]{:S(2)}) collective-permute-start(bf16[128,2048]{1,0:T(8,128)(2,1)S(1)} %get-tuple-element.36), channel_id=1, source_target_pairs={{0,4},{4,0},{8,12},{12,8},{16,20},{20,16},{24,28},{28,24},{1,5},{5... | collective-permute-start | bytes 1572872 | tf_op jit(solution)/shard_map/ppermute | solution.py:385
  48.5 15.8 %collective-permute-start.15 = (s16[1616,128]{1,0:T(8,128)(2,1)S(1)}, s16[1616,128]{1,0:T(8,128)(2,1)S(1)}, u32[]{:S(2)}, u32[]{:S(2)}) collective-permute-start(s16[1616,128]{1,0:T(8,128)(2,1)S(1)} %sum_step_04.1.rest_2_), channel_id=1, source_target_pairs={{8,16},{12,20},{16,8},{20,12},{9,17},{13,21},{17,9},{21,13},{10,18... | collective-permute-start | bytes 1241096 | tf_op jit(solution)/shard_map/ppermute | solution.py:436
  49.2 15.1 %collective-permute-start.13 = (s16[1616,128]{1,0:T(8,128)(2,1)S(1)}, s16[1616,128]{1,0:T(8,128)(2,1)S(1)}, u32[]{:S(2)}, u32[]{:S(2)}) collective-permute-start(s16[1616,128]{1,0:T(8,128)(2,1)S(1)} %sum_step_04.1.rest_2_), channel_id=1, source_target_pairs={{0,8},{4,12},{24,16},{28,20},{1,9},{5,13},{25,17},{29,21},{2,10},{... | collective-permute-start | bytes 1241096 | tf_op jit(solution)/shard_map/ppermute | solution.py:436
  56.8 13.5 %collective-permute-start.16 = (s16[1616,128]{1,0:T(8,128)(2,1)S(1)}, s16[1616,128]{1,0:T(8,128)(2,1)S(1)}, u32[]{:S(2)}, u32[]{:S(2)}) collective-permute-start(s16[1616,128]{1,0:T(8,128)(2,1)S(1)} %get-tuple-element.35.rest_1_), channel_id=1, source_target_pairs={{8,16},{12,20},{16,8},{20,12},{9,17},{13,21},{17,9},{21,13},{10,18... | collective-permute-start | bytes 1241096 | tf_op jit(solution)/shard_map/ppermute | solution.py:436
  57.5 15.5 %collective-permute-start.12 = (s16[1616,128]{1,0:T(8,128)(2,1)S(1)}, s16[1616,128]{1,0:T(8,128)(2,1)S(1)}, u32[]{:S(2)}, u32[]{:S(2)}) collective-permute-start(s16[1616,128]{1,0:T(8,128)(2,1)S(1)} %get-tuple-element.35.rest_1_), channel_id=1, source_target_pairs={{0,8},{4,12},{24,16},{28,20},{1,9},{5,13},{25,17},{29,21},{2,10},{... | collective-permute-start | bytes 1241096 | tf_op jit(solution)/shard_map/ppermute | solution.py:436
  63.1 19.9 %collective-permute-start.11 = (bf16[128,2048]{1,0:T(8,128)(2,1)S(1)}, bf16[128,2048]{1,0:T(8,128)(2,1)S(1)}, u32[]{:S(2)}, u32[]{:S(2)}) collective-permute-start(bf16[128,2048]{1,0:T(8,128)(2,1)S(1)} %get-tuple-element.34), channel_id=1, source_target_pairs={{0,4},{4,0},{8,12},{12,8},{16,20},{20,16},{24,28},{28,24},{1,5},{5... | collective-permute-start | bytes 1572872 | tf_op jit(solution)/shard_map/ppermute | solution.py:385
  66.3 15.6 %collective-permute-start.18 = (s16[1616,128]{1,0:T(8,128)(2,1)S(1)}, s16[1616,128]{1,0:T(8,128)(2,1)S(1)}, u32[]{:S(2)}, u32[]{:S(2)}) collective-permute-start(s16[1616,128]{1,0:T(8,128)(2,1)S(1)} %sum_step_06.1.rest_3_), channel_id=1, source_target_pairs={{0,8},{4,12},{24,16},{28,20},{1,9},{5,13},{25,17},{29,21},{2,10},{... | collective-permute-start | bytes 1241096 | tf_op jit(solution)/shard_map/ppermute | solution.py:436
  69.6 13.4 %collective-permute-start.17 = (s16[1616,128]{1,0:T(8,128)(2,1)S(1)}, s16[1616,128]{1,0:T(8,128)(2,1)S(1)}, u32[]{:S(2)}, u32[]{:S(2)}) collective-permute-start(s16[1616,128]{1,0:T(8,128)(2,1)S(1)} %sum_step_06.1.rest_3_), channel_id=1, source_target_pairs={{8,16},{12,20},{16,8},{20,12},{9,17},{13,21},{17,9},{21,13},{10,18... | collective-permute-start | bytes 1241096 | tf_op jit(solution)/shard_map/ppermute | solution.py:436
  75.4 15.4 %collective-permute-start.20 = (s16[1616,128]{1,0:T(8,128)(2,1)S(1)}, s16[1616,128]{1,0:T(8,128)(2,1)S(1)}, u32[]{:S(2)}, u32[]{:S(2)}) collective-permute-start(s16[1616,128]{1,0:T(8,128)(2,1)S(1)} %get-tuple-element.37.rest_2_), channel_id=1, source_target_pairs={{0,8},{4,12},{24,16},{28,20},{1,9},{5,13},{25,17},{29,21},{2,10},{... | collective-permute-start | bytes 1241096 | tf_op jit(solution)/shard_map/ppermute | solution.py:436
  79.8 11.0 %collective-permute-start.19 = (s16[1616,128]{1,0:T(8,128)(2,1)S(1)}, s16[1616,128]{1,0:T(8,128)(2,1)S(1)}, u32[]{:S(2)}, u32[]{:S(2)}) collective-permute-start(s16[1616,128]{1,0:T(8,128)(2,1)S(1)} %get-tuple-element.37.rest_2_), channel_id=1, source_target_pairs={{8,16},{12,20},{16,8},{20,12},{9,17},{13,21},{17,9},{21,13},{10,18... | collective-permute-start | bytes 1241096 | tf_op jit(solution)/shard_map/ppermute | solution.py:436
  81.9 14.9 %collective-permute-start.22 = (bf16[128,2048]{1,0:T(8,128)(2,1)S(1)}, bf16[128,2048]{1,0:T(8,128)(2,1)S(1)}, u32[]{:S(2)}, u32[]{:S(2)}) collective-permute-start(bf16[128,2048]{1,0:T(8,128)(2,1)S(1)} %get-tuple-element.40), channel_id=1, source_target_pairs={{0,4},{4,0},{8,12},{12,8},{16,20},{20,16},{24,28},{28,24},{1,5},{5... | collective-permute-start | bytes 1572872 | tf_op jit(solution)/shard_map/ppermute | solution.py:385
  85.3 16.6 %collective-permute-start.23 = (s16[1616,128]{1,0:T(8,128)(2,1)S(1)}, s16[1616,128]{1,0:T(8,128)(2,1)S(1)}, u32[]{:S(2)}, u32[]{:S(2)}) collective-permute-start(s16[1616,128]{1,0:T(8,128)(2,1)S(1)} %get-tuple-element.38.rest_2_), channel_id=1, source_target_pairs={{0,8},{4,12},{8,24},{12,28},{16,0},{20,4},{24,16},{28,20},{1,9},{5... | collective-permute-start | bytes 1241096 | tf_op jit(solution)/shard_map/ppermute | solution.py:436
  87.8 17.4 %collective-permute-start.25 = (bf16[128,2048]{1,0:T(8,128)(2,1)S(1)}, bf16[128,2048]{1,0:T(8,128)(2,1)S(1)}, u32[]{:S(2)}, u32[]{:S(2)}) collective-permute-start(bf16[128,2048]{1,0:T(8,128)(2,1)S(1)} %get-tuple-element.42), channel_id=1, source_target_pairs={{0,4},{4,0},{8,12},{12,8},{16,20},{20,16},{24,28},{28,24},{1,5},{5... | collective-permute-start | bytes 1572872 | tf_op jit(solution)/shard_map/ppermute | solution.py:385
  93.0 17.7 %collective-permute-start.24 = (s16[1616,128]{1,0:T(8,128)(2,1)S(1)}, s16[1616,128]{1,0:T(8,128)(2,1)S(1)}, u32[]{:S(2)}, u32[]{:S(2)}) collective-permute-start(s16[1616,128]{1,0:T(8,128)(2,1)S(1)} %get-tuple-element.41.rest_1_), channel_id=1, source_target_pairs={{0,8},{4,12},{8,24},{12,28},{16,0},{20,4},{24,16},{28,20},{1,9},{5... | collective-permute-start | bytes 1241096 | tf_op jit(solution)/shard_map/ppermute | solution.py:436
  95.8 22.4 %collective-permute-start.21 = (bf16[128,2048]{1,0:T(8,128)(2,1)S(1)}, bf16[128,2048]{1,0:T(8,128)(2,1)S(1)}, u32[]{:S(2)}, u32[]{:S(2)}) collective-permute-start(bf16[128,2048]{1,0:T(8,128)(2,1)S(1)} %get-tuple-element.39), channel_id=1, source_target_pairs={{0,4},{4,0},{8,12},{12,8},{16,20},{20,16},{24,28},{28,24},{1,5},{5... | collective-permute-start | bytes 1572872 | tf_op jit(solution)/shard_map/ppermute | solution.py:385
  103.8 14.4 %collective-permute-start.27 = (s16[1616,128]{1,0:T(8,128)(2,1)S(1)}, s16[1616,128]{1,0:T(8,128)(2,1)S(1)}, u32[]{:S(2)}, u32[]{:S(2)}) collective-permute-start(s16[1616,128]{1,0:T(8,128)(2,1)S(1)} %sum_step_10.1.rest_1_), channel_id=1, source_target_pairs={{0,8},{4,12},{8,24},{12,28},{16,0},{20,4},{24,16},{28,20},{1,9},{5... | collective-permute-start | bytes 1241096 | tf_op jit(solution)/shard_map/ppermute | solution.py:436
  112.7 9.9 %collective-permute-start.26 = (s16[1616,128]{1,0:T(8,128)(2,1)S(1)}, s16[1616,128]{1,0:T(8,128)(2,1)S(1)}, u32[]{:S(2)}, u32[]{:S(2)}) collective-permute-start(s16[1616,128]{1,0:T(8,128)(2,1)S(1)} %sum_step_11.1), channel_id=1, source_target_pairs={{0,8},{4,12},{8,24},{12,28},{16,0},{20,4},{24,16},{28,20},{1,9},{5... | collective-permute-start | bytes 1241096 | tf_op jit(solution)/shard_map/ppermute | solution.py:436
